TPU v7x, 32 devices: a whole 2x2x4 slice. The times are simulated.
32 devices in a mesh: scan: 2 (over x), coil: 4 (over z), pencil: 4 (over y, core).
Axes of the slice: x: 2, y: 2, z: 4, core: 2. Of those that a mesh axis runs over, the one named last changes fastest.
Arguments:
- kspace: bfloat16 [4, 16, 2, 4096], P('coil', 'scan', None, 'pencil'), parts along dimension 1, may hold values from -6 to 6
- sens_maps: bfloat16 [4, 16, 2, 512, 512], P('coil', 'scan', None, 'pencil'), parts along dimension 1, may hold values from -5 to 5
- weights: bfloat16 [128, 128, 128], P('pencil'), may hold values from -0.25 to 0.25
- tile_slot: int32 [128], P('pencil'), may hold values from 0 to 31, as said below
- tile_block: int32 [128], P('pencil'), may hold values from 0 to 7
- send_list: int32 [4, 4, 8], P('pencil'), may hold values from 0 to 511
Outputs:
- solution: float32 [16, 2, 512, 512], P('scan', None, 'pencil'), parts along dimension 0
- residual: float32 [16, 2, 512, 512], P('scan', None, 'pencil'), parts along dimension 0
There are 2 independent parts, one for each index of `scan`. A program takes and returns all parts, laid end to end along the dimension named above; an argument that names none is the same for every part. Nothing has to cross between parts.
Inputs may be any that keep to these rules, and one draw needn't show every extreme that they name: For the tiles of one device, tile_slot // 8 is the device that owns the tile's brick and tile_slot % 8 the place of that brick in the owner's list for this device; every place up to the largest used one for an owner has a tile, and every device uses all 8 places of some owners.
All inputs are finite; a program needn't handle non-finite values.
Results may differ from a plain program's by a relative error of at most 0.0075.
Values may be sent and summed in bfloat16 or wider, within the bound.
No kernel may reach another device: no remote copies, remote signals or barrier semaphores. Data moves between devices by JAX's collectives and lax.ppermute only.
A program may use at most 192 MiB of HBM per device.

v0:
```python
import functools
import math

import jax
import jax.numpy as jnp
from jax import lax
from jax.experimental import pallas as pl
from jax.experimental.pallas import tpu as pltpu
from jax.sharding import PartitionSpec as P


damping = 0.5
f32, bf16 = jnp.float32, jnp.bfloat16
vmem_limit = 56 * 1024 * 1024


def wave(left, right, length):
    phases = left[:, None] * right[None, :] % length
    angles = phases.astype(f32) * (2.0 * math.pi / length)
    return jnp.cos(angles) / math.sqrt(length), jnp.sin(angles) / math.sqrt(length)


def quarter_turns(left, right, count):
    turns = left[:, None] * right[None, :] % count
    if count == 4:
        cosine = jnp.where(turns == 0, 1.0, 0.0) - jnp.where(turns == 2, 1.0, 0.0)
        sine = jnp.where(turns == 1, 1.0, 0.0) - jnp.where(turns == 3, 1.0, 0.0)
        return cosine.astype(f32), sine.astype(f32)
    angles = turns.astype(f32) * (2.0 * math.pi / count)
    return jnp.cos(angles), jnp.sin(angles)


def split(value):
    high = value.astype(bf16)
    return high, (value - high.astype(f32)).astype(bf16)


def split_table(table):
    high = lax.reduce_precision(table, 8, 7)
    return high.astype(bf16), (table - high).astype(bf16)


def nt(left, right):
    return lax.dot_general(left, right, (((1,), (1,)), ((), ())), preferred_element_type=f32)


def nn(left, right):
    return jnp.dot(left, right, preferred_element_type=f32)


def three(product, left, right):
    return (
        product(left[0], right[0]) + product(left[0], right[1]) + product(left[1], right[0])
    )


def tree_sum(values):
    while len(values) > 1:
        values = [left + right for left, right in zip(values[::2], values[1::2])]
    return values[0]


def forward_image(step, real, imag, sens_ref, ey, mx, turn_ref, grid_ref):
    tiles = turn_ref.shape[1]
    rows = turn_ref.shape[2]
    channels = grid_ref.shape[0] // tiles
    sens_real = sens_ref[0].astype(f32)
    sens_imag = sens_ref[1].astype(f32)
    coil = jnp.concatenate(
        [sens_real * real - sens_imag * imag, sens_real * imag + sens_imag * real], 0
    )
    both = three(nt, (ey[0][...], ey[1][...]), split(coil))
    half_real = both[:tiles, :rows] + both[tiles:, rows:]
    half_imag = both[:tiles, rows:] - both[tiles:, :rows]
    turned = jnp.concatenate(
        [
            half_real * turn_ref[0] + half_imag * turn_ref[1],
            half_imag * turn_ref[0] - half_real * turn_ref[1],
        ],
        1,
    )
    grid = three(nn, split(turned), (mx[0][...], mx[1][...]))
    size = grid.shape[1] // 2
    grid_ref[pl.ds(2 * step, tiles, stride=channels), :] = grid[:, :size]
    grid_ref[pl.ds(2 * step + 1, tiles, stride=channels), :] = grid[:, size:]


def sample_tiles(block_ref, weights_ref, grid_ref, sums_ref, out_ref):
    tiles = weights_ref.shape[0]
    channels = grid_ref.shape[0] // tiles
    sums_ref[...] = jnp.zeros_like(sums_ref)

    def one(tile, carry):
        start = pl.multiple_of(tile * channels, channels)
        high, low = split(grid_ref[pl.ds(start, channels), :])
        product = nn(jnp.concatenate([high, low], 0), weights_ref[tile])
        sums_ref[block_ref[tile]] += product[:channels] + product[channels:]
        return carry

    lax.fori_loop(0, tiles, one, 0, unroll=8)
    out_ref[...] = sums_ref[...].astype(bf16)


def spread_tiles(block_ref, weights_ref, parts_ref, grid_ref):
    tiles = weights_ref.shape[0]
    channels = grid_ref.shape[0] // tiles

    def one(tile, carry):
        start = pl.multiple_of(tile * channels, channels)
        product = nt(parts_ref[block_ref[tile]], weights_ref[tile])
        if product.shape[0] > channels:
            product = product[:channels] + product[channels:]
        grid_ref[pl.ds(start, channels), :] = product
        return carry

    lax.fori_loop(0, tiles, one, 0, unroll=8)


def adjoint_image(step, tiles, ey_back, mx, turn_ref, grid_ref):
    channels = grid_ref.shape[0] // tiles
    rows = turn_ref.shape[1]
    grid = jnp.concatenate(
        [
            grid_ref[pl.ds(2 * step, tiles, stride=channels), :],
            grid_ref[pl.ds(2 * step + 1, tiles, stride=channels), :],
        ],
        1,
    )
    back = three(nt, (mx[0][...], mx[1][...]), split(grid))
    turned = jnp.concatenate(
        [
            back[:rows] * turn_ref[0] - back[rows:] * turn_ref[1],
            back[rows:] * turn_ref[0] + back[:rows] * turn_ref[1],
        ],
        1,
    )
    image = three(nn, split(turned), (ey_back[0][...], ey_back[1][...]))
    columns = image.shape[1] // 2
    return image[:, :columns], image[:, columns:]


def add_dots(dots_ref, products):
    rows = lax.broadcasted_iota(jnp.int32, dots_ref.shape, 0)
    total = dots_ref[...]
    for place, (left, right) in enumerate(products):
        total += jnp.where(rows == place, jnp.sum(left * right), 0.0)
    dots_ref[...] = total


def measured_kernel(block, samples, weights, mx0, mx1, eb0, eb1, turn, images, grid):
    step = pl.program_id(0)

    @pl.when(step == 0)
    def _():
        spread_tiles(block, weights, samples, grid)

    real, imag = adjoint_image(step, weights.shape[0], (eb0, eb1), (mx0, mx1), turn, grid)
    images[0, 0] = real
    images[0, 1] = imag


def start_kernel(
    block,
    images,
    sens,
    weights,
    ey0,
    ey1,
    mx0,
    mx1,
    turn,
    right_side,
    samples,
    rounded,
    dots,
    grid,
    sums,
):
    plane, coil = pl.program_id(0), pl.program_id(1)
    coils = pl.num_programs(1)

    @pl.when(coil == 0)
    def _():
        total_real = jnp.zeros(right_side.shape[2:], f32)
        total_imag = jnp.zeros(right_side.shape[2:], f32)
        for other in range(images.shape[0]):
            sens_real = sens[other, 0, 0].astype(f32)
            sens_imag = sens[other, 0, 1].astype(f32)
            total_real += sens_real * images[other, 0, 0] + sens_imag * images[other, 0, 1]
            total_imag += sens_real * images[other, 0, 1] - sens_imag * images[other, 0, 0]
        right_side[0, 0] = total_real
        right_side[0, 1] = total_imag
        rounded[0, 0] = total_real.astype(bf16)
        rounded[0, 1] = total_imag.astype(bf16)

        @pl.when(plane == 0)
        def _():
            dots[...] = jnp.zeros_like(dots)

        add_dots(dots, [(right_side[0], right_side[0])])

    forward_image(
        coil * pl.num_programs(0) + plane,
        right_side[0, 0],
        right_side[0, 1],
        sens.at[coil, 0],
        (ey0, ey1),
        (mx0, mx1),
        turn,
        grid,
    )

    @pl.when((plane == pl.num_programs(0) - 1) & (coil == coils - 1))
    def _():
        sample_tiles(block, weights, grid, sums, samples)


def forward_kernel(
    block,
    totals,
    right_side,
    applied,
    sens,
    weights,
    ey0,
    ey1,
    mx0,
    mx1,
    turn,
    residual,
    samples,
    rounded,
    grid,
    sums,
):
    plane, coil = pl.program_id(0), pl.program_id(1)

    @pl.when(coil == 0)
    def _():
        scale = first_step_of(totals).reshape(1, 1, 1)
        value = right_side[0] - scale * applied[0]
        residual[0] = value
        rounded[0] = value.astype(bf16)

    forward_image(
        coil * pl.num_programs(0) + plane,
        residual[0, 0],
        residual[0, 1],
        sens.at[0, 0],
        (ey0, ey1),
        (mx0, mx1),
        turn,
        grid,
    )

    @pl.when((plane == pl.num_programs(0) - 1) & (coil == pl.num_programs(1) - 1))
    def _():
        sample_tiles(block, weights, grid, sums, samples)


def first_step_of(totals):
    return totals[0:1, 0:1] / (totals[1:2, 0:1] + damping * totals[0:1, 0:1])


def combine(coil, image, sens, out):
    sens_real = sens[0, 0, 0].astype(f32)
    sens_imag = sens[0, 0, 1].astype(f32)
    real = sens_real * image[0] + sens_imag * image[1]
    imag = sens_real * image[1] - sens_imag * image[0]

    @pl.when(coil == 0)
    def _():
        out[0, 0] = real
        out[0, 1] = imag

    @pl.when(coil > 0)
    def _():
        out[0, 0] += real
        out[0, 1] += imag


def first_kernel(peers, block, *refs):
    samples = refs[:peers]
    right_side, sens, weights, mx0, mx1, eb0, eb1, turn, applied, grid, parts = refs[peers:]
    plane, coil = pl.program_id(0), pl.program_id(1)

    @pl.when((plane == 0) & (coil == 0))
    def _():
        summed = tree_sum([part[...].astype(f32) for part in samples])
        channels = summed.shape[1]
        high, low = split(summed)
        parts[:, :channels] = high
        parts[:, channels:] = low
        spread_tiles(block, weights, parts, grid)

    image = adjoint_image(
        coil * pl.num_programs(0) + plane, weights.shape[0], (eb0, eb1), (mx0, mx1), turn, grid
    )
    combine(coil, image, sens, applied)

    @pl.when(coil == pl.num_programs(1) - 1)
    def _():
        applied[...] += damping * right_side[...]


def second_kernel(peers, block, *refs):
    samples = refs[:peers]
    (
        totals,
        right_side,
        first_applied,
        residual,
        sens,
        weights,
        mx0,
        mx1,
        eb0,
        eb1,
        turn,
        rounded,
        dots,
        grid,
        parts,
        applied,
    ) = refs[peers:]
    plane, coil = pl.program_id(0), pl.program_id(1)

    @pl.when((plane == 0) & (coil == 0))
    def _():
        summed = tree_sum([part[...].astype(f32) for part in samples])
        channels = summed.shape[1]
        high, low = split(summed)
        parts[:, :channels] = high
        parts[:, channels:] = low
        dots[...] = jnp.zeros_like(dots)
        spread_tiles(block, weights, parts, grid)

    image = adjoint_image(
        coil * pl.num_programs(0) + plane, weights.shape[0], (eb0, eb1), (mx0, mx1), turn, grid
    )
    combine(coil, image, sens, applied)

    @pl.when(coil == pl.num_programs(1) - 1)
    def _():
        vector = residual[0]
        again = applied[0] + damping * vector
        rounded[0] = (vector - first_step_of(totals).reshape(1, 1, 1) * again).astype(bf16)
        add_dots(
            dots,
            [
                (vector, vector),
                (vector, again),
                (vector, first_applied[0]),
                (right_side[0], again),
            ],
        )


def whole_block(array):
    rank = len(array.shape)
    return pl.BlockSpec(array.shape, lambda *_: (0,) * rank)


def on_device(kspace, sens_maps, weights, tile_slot, tile_block, send_list):
    coil_count = lax.axis_size("coil")
    peers = lax.axis_size("pencil")
    planes = sens_maps.shape[1]
    own_planes = planes // coil_count
    rows = sens_maps.shape[3]
    columns = sens_maps.shape[4]
    rows_total = rows * peers
    size = weights.shape[1]
    tile_count = tile_slot.shape[0]
    tiles = tile_count * peers
    blocks_dev = kspace.shape[3] // size
    blocks = blocks_dev * peers
    cap = send_list.shape[2]
    runs = rows_total // size
    brick_dev = columns // peers * runs
    images_count = coil_count * own_planes
    channels = 2 * images_count

    sens = lax.all_to_all(sens_maps[0], "coil", split_axis=0, concat_axis=0, tiled=True)
    sens = sens.reshape(coil_count, own_planes, 2, rows, columns)

    packed = jnp.concatenate([tile_slot, tile_block, send_list.reshape(-1)])
    places = lax.all_gather(packed, "pencil")
    slots = places[:, :tile_count]
    block_of = (
        places[:, tile_count : 2 * tile_count]
        + blocks_dev * jnp.arange(peers, dtype=jnp.int32)[:, None]
    ).reshape(-1)
    lists = places[:, 2 * tile_count :].reshape(peers, peers, cap)
    holder = jnp.arange(peers, dtype=jnp.int32)[:, None]
    brick = (slots // cap * brick_dev + lists[slots // cap, holder, slots % cap]).reshape(-1)
    line = brick // runs
    run = brick % runs

    measured = lax.all_to_all(kspace[0], "coil", split_axis=0, concat_axis=0, tiled=True)
    measured = lax.all_gather(
        measured.reshape(channels, blocks_dev, size), "pencil", axis=1, tiled=True
    )
    measured = jnp.swapaxes(measured, 0, 1)
    all_weights = lax.all_gather(weights, "pencil", axis=0, tiled=True)

    cos_y, sin_y = wave(
        line - columns // 2, jnp.arange(columns, dtype=jnp.int32) - columns // 2, columns
    )
    row_ids = jnp.arange(rows, dtype=jnp.int32) + lax.axis_index("pencil") * rows - rows_total // 2
    cos_x, sin_x = wave(
        row_ids, jnp.arange(size, dtype=jnp.int32) - rows_total // 2, rows_total
    )
    turn = jnp.stack(quarter_turns(run, row_ids, runs))
    turn_back = jnp.stack(quarter_turns(row_ids, run, runs))

    def exchanged(partial, axis="pencil"):
        count = lax.axis_size(axis)
        return [partial] + [
            lax.ppermute(partial, axis, [(i, i ^ k) for i in range(count)])
            for k in range(1, count)
        ]

    def summed_over(axes, dots):
        for axis in axes:
            dots = tree_sum(exchanged(dots, axis))
        return dots

    def added(samples):
        return tree_sum([part.astype(f32) for part in samples])

    def gathered(own):
        return lax.all_gather(own, "coil", axis=0, tiled=True)

    picture_shape = (own_planes, 2, rows, columns)

    if rows % 128 == 0 and columns % 128 == 0 and size % 128 == 0 and channels % 16 == 0:
        ey = split_table(jnp.concatenate([cos_y, sin_y], 0))
        eb = split_table(
            jnp.concatenate(
                [jnp.concatenate([cos_y, sin_y], 1), jnp.concatenate([-sin_y, cos_y], 1)], 0
            )
        )
        mx = split_table(
            jnp.concatenate(
                [jnp.concatenate([cos_x, -sin_x], 1), jnp.concatenate([sin_x, cos_x], 1)], 0
            )
        )
        places_spec = pl.BlockSpec(memory_space=pltpu.SMEM)
        plane_spec = pl.BlockSpec((1, 2, rows, columns), lambda p, c: (p, 0, 0, 0))
        sens_spec = pl.BlockSpec((1, 1, 2, rows, columns), lambda p, c: (c, p, 0, 0, 0))
        grid_scratch = pltpu.VMEM((tiles * channels, size), f32)
        sums_shape = (blocks, channels, size)
        params = pltpu.CompilerParams(vmem_limit_bytes=vmem_limit)

        def call(kernel, grid, inputs, specs, outs, out_specs, scratch, flops):
            read = sum(math.prod(i.shape) * i.dtype.itemsize for i in inputs)
            return pl.pallas_call(
                kernel,
                grid=grid,
                in_specs=specs,
                out_specs=out_specs,
                out_shape=outs,
                scratch_shapes=scratch,
                compiler_params=params,
                cost_estimate=pl.CostEstimate(
                    flops=flops, bytes_accessed=read, transcendentals=0
                ),
            )(*inputs)

        def shaped(shape, dtype=f32):
            return jax.ShapeDtypeStruct(shape, dtype)

        image_flops = 3 * images_count * 8 * tiles * rows * (columns + size)
        tile_flops = 4 * tiles * channels * size * size
        grid = (own_planes, coil_count)

        def measured_images():
            inputs = [block_of, measured, all_weights, *mx, *eb, turn_back]
            return call(
                measured_kernel,
                (images_count,),
                inputs,
                [places_spec] + [whole_block(i) for i in inputs[1:]],
                shaped((images_count, 2, rows, columns)),
                pl.BlockSpec((1, 2, rows, columns), lambda i: (i, 0, 0, 0)),
                [grid_scratch],
                image_flops + tile_flops,
            )

        def start(images):
            images = images.reshape(coil_count, own_planes, 2, rows, columns)
            inputs = [block_of, images, sens, all_weights, *ey, *mx, turn]
            all_coils = pl.BlockSpec(
                (coil_count, 1, 2, rows, columns), lambda p, c: (0, p, 0, 0, 0)
            )
            return call(
                start_kernel,
                grid,
                inputs,
                [places_spec, all_coils, all_coils] + [whole_block(i) for i in inputs[3:]],
                [
                    shaped(picture_shape),
                    shaped(sums_shape, bf16),
                    shaped(picture_shape, bf16),
                    shaped((8, 128)),
                ],
                [
                    plane_spec,
                    whole_block(shaped(sums_shape)),
                    plane_spec,
                    whole_block(shaped((8, 128))),
                ],
                [grid_scratch, pltpu.VMEM(sums_shape, f32)],
                image_flops + tile_flops,
            )

        def forward(totals, right_side, applied):
            tail = [all_weights, *ey, *mx, turn]
            inputs = [block_of, totals, right_side, applied, sens, *tail]
            return call(
                forward_kernel,
                grid,
                inputs,
                [places_spec, whole_block(totals), plane_spec, plane_spec, sens_spec]
                + [whole_block(i) for i in tail],
                [shaped(picture_shape), shaped(sums_shape, bf16), shaped(picture_shape, bf16)],
                [plane_spec, whole_block(shaped(sums_shape)), plane_spec],
                [grid_scratch, pltpu.VMEM(sums_shape, f32)],
                image_flops + tile_flops,
            )

        parts_scratch = pltpu.VMEM((blocks, 2 * channels, size), bf16)

        def first(samples, right_side):
            tail = [all_weights, *mx, *eb, turn_back]
            inputs = [block_of, *samples, right_side, sens, *tail]
            return call(
                functools.partial(first_kernel, peers),
                grid,
                inputs,
                [places_spec]
                + [whole_block(i) for i in samples]
                + [plane_spec, sens_spec]
                + [whole_block(i) for i in tail],
                shaped(picture_shape),
                plane_spec,
                [grid_scratch, parts_scratch],
                image_flops + tile_flops,
            )

        def second(samples, totals, right_side, applied, residual):
            tail = [all_weights, *mx, *eb, turn_back]
            inputs = [
                block_of,
                *samples,
                totals,
                right_side,
                applied,
                residual,
                sens,
                *tail,
            ]
            return call(
                functools.partial(second_kernel, peers),
                grid,
                inputs,
                [places_spec]
                + [whole_block(i) for i in samples]
                + [whole_block(totals), plane_spec, plane_spec, plane_spec, sens_spec]
                + [whole_block(i) for i in tail],
                [shaped(picture_shape, bf16), shaped((8, 128))],
                [plane_spec, whole_block(shaped((8, 128)))],
                [grid_scratch, parts_scratch, pltpu.VMEM((1, 2, rows, columns), f32)],
                image_flops + tile_flops,
            )

    else:
        ein = functools.partial(jnp.einsum, precision=lax.Precision.HIGH)
        map_real = sens[:, :, 0].astype(f32)
        map_imag = sens[:, :, 1].astype(f32)
        shape = (coil_count, own_planes)
        block_map = (block_of[:, None] == jnp.arange(blocks, dtype=jnp.int32)).astype(f32)
        tc, ts = turn[0][:, None, None], turn[1][:, None, None]
        wide_weights = all_weights.astype(f32)

        def sampled(picture):
            coil_real = map_real * picture[None, :, 0] - map_imag * picture[None, :, 1]
            coil_imag = map_real * picture[None, :, 1] + map_imag * picture[None, :, 0]
            half_real = ein("ty,cpxy->tcpx", cos_y, coil_real) + ein(
                "ty,cpxy->tcpx", sin_y, coil_imag
            )
            half_imag = ein("ty,cpxy->tcpx", cos_y, coil_imag) - ein(
                "ty,cpxy->tcpx", sin_y, coil_real
            )
            real = half_real * tc + half_imag * ts
            imag = half_imag * tc - half_real * ts
            grid = jnp.stack(
                [
                    ein("tcpx,xi->tcpi", real, cos_x) + ein("tcpx,xi->tcpi", imag, sin_x),
                    ein("tcpx,xi->tcpi", imag, cos_x) - ein("tcpx,xi->tcpi", real, sin_x),
                ],
                3,
            ).reshape(tiles, channels, size)
            product = ein("tgi,tis->tgs", grid, wide_weights)
            return ein("tb,tgs->bgs", block_map, product).astype(bf16)

        def images_of(samples):
            spread = ein("tgs,tis->tgi", jnp.take(samples, block_of, axis=0), wide_weights)
            spread = spread.reshape(tiles, *shape, 2, size)
            back_real = ein("tcpi,xi->tcpx", spread[:, :, :, 0], cos_x) - ein(
                "tcpi,xi->tcpx", spread[:, :, :, 1], sin_x
            )
            back_imag = ein("tcpi,xi->tcpx", spread[:, :, :, 1], cos_x) + ein(
                "tcpi,xi->tcpx", spread[:, :, :, 0], sin_x
            )
            real = back_real * tc - back_imag * ts
            imag = back_imag * tc + back_real * ts
            return (
                ein("tcpx,ty->cpxy", real, cos_y) - ein("tcpx,ty->cpxy", imag, sin_y),
                ein("tcpx,ty->cpxy", imag, cos_y) + ein("tcpx,ty->cpxy", real, sin_y),
            )

        def combined(images):
            real, imag = images
            return jnp.stack(
                [
                    jnp.sum(map_real * real + map_imag * imag, 0),
                    jnp.sum(map_real * imag - map_imag * real, 0),
                ],
                1,
            )

        def stacked_dots(products):
            values = [jnp.sum(left * right) for left, right in products]
            values += [jnp.zeros((), f32)] * (8 - len(values))
            return jnp.broadcast_to(jnp.stack(values)[:, None], (8, 128))

        def measured_images():
            return images_of(measured.astype(f32))

        def start(images):
            right_side = combined(images)
            dots = stacked_dots([(right_side, right_side)])
            return right_side, sampled(right_side), right_side.astype(bf16), dots

        def forward(totals, right_side, applied):
            scale = totals[0, 0] / (totals[1, 0] + damping * totals[0, 0])
            residual = right_side - scale * applied
            return residual, sampled(residual), residual.astype(bf16)

        def first(samples, right_side):
            return combined(images_of(added(samples))) + damping * right_side

        def second(samples, totals, right_side, applied, residual):
            scale = totals[0, 0] / (totals[1, 0] + damping * totals[0, 0])
            again = combined(images_of(added(samples))) + damping * residual
            dots = stacked_dots(
                [
                    (residual, residual),
                    (residual, again),
                    (residual, applied),
                    (right_side, again),
                ]
            )
            return (residual - scale * again).astype(bf16), dots

    right_side, start_samples, start_rounded, dots = start(measured_images())
    start_everywhere = gathered(start_rounded)
    samples = exchanged(start_samples)
    dots = summed_over(["pencil"], dots)
    energy = jnp.sum(jnp.square(added(samples)))
    place = lax.broadcasted_iota(jnp.int32, dots.shape, 0)
    first_totals = summed_over(["coil"], jnp.where(place == 1, energy, dots))
    applied = first(samples, right_side)
    residual, samples, residual_rounded = forward(first_totals, right_side, applied)
    residual_everywhere = gathered(residual_rounded)
    mixed_rounded, dots = second(
        exchanged(samples), first_totals, right_side, applied, residual
    )
    mixed_everywhere = gathered(mixed_rounded)
    totals = summed_over(["coil", "pencil"], dots)
    start_norm = first_totals[0, 0]
    start_curve = first_totals[1, 0] + damping * start_norm
    first_step = start_norm / start_curve
    ratio = totals[0, 0] / start_norm
    curve = totals[1, 0] + ratio * (totals[2, 0] + totals[3, 0]) + ratio * ratio * start_curve
    second_step = totals[0, 0] / curve
    start_all = start_everywhere.astype(f32)
    residual_all = residual_everywhere.astype(f32)
    mixed_all = mixed_everywhere.astype(f32)
    picture = (first_step + second_step * ratio) * start_all + second_step * residual_all
    share = second_step / first_step
    residual = (
        (1.0 - share + share * ratio) * residual_all
        + share * mixed_all
        - share * ratio * start_all
    )
    return picture, residual


def solution(mesh):
    in_specs = (
        P("coil", "scan", None, "pencil"),
        P("coil", "scan", None, "pencil", None),
        P("pencil", None, None),
        P("pencil"),
        P("pencil"),
        P("pencil", None, None),
    )
    out_specs = (P("scan", None, "pencil", None), P("scan", None, "pencil", None))
    return jax.shard_map(
        on_device, mesh=mesh, in_specs=in_specs, out_specs=out_specs, check_vma=False
    )
```

profile of v0, /device:TPU:0, one launch (start us, length us, event | category | flops | bytes accessed | tf_op | source)
XLA Modules:
  0.0 240.7 jit_solution(4993181843356627604)
XLA Ops:
  7.9 12.0 %all_to_all.10 = bf16[8,2,1024]{2,1,0:T(2,128)(2,1)S(1)} all-to-all(bf16[8,2,1024]{2,1,0:T(2,128)(2,1)} %bitcast.30), channel_id=1, replica_groups=mesh['scan'=2,'coil'=4,'pencil'=4] {'coil'}, dimensions={0} | all-to-all | bytes 65536 | tf_op jit(solution)/shard_map/all_to_all | solution.py:399
  19.9 3.6 %all-to-all-start.1 = ((bf16[8,2,128,512]{3,2,1,0:T(8,128)(2,1)}), bf16[8,2,128,512]{3,2,1,0:T(8,128)(2,1)S(1)}, u32[]{:S(2)}, u32[]{:S(2)}) async-start(bf16[8,2,128,512]{3,2,1,0:T(8,128)(2,1)} %bitcast.28), calls=%async_computation.1 | async-start | bytes 4194304 | tf_op jit(solution)/shard_map/all_to_all | solution.py:383
  25.2 5.0 %all-reduce = s32[384]{0:T(512)S(1)} all-reduce(s32[384]{0:T(512)S(1)} %add_dynamic-update-slice_fusion), channel_id=2, replica_groups=mesh['scan'=2,'coil'=4,'pencil'=4] {'pencil'}, use_global_device_ids=true, to_apply=%add | all-reduce | flops 384 | bytes 3072
  30.5 1.7 gather_fusion
  38.9 6.5 %all_gather.23 = bf16[16,32,128]{2,0,1:T(8,128)(2,1)} all-gather(bf16[16,8,128]{2,0,1:T(8,128)(2,1)S(1)} %copy.9), channel_id=1, replica_groups=mesh['scan'=2,'coil'=4,'pencil'=4] {'pencil'}, dimensions={1}, use_global_device_ids=true | all-gather | bytes 163840 | tf_op jit(solution)/shard_map/all_gather | solution.py:400
  45.5 2.1 all-gather.6.cloned.1.call-done.weights.refs_6_.refs_9_
  47.6 13.9 %shard_map.77 = f32[8,2,128,512]{3,2,1,0:T(8,128)} custom-call(s32[128]{0:T(128)} %reshape.415.block, bf16[32,16,128]{2,1,0:T(8,128)(2,1)} %bitcast.29, bf16[128,128,128]{2,1,0:T(8,128)(2,1)} %all-gather.6.cloned.1.call-done.weights.refs_6_.refs_9_, bf16[256,256]{1,0:T(8,128)(2,1)} %get-tuple-element.29.mx0.refs_7_.refs_10_, ...), custom_call_target="tpu_custom_call" | custom-call | flops 2147483648 | bytes 5767680 | tf_op jit(solution)/shard_map/pallas_call | solution.py:457
  61.5 9.1 %all-to-all-done.1 = bf16[8,2,128,512]{3,2,1,0:T(8,128)(2,1)S(1)} async-done(((bf16[8,2,128,512]{3,2,1,0:T(8,128)(2,1)}), bf16[8,2,128,512]{3,2,1,0:T(8,128)(2,1)S(1)}, u32[]{:S(2)}, u32[]{:S(2)}) %all-to-all-start.1) | async-done | bytes 2097184 | tf_op jit(solution)/shard_map/all_to_all | solution.py:383
  71.9 16.1 %shard_map.78 = (f32[2,2,128,512]{3,2,1,0:T(8,128)}, bf16[32,16,128]{2,1,0:T(8,128)(2,1)}, bf16[2,2,128,512]{3,2,1,0:T(8,128)(2,1)}, f32[8,128]{1,0:T(8,128)}) custom-call(s32[128]{0:T(128)} %reshape.415.block, f32[4,2,2,128,512]{4,3,2,1,0:T(8,128)} %bitcast.27, bf16[4,2,2,128,512]{4,3,2,1,0:T(8,128)(2,1)} %bitcast.23, ...), custom_call_target="tpu_custom_call" | custom-call | flops 2147483648 | bytes 11403776 | tf_op jit(solution)/shard_map/pallas_call | solution.py:457
  91.9 2.8 %collective-permute-done.1.refs_2_ = bf16[32,16,128]{2,1,0:T(8,128)(2,1)S(1)} collective-permute-done((bf16[32,16,128]{2,1,0:T(8,128)(2,1)}, bf16[32,16,128]{2,1,0:T(8,128)(2,1)S(1)}, u32[]{:S(2)}, u32[]{:S(2)}) %collective-permute-start.1) | collective-permute-done | bytes 131104 | tf_op jit(solution)/shard_map/ppermute | solution.py:419
  94.8 1.9 collective-permute-done.2.refs_3_
  96.7 1.6 multiply_reduce_fusion
  99.7 2.0 collective-permute-start.7
  101.7 2.4 collective-permute-start.8
  104.1 15.6 %shard_map.79.applied.refs_6_ = f32[2,2,128,512]{3,2,1,0:T(8,128)} custom-call(s32[128]{0:T(128)} %reshape.415.block, bf16[32,16,128]{2,1,0:T(8,128)(2,1)} %get-tuple-element.11.refs_0_, bf16[32,16,128]{2,1,0:T(8,128)(2,1)} %copy-done.1, bf16[32,16,128]{2,1,0:T(8,128)(2,1)} %copy-done.2, bf16[32,16,128]{2,1,0:T(8,128)(2,1)} %copy-done.3, ...), custom_call_target="tpu_custom_call" | custom-call | flops 2147483648 | bytes 9306624 | tf_op jit(solution)/shard_map/pallas_call | solution.py:457
  120.3 14.0 %shard_map.80 = (f32[2,2,128,512]{3,2,1,0:T(8,128)}, bf16[32,16,128]{2,1,0:T(8,128)(2,1)}, bf16[2,2,128,512]{3,2,1,0:T(8,128)(2,1)}) custom-call(s32[128]{0:T(128)} %reshape.415.block, f32[8,128]{1,0:T(8,128)} %add_add_fusion.2.totals.refs_4_, f32[2,2,128,512]{3,2,1,0:T(8,128)} %get-tuple-element.13.refs_4_.right_side.refs_5_, ...), custom_call_target="tpu_custom_call" | custom-call | flops 2147483648 | bytes 9310720 | tf_op jit(solution)/shard_map/pallas_call | solution.py:457
  136.8 3.5 %collective-permute-done.10.refs_2_ = bf16[32,16,128]{2,1,0:T(8,128)(2,1)S(1)} collective-permute-done((bf16[32,16,128]{2,1,0:T(8,128)(2,1)}, bf16[32,16,128]{2,1,0:T(8,128)(2,1)S(1)}, u32[]{:S(2)}, u32[]{:S(2)}) %collective-permute-start.10) | collective-permute-done | bytes 131104 | tf_op jit(solution)/shard_map/ppermute | solution.py:419
  140.4 1.8 collective-permute-done.11.refs_3_
  142.9 16.5 %shard_map.81 = (bf16[2,2,128,512]{3,2,1,0:T(8,128)(2,1)}, f32[8,128]{1,0:T(8,128)}) custom-call(s32[128]{0:T(128)} %reshape.415.block, bf16[32,16,128]{2,1,0:T(8,128)(2,1)} %get-tuple-element.14.refs_0_, bf16[32,16,128]{2,1,0:T(8,128)(2,1)} %copy-done.6, bf16[32,16,128]{2,1,0:T(8,128)(2,1)} %copy-done.4, bf16[32,16,128]{2,1,0:T(8,128)(2,1)} %copy-done.5, ...), custom_call_target="tpu_custom_call" | custom-call | flops 2147483648 | bytes 11407872 | tf_op jit(solution)/shard_map/pallas_call | solution.py:457
  159.5 2.4 collective-permute-start.13
  161.8 2.0 collective-permute-start.14
  164.6 2.9 %collective-permute-done.14 = f32[8,128]{1,0:T(8,128)S(1)} collective-permute-done((f32[8,128]{1,0:T(8,128)}, f32[8,128]{1,0:T(8,128)S(1)}, u32[]{:S(2)}, u32[]{:S(2)}) %collective-permute-start.14) | collective-permute-done | bytes 4128 | tf_op jit(solution)/shard_map/ppermute | solution.py:419
  180.2 46.1 %all-gather.12.cloned.1.call-done = bf16[8,2,128,512]{3,2,1,0:T(8,128)(2,1)} async-done(((bf16[2,2,128,512]{3,2,1,0:T(8,128)(2,1)}), bf16[8,2,128,512]{3,2,1,0:T(8,128)(2,1)}) %all-gather.12.cloned.1.call-update) | async-done | bytes 2097168 | tf_op jit(solution)/shard_map/all_gather | solution.py:432
  226.4 7.9 %fusion.1 = (f32[8,2,128,512]{3,2,1,0:T(8,128)}, f32[8,2,128,512]{3,2,1,0:T(8,128)}) fusion(bf16[8,2,128,512]{3,2,1,0:T(8,128)(2,1)} %all-gather.8.cloned.1.call-done, bf16[8,2,128,512]{3,2,1,0:T(8,128)(2,1)} %all-gather.10.cloned.1.call-done, bf16[8,2,128,512]{3,2,1,0:T(8,128)(2,1)} %all-gather.12.cloned.1.call-done, f32[]{:T(128)S(6)} %mul.177, ...), kind=kLoop, calls=%fused_computation.6 | loop fusion | flops 11534336 | bytes 14680084 | tf_op jit(solution)/shard_map/sub | solution.py:694
  (93 shorter events, 25.7 us)
Async XLA Ops:
  7.2 17.8 %copy-start.8 = (s32[32]{0:T(128)S(1)}, s32[32]{0:T(128)}, u32[]{:S(2)}) copy-start(s32[32]{0:T(128)} %param.10) | copy-start | bytes 388
  7.2 40.4 %all-gather.6.cloned.1.call-start = ((), (), s32[]{:S(2)}) async-start(), calls=%async_computation.2 | async-start | bytes 5242880 | tf_op jit(solution)/shard_map/all_gather | solution.py:404
  19.9 50.7 %all-to-all-start.1 = ((bf16[8,2,128,512]{3,2,1,0:T(8,128)(2,1)}), bf16[8,2,128,512]{3,2,1,0:T(8,128)(2,1)S(1)}, u32[]{:S(2)}, u32[]{:S(2)}) async-start(bf16[8,2,128,512]{3,2,1,0:T(8,128)(2,1)} %bitcast.28), calls=%async_computation.1 | async-start | bytes 4194304 | tf_op jit(solution)/shard_map/all_to_all | solution.py:383
  23.6 155.2 %all-gather.8.cloned.1.call-start = ((), (), s32[]{:S(2)}) async-start(), calls=%async_computation.3 | async-start | bytes 2621440 | tf_op jit(solution)/shard_map/all_gather | solution.py:432
  88.1 92.2 %all-gather.10.cloned.1.call-start = ((), (), s32[]{:S(2)}) async-start(), calls=%async_computation.4 | async-start | bytes 2621440 | tf_op jit(solution)/shard_map/all_gather | solution.py:432
  88.1 3.8 %collective-permute-start = (bf16[32,16,128]{2,1,0:T(8,128)(2,1)}, bf16[32,16,128]{2,1,0:T(8,128)(2,1)S(1)}, u32[]{:S(2)}, u32[]{:S(2)}) collective-permute-start(bf16[32,16,128]{2,1,0:T(8,128)(2,1)} %get-tuple-element.11.refs_0_), channel_id=1, source_target_pairs={{0,1},{1,0},{2,3},{3,2},{4,5},{5,4},{6,7},{7,6},{8,9},{9,8},{10,11... | collective-permute-start | bytes 393224 | tf_op jit(solution)/shard_map/ppermute | solution.py:419
  88.2 6.6 %collective-permute-start.1 = (bf16[32,16,128]{2,1,0:T(8,128)(2,1)}, bf16[32,16,128]{2,1,0:T(8,128)(2,1)S(1)}, u32[]{:S(2)}, u32[]{:S(2)}) collective-permute-start(bf16[32,16,128]{2,1,0:T(8,128)(2,1)} %get-tuple-element.11.refs_0_), channel_id=1, source_target_pairs={{0,2},{1,3},{2,0},{3,1},{4,6},{5,7},{6,4},{7,5},{8,10},{9,11},{10,... | collective-permute-start | bytes 393224 | tf_op jit(solution)/shard_map/ppermute | solution.py:419
  89.8 6.9 %collective-permute-start.2 = (bf16[32,16,128]{2,1,0:T(8,128)(2,1)}, bf16[32,16,128]{2,1,0:T(8,128)(2,1)S(1)}, u32[]{:S(2)}, u32[]{:S(2)}) collective-permute-start(bf16[32,16,128]{2,1,0:T(8,128)(2,1)} %get-tuple-element.11.refs_0_), channel_id=1, source_target_pairs={{0,3},{1,2},{2,1},{3,0},{4,7},{5,6},{6,5},{7,4},{8,11},{9,10},{10,... | collective-permute-start | bytes 393224 | tf_op jit(solution)/shard_map/ppermute | solution.py:419
  90.1 8.2 %collective-permute-start.3 = (f32[8,128]{1,0:T(8,128)}, f32[8,128]{1,0:T(8,128)S(1)}, u32[]{:S(2)}, u32[]{:S(2)}) collective-permute-start(f32[8,128]{1,0:T(8,128)} %get-tuple-element.12), channel_id=1, source_target_pairs={{0,1},{1,0},{2,3},{3,2},{4,5},{5,4},{6,7},{7,6},{8,9},{9,8},{10,11... | collective-permute-start | bytes 12296 | tf_op jit(solution)/shard_map/ppermute | solution.py:419
  90.4 7.9 %collective-permute-start.4 = (f32[8,128]{1,0:T(8,128)}, f32[8,128]{1,0:T(8,128)S(1)}, u32[]{:S(2)}, u32[]{:S(2)}) collective-permute-start(f32[8,128]{1,0:T(8,128)} %get-tuple-element.12), channel_id=1, source_target_pairs={{0,2},{1,3},{2,0},{3,1},{4,6},{5,7},{6,4},{7,5},{8,10},{9,11},{10,... | collective-permute-start | bytes 12296 | tf_op jit(solution)/shard_map/ppermute | solution.py:419
  91.9 6.4 %collective-permute-start.5 = (f32[8,128]{1,0:T(8,128)}, f32[8,128]{1,0:T(8,128)S(1)}, u32[]{:S(2)}, u32[]{:S(2)}) collective-permute-start(f32[8,128]{1,0:T(8,128)} %get-tuple-element.12), channel_id=1, source_target_pairs={{0,3},{1,2},{2,1},{3,0},{4,7},{5,6},{6,5},{7,4},{8,11},{9,10},{10,... | collective-permute-start | bytes 12296 | tf_op jit(solution)/shard_map/ppermute | solution.py:419
  99.7 20.0 %collective-permute-start.6 = (f32[8,128]{1,0:T(8,128)S(1)}, f32[8,128]{1,0:T(8,128)S(1)}, u32[]{:S(2)}, u32[]{:S(2)}) collective-permute-start(f32[8,128]{1,0:T(8,128)S(1)} %add_select_fusion.4), channel_id=1, source_target_pairs={{0,4},{4,0},{8,12},{12,8},{1,5},{5,1},{9,13},{13,9},{2,6},{6,2},{1... | collective-permute-start | bytes 12296 | tf_op jit(solution)/shard_map/ppermute | solution.py:419
  99.7 20.0 %collective-permute-start.7 = (f32[8,128]{1,0:T(8,128)S(1)}, f32[8,128]{1,0:T(8,128)S(1)}, u32[]{:S(2)}, u32[]{:S(2)}) collective-permute-start(f32[8,128]{1,0:T(8,128)S(1)} %add_select_fusion.4), channel_id=1, source_target_pairs={{0,8},{4,12},{8,0},{12,4},{1,9},{5,13},{9,1},{13,5},{2,10},{6,14},... | collective-permute-start | bytes 12296 | tf_op jit(solution)/shard_map/ppermute | solution.py:419
  101.7 18.0 %collective-permute-start.8 = (f32[8,128]{1,0:T(8,128)S(1)}, f32[8,128]{1,0:T(8,128)S(1)}, u32[]{:S(2)}, u32[]{:S(2)}) collective-permute-start(f32[8,128]{1,0:T(8,128)S(1)} %add_select_fusion.4), channel_id=1, source_target_pairs={{0,12},{4,8},{8,4},{12,0},{1,13},{5,9},{9,5},{13,1},{2,14},{6,10},... | collective-permute-start | bytes 12296 | tf_op jit(solution)/shard_map/ppermute | solution.py:419
  134.4 92.0 %all-gather.12.cloned.1.call-start = ((), (), s32[]{:S(2)}) async-start(), calls=%async_computation.5 | async-start | bytes 2621440 | tf_op jit(solution)/shard_map/all_gather | solution.py:432
  134.6 5.7 %collective-permute-start.10 = (bf16[32,16,128]{2,1,0:T(8,128)(2,1)}, bf16[32,16,128]{2,1,0:T(8,128)(2,1)S(1)}, u32[]{:S(2)}, u32[]{:S(2)}) collective-permute-start(bf16[32,16,128]{2,1,0:T(8,128)(2,1)} %get-tuple-element.14.refs_0_), channel_id=1, source_target_pairs={{0,2},{1,3},{2,0},{3,1},{4,6},{5,7},{6,4},{7,5},{8,10},{9,11},{10,... | collective-permute-start | bytes 393224 | tf_op jit(solution)/shard_map/ppermute | solution.py:419
  136.2 6.0 %collective-permute-start.11 = (bf16[32,16,128]{2,1,0:T(8,128)(2,1)}, bf16[32,16,128]{2,1,0:T(8,128)(2,1)S(1)}, u32[]{:S(2)}, u32[]{:S(2)}) collective-permute-start(bf16[32,16,128]{2,1,0:T(8,128)(2,1)} %get-tuple-element.14.refs_0_), channel_id=1, source_target_pairs={{0,3},{1,2},{2,1},{3,0},{4,7},{5,6},{6,5},{7,4},{8,11},{9,10},{10,... | collective-permute-start | bytes 393224 | tf_op jit(solution)/shard_map/ppermute | solution.py:419
  136.2 6.0 %collective-permute-start.9 = (bf16[32,16,128]{2,1,0:T(8,128)(2,1)}, bf16[32,16,128]{2,1,0:T(8,128)(2,1)S(1)}, u32[]{:S(2)}, u32[]{:S(2)}) collective-permute-start(bf16[32,16,128]{2,1,0:T(8,128)(2,1)} %get-tuple-element.14.refs_0_), channel_id=1, source_target_pairs={{0,1},{1,0},{2,3},{3,2},{4,5},{5,4},{6,7},{7,6},{8,9},{9,8},{10,11... | collective-permute-start | bytes 393224 | tf_op jit(solution)/shard_map/ppermute | solution.py:419
  159.4 4.5 %collective-permute-start.12 = (f32[8,128]{1,0:T(8,128)}, f32[8,128]{1,0:T(8,128)S(1)}, u32[]{:S(2)}, u32[]{:S(2)}) collective-permute-start(f32[8,128]{1,0:T(8,128)} %get-tuple-element.16), channel_id=1, source_target_pairs={{0,4},{4,0},{8,12},{12,8},{1,5},{5,1},{9,13},{13,9},{2,6},{6,2},{1... | collective-permute-start | bytes 12296 | tf_op jit(solution)/shard_map/ppermute | solution.py:419
  159.5 5.2 %collective-permute-start.13 = (f32[8,128]{1,0:T(8,128)}, f32[8,128]{1,0:T(8,128)S(1)}, u32[]{:S(2)}, u32[]{:S(2)}) collective-permute-start(f32[8,128]{1,0:T(8,128)} %get-tuple-element.16), channel_id=1, source_target_pairs={{0,8},{4,12},{8,0},{12,4},{1,9},{5,13},{9,1},{13,5},{2,10},{6,14},... | collective-permute-start | bytes 12296 | tf_op jit(solution)/shard_map/ppermute | solution.py:419
  161.8 5.7 %collective-permute-start.14 = (f32[8,128]{1,0:T(8,128)}, f32[8,128]{1,0:T(8,128)S(1)}, u32[]{:S(2)}, u32[]{:S(2)}) collective-permute-start(f32[8,128]{1,0:T(8,128)} %get-tuple-element.16), channel_id=1, source_target_pairs={{0,12},{4,8},{8,4},{12,0},{1,13},{5,9},{9,5},{13,1},{2,14},{6,10},... | collective-permute-start | bytes 12296 | tf_op jit(solution)/shard_map/ppermute | solution.py:419
  168.3 4.9 %collective-permute-start.15 = (f32[8,128]{1,0:T(8,128)S(1)}, f32[8,128]{1,0:T(8,128)S(1)}, u32[]{:S(2)}, u32[]{:S(2)}) collective-permute-start(f32[8,128]{1,0:T(8,128)S(1)} %add_add_fusion.1), channel_id=1, source_target_pairs={{0,1},{1,0},{2,3},{3,2},{4,5},{5,4},{6,7},{7,6},{8,9},{9,8},{10,11... | collective-permute-start | bytes 12296 | tf_op jit(solution)/shard_map/ppermute | solution.py:419
  168.3 4.9 %collective-permute-start.16 = (f32[8,128]{1,0:T(8,128)S(1)}, f32[8,128]{1,0:T(8,128)S(1)}, u32[]{:S(2)}, u32[]{:S(2)}) collective-permute-start(f32[8,128]{1,0:T(8,128)S(1)} %add_add_fusion.1), channel_id=1, source_target_pairs={{0,2},{1,3},{2,0},{3,1},{4,6},{5,7},{6,4},{7,5},{8,10},{9,11},{10,... | collective-permute-start | bytes 12296 | tf_op jit(solution)/shard_map/ppermute | solution.py:419
  168.9 4.3 %collective-permute-start.17 = (f32[8,128]{1,0:T(8,128)S(1)}, f32[8,128]{1,0:T(8,128)S(1)}, u32[]{:S(2)}, u32[]{:S(2)}) collective-permute-start(f32[8,128]{1,0:T(8,128)S(1)} %add_add_fusion.1), channel_id=1, source_target_pairs={{0,3},{1,2},{2,1},{3,0},{4,7},{5,6},{6,5},{7,4},{8,11},{9,10},{10,... | collective-permute-start | bytes 12296 | tf_op jit(solution)/shard_map/ppermute | solution.py:419
  (10 other events, 84.3 us)
Sparse Core Ops, SparseCore 0:
  9.6 37.9 all-gather.5
  88.2 45.3 all-gather.7
  135.2 44.9 all-gather.9
  181.6 44.6 all-gather.11
where the time goes:
time: 242 us; the launch traced here: 241 us
  Pallas kernels  76.1 us (31%)
  waiting for transfers between devices  73.3 us (30%)
  blocking collectives  23.5 us (10%)
  between operations  21.5 us (9%)
  starting transfers between devices  20.7 us (9%)
  other arithmetic  18.2 us (8%)
  local copies, waits for them, and re-layouts  7.4 us (3%)
    pallas_call x5, Pallas kernels, call(): pl.pallas_call(kernel, grid=grid, in_specs=specs, out_specs=out_specs, ou...  76.1 us
    all_gather x3, waiting for transfers between devices, gathered(): return lax.all_gather(own, 'coil', axis=0, tiled=True)  47.6 us
    ppermute x18, starting transfers between devices, exchanged(): lax.ppermute(partial, axis, [(i, i ^ k) for i in range(count)])  16.7 us
    ppermute x18, waiting for transfers between devices, exchanged(): lax.ppermute(partial, axis, [(i, i ^ k) for i in range(count)])  13.8 us
    all_to_all x1, blocking collectives, on_device(): lax.all_to_all(kspace[0], 'coil', split_axis=0, concat_axis=0, tiled=True)  12 us
    all_to_all x1, waiting for transfers between devices, on_device(): lax.all_to_all(sens_maps[0], 'coil', split_axis=0, concat_axis=0, tiled=T...  9.07 us
    sub x1, other arithmetic, on_device(): (1.0 - share + share * ratio) * residual_all + share * mixed_all  7.86 us
    all_gather x1, blocking collectives, on_device(): lax.all_gather(measured.reshape(channels, blocks_dev, size), 'pencil', ax...  6.55 us
  transfers between devices with their start and end apart: 23, of which 10 were waited for; matrix products, arithmetic and copies ran while one was open for 7% of the time, Pallas kernels for 25%

commit v1 on v0

v1 whole, which is shorter than its diff:
```python
import functools
import math

import jax
import jax.numpy as jnp
from jax import lax
from jax.experimental import pallas as pl
from jax.experimental.pallas import tpu as pltpu
from jax.sharding import PartitionSpec as P


damping = 0.5
f32, bf16 = jnp.float32, jnp.bfloat16
vmem_limit = 56 * 1024 * 1024


def wave(left, right, length):
    phases = left[:, None] * right[None, :] % length
    angles = phases.astype(f32) * (2.0 * math.pi / length)
    return jnp.cos(angles) / math.sqrt(length), jnp.sin(angles) / math.sqrt(length)


def quarter_turns(left, right, count):
    turns = left[:, None] * right[None, :] % count
    if count == 4:
        cosine = jnp.where(turns == 0, 1.0, 0.0) - jnp.where(turns == 2, 1.0, 0.0)
        sine = jnp.where(turns == 1, 1.0, 0.0) - jnp.where(turns == 3, 1.0, 0.0)
        return cosine.astype(f32), sine.astype(f32)
    angles = turns.astype(f32) * (2.0 * math.pi / count)
    return jnp.cos(angles), jnp.sin(angles)


def split(value):
    high = value.astype(bf16)
    return high, (value - high.astype(f32)).astype(bf16)


def table_parts(table, axis):
    high = lax.reduce_precision(table, 8, 7)
    low = (table - high).astype(bf16)
    high = high.astype(bf16)
    return jnp.concatenate([high, high, low], axis)


def data_parts(value):
    high, low = split(value)
    return jnp.concatenate([high, low, high], 1)


def nt(left, right):
    return lax.dot_general(left, right, (((1,), (1,)), ((), ())), preferred_element_type=f32)


def nn(left, right):
    return jnp.dot(left, right, preferred_element_type=f32)


def tree_sum(values):
    while len(values) > 1:
        values = [left + right for left, right in zip(values[::2], values[1::2])]
    return values[0]


def forward_image(step, real, imag, sens_ref, ey, mx, turn_ref, grid_ref):
    tiles = turn_ref.shape[1]
    rows = turn_ref.shape[2]
    channels = grid_ref.shape[0] // tiles
    sens_real = sens_ref[0, 0].astype(f32)
    sens_imag = sens_ref[0, 1].astype(f32)
    coil = jnp.concatenate(
        [sens_real * real - sens_imag * imag, sens_real * imag + sens_imag * real], 0
    )
    both = nt(ey[...], data_parts(coil))
    half_real = both[:tiles, :rows] + both[tiles:, rows:]
    half_imag = both[:tiles, rows:] - both[tiles:, :rows]
    turned = jnp.concatenate(
        [
            half_real * turn_ref[0] + half_imag * turn_ref[1],
            half_imag * turn_ref[0] - half_real * turn_ref[1],
        ],
        1,
    )
    grid = nn(data_parts(turned), mx[...])
    size = grid.shape[1] // 2
    grid_ref[pl.ds(2 * step, tiles, stride=channels), :] = grid[:, :size]
    grid_ref[pl.ds(2 * step + 1, tiles, stride=channels), :] = grid[:, size:]


def sample_tiles(block_ref, weights_ref, grid_ref, sums_ref, out_ref):
    tiles = weights_ref.shape[0]
    channels = grid_ref.shape[0] // tiles
    sums_ref[...] = jnp.zeros_like(sums_ref)

    def one(tile, carry):
        start = pl.multiple_of(tile * channels, channels)
        high, low = split(grid_ref[pl.ds(start, channels), :])
        product = nn(jnp.concatenate([high, low], 0), weights_ref[tile])
        sums_ref[block_ref[tile]] += product[:channels] + product[channels:]
        return carry

    lax.fori_loop(0, tiles, one, 0, unroll=32)
    out_ref[...] = sums_ref[...].astype(bf16)


def spread_tiles(block_ref, weights_ref, parts_ref, grid_ref):
    tiles = weights_ref.shape[0]
    channels = grid_ref.shape[0] // tiles

    def one(tile, carry):
        start = pl.multiple_of(tile * channels, channels)
        product = nt(parts_ref[block_ref[tile]], weights_ref[tile])
        if product.shape[0] > channels:
            product = product[:channels] + product[channels:]
        grid_ref[pl.ds(start, channels), :] = product
        return carry

    lax.fori_loop(0, tiles, one, 0, unroll=32)


def adjoint_image(step, tiles, ey_back, mx_back, turn_ref, grid_ref):
    channels = grid_ref.shape[0] // tiles
    rows = turn_ref.shape[1]
    grid = jnp.concatenate(
        [
            grid_ref[pl.ds(2 * step, tiles, stride=channels), :],
            grid_ref[pl.ds(2 * step + 1, tiles, stride=channels), :],
        ],
        1,
    )
    back = nt(mx_back[...], data_parts(grid))
    turned = jnp.concatenate(
        [
            back[:rows] * turn_ref[0] - back[rows:] * turn_ref[1],
            back[rows:] * turn_ref[0] + back[:rows] * turn_ref[1],
        ],
        1,
    )
    image = nn(data_parts(turned), ey_back[...])
    columns = image.shape[1] // 2
    return image[:, :columns], image[:, columns:]


def add_dots(dots_ref, products):
    rows = lax.broadcasted_iota(jnp.int32, dots_ref.shape, 0)
    total = dots_ref[...]
    for place, (left, right) in enumerate(products):
        total += jnp.where(rows == place, jnp.sum(left * right), 0.0)
    dots_ref[...] = total


def measured_kernel(block, samples, weights, mx, eb, turn, images, grid):
    plane = pl.program_id(0)
    coils = images.shape[0]

    @pl.when(plane == 0)
    def _():
        spread_tiles(block, weights, samples, grid)

    for coil in range(coils):
        real, imag = adjoint_image(
            coil * pl.num_programs(0) + plane, weights.shape[0], eb, mx, turn, grid
        )
        images[coil, 0, 0] = real
        images[coil, 0, 1] = imag


def combine(images, sens):
    total_real = total_imag = 0.0
    for (real, imag), sens_ref in zip(images, sens):
        sens_real = sens_ref[0, 0].astype(f32)
        sens_imag = sens_ref[0, 1].astype(f32)
        total_real += sens_real * real + sens_imag * imag
        total_imag += sens_real * imag - sens_imag * real
    return total_real, total_imag


def start_kernel(images, *refs):
    *sens, right_side, rounded, dots = refs
    total = combine([(images[c, 0, 0], images[c, 0, 1]) for c in range(len(sens))], sens)
    for part in range(2):
        right_side[0, part] = total[part]
        rounded[0, part] = total[part].astype(bf16)

    @pl.when((pl.program_id(0) == 0) & (pl.program_id(1) == 0))
    def _():
        dots[...] = jnp.zeros_like(dots)

    add_dots(dots, [(right_side[0], right_side[0])])


def forward_kernel(block, picture, *refs):
    *sens, weights, ey, mx, turn, samples, grid, sums = refs
    plane = pl.program_id(0)
    for coil, sens_ref in enumerate(sens):
        forward_image(
            coil * pl.num_programs(0) + plane,
            picture[0, 0],
            picture[0, 1],
            sens_ref,
            ey,
            mx,
            turn,
            grid,
        )

    @pl.when(plane == pl.num_programs(0) - 1)
    def _():
        sample_tiles(block, weights, grid, sums, samples)


def spread_sum(block, samples, weights, grid, parts):
    summed = tree_sum([part[...].astype(f32) for part in samples])
    channels = summed.shape[1]
    high, low = split(summed)
    parts[:, :channels] = high
    parts[:, channels:] = low
    spread_tiles(block, weights, parts, grid)


def back_images(coils, plane, tiles, eb, mx, turn, grid):
    return [
        adjoint_image(coil * pl.num_programs(0) + plane, tiles, eb, mx, turn, grid)
        for coil in range(coils)
    ]


def first_kernel(peers, block, *refs):
    samples = refs[:peers]
    right_side, *sens, weights, mx, eb, turn, applied, grid, parts = refs[peers:]
    plane = pl.program_id(0)

    @pl.when(plane == 0)
    def _():
        spread_sum(block, samples, weights, grid, parts)

    images = back_images(len(sens), plane, weights.shape[0], eb, mx, turn, grid)
    total = combine(images, sens)
    for part in range(2):
        applied[0, part] = total[part] + damping * right_side[0, part]


def first_step_of(totals):
    return totals[0:1, 0:1] / (totals[1:2, 0:1] + damping * totals[0:1, 0:1])


def second_kernel(peers, block, *refs):
    samples = refs[:peers]
    totals, right_side, applied, residual, *sens = refs[peers:-8]
    weights, mx, eb, turn, rounded, dots, grid, parts = refs[-8:]
    plane = pl.program_id(0)

    @pl.when(plane == 0)
    def _():
        dots[...] = jnp.zeros_like(dots)
        spread_sum(block, samples, weights, grid, parts)

    images = back_images(len(sens), plane, weights.shape[0], eb, mx, turn, grid)
    total = combine(images, sens)
    for part in range(2):
        vector = residual[0, part]
        again = total[part] + damping * vector
        rounded[0, part] = (vector - first_step_of(totals) * again).astype(bf16)
        add_dots(
            dots,
            [
                (vector, vector),
                (vector, again),
                (vector, applied[0, part]),
                (right_side[0, part], again),
            ],
        )


def whole_block(array):
    rank = len(array.shape)
    return pl.BlockSpec(array.shape, lambda *_: (0,) * rank)


def on_device(kspace, sens_maps, weights, tile_slot, tile_block, send_list):
    coil_count = lax.axis_size("coil")
    peers = lax.axis_size("pencil")
    planes = sens_maps.shape[1]
    own_planes = planes // coil_count
    rows = sens_maps.shape[3]
    columns = sens_maps.shape[4]
    rows_total = rows * peers
    size = weights.shape[1]
    tile_count = tile_slot.shape[0]
    tiles = tile_count * peers
    blocks_dev = kspace.shape[3] // size
    blocks = blocks_dev * peers
    cap = send_list.shape[2]
    runs = rows_total // size
    brick_dev = columns // peers * runs
    images_count = coil_count * own_planes
    channels = 2 * images_count

    coil_index = lax.axis_index("coil")

    def to_planes(array):
        pieces = []
        for k in range(coil_count):
            part = lax.dynamic_slice_in_dim(array, (coil_index ^ k) * own_planes, own_planes, 0)
            if k > 0:
                part = lax.ppermute(part, "coil", [(i, i ^ k) for i in range(coil_count)])
            pieces.append(part)
        return pieces

    sens = to_planes(sens_maps[0])

    packed = jnp.concatenate([tile_slot, tile_block, send_list.reshape(-1)])
    places = lax.all_gather(packed, "pencil")
    slots = places[:, :tile_count]
    block_of = (
        places[:, tile_count : 2 * tile_count]
        + blocks_dev * jnp.arange(peers, dtype=jnp.int32)[:, None]
    ).reshape(-1)
    lists = places[:, 2 * tile_count :].reshape(peers, peers, cap)
    holder = jnp.arange(peers, dtype=jnp.int32)[:, None]
    brick = (slots // cap * brick_dev + lists[slots // cap, holder, slots % cap]).reshape(-1)
    line = brick // runs
    run = brick % runs

    measured = jnp.stack(to_planes(kspace[0]))
    measured = lax.all_gather(
        measured.reshape(channels, blocks_dev, size), "pencil", axis=1, tiled=True
    )
    measured = jnp.swapaxes(measured, 0, 1)
    all_weights = lax.all_gather(weights, "pencil", axis=0, tiled=True)

    cos_y, sin_y = wave(
        line - columns // 2, jnp.arange(columns, dtype=jnp.int32) - columns // 2, columns
    )
    row_ids = jnp.arange(rows, dtype=jnp.int32) + lax.axis_index("pencil") * rows - rows_total // 2
    cos_x, sin_x = wave(
        row_ids, jnp.arange(size, dtype=jnp.int32) - rows_total // 2, rows_total
    )
    turn = jnp.stack(quarter_turns(run, row_ids, runs))
    turn_back = jnp.stack(quarter_turns(row_ids, run, runs))

    def exchanged(partial, axis="pencil"):
        count = lax.axis_size(axis)
        return [partial] + [
            lax.ppermute(partial, axis, [(i, i ^ k) for i in range(count)])
            for k in range(1, count)
        ]

    def summed_over(axes, dots):
        for axis in axes:
            dots = tree_sum(exchanged(dots, axis))
        return dots

    def added(samples):
        return tree_sum([part.astype(f32) for part in samples])

    def gathered(own):
        ahead = [(i, i + 1) for i in range(coil_count - 1)]
        behind = [(i + 1, i) for i in range(coil_count - 1)]
        lines = []
        for plane in range(own_planes):
            piece = own[plane : plane + 1]
            lower, upper = [piece], [piece]
            for _ in range(1, coil_count):
                lower.append(lax.ppermute(lower[-1], "coil", ahead))
                upper.append(lax.ppermute(upper[-1], "coil", behind))
            lines.append([(lower[k], upper[-k]) for k in range(coil_count)])
        return [[line[k] for line in lines] for k in range(coil_count)]

    def chosen(k, pair):
        return (pair[0] if k == 0 else jnp.where(coil_index >= k, *pair)).astype(f32)

    def assembled(value_of):
        out = jnp.zeros((planes, 2, rows, columns), f32)
        for k in range(coil_count):
            for plane in range(own_planes):
                place = (coil_index + coil_count - k) % coil_count * own_planes + plane
                out = lax.dynamic_update_slice(out, value_of(k, plane), (place, 0, 0, 0))
        return out

    picture_shape = (own_planes, 2, rows, columns)

    if rows % 128 == 0 and columns % 128 == 0 and size % 128 == 0 and channels % 16 == 0:
        ey = table_parts(jnp.concatenate([cos_y, sin_y], 0), 1)
        eb = jnp.concatenate(
            [jnp.concatenate([cos_y, sin_y], 1), jnp.concatenate([-sin_y, cos_y], 1)], 0
        )
        eb = table_parts(eb, 0)
        mx = jnp.concatenate(
            [jnp.concatenate([cos_x, -sin_x], 1), jnp.concatenate([sin_x, cos_x], 1)], 0
        )
        mx, mx_back = table_parts(mx, 0), table_parts(mx, 1)
        places_spec = pl.BlockSpec(memory_space=pltpu.SMEM)
        plane_spec = pl.BlockSpec((1, 2, rows, columns), lambda p: (p, 0, 0, 0))
        all_coils = pl.BlockSpec(
            (coil_count, 1, 2, rows, columns), lambda p: (0, p, 0, 0, 0)
        )
        grid_scratch = pltpu.VMEM((tiles * channels, size), f32)
        sums_shape = (blocks, channels, size)
        params = pltpu.CompilerParams(vmem_limit_bytes=vmem_limit)

        def call(kernel, grid, inputs, specs, outs, out_specs, scratch, flops):
            read = sum(math.prod(i.shape) * i.dtype.itemsize for i in inputs)
            return pl.pallas_call(
                kernel,
                grid=grid,
                in_specs=specs,
                out_specs=out_specs,
                out_shape=outs,
                scratch_shapes=scratch,
                compiler_params=params,
                cost_estimate=pl.CostEstimate(
                    flops=flops, bytes_accessed=read, transcendentals=0
                ),
            )(*inputs)

        def shaped(shape, dtype=f32):
            return jax.ShapeDtypeStruct(shape, dtype)

        image_flops = 3 * images_count * 8 * tiles * rows * (columns + size)
        tile_flops = 4 * tiles * channels * size * size
        grid = (own_planes,)

        def measured_images():
            inputs = [block_of, measured, all_weights, mx_back, eb, turn_back]
            return call(
                measured_kernel,
                grid,
                inputs,
                [places_spec] + [whole_block(i) for i in inputs[1:]],
                shaped((coil_count,) + picture_shape),
                all_coils,
                [grid_scratch],
                image_flops + tile_flops,
            )

        def start(images):
            chunk = 64
            spec = pl.BlockSpec((1, 2, chunk, columns), lambda p, r: (p, 0, r, 0))
            coils_spec = pl.BlockSpec(
                (coil_count, 1, 2, chunk, columns), lambda p, r: (0, p, 0, r, 0)
            )
            return call(
                start_kernel,
                (own_planes, rows // chunk),
                [images, *sens],
                [coils_spec] + [spec] * coil_count,
                [shaped(picture_shape), shaped(picture_shape, bf16), shaped((8, 128))],
                [spec, spec, whole_block(shaped((8, 128)))],
                [],
                8 * images_count * rows * columns,
            )

        def forward(picture):
            tail = [all_weights, ey, mx, turn]
            return call(
                forward_kernel,
                grid,
                [block_of, picture, *sens, *tail],
                [places_spec] + [plane_spec] * (1 + coil_count) + [whole_block(i) for i in tail],
                shaped(sums_shape, bf16),
                whole_block(shaped(sums_shape)),
                [grid_scratch, pltpu.VMEM(sums_shape, f32)],
                image_flops + tile_flops,
            )

        parts_scratch = pltpu.VMEM((blocks, 2 * channels, size), bf16)

        def first(samples, right_side):
            tail = [all_weights, mx_back, eb, turn_back]
            inputs = [block_of, *samples, right_side, *sens, *tail]
            return call(
                functools.partial(first_kernel, peers),
                grid,
                inputs,
                [places_spec]
                + [whole_block(i) for i in samples]
                + [plane_spec] * (1 + coil_count)
                + [whole_block(i) for i in tail],
                shaped(picture_shape),
                plane_spec,
                [grid_scratch, parts_scratch],
                image_flops + tile_flops,
            )

        def second(samples, totals, right_side, applied, residual):
            tail = [all_weights, mx_back, eb, turn_back]
            inputs = [block_of, *samples, totals, right_side, applied, residual, *sens, *tail]
            return call(
                functools.partial(second_kernel, peers),
                grid,
                inputs,
                [places_spec]
                + [whole_block(i) for i in samples]
                + [whole_block(totals)]
                + [plane_spec] * (3 + coil_count)
                + [whole_block(i) for i in tail],
                [shaped(picture_shape, bf16), shaped((8, 128))],
                [plane_spec, whole_block(shaped((8, 128)))],
                [grid_scratch, parts_scratch],
                image_flops + tile_flops,
            )

    else:
        ein = functools.partial(jnp.einsum, precision=lax.Precision.HIGH)
        all_sens = jnp.stack(sens).astype(f32)
        map_real, map_imag = all_sens[:, :, 0], all_sens[:, :, 1]
        shape = (coil_count, own_planes)
        block_map = (block_of[:, None] == jnp.arange(blocks, dtype=jnp.int32)).astype(f32)
        tc, ts = turn[0][:, None, None], turn[1][:, None, None]
        wide_weights = all_weights.astype(f32)

        def forward(picture):
            coil_real = map_real * picture[None, :, 0] - map_imag * picture[None, :, 1]
            coil_imag = map_real * picture[None, :, 1] + map_imag * picture[None, :, 0]
            half_real = ein("ty,cpxy->tcpx", cos_y, coil_real) + ein(
                "ty,cpxy->tcpx", sin_y, coil_imag
            )
            half_imag = ein("ty,cpxy->tcpx", cos_y, coil_imag) - ein(
                "ty,cpxy->tcpx", sin_y, coil_real
            )
            real = half_real * tc + half_imag * ts
            imag = half_imag * tc - half_real * ts
            grid = jnp.stack(
                [
                    ein("tcpx,xi->tcpi", real, cos_x) + ein("tcpx,xi->tcpi", imag, sin_x),
                    ein("tcpx,xi->tcpi", imag, cos_x) - ein("tcpx,xi->tcpi", real, sin_x),
                ],
                3,
            ).reshape(tiles, channels, size)
            product = ein("tgi,tis->tgs", grid, wide_weights)
            return ein("tb,tgs->bgs", block_map, product).astype(bf16)

        def images_of(samples):
            spread = ein("tgs,tis->tgi", jnp.take(samples, block_of, axis=0), wide_weights)
            spread = spread.reshape(tiles, *shape, 2, size)
            back_real = ein("tcpi,xi->tcpx", spread[:, :, :, 0], cos_x) - ein(
                "tcpi,xi->tcpx", spread[:, :, :, 1], sin_x
            )
            back_imag = ein("tcpi,xi->tcpx", spread[:, :, :, 1], cos_x) + ein(
                "tcpi,xi->tcpx", spread[:, :, :, 0], sin_x
            )
            real = back_real * tc - back_imag * ts
            imag = back_imag * tc + back_real * ts
            return (
                ein("tcpx,ty->cpxy", real, cos_y) - ein("tcpx,ty->cpxy", imag, sin_y),
                ein("tcpx,ty->cpxy", imag, cos_y) + ein("tcpx,ty->cpxy", real, sin_y),
            )

        def combined(images):
            real, imag = images
            return jnp.stack(
                [
                    jnp.sum(map_real * real + map_imag * imag, 0),
                    jnp.sum(map_real * imag - map_imag * real, 0),
                ],
                1,
            )

        def stacked_dots(products):
            values = [jnp.sum(left * right) for left, right in products]
            values += [jnp.zeros((), f32)] * (8 - len(values))
            return jnp.broadcast_to(jnp.stack(values)[:, None], (8, 128))

        def measured_images():
            return images_of(measured.astype(f32))

        def start(images):
            right_side = combined(images)
            dots = stacked_dots([(right_side, right_side)])
            return right_side, right_side.astype(bf16), dots

        def first(samples, right_side):
            return combined(images_of(added(samples))) + damping * right_side

        def second(samples, totals, right_side, applied, residual):
            scale = totals[0, 0] / (totals[1, 0] + damping * totals[0, 0])
            again = combined(images_of(added(samples))) + damping * residual
            dots = stacked_dots(
                [
                    (residual, residual),
                    (residual, again),
                    (residual, applied),
                    (right_side, again),
                ]
            )
            return (residual - scale * again).astype(bf16), dots

    right_side, rounded, dots = start(measured_images())
    start_everywhere = gathered(rounded)
    samples = exchanged(forward(right_side))
    dots = summed_over(["pencil"], dots)
    energy = jnp.sum(jnp.square(added(samples)))
    place = lax.broadcasted_iota(jnp.int32, dots.shape, 0)
    first_totals = summed_over(["coil"], jnp.where(place == 1, energy, dots))
    start_norm = first_totals[0, 0]
    start_curve = first_totals[1, 0] + damping * start_norm
    first_step = start_norm / start_curve
    applied = first(samples, right_side)
    residual = right_side - first_step * applied
    residual_everywhere = gathered(residual.astype(bf16))
    samples = exchanged(forward(residual))
    rounded, dots = second(samples, first_totals, right_side, applied, residual)
    mixed_everywhere = gathered(rounded)
    totals = summed_over(["coil", "pencil"], dots)
    ratio = totals[0, 0] / start_norm
    curve = totals[1, 0] + ratio * (totals[2, 0] + totals[3, 0]) + ratio * ratio * start_curve
    second_step = totals[0, 0] / curve
    share = second_step / first_step

    def picture_of(k, plane):
        return (first_step + second_step * ratio) * chosen(
            k, start_everywhere[k][plane]
        ) + second_step * chosen(k, residual_everywhere[k][plane])

    def residual_of(k, plane):
        return (
            (1.0 - share + share * ratio) * chosen(k, residual_everywhere[k][plane])
            + share * chosen(k, mixed_everywhere[k][plane])
            - share * ratio * chosen(k, start_everywhere[k][plane])
        )

    return assembled(picture_of), assembled(residual_of)


def solution(mesh):
    in_specs = (
        P("coil", "scan", None, "pencil"),
        P("coil", "scan", None, "pencil", None),
        P("pencil", None, None),
        P("pencil"),
        P("pencil"),
        P("pencil", None, None),
    )
    out_specs = (P("scan", None, "pencil", None), P("scan", None, "pencil", None))
    return jax.shard_map(
        on_device, mesh=mesh, in_specs=in_specs, out_specs=out_specs, check_vma=False
    )
```

time: 242 us -> 336 us (1.39)
  starting transfers between devices: 20.7 us -> 132 us
  Pallas kernels: 76.1 us -> 61.2 us
  blocking collectives: 23.5 us -> 11 us
  local copies, waits for them, and re-layouts: 7.4 us -> 16.8 us
    ppermute x0 -> x42, starting transfers between devices: none -> 104 us  [the longest x18 70.4 us: gathered(): lower.append(lax.ppermute(lower[-1], 'coil', ahead))]
    ppermute x0 -> x42, waiting for transfers between devices: none -> 60.8 us  [the longest x18 26.2 us: gathered(): upper.append(lax.ppermute(upper[-1], 'coil', behind))]
    all_gather x3 -> x0, waiting for transfers between devices: 47.6 us -> none  [gathered(): return lax.all_gather(own, 'coil', axis=0, tiled=True)]
    pallas_call x5 -> x6, Pallas kernels: 76.1 us -> 61.2 us  [call(): pl.pallas_call(kernel, grid=grid, in_specs=specs, out_specs=out_specs, ou...]
    all_to_all x1 -> x0, blocking collectives: 12 us -> none  [on_device(): lax.all_to_all(kspace[0], 'coil', split_axis=0, concat_axis=0, tiled=True)]
    ppermute x18, starting transfers between devices: 16.7 us -> 27.8 us  [exchanged(): lax.ppermute(partial, axis, [(i, i ^ k) for i in range(count)])]
    all_to_all x1 -> x0, waiting for transfers between devices: 9.07 us -> none  [on_device(): lax.all_to_all(sens_maps[0], 'coil', split_axis=0, concat_axis=0, tiled=T...]
    sub x1 -> x0, other arithmetic: 7.86 us -> none  [on_device(): (1.0 - share + share * ratio) * residual_all + share * mixed_all]
  transfers between devices with their start and end apart: 23 -> 61, of which waited for: 10 -> 18; matrix products, arithmetic and copies ran while one was open for 7% -> 8% of each run, Pallas kernels for 25% -> 10%
where the time goes in v1:
time: 336 us; the launch traced here: 335 us
  starting transfers between devices  132 us (39%)
  waiting for transfers between devices  72.8 us (22%)
  Pallas kernels  61.2 us (18%)
  between operations  22.6 us (7%)
  other arithmetic  18.6 us (6%)
  local copies, waits for them, and re-layouts  16.8 us (5%)
  blocking collectives  11 us (3%)
    ppermute x18, starting transfers between devices, gathered(): lower.append(lax.ppermute(lower[-1], 'coil', ahead))  70.4 us
    pallas_call x6, Pallas kernels, call(): pl.pallas_call(kernel, grid=grid, in_specs=specs, out_specs=out_specs, ou...  61.2 us
    ppermute x18, starting transfers between devices, exchanged(): lax.ppermute(partial, axis, [(i, i ^ k) for i in range(count)])  27.8 us
    ppermute x18, waiting for transfers between devices, gathered(): upper.append(lax.ppermute(upper[-1], 'coil', behind))  26.2 us
    ppermute x18, starting transfers between devices, gathered(): upper.append(lax.ppermute(upper[-1], 'coil', behind))  23.4 us
    ppermute x18, waiting for transfers between devices, gathered(): lower.append(lax.ppermute(lower[-1], 'coil', ahead))  20.1 us
    ppermute x6, waiting for transfers between devices, to_planes(): part = lax.ppermute(part, 'coil', [(i, i ^ k) for i in range(coil_count)])  14.5 us
    ppermute x18, waiting for transfers between devices, exchanged(): lax.ppermute(partial, axis, [(i, i ^ k) for i in range(count)])  11.3 us
  transfers between devices with their start and end apart: 61, of which 18 were waited for; matrix products, arithmetic and copies ran while one was open for 8% of the time, Pallas kernels for 10%

profile of v1, /device:TPU:0, one launch (start us, length us, event | category | flops | bytes accessed | tf_op | source)
XLA Modules:
  0.0 334.8 jit_solution(6512179920666613830)
XLA Ops:
  22.9 5.0 %all-reduce = s32[384]{0:T(512)S(1)} all-reduce(s32[384]{0:T(512)S(1)} %add_dynamic-update-slice_fusion), channel_id=2, replica_groups=mesh['scan'=2,'coil'=4,'pencil'=4] {'pencil'}, use_global_device_ids=true, to_apply=%add | all-reduce | flops 384 | bytes 3072
  38.2 14.4 %collective-permute-done.2 = bf16[2,2,1024]{2,1,0:T(2,128)(2,1)S(1)} collective-permute-done((bf16[2,2,1024]{2,1,0:T(2,128)(2,1)S(1)}, bf16[2,2,1024]{2,1,0:T(2,128)(2,1)S(1)}, u32[]{:S(2)}, u32[]{:S(2)}) %collective-permute-start.2) | collective-permute-done | bytes 8224 | tf_op jit(solution)/shard_map/ppermute | solution.py:305
  52.8 6.1 %all_gather.14 = bf16[16,32,128]{2,0,1:T(8,128)(2,1)} all-gather(bf16[16,8,128]{2,0,1:T(8,128)(2,1)S(1)} %copy.9), channel_id=1, replica_groups=mesh['scan'=2,'coil'=4,'pencil'=4] {'pencil'}, dimensions={1}, use_global_device_ids=true | all-gather | bytes 163840 | tf_op jit(solution)/shard_map/all_gather | solution.py:325
  58.8 10.9 %shard_map.77.images = f32[4,2,2,128,512]{4,3,2,1,0:T(8,128)} custom-call(s32[128]{0:T(128)} %reshape.418.block, bf16[32,16,128]{2,1,0:T(8,128)(2,1)} %bitcast.36, bf16[128,128,128]{2,1,0:T(8,128)(2,1)} %all-gather.3.cloned.1.call-done.weights.refs_4_.refs_9_.refs_12_, bf16[256,768]{1,0:T(8,128)(2,1)} %pad_maximum_fusion.3.mx.refs_10_.refs_13_, ...), custom_call_target="tpu_custom_call" | custom-call | flops 2147483648 | bytes 6423040 | tf_op jit(solution)/shard_map/pallas_call | solution.py:403
  70.9 5.1 %shard_map.78 = (f32[2,2,128,512]{3,2,1,0:T(8,128)}, bf16[2,2,128,512]{3,2,1,0:T(8,128)(2,1)}, f32[8,128]{1,0:T(8,128)}) custom-call(f32[4,2,2,128,512]{4,3,2,1,0:T(8,128)} %shard_map.77.images, bf16[2,2,128,512]{3,2,1,0:T(8,128)(2,1)} %get-tuple-element.18.refs_0_.refs_5_.refs_8_, bf16[2,2,128,512]{3,2,1,0:T(8,128)(2,1)} %copy-done.1, ...), custom_call_target="tpu_custom_call" | custom-call | flops 4194304 | bytes 6291456 | tf_op jit(solution)/shard_map/pallas_call | solution.py:403
  76.0 10.5 %shard_map.79.refs_0_ = bf16[32,16,128]{2,1,0:T(8,128)(2,1)} custom-call(s32[128]{0:T(128)} %reshape.418.block, f32[2,2,128,512]{3,2,1,0:T(8,128)} %get-tuple-element.7.picture.refs_4_.refs_5_, bf16[2,2,128,512]{3,2,1,0:T(8,128)(2,1)} %get-tuple-element.18.refs_0_.refs_5_.refs_8_, bf16[2,2,128,512]{3,2,1,0:T(8,128)(2,1)} %copy-done.1, ...), custom_call_target="tpu_custom_call" | custom-call | flops 2147483648 | bytes 8651264 | tf_op jit(solution)/shard_map/pallas_call | solution.py:403
  97.1 13.2 %collective-permute-start.12 = (f32[8,128]{1,0:T(8,128)S(1)}, f32[8,128]{1,0:T(8,128)S(1)}, u32[]{:S(2)}, u32[]{:S(2)}) collective-permute-start(f32[8,128]{1,0:T(8,128)S(1)} %add_select_fusion.4), channel_id=1, source_target_pairs={{0,4},{4,0},{8,12},{12,8},{1,5},{5,1},{9,13},{13,9},{2,6},{6,2},{1... | collective-permute-start | bytes 12296 | tf_op jit(solution)/shard_map/ppermute | solution.py:344
  112.7 11.6 %shard_map.80.refs_6_ = f32[2,2,128,512]{3,2,1,0:T(8,128)} custom-call(s32[128]{0:T(128)} %reshape.418.block, bf16[32,16,128]{2,1,0:T(8,128)(2,1)} %shard_map.79.refs_0_, bf16[32,16,128]{2,1,0:T(8,128)(2,1)} %copy-done.8, bf16[32,16,128]{2,1,0:T(8,128)(2,1)} %copy-done.9, bf16[32,16,128]{2,1,0:T(8,128)(2,1)} %copy-done.10, ...), custom_call_target="tpu_custom_call" | custom-call | flops 2147483648 | bytes 9961984 | tf_op jit(solution)/shard_map/pallas_call | solution.py:403
  129.2 10.5 %shard_map.81.refs_0_ = bf16[32,16,128]{2,1,0:T(8,128)(2,1)} custom-call(s32[128]{0:T(128)} %reshape.418.block, f32[2,2,128,512]{3,2,1,0:T(8,128)} %get-tuple-element.13.picture.refs_7_, bf16[2,2,128,512]{3,2,1,0:T(8,128)(2,1)} %get-tuple-element.18.refs_0_.refs_5_.refs_8_, bf16[2,2,128,512]{3,2,1,0:T(8,128)(2,1)} %copy-done.1, ...), custom_call_target="tpu_custom_call" | custom-call | flops 2147483648 | bytes 8651264 | tf_op jit(solution)/shard_map/pallas_call | solution.py:403
  148.8 12.5 %shard_map.82 = (bf16[2,2,128,512]{3,2,1,0:T(8,128)(2,1)}, f32[8,128]{1,0:T(8,128)}) custom-call(s32[128]{0:T(128)} %reshape.418.block, bf16[32,16,128]{2,1,0:T(8,128)(2,1)} %shard_map.81.refs_0_, bf16[32,16,128]{2,1,0:T(8,128)(2,1)} %copy-done.14, bf16[32,16,128]{2,1,0:T(8,128)(2,1)} %copy-done.15, bf16[32,16,128]{2,1,0:T(8,128)(2,1)} %copy-done.16, ...), custom_call_target="tpu_custom_call" | custom-call | flops 2147483648 | bytes 12063232 | tf_op jit(solution)/shard_map/pallas_call | solution.py:403
  166.6 4.6 %collective-permute-start.32 = (bf16[1,2,128,512]{3,2,1,0:T(8,128)(2,1)S(1)}, bf16[1,2,128,512]{3,2,1,0:T(8,128)(2,1)S(1)}, u32[]{:S(2)}, u32[]{:S(2)}) collective-permute-start(bf16[1,2,128,512]{3,2,1,0:T(8,128)(2,1)S(1)} %get-tuple-element.40), channel_id=1, source_target_pairs={{0,4},{4,8},{8,12},{1,5},{5,9},{9,13},{2,6},{6,10},{10,14},{3,7},{... | collective-permute-start | bytes 786440 | tf_op jit(solution)/shard_map/ppermute | solution.py:364
  178.5 4.6 %collective-permute-start.28 = (bf16[1,2,128,512]{3,2,1,0:T(8,128)(2,1)S(1)}, bf16[1,2,128,512]{3,2,1,0:T(8,128)(2,1)S(1)}, u32[]{:S(2)}, u32[]{:S(2)}) collective-permute-start(bf16[1,2,128,512]{3,2,1,0:T(8,128)(2,1)S(1)} %get-tuple-element.39), channel_id=1, source_target_pairs={{0,4},{4,8},{8,12},{1,5},{5,9},{9,13},{2,6},{6,10},{10,14},{3,7},{... | collective-permute-start | bytes 786440 | tf_op jit(solution)/shard_map/ppermute | solution.py:364
  188.9 5.3 %collective-permute-start.36 = (bf16[1,2,128,512]{3,2,1,0:T(8,128)(2,1)}, bf16[1,2,128,512]{3,2,1,0:T(8,128)(2,1)}, u32[]{:S(2)}, u32[]{:S(2)}) collective-permute-start(bf16[1,2,128,512]{3,2,1,0:T(8,128)(2,1)} %get-tuple-element.38), channel_id=1, source_target_pairs={{0,4},{4,8},{8,12},{1,5},{5,9},{9,13},{2,6},{6,10},{10,14},{3,7},{... | collective-permute-start | bytes 786440 | tf_op jit(solution)/shard_map/ppermute | solution.py:364
  198.4 6.3 %collective-permute-start.40 = (bf16[1,2,128,512]{3,2,1,0:T(8,128)(2,1)}, bf16[1,2,128,512]{3,2,1,0:T(8,128)(2,1)}, u32[]{:S(2)}, u32[]{:S(2)}) collective-permute-start(bf16[1,2,128,512]{3,2,1,0:T(8,128)(2,1)} %copy-done.11), channel_id=1, source_target_pairs={{0,4},{4,8},{8,12},{1,5},{5,9},{9,13},{2,6},{6,10},{10,14},{3,7},{... | collective-permute-start | bytes 786440 | tf_op jit(solution)/shard_map/ppermute | solution.py:364
  212.2 4.2 %collective-permute-done.49 = bf16[1,2,128,512]{3,2,1,0:T(8,128)(2,1)S(1)} collective-permute-done((bf16[1,2,128,512]{3,2,1,0:T(8,128)(2,1)}, bf16[1,2,128,512]{3,2,1,0:T(8,128)(2,1)S(1)}, u32[]{:S(2)}, u32[]{:S(2)}) %collective-permute-start.49) | collective-permute-done | bytes 262176 | tf_op jit(solution)/shard_map/ppermute | solution.py:365
  229.4 4.0 %collective-permute-done.50 = bf16[1,2,128,512]{3,2,1,0:T(8,128)(2,1)} collective-permute-done((bf16[1,2,128,512]{3,2,1,0:T(8,128)(2,1)S(1)}, bf16[1,2,128,512]{3,2,1,0:T(8,128)(2,1)}, u32[]{:S(2)}, u32[]{:S(2)}) %collective-permute-start.50) | collective-permute-done | bytes 262176 | tf_op jit(solution)/shard_map/ppermute | solution.py:365
  251.5 4.3 %collective-permute-done.31 = bf16[1,2,128,512]{3,2,1,0:T(8,128)(2,1)S(1)} collective-permute-done((bf16[1,2,128,512]{3,2,1,0:T(8,128)(2,1)}, bf16[1,2,128,512]{3,2,1,0:T(8,128)(2,1)S(1)}, u32[]{:S(2)}, u32[]{:S(2)}) %collective-permute-start.31) | collective-permute-done | bytes 262176 | tf_op jit(solution)/shard_map/ppermute | solution.py:365
  257.1 4.3 %collective-permute-done.51 = bf16[1,2,128,512]{3,2,1,0:T(8,128)(2,1)S(1)} collective-permute-done((bf16[1,2,128,512]{3,2,1,0:T(8,128)(2,1)}, bf16[1,2,128,512]{3,2,1,0:T(8,128)(2,1)S(1)}, u32[]{:S(2)}, u32[]{:S(2)}) %collective-permute-start.51) | collective-permute-done | bytes 262176 | tf_op jit(solution)/shard_map/ppermute | solution.py:365
  263.1 5.5 %collective-permute-start.41 = (bf16[1,2,128,512]{3,2,1,0:T(8,128)(2,1)S(1)}, bf16[1,2,128,512]{3,2,1,0:T(8,128)(2,1)S(1)}, u32[]{:S(2)}, u32[]{:S(2)}) collective-permute-start(bf16[1,2,128,512]{3,2,1,0:T(8,128)(2,1)S(1)} %collective-permute-done.28), channel_id=1, source_target_pairs={{0,4},{4,8},{8,12},{1,5},{5,9},{9,13},{2,6},{6,10},{10,14},{3,7},{... | collective-permute-start | bytes 786440 | tf_op jit(solution)/shard_map/ppermute | solution.py:364
  281.4 4.6 %collective-permute-start.57 = (bf16[1,2,128,512]{3,2,1,0:T(8,128)(2,1)S(1)}, bf16[1,2,128,512]{3,2,1,0:T(8,128)(2,1)S(1)}, u32[]{:S(2)}, u32[]{:S(2)}) collective-permute-start(bf16[1,2,128,512]{3,2,1,0:T(8,128)(2,1)S(1)} %collective-permute-done.52), channel_id=1, source_target_pairs={{0,4},{4,8},{8,12},{1,5},{5,9},{9,13},{2,6},{6,10},{10,14},{3,7},{... | collective-permute-start | bytes 786440 | tf_op jit(solution)/shard_map/ppermute | solution.py:364
  287.9 9.4 %collective-permute-done.56 = bf16[1,2,128,512]{3,2,1,0:T(8,128)(2,1)S(1)} collective-permute-done((bf16[1,2,128,512]{3,2,1,0:T(8,128)(2,1)}, bf16[1,2,128,512]{3,2,1,0:T(8,128)(2,1)S(1)}, u32[]{:S(2)}, u32[]{:S(2)}) %collective-permute-start.56) | collective-permute-done | bytes 262176 | tf_op jit(solution)/shard_map/ppermute | solution.py:364
  297.3 4.3 %collective-permute-start.47 = (bf16[1,2,128,512]{3,2,1,0:T(8,128)(2,1)S(1)}, bf16[1,2,128,512]{3,2,1,0:T(8,128)(2,1)S(1)}, u32[]{:S(2)}, u32[]{:S(2)}) collective-permute-start(bf16[1,2,128,512]{3,2,1,0:T(8,128)(2,1)S(1)} %collective-permute-done.43), channel_id=1, source_target_pairs={{0,4},{4,8},{8,12},{1,5},{5,9},{9,13},{2,6},{6,10},{10,14},{3,7},{... | collective-permute-start | bytes 786440 | tf_op jit(solution)/shard_map/ppermute | solution.py:364
  303.1 4.1 %collective-permute-start.58 = (bf16[1,2,128,512]{3,2,1,0:T(8,128)(2,1)S(1)}, bf16[1,2,128,512]{3,2,1,0:T(8,128)(2,1)S(1)}, u32[]{:S(2)}, u32[]{:S(2)}) collective-permute-start(bf16[1,2,128,512]{3,2,1,0:T(8,128)(2,1)S(1)} %collective-permute-done.56), channel_id=1, source_target_pairs={{0,4},{4,8},{8,12},{1,5},{5,9},{9,13},{2,6},{6,10},{10,14},{3,7},{... | collective-permute-start | bytes 786440 | tf_op jit(solution)/shard_map/ppermute | solution.py:364
  312.3 7.4 %collective-permute-done.58 = bf16[1,2,128,512]{3,2,1,0:T(8,128)(2,1)S(1)} collective-permute-done((bf16[1,2,128,512]{3,2,1,0:T(8,128)(2,1)S(1)}, bf16[1,2,128,512]{3,2,1,0:T(8,128)(2,1)S(1)}, u32[]{:S(2)}, u32[]{:S(2)}) %collective-permute-start.58) | collective-permute-done | bytes 262176 | tf_op jit(solution)/shard_map/ppermute | solution.py:364
  (211 shorter events, 139.5 us)
Async XLA Ops:
  7.2 51.6 %all-gather.3.cloned.1.call-start = ((), (), s32[]{:S(2)}) async-start(), calls=%async_computation | async-start | bytes 5242880 | tf_op jit(solution)/shard_map/all_gather | solution.py:329
  8.8 28.0 %collective-permute-start = (bf16[2,2,1024]{2,1,0:T(2,128)(2,1)S(1)}, bf16[2,2,1024]{2,1,0:T(2,128)(2,1)S(1)}, u32[]{:S(2)}, u32[]{:S(2)}) collective-permute-start(bf16[2,2,1024]{2,1,0:T(2,128)(2,1)S(1)} %get-tuple-element.47), channel_id=1, source_target_pairs={{0,4},{4,0},{8,12},{12,8},{1,5},{5,1},{9,13},{13,9},{2,6},{6,2},{1... | collective-permute-start | bytes 24584 | tf_op jit(solution)/shard_map/ppermute | solution.py:305
  11.8 26.4 %collective-permute-start.1 = (bf16[2,2,1024]{2,1,0:T(2,128)(2,1)S(1)}, bf16[2,2,1024]{2,1,0:T(2,128)(2,1)S(1)}, u32[]{:S(2)}, u32[]{:S(2)}) collective-permute-start(bf16[2,2,1024]{2,1,0:T(2,128)(2,1)S(1)} %get-tuple-element.49), channel_id=1, source_target_pairs={{0,8},{4,12},{8,0},{12,4},{1,9},{5,13},{9,1},{13,5},{2,10},{6,14},... | collective-permute-start | bytes 24584 | tf_op jit(solution)/shard_map/ppermute | solution.py:305
  17.0 52.7 %collective-permute-start.3 = (bf16[2,2,128,512]{3,2,1,0:T(8,128)(2,1)S(1)}, bf16[2,2,128,512]{3,2,1,0:T(8,128)(2,1)S(1)}, u32[]{:S(2)}, u32[]{:S(2)}) collective-permute-start(bf16[2,2,128,512]{3,2,1,0:T(8,128)(2,1)S(1)} %get-tuple-element.17), channel_id=1, source_target_pairs={{0,4},{4,0},{8,12},{12,8},{1,5},{5,1},{9,13},{13,9},{2,6},{6,2},{1... | collective-permute-start | bytes 1572872 | tf_op jit(solution)/shard_map/ppermute | solution.py:305
  17.5 52.2 %collective-permute-start.4 = (bf16[2,2,128,512]{3,2,1,0:T(8,128)(2,1)S(1)}, bf16[2,2,128,512]{3,2,1,0:T(8,128)(2,1)S(1)}, u32[]{:S(2)}, u32[]{:S(2)}) collective-permute-start(bf16[2,2,128,512]{3,2,1,0:T(8,128)(2,1)S(1)} %get-tuple-element.19), channel_id=1, source_target_pairs={{0,8},{4,12},{8,0},{12,4},{1,9},{5,13},{9,1},{13,5},{2,10},{6,14},... | collective-permute-start | bytes 1572872 | tf_op jit(solution)/shard_map/ppermute | solution.py:305
  17.5 52.2 %collective-permute-start.5 = (bf16[2,2,128,512]{3,2,1,0:T(8,128)(2,1)S(1)}, bf16[2,2,128,512]{3,2,1,0:T(8,128)(2,1)S(1)}, u32[]{:S(2)}, u32[]{:S(2)}) collective-permute-start(bf16[2,2,128,512]{3,2,1,0:T(8,128)(2,1)S(1)} %get-tuple-element.16), channel_id=1, source_target_pairs={{0,12},{4,8},{8,4},{12,0},{1,13},{5,9},{9,5},{13,1},{2,14},{6,10},... | collective-permute-start | bytes 1572872 | tf_op jit(solution)/shard_map/ppermute | solution.py:305
  97.1 27.3 %collective-permute-start.12 = (f32[8,128]{1,0:T(8,128)S(1)}, f32[8,128]{1,0:T(8,128)S(1)}, u32[]{:S(2)}, u32[]{:S(2)}) collective-permute-start(f32[8,128]{1,0:T(8,128)S(1)} %add_select_fusion.4), channel_id=1, source_target_pairs={{0,4},{4,0},{8,12},{12,8},{1,5},{5,1},{9,13},{13,9},{2,6},{6,2},{1... | collective-permute-start | bytes 12296 | tf_op jit(solution)/shard_map/ppermute | solution.py:344
  141.7 29.5 %collective-permute-start.25 = (bf16[1,2,128,512]{3,2,1,0:T(8,128)(2,1)S(1)}, bf16[1,2,128,512]{3,2,1,0:T(8,128)(2,1)S(1)}, u32[]{:S(2)}, u32[]{:S(2)}) collective-permute-start(bf16[1,2,128,512]{3,2,1,0:T(8,128)(2,1)S(1)} %get-tuple-element.41), channel_id=1, source_target_pairs={{4,0},{8,4},{12,8},{5,1},{9,5},{13,9},{6,2},{10,6},{14,10},{7,3},{... | collective-permute-start | bytes 786440 | tf_op jit(solution)/shard_map/ppermute | solution.py:365
  162.6 21.2 %collective-permute-start.24 = (bf16[1,2,128,512]{3,2,1,0:T(8,128)(2,1)S(1)}, bf16[1,2,128,512]{3,2,1,0:T(8,128)(2,1)S(1)}, u32[]{:S(2)}, u32[]{:S(2)}) collective-permute-start(bf16[1,2,128,512]{3,2,1,0:T(8,128)(2,1)S(1)} %get-tuple-element.41), channel_id=1, source_target_pairs={{0,4},{4,8},{8,12},{1,5},{5,9},{9,13},{2,6},{6,10},{10,14},{3,7},{... | collective-permute-start | bytes 786440 | tf_op jit(solution)/shard_map/ppermute | solution.py:364
  196.8 19.7 %collective-permute-start.49 = (bf16[1,2,128,512]{3,2,1,0:T(8,128)(2,1)}, bf16[1,2,128,512]{3,2,1,0:T(8,128)(2,1)S(1)}, u32[]{:S(2)}, u32[]{:S(2)}) collective-permute-start(bf16[1,2,128,512]{3,2,1,0:T(8,128)(2,1)} %get-tuple-element.37), channel_id=1, source_target_pairs={{4,0},{8,4},{12,8},{5,1},{9,5},{13,9},{6,2},{10,6},{14,10},{7,3},{... | collective-permute-start | bytes 786440 | tf_op jit(solution)/shard_map/ppermute | solution.py:365
  198.4 25.8 %collective-permute-start.40 = (bf16[1,2,128,512]{3,2,1,0:T(8,128)(2,1)}, bf16[1,2,128,512]{3,2,1,0:T(8,128)(2,1)}, u32[]{:S(2)}, u32[]{:S(2)}) collective-permute-start(bf16[1,2,128,512]{3,2,1,0:T(8,128)(2,1)} %copy-done.11), channel_id=1, source_target_pairs={{0,4},{4,8},{8,12},{1,5},{5,9},{9,13},{2,6},{6,10},{10,14},{3,7},{... | collective-permute-start | bytes 786440 | tf_op jit(solution)/shard_map/ppermute | solution.py:364
  204.7 20.8 %collective-permute-start.48 = (bf16[1,2,128,512]{3,2,1,0:T(8,128)(2,1)}, bf16[1,2,128,512]{3,2,1,0:T(8,128)(2,1)}, u32[]{:S(2)}, u32[]{:S(2)}) collective-permute-start(bf16[1,2,128,512]{3,2,1,0:T(8,128)(2,1)} %get-tuple-element.37), channel_id=1, source_target_pairs={{0,4},{4,8},{8,12},{1,5},{5,9},{9,13},{2,6},{6,10},{10,14},{3,7},{... | collective-permute-start | bytes 786440 | tf_op jit(solution)/shard_map/ppermute | solution.py:364
  226.8 23.3 %collective-permute-start.54 = (bf16[1,2,128,512]{3,2,1,0:T(8,128)(2,1)}, bf16[1,2,128,512]{3,2,1,0:T(8,128)(2,1)S(1)}, u32[]{:S(2)}, u32[]{:S(2)}) collective-permute-start(bf16[1,2,128,512]{3,2,1,0:T(8,128)(2,1)} %collective-permute-done.53), channel_id=1, source_target_pairs={{4,0},{8,4},{12,8},{5,1},{9,5},{13,9},{6,2},{10,6},{14,10},{7,3},{... | collective-permute-start | bytes 786440 | tf_op jit(solution)/shard_map/ppermute | solution.py:365
  228.1 27.7 %collective-permute-start.31 = (bf16[1,2,128,512]{3,2,1,0:T(8,128)(2,1)}, bf16[1,2,128,512]{3,2,1,0:T(8,128)(2,1)S(1)}, u32[]{:S(2)}, u32[]{:S(2)}) collective-permute-start(bf16[1,2,128,512]{3,2,1,0:T(8,128)(2,1)} %collective-permute-done.30), channel_id=1, source_target_pairs={{4,0},{8,4},{12,8},{5,1},{9,5},{13,9},{6,2},{10,6},{14,10},{7,3},{... | collective-permute-start | bytes 786440 | tf_op jit(solution)/shard_map/ppermute | solution.py:365
  233.4 28.0 %collective-permute-start.51 = (bf16[1,2,128,512]{3,2,1,0:T(8,128)(2,1)}, bf16[1,2,128,512]{3,2,1,0:T(8,128)(2,1)S(1)}, u32[]{:S(2)}, u32[]{:S(2)}) collective-permute-start(bf16[1,2,128,512]{3,2,1,0:T(8,128)(2,1)} %collective-permute-done.50), channel_id=1, source_target_pairs={{4,0},{8,4},{12,8},{5,1},{9,5},{13,9},{6,2},{10,6},{14,10},{7,3},{... | collective-permute-start | bytes 786440 | tf_op jit(solution)/shard_map/ppermute | solution.py:365
  238.9 24.1 %collective-permute-start.42 = (bf16[1,2,128,512]{3,2,1,0:T(8,128)(2,1)S(1)}, bf16[1,2,128,512]{3,2,1,0:T(8,128)(2,1)S(1)}, u32[]{:S(2)}, u32[]{:S(2)}) collective-permute-start(bf16[1,2,128,512]{3,2,1,0:T(8,128)(2,1)S(1)} %collective-permute-done.32), channel_id=1, source_target_pairs={{0,4},{4,8},{8,12},{1,5},{5,9},{9,13},{2,6},{6,10},{10,14},{3,7},{... | collective-permute-start | bytes 786440 | tf_op jit(solution)/shard_map/ppermute | solution.py:364
  244.6 24.0 %collective-permute-start.52 = (bf16[1,2,128,512]{3,2,1,0:T(8,128)(2,1)S(1)}, bf16[1,2,128,512]{3,2,1,0:T(8,128)(2,1)S(1)}, u32[]{:S(2)}, u32[]{:S(2)}) collective-permute-start(bf16[1,2,128,512]{3,2,1,0:T(8,128)(2,1)S(1)} %copy-done.13), channel_id=1, source_target_pairs={{0,4},{4,8},{8,12},{1,5},{5,9},{9,13},{2,6},{6,10},{10,14},{3,7},{... | collective-permute-start | bytes 786440 | tf_op jit(solution)/shard_map/ppermute | solution.py:364
  250.2 21.7 %collective-permute-start.35 = (bf16[1,2,128,512]{3,2,1,0:T(8,128)(2,1)}, bf16[1,2,128,512]{3,2,1,0:T(8,128)(2,1)S(1)}, u32[]{:S(2)}, u32[]{:S(2)}) collective-permute-start(bf16[1,2,128,512]{3,2,1,0:T(8,128)(2,1)} %collective-permute-done.34), channel_id=1, source_target_pairs={{4,0},{8,4},{12,8},{5,1},{9,5},{13,9},{6,2},{10,6},{14,10},{7,3},{... | collective-permute-start | bytes 786440 | tf_op jit(solution)/shard_map/ppermute | solution.py:365
  255.8 19.9 %collective-permute-start.39 = (bf16[1,2,128,512]{3,2,1,0:T(8,128)(2,1)S(1)}, bf16[1,2,128,512]{3,2,1,0:T(8,128)(2,1)S(1)}, u32[]{:S(2)}, u32[]{:S(2)}) collective-permute-start(bf16[1,2,128,512]{3,2,1,0:T(8,128)(2,1)S(1)} %collective-permute-done.38), channel_id=1, source_target_pairs={{4,0},{8,4},{12,8},{5,1},{9,5},{13,9},{6,2},{10,6},{14,10},{7,3},{... | collective-permute-start | bytes 786440 | tf_op jit(solution)/shard_map/ppermute | solution.py:365
  271.8 36.7 %collective-permute-start.44 = (bf16[1,2,128,512]{3,2,1,0:T(8,128)(2,1)}, bf16[1,2,128,512]{3,2,1,0:T(8,128)(2,1)S(1)}, u32[]{:S(2)}, u32[]{:S(2)}) collective-permute-start(bf16[1,2,128,512]{3,2,1,0:T(8,128)(2,1)} %collective-permute-done.40), channel_id=1, source_target_pairs={{0,4},{4,8},{8,12},{1,5},{5,9},{9,13},{2,6},{6,10},{10,14},{3,7},{... | collective-permute-start | bytes 786440 | tf_op jit(solution)/shard_map/ppermute | solution.py:364
  275.7 44.3 %collective-permute-start.46 = (bf16[1,2,128,512]{3,2,1,0:T(8,128)(2,1)S(1)}, bf16[1,2,128,512]{3,2,1,0:T(8,128)(2,1)S(1)}, u32[]{:S(2)}, u32[]{:S(2)}) collective-permute-start(bf16[1,2,128,512]{3,2,1,0:T(8,128)(2,1)S(1)} %collective-permute-done.42), channel_id=1, source_target_pairs={{0,4},{4,8},{8,12},{1,5},{5,9},{9,13},{2,6},{6,10},{10,14},{3,7},{... | collective-permute-start | bytes 786440 | tf_op jit(solution)/shard_map/ppermute | solution.py:364
  281.4 21.7 %collective-permute-start.57 = (bf16[1,2,128,512]{3,2,1,0:T(8,128)(2,1)S(1)}, bf16[1,2,128,512]{3,2,1,0:T(8,128)(2,1)S(1)}, u32[]{:S(2)}, u32[]{:S(2)}) collective-permute-start(bf16[1,2,128,512]{3,2,1,0:T(8,128)(2,1)S(1)} %collective-permute-done.52), channel_id=1, source_target_pairs={{0,4},{4,8},{8,12},{1,5},{5,9},{9,13},{2,6},{6,10},{10,14},{3,7},{... | collective-permute-start | bytes 786440 | tf_op jit(solution)/shard_map/ppermute | solution.py:364
  286.0 26.4 %collective-permute-start.45 = (bf16[1,2,128,512]{3,2,1,0:T(8,128)(2,1)S(1)}, bf16[1,2,128,512]{3,2,1,0:T(8,128)(2,1)S(1)}, u32[]{:S(2)}, u32[]{:S(2)}) collective-permute-start(bf16[1,2,128,512]{3,2,1,0:T(8,128)(2,1)S(1)} %collective-permute-done.41), channel_id=1, source_target_pairs={{0,4},{4,8},{8,12},{1,5},{5,9},{9,13},{2,6},{6,10},{10,14},{3,7},{... | collective-permute-start | bytes 786440 | tf_op jit(solution)/shard_map/ppermute | solution.py:364
  297.3 22.7 %collective-permute-start.47 = (bf16[1,2,128,512]{3,2,1,0:T(8,128)(2,1)S(1)}, bf16[1,2,128,512]{3,2,1,0:T(8,128)(2,1)S(1)}, u32[]{:S(2)}, u32[]{:S(2)}) collective-permute-start(bf16[1,2,128,512]{3,2,1,0:T(8,128)(2,1)S(1)} %collective-permute-done.43), channel_id=1, source_target_pairs={{0,4},{4,8},{8,12},{1,5},{5,9},{9,13},{2,6},{6,10},{10,14},{3,7},{... | collective-permute-start | bytes 786440 | tf_op jit(solution)/shard_map/ppermute | solution.py:364
  (60 other events, 788.5 us)
Sparse Core Ops, SparseCore 0:
  9.6 37.2 all-gather.2

commit v2 on v1

--- a/solution.py
+++ b/solution.py
@@ -70,7 +70,7 @@
     coil = jnp.concatenate(
         [sens_real * real - sens_imag * imag, sens_real * imag + sens_imag * real], 0
     )
-    both = nt(ey[...], data_parts(coil))
+    both = nt(ey[...], coil.astype(bf16))
     half_real = both[:tiles, :rows] + both[tiles:, rows:]
     half_imag = both[:tiles, rows:] - both[tiles:, :rows]
     turned = jnp.concatenate(
@@ -80,41 +80,47 @@
         ],
         1,
     )
-    grid = nn(data_parts(turned), mx[...])
+    grid = nn(turned.astype(bf16), mx[...])
     size = grid.shape[1] // 2
     grid_ref[pl.ds(2 * step, tiles, stride=channels), :] = grid[:, :size]
     grid_ref[pl.ds(2 * step + 1, tiles, stride=channels), :] = grid[:, size:]
 
 
-def sample_tiles(block_ref, weights_ref, grid_ref, sums_ref, out_ref):
-    tiles = weights_ref.shape[0]
-    channels = grid_ref.shape[0] // tiles
+def sample_tiles(block_ref, weights, grid_ref, sums_ref, out_ref):
+    count = weights[0].shape[0]
+    channels = sums_ref.shape[1]
     sums_ref[...] = jnp.zeros_like(sums_ref)
 
-    def one(tile, carry):
-        start = pl.multiple_of(tile * channels, channels)
-        high, low = split(grid_ref[pl.ds(start, channels), :])
-        product = nn(jnp.concatenate([high, low], 0), weights_ref[tile])
-        sums_ref[block_ref[tile]] += product[:channels] + product[channels:]
-        return carry
-
-    lax.fori_loop(0, tiles, one, 0, unroll=32)
+    for group, weights_ref in enumerate(weights):
+
+        def one(place, carry):
+            tile = group * count + place
+            start = pl.multiple_of(tile * channels, channels)
+            high, low = split(grid_ref[pl.ds(start, channels), :])
+            product = nn(jnp.concatenate([high, low], 0), weights_ref[place])
+            sums_ref[block_ref[tile]] += product[:channels] + product[channels:]
+            return carry
+
+        lax.fori_loop(0, count, one, 0, unroll=True)
     out_ref[...] = sums_ref[...].astype(bf16)
 
 
-def spread_tiles(block_ref, weights_ref, parts_ref, grid_ref):
-    tiles = weights_ref.shape[0]
-    channels = grid_ref.shape[0] // tiles
-
-    def one(tile, carry):
-        start = pl.multiple_of(tile * channels, channels)
-        product = nt(parts_ref[block_ref[tile]], weights_ref[tile])
-        if product.shape[0] > channels:
-            product = product[:channels] + product[channels:]
-        grid_ref[pl.ds(start, channels), :] = product
-        return carry
-
-    lax.fori_loop(0, tiles, one, 0, unroll=32)
+def spread_tiles(block_ref, weights, parts_ref, grid_ref):
+    count = weights[0].shape[0]
+    channels = grid_ref.shape[0] // (count * len(weights))
+
+    for group, weights_ref in enumerate(weights):
+
+        def one(place, carry):
+            tile = group * count + place
+            start = pl.multiple_of(tile * channels, channels)
+            product = nt(parts_ref[block_ref[tile]], weights_ref[place])
+            if product.shape[0] > channels:
+                product = product[:channels] + product[channels:]
+            grid_ref[pl.ds(start, channels), :] = product
+            return carry
+
+        lax.fori_loop(0, count, one, 0, unroll=True)
 
 
 def adjoint_image(step, tiles, ey_back, mx_back, turn_ref, grid_ref):
@@ -148,7 +154,8 @@
     dots_ref[...] = total
 
 
-def measured_kernel(block, samples, weights, mx, eb, turn, images, grid):
+def measured_kernel(block, samples, *refs):
+    *weights, mx, eb, turn, images, grid = refs
     plane = pl.program_id(0)
     coils = images.shape[0]
 
@@ -158,7 +165,7 @@
 
     for coil in range(coils):
         real, imag = adjoint_image(
-            coil * pl.num_programs(0) + plane, weights.shape[0], eb, mx, turn, grid
+            coil * pl.num_programs(0) + plane, turn.shape[2], eb, mx, turn, grid
         )
         images[coil, 0, 0] = real
         images[coil, 0, 1] = imag
@@ -188,8 +195,9 @@
     add_dots(dots, [(right_side[0], right_side[0])])
 
 
-def forward_kernel(block, picture, *refs):
-    *sens, weights, ey, mx, turn, samples, grid, sums = refs
+def forward_kernel(coils, block, picture, *refs):
+    sens = refs[:coils]
+    *weights, ey, mx, turn, samples, grid, sums = refs[coils:]
     plane = pl.program_id(0)
     for coil, sens_ref in enumerate(sens):
         forward_image(
@@ -224,16 +232,16 @@
     ]
 
 
-def first_kernel(peers, block, *refs):
-    samples = refs[:peers]
-    right_side, *sens, weights, mx, eb, turn, applied, grid, parts = refs[peers:]
+def first_kernel(peers, coils, block, *refs):
+    samples, weights, sens = refs[:peers], refs[peers : 2 * peers], refs[2 * peers :][:coils]
+    mx, eb, turn, right_side, applied, grid, parts = refs[2 * peers + coils :]
     plane = pl.program_id(0)
 
     @pl.when(plane == 0)
     def _():
         spread_sum(block, samples, weights, grid, parts)
 
-    images = back_images(len(sens), plane, weights.shape[0], eb, mx, turn, grid)
+    images = back_images(len(sens), plane, turn.shape[2], eb, mx, turn, grid)
     total = combine(images, sens)
     for part in range(2):
         applied[0, part] = total[part] + damping * right_side[0, part]
@@ -243,10 +251,10 @@
     return totals[0:1, 0:1] / (totals[1:2, 0:1] + damping * totals[0:1, 0:1])
 
 
-def second_kernel(peers, block, *refs):
-    samples = refs[:peers]
-    totals, right_side, applied, residual, *sens = refs[peers:-8]
-    weights, mx, eb, turn, rounded, dots, grid, parts = refs[-8:]
+def second_kernel(peers, coils, block, *refs):
+    samples, weights, sens = refs[:peers], refs[peers : 2 * peers], refs[2 * peers :][:coils]
+    mx, eb, turn, totals, right_side, applied, residual = refs[2 * peers + coils :][:7]
+    rounded, dots, grid, parts = refs[-4:]
     plane = pl.program_id(0)
 
     @pl.when(plane == 0)
@@ -254,7 +262,7 @@
         dots[...] = jnp.zeros_like(dots)
         spread_sum(block, samples, weights, grid, parts)
 
-    images = back_images(len(sens), plane, weights.shape[0], eb, mx, turn, grid)
+    images = back_images(len(sens), plane, turn.shape[2], eb, mx, turn, grid)
     total = combine(images, sens)
     for part in range(2):
         vector = residual[0, part]
@@ -297,36 +305,48 @@
 
     coil_index = lax.axis_index("coil")
 
+    def swapped(array, axis, k):
+        return lax.ppermute(array, axis, [(i, i ^ k) for i in range(lax.axis_size(axis))])
+
+    def everywhere(array, axis):
+        bit = 1
+        while bit < lax.axis_size(axis):
+            bit *= 2
+        pieces = {0: array}
+        while bit > 1:
+            bit //= 2
+            for k in sorted(pieces):
+                pieces[k ^ bit] = swapped(pieces[k], axis, bit)
+        return [pieces[k] for k in sorted(pieces)]
+
     def to_planes(array):
         pieces = []
         for k in range(coil_count):
             part = lax.dynamic_slice_in_dim(array, (coil_index ^ k) * own_planes, own_planes, 0)
-            if k > 0:
-                part = lax.ppermute(part, "coil", [(i, i ^ k) for i in range(coil_count)])
-            pieces.append(part)
+            pieces.append(swapped(part, "coil", k) if k > 0 else part)
         return pieces
 
-    sens = to_planes(sens_maps[0])
+    measured = to_planes(kspace[0])
+    sens_source, *measured = lax.optimization_barrier((sens_maps[0], *measured))
+    sens = to_planes(sens_source)
+    all_weights = everywhere(weights, "pencil")
 
     packed = jnp.concatenate([tile_slot, tile_block, send_list.reshape(-1)])
     places = lax.all_gather(packed, "pencil")
-    slots = places[:, :tile_count]
-    block_of = (
-        places[:, tile_count : 2 * tile_count]
-        + blocks_dev * jnp.arange(peers, dtype=jnp.int32)[:, None]
-    ).reshape(-1)
     lists = places[:, 2 * tile_count :].reshape(peers, peers, cap)
-    holder = jnp.arange(peers, dtype=jnp.int32)[:, None]
+    holder = (jnp.arange(peers, dtype=jnp.int32) ^ lax.axis_index("pencil"))[:, None]
+    own_places = jnp.take(places, holder[:, 0], axis=0)
+    slots = own_places[:, :tile_count]
+    block_of = (own_places[:, tile_count : 2 * tile_count] + blocks_dev * holder).reshape(-1)
     brick = (slots // cap * brick_dev + lists[slots // cap, holder, slots % cap]).reshape(-1)
     line = brick // runs
     run = brick % runs
 
-    measured = jnp.stack(to_planes(kspace[0]))
+    measured = jnp.stack(measured)
     measured = lax.all_gather(
         measured.reshape(channels, blocks_dev, size), "pencil", axis=1, tiled=True
     )
     measured = jnp.swapaxes(measured, 0, 1)
-    all_weights = lax.all_gather(weights, "pencil", axis=0, tiled=True)
 
     cos_y, sin_y = wave(
         line - columns // 2, jnp.arange(columns, dtype=jnp.int32) - columns // 2, columns
@@ -340,10 +360,7 @@
 
     def exchanged(partial, axis="pencil"):
         count = lax.axis_size(axis)
-        return [partial] + [
-            lax.ppermute(partial, axis, [(i, i ^ k) for i in range(count)])
-            for k in range(1, count)
-        ]
+        return [partial] + [swapped(partial, axis, k) for k in range(1, count)]
 
     def summed_over(axes, dots):
         for axis in axes:
@@ -354,33 +371,12 @@
         return tree_sum([part.astype(f32) for part in samples])
 
     def gathered(own):
-        ahead = [(i, i + 1) for i in range(coil_count - 1)]
-        behind = [(i + 1, i) for i in range(coil_count - 1)]
-        lines = []
-        for plane in range(own_planes):
-            piece = own[plane : plane + 1]
-            lower, upper = [piece], [piece]
-            for _ in range(1, coil_count):
-                lower.append(lax.ppermute(lower[-1], "coil", ahead))
-                upper.append(lax.ppermute(upper[-1], "coil", behind))
-            lines.append([(lower[k], upper[-k]) for k in range(coil_count)])
-        return [[line[k] for line in lines] for k in range(coil_count)]
-
-    def chosen(k, pair):
-        return (pair[0] if k == 0 else jnp.where(coil_index >= k, *pair)).astype(f32)
-
-    def assembled(value_of):
-        out = jnp.zeros((planes, 2, rows, columns), f32)
-        for k in range(coil_count):
-            for plane in range(own_planes):
-                place = (coil_index + coil_count - k) % coil_count * own_planes + plane
-                out = lax.dynamic_update_slice(out, value_of(k, plane), (place, 0, 0, 0))
-        return out
+        return lax.all_gather(own, "coil", axis=0, tiled=True).astype(f32)
 
     picture_shape = (own_planes, 2, rows, columns)
 
     if rows % 128 == 0 and columns % 128 == 0 and size % 128 == 0 and channels % 16 == 0:
-        ey = table_parts(jnp.concatenate([cos_y, sin_y], 0), 1)
+        ey = jnp.concatenate([cos_y, sin_y], 0).astype(bf16)
         eb = jnp.concatenate(
             [jnp.concatenate([cos_y, sin_y], 1), jnp.concatenate([-sin_y, cos_y], 1)], 0
         )
@@ -388,7 +384,7 @@
         mx = jnp.concatenate(
             [jnp.concatenate([cos_x, -sin_x], 1), jnp.concatenate([sin_x, cos_x], 1)], 0
         )
-        mx, mx_back = table_parts(mx, 0), table_parts(mx, 1)
+        mx, mx_back = mx.astype(bf16), table_parts(mx, 1)
         places_spec = pl.BlockSpec(memory_space=pltpu.SMEM)
         plane_spec = pl.BlockSpec((1, 2, rows, columns), lambda p: (p, 0, 0, 0))
         all_coils = pl.BlockSpec(
@@ -416,12 +412,12 @@
         def shaped(shape, dtype=f32):
             return jax.ShapeDtypeStruct(shape, dtype)
 
-        image_flops = 3 * images_count * 8 * tiles * rows * (columns + size)
+        image_flops = 2 * images_count * 8 * tiles * rows * (columns + size)
         tile_flops = 4 * tiles * channels * size * size
         grid = (own_planes,)
 
         def measured_images():
-            inputs = [block_of, measured, all_weights, mx_back, eb, turn_back]
+            inputs = [block_of, measured, *all_weights, mx_back, eb, turn_back]
             return call(
                 measured_kernel,
                 grid,
@@ -451,9 +447,9 @@
             )
 
         def forward(picture):
-            tail = [all_weights, ey, mx, turn]
+            tail = [*all_weights, ey, mx, turn]
             return call(
-                forward_kernel,
+                functools.partial(forward_kernel, coil_count),
                 grid,
                 [block_of, picture, *sens, *tail],
                 [places_spec] + [plane_spec] * (1 + coil_count) + [whole_block(i) for i in tail],
@@ -465,39 +461,37 @@
 
         parts_scratch = pltpu.VMEM((blocks, 2 * channels, size), bf16)
 
-        def first(samples, right_side):
-            tail = [all_weights, mx_back, eb, turn_back]
-            inputs = [block_of, *samples, right_side, *sens, *tail]
+        def back(kernel, samples, tables, vectors, outs, out_specs):
+            inputs = [*samples, *all_weights]
+            tables = [mx_back, eb, turn_back, *tables]
             return call(
-                functools.partial(first_kernel, peers),
+                functools.partial(kernel, peers, coil_count),
                 grid,
-                inputs,
+                [block_of, *inputs, *sens, *tables, *vectors],
                 [places_spec]
-                + [whole_block(i) for i in samples]
-                + [plane_spec] * (1 + coil_count)
-                + [whole_block(i) for i in tail],
-                shaped(picture_shape),
-                plane_spec,
+                + [whole_block(i) for i in inputs]
+                + [plane_spec] * coil_count
+                + [whole_block(i) for i in tables]
+                + [plane_spec] * len(vectors),
+                outs,
+                out_specs,
                 [grid_scratch, parts_scratch],
                 image_flops + tile_flops,
             )
 
+        def first(samples, right_side):
+            return back(
+                first_kernel, samples, [], [right_side], shaped(picture_shape), plane_spec
+            )
+
         def second(samples, totals, right_side, applied, residual):
-            tail = [all_weights, mx_back, eb, turn_back]
-            inputs = [block_of, *samples, totals, right_side, applied, residual, *sens, *tail]
-            return call(
-                functools.partial(second_kernel, peers),
-                grid,
-                inputs,
-                [places_spec]
-                + [whole_block(i) for i in samples]
-                + [whole_block(totals)]
-                + [plane_spec] * (3 + coil_count)
-                + [whole_block(i) for i in tail],
+            return back(
+                second_kernel,
+                samples,
+                [totals],
+                [right_side, applied, residual],
                 [shaped(picture_shape, bf16), shaped((8, 128))],
                 [plane_spec, whole_block(shaped((8, 128)))],
-                [grid_scratch, parts_scratch],
-                image_flops + tile_flops,
             )
 
     else:
@@ -507,7 +501,7 @@
         shape = (coil_count, own_planes)
         block_map = (block_of[:, None] == jnp.arange(blocks, dtype=jnp.int32)).astype(f32)
         tc, ts = turn[0][:, None, None], turn[1][:, None, None]
-        wide_weights = all_weights.astype(f32)
+        wide_weights = jnp.concatenate(all_weights, 0).astype(f32)
 
         def forward(picture):
             coil_real = map_real * picture[None, :, 0] - map_imag * picture[None, :, 1]
@@ -586,7 +580,7 @@
             return (residual - scale * again).astype(bf16), dots
 
     right_side, rounded, dots = start(measured_images())
-    start_everywhere = gathered(rounded)
+    start_all = gathered(rounded)
     samples = exchanged(forward(right_side))
     dots = summed_over(["pencil"], dots)
     energy = jnp.sum(jnp.square(added(samples)))
@@ -597,29 +591,22 @@
     first_step = start_norm / start_curve
     applied = first(samples, right_side)
     residual = right_side - first_step * applied
-    residual_everywhere = gathered(residual.astype(bf16))
+    residual_all = gathered(residual.astype(bf16))
     samples = exchanged(forward(residual))
     rounded, dots = second(samples, first_totals, right_side, applied, residual)
-    mixed_everywhere = gathered(rounded)
+    mixed = everywhere(rounded, "coil")
     totals = summed_over(["coil", "pencil"], dots)
     ratio = totals[0, 0] / start_norm
     curve = totals[1, 0] + ratio * (totals[2, 0] + totals[3, 0]) + ratio * ratio * start_curve
     second_step = totals[0, 0] / curve
     share = second_step / first_step
-
-    def picture_of(k, plane):
-        return (first_step + second_step * ratio) * chosen(
-            k, start_everywhere[k][plane]
-        ) + second_step * chosen(k, residual_everywhere[k][plane])
-
-    def residual_of(k, plane):
-        return (
-            (1.0 - share + share * ratio) * chosen(k, residual_everywhere[k][plane])
-            + share * chosen(k, mixed_everywhere[k][plane])
-            - share * ratio * chosen(k, start_everywhere[k][plane])
-        )
-
-    return assembled(picture_of), assembled(residual_of)
+    picture = (first_step + second_step * ratio) * start_all + second_step * residual_all
+    out = (1.0 - share + share * ratio) * residual_all - share * ratio * start_all
+    for k, piece in enumerate(mixed):
+        place = ((coil_index ^ k) * own_planes, 0, 0, 0)
+        known = lax.dynamic_slice(out, place, piece.shape)
+        out = lax.dynamic_update_slice(out, known + share * piece.astype(f32), place)
+    return picture, out
 
 
 def solution(mesh):

time: 336 us -> 241 us (0.72)
  starting transfers between devices: 132 us -> 40.5 us
  waiting for transfers between devices: 72.8 us -> 61.8 us
  blocking collectives: 11 us -> 20 us
  Pallas kernels: 61.2 us -> 54.3 us
  other arithmetic: 18.6 us -> 24.3 us
    ppermute x60 -> x30, starting transfers between devices: 132 us -> 40.3 us  [swapped(): lax.ppermute(array, axis, [(i, i ^ k) for i in range(lax.axis_size(axis))])]
    ppermute x60 -> x30, waiting for transfers between devices: 72.1 us -> 61.8 us  [swapped(): lax.ppermute(array, axis, [(i, i ^ k) for i in range(lax.axis_size(axis))])]
    unnamed x1, blocking collectives: 4.99 us -> 14.1 us
    pallas_call x6, Pallas kernels: 61.2 us -> 54.3 us  [call(): pl.pallas_call(kernel, grid=grid, in_specs=specs, out_specs=out_specs, ou...]
    sub x0 -> x1, other arithmetic: none -> 5.35 us  [on_device(): (1.0 - share + share * ratio) * residual_all - share * ratio * start_all]
    dynamic_update_slice x9 -> x4, other arithmetic: 5.6 us -> 0.93 us  [on_device(): lax.dynamic_update_slice(out, known + share * piece.astype(f32), place)]
  transfers between devices with their start and end apart: 61 -> 32, of which waited for: 18 -> 11; matrix products, arithmetic and copies ran while one was open for 8% -> 16% of each run, Pallas kernels for 10% -> 20%
where the time goes in v2:
time: 241 us; the launch traced here: 240 us
  waiting for transfers between devices  61.8 us (26%)
  Pallas kernels  54.3 us (23%)
  starting transfers between devices  40.5 us (17%)
  other arithmetic  24.3 us (10%)
  between operations  21.6 us (9%)
  blocking collectives  20 us (8%)
  local copies, waits for them, and re-layouts  17.8 us (7%)
    ppermute x30, waiting for transfers between devices, swapped(): lax.ppermute(array, axis, [(i, i ^ k) for i in range(lax.axis_size(axis))])  61.8 us
    pallas_call x6, Pallas kernels, call(): pl.pallas_call(kernel, grid=grid, in_specs=specs, out_specs=out_specs, ou...  54.3 us
    ppermute x30, starting transfers between devices, swapped(): lax.ppermute(array, axis, [(i, i ^ k) for i in range(lax.axis_size(axis))])  40.3 us
    unnamed x1, blocking collectives  14.1 us
    all_gather x1, blocking collectives, on_device(): lax.all_gather(measured.reshape(channels, blocks_dev, size), 'pencil', ax...  5.86 us
    sub x1, other arithmetic, on_device(): (1.0 - share + share * ratio) * residual_all - share * ratio * start_all  5.35 us
    unnamed x42, local copies, waits for them, and re-layouts  5.28 us
  transfers between devices with their start and end apart: 32, of which 11 were waited for; matrix products, arithmetic and copies ran while one was open for 16% of the time, Pallas kernels for 20%

profile of v2, /device:TPU:0, one launch (start us, length us, event | category | flops | bytes accessed | tf_op | source)
XLA Modules:
  0.0 240.2 jit_solution(1556454927128226740)
XLA Ops:
  7.2 3.0 %collective-permute-start.4 = (bf16[32,128,128]{2,1,0:T(8,128)(2,1)}, bf16[32,128,128]{2,1,0:T(8,128)(2,1)S(1)}, u32[]{:S(2)}, u32[]{:S(2)}) collective-permute-start(bf16[32,128,128]{2,1,0:T(8,128)(2,1)} %refs_4_.7), channel_id=1, source_target_pairs={{0,2},{1,3},{2,0},{3,1},{4,6},{5,7},{6,4},{7,5},{8,10},{9,11},{10,... | collective-permute-start | bytes 3145736 | tf_op jit(solution)/shard_map/ppermute | solution.py:309
  13.2 2.6 %collective-permute-start.1 = (bf16[2,2,1024]{2,1,0:T(2,128)(2,1)}, bf16[2,2,1024]{2,1,0:T(2,128)(2,1)}, u32[]{:S(2)}, u32[]{:S(2)}) collective-permute-start(bf16[2,2,1024]{2,1,0:T(2,128)(2,1)} %get-tuple-element.39), channel_id=1, source_target_pairs={{0,8},{4,12},{8,0},{12,4},{1,9},{5,13},{9,1},{13,5},{2,10},{6,14},... | collective-permute-start | bytes 24584 | tf_op jit(solution)/shard_map/ppermute | solution.py:309
  19.6 14.1 %all-reduce = s32[384]{0:T(512)S(1)} all-reduce(s32[384]{0:T(512)S(1)} %add_dynamic-update-slice_fusion.4), channel_id=2, replica_groups=mesh['scan'=2,'coil'=4,'pencil'=4] {'pencil'}, use_global_device_ids=true, to_apply=%add | all-reduce | flops 384 | bytes 3072
  37.2 1.9 fusion.10
  43.8 3.1 %constant_dynamic-slice_fusion = (bf16[2,2,128,512]{3,2,1,0:T(8,128)(2,1)}, bf16[2,2,128,512]{3,2,1,0:T(8,128)(2,1)}, bf16[2,2,128,512]{3,2,1,0:T(8,128)(2,1)}, bf16[2,2,128,512]{3,2,1,0:T(8,128)(2,1)}) fusion(bf16[8,2,128,512]{3,2,1,0:T(8,128)(2,1)} %bitcast.34, s32[]{:T(128)S(6)} %select_n.223, s32[]{:T(128)S(6)} %select_n.222, s32[]{:T(128)S(6)} %select_n.221, ...), kind=kLoop, calls=%fused_computation.80 | loop fusion | bytes 4194320 | tf_op jit(solution)/shard_map/dynamic_slice | solution.py:325
  48.7 2.6 %collective-permute-start.7 = (bf16[2,2,128,512]{3,2,1,0:T(8,128)(2,1)}, bf16[2,2,128,512]{3,2,1,0:T(8,128)(2,1)}, u32[]{:S(2)}, u32[]{:S(2)}) collective-permute-start(bf16[2,2,128,512]{3,2,1,0:T(8,128)(2,1)} %get-tuple-element.29), channel_id=1, source_target_pairs={{0,8},{4,12},{8,0},{12,4},{1,9},{5,13},{9,1},{13,5},{2,10},{6,14},... | collective-permute-start | bytes 1572872 | tf_op jit(solution)/shard_map/ppermute | solution.py:309
  56.8 5.9 %all_gather.17 = bf16[16,32,128]{2,0,1:T(8,128)(2,1)} all-gather(bf16[16,8,128]{2,0,1:T(8,128)(2,1)S(1)} %copy.9), channel_id=1, replica_groups=mesh['scan'=2,'coil'=4,'pencil'=4] {'pencil'}, dimensions={1}, use_global_device_ids=true | all-gather | bytes 163840 | tf_op jit(solution)/shard_map/all_gather | solution.py:346
  64.0 10.6 %shard_map.77.images = f32[4,2,2,128,512]{4,3,2,1,0:T(8,128)} custom-call(s32[128]{0:T(128)} %reshape.439.block, bf16[32,16,128]{2,1,0:T(8,128)(2,1)} %bitcast.35, bf16[32,128,128]{2,1,0:T(8,128)(2,1)} %refs_4_.7, bf16[32,128,128]{2,1,0:T(8,128)(2,1)} %copy-done.1, bf16[32,128,128]{2,1,0:T(8,128)(2,1)} %copy-done, bf16[32,128,128]{2,1,0:T(8,128)(2,1)} %copy-done.2, ...), custom_call_target="tpu_custom_call" | custom-call | flops 1476395008 | bytes 6423040 | tf_op jit(solution)/shard_map/pallas_call | solution.py:399
  74.7 12.6 %collective-permute-done.7.refs_2_.refs_10_ = bf16[2,2,128,512]{3,2,1,0:T(8,128)(2,1)} collective-permute-done((bf16[2,2,128,512]{3,2,1,0:T(8,128)(2,1)}, bf16[2,2,128,512]{3,2,1,0:T(8,128)(2,1)}, u32[]{:S(2)}, u32[]{:S(2)}) %collective-permute-start.7) | collective-permute-done | bytes 524320 | tf_op jit(solution)/shard_map/ppermute | solution.py:309
  87.2 5.2 %shard_map.78 = (f32[2,2,128,512]{3,2,1,0:T(8,128)}, bf16[2,2,128,512]{3,2,1,0:T(8,128)(2,1)}, f32[8,128]{1,0:T(8,128)}) custom-call(f32[4,2,2,128,512]{4,3,2,1,0:T(8,128)} %shard_map.77.images, bf16[2,2,128,512]{3,2,1,0:T(8,128)(2,1)} %get-tuple-element.31.refs_0_.refs_8_, bf16[2,2,128,512]{3,2,1,0:T(8,128)(2,1)} %collective-permute-done.6.refs_1_.refs_9_, ...), custom_call_target="tpu_custom_call" | custom-call | flops 4194304 | bytes 6291456 | tf_op jit(solution)/shard_map/pallas_call | solution.py:399
  94.7 7.4 %shard_map.79.refs_0_ = bf16[32,16,128]{2,1,0:T(8,128)(2,1)} custom-call(s32[128]{0:T(128)} %reshape.439.block, f32[2,2,128,512]{3,2,1,0:T(8,128)} %get-tuple-element.17.picture.refs_15_.refs_16_, bf16[2,2,128,512]{3,2,1,0:T(8,128)(2,1)} %get-tuple-element.31.refs_0_.refs_8_, bf16[2,2,128,512]{3,2,1,0:T(8,128)(2,1)} %collective-permute-done.6.refs_1_.refs_9_, ...), custom_call_target="tpu_custom_call" | custom-call | flops 1476395008 | bytes 7864832 | tf_op jit(solution)/shard_map/pallas_call | solution.py:399
  105.8 2.0 collective-permute-done.10.refs_2_
  112.0 10.9 %collective-permute-start.15 = (f32[8,128]{1,0:T(8,128)S(1)}, f32[8,128]{1,0:T(8,128)S(1)}, u32[]{:S(2)}, u32[]{:S(2)}) collective-permute-start(f32[8,128]{1,0:T(8,128)S(1)} %add_select_fusion.4), channel_id=1, source_target_pairs={{0,4},{4,0},{8,12},{12,8},{1,5},{5,1},{9,13},{13,9},{2,6},{6,2},{1... | collective-permute-start | bytes 12296 | tf_op jit(solution)/shard_map/ppermute | solution.py:309
  125.4 11.3 %shard_map.80.refs_17_ = f32[2,2,128,512]{3,2,1,0:T(8,128)} custom-call(s32[128]{0:T(128)} %reshape.439.block, bf16[32,16,128]{2,1,0:T(8,128)(2,1)} %shard_map.79.refs_0_, bf16[32,16,128]{2,1,0:T(8,128)(2,1)} %copy-done.9, bf16[32,16,128]{2,1,0:T(8,128)(2,1)} %copy-done.7, bf16[32,16,128]{2,1,0:T(8,128)(2,1)} %copy-done.8, bf16[32,128,128]{2,1,0:T(8,128)(2,1)} %refs_4_.7, ...), custom_call_target="tpu_custom_call" | custom-call | flops 1476395008 | bytes 9961984 | tf_op jit(solution)/shard_map/pallas_call | solution.py:399
  139.1 2.7 %fusion.29 = (bf16[2,2,128,512]{3,2,1,0:T(8,128)(2,1)}, f32[2,2,128,512]{3,2,1,0:T(8,128)}) fusion(f32[2,2,128,512]{3,2,1,0:T(8,128)S(1)} %copy-done.4, f32[2,2,128,512]{3,2,1,0:T(8,128)} %shard_map.80.refs_17_, f32[]{:T(128)S(6)} %div.62), kind=kLoop, calls=%fused_computation.122 | loop fusion | flops 786432 | bytes 3670020 | tf_op jit(solution)/shard_map/convert_element_type | solution.py:594
  141.7 7.4 %shard_map.81.refs_0_ = bf16[32,16,128]{2,1,0:T(8,128)(2,1)} custom-call(s32[128]{0:T(128)} %reshape.439.block, f32[2,2,128,512]{3,2,1,0:T(8,128)} %get-tuple-element.23.picture.refs_18_, bf16[2,2,128,512]{3,2,1,0:T(8,128)(2,1)} %get-tuple-element.31.refs_0_.refs_8_, bf16[2,2,128,512]{3,2,1,0:T(8,128)(2,1)} %collective-permute-done.6.refs_1_.refs_9_, ...), custom_call_target="tpu_custom_call" | custom-call | flops 1476395008 | bytes 7864832 | tf_op jit(solution)/shard_map/pallas_call | solution.py:399
  151.3 4.6 %collective-permute-done.19.refs_2_ = bf16[32,16,128]{2,1,0:T(8,128)(2,1)S(1)} collective-permute-done((bf16[32,16,128]{2,1,0:T(8,128)(2,1)}, bf16[32,16,128]{2,1,0:T(8,128)(2,1)S(1)}, u32[]{:S(2)}, u32[]{:S(2)}) %collective-permute-start.19) | collective-permute-done | bytes 131104 | tf_op jit(solution)/shard_map/ppermute | solution.py:309
  155.9 2.0 collective-permute-done.20.refs_3_
  158.6 12.4 %shard_map.82 = (bf16[2,2,128,512]{3,2,1,0:T(8,128)(2,1)}, f32[8,128]{1,0:T(8,128)}) custom-call(s32[128]{0:T(128)} %reshape.439.block, bf16[32,16,128]{2,1,0:T(8,128)(2,1)} %shard_map.81.refs_0_, bf16[32,16,128]{2,1,0:T(8,128)(2,1)} %copy-done.15, bf16[32,16,128]{2,1,0:T(8,128)(2,1)} %copy-done.16, bf16[32,16,128]{2,1,0:T(8,128)(2,1)} %copy-done.17, ...), custom_call_target="tpu_custom_call" | custom-call | flops 1476395008 | bytes 12063232 | tf_op jit(solution)/shard_map/pallas_call | solution.py:399
  177.0 2.7 %collective-permute-done.23 = f32[8,128]{1,0:T(8,128)S(1)} collective-permute-done((f32[8,128]{1,0:T(8,128)}, f32[8,128]{1,0:T(8,128)S(1)}, u32[]{:S(2)}, u32[]{:S(2)}) %collective-permute-start.23) | collective-permute-done | bytes 4128 | tf_op jit(solution)/shard_map/ppermute | solution.py:309
  190.6 26.6 %collective-permute-done.28 = bf16[2,2,128,512]{3,2,1,0:T(8,128)(2,1)S(1)} collective-permute-done((bf16[2,2,128,512]{3,2,1,0:T(8,128)(2,1)}, bf16[2,2,128,512]{3,2,1,0:T(8,128)(2,1)S(1)}, u32[]{:S(2)}, u32[]{:S(2)}) %collective-permute-start.28) | collective-permute-done | bytes 524320 | tf_op jit(solution)/shard_map/ppermute | solution.py:309
  217.2 5.4 %fusion.1 = (f32[8,2,128,512]{3,2,1,0:T(8,128)S(1)}, f32[8,2,128,512]{3,2,1,0:T(8,128)}) fusion(bf16[8,2,128,512]{3,2,1,0:T(8,128)(2,1)} %all-gather.4.cloned.1.call-done, bf16[8,2,128,512]{3,2,1,0:T(8,128)(2,1)} %all-gather.6.cloned.1.call-done, f32[]{:T(128)S(6)} %mul.221, f32[]{:T(128)S(6)} %add.293, f32[]{:T(128)S(6)} %div.64, f32[]{:T(128)S(6)} %add.291), kind=kLoop, calls=%fused_computation.7 | loop fusion | flops 8388608 | bytes 12582928 | tf_op jit(solution)/shard_map/sub | solution.py:604
  223.3 7.8 %collective-permute-done.29 = bf16[2,2,128,512]{3,2,1,0:T(8,128)(2,1)S(1)} collective-permute-done((bf16[2,2,128,512]{3,2,1,0:T(8,128)(2,1)S(1)}, bf16[2,2,128,512]{3,2,1,0:T(8,128)(2,1)S(1)}, u32[]{:S(2)}, u32[]{:S(2)}) %collective-permute-start.29) | collective-permute-done | bytes 524320 | tf_op jit(solution)/shard_map/ppermute | solution.py:309
  231.4 2.0 copy-done.3
  (143 shorter events, 52.0 us)
Async XLA Ops:
  7.2 210.1 %all-gather.4.cloned.1.call-start = ((), (), s32[]{:S(2)}) async-start(), calls=%async_computation | async-start | bytes 2621440 | tf_op jit(solution)/shard_map/all_gather | solution.py:374
  7.2 33.4 %collective-permute-start.4 = (bf16[32,128,128]{2,1,0:T(8,128)(2,1)}, bf16[32,128,128]{2,1,0:T(8,128)(2,1)S(1)}, u32[]{:S(2)}, u32[]{:S(2)}) collective-permute-start(bf16[32,128,128]{2,1,0:T(8,128)(2,1)} %refs_4_.7), channel_id=1, source_target_pairs={{0,2},{1,3},{2,0},{3,1},{4,6},{5,7},{6,4},{7,5},{8,10},{9,11},{10,... | collective-permute-start | bytes 3145736 | tf_op jit(solution)/shard_map/ppermute | solution.py:309
  10.2 52.5 %collective-permute-start.3 = (bf16[32,128,128]{2,1,0:T(8,128)(2,1)}, bf16[32,128,128]{2,1,0:T(8,128)(2,1)S(1)}, u32[]{:S(2)}, u32[]{:S(2)}) collective-permute-start(bf16[32,128,128]{2,1,0:T(8,128)(2,1)} %refs_4_.7), channel_id=1, source_target_pairs={{0,1},{1,0},{2,3},{3,2},{4,5},{5,4},{6,7},{7,6},{8,9},{9,8},{10,11... | collective-permute-start | bytes 3145736 | tf_op jit(solution)/shard_map/ppermute | solution.py:309
  11.6 32.2 %collective-permute-start = (bf16[2,2,1024]{2,1,0:T(2,128)(2,1)}, bf16[2,2,1024]{2,1,0:T(2,128)(2,1)}, u32[]{:S(2)}, u32[]{:S(2)}) collective-permute-start(bf16[2,2,1024]{2,1,0:T(2,128)(2,1)} %get-tuple-element.37), channel_id=1, source_target_pairs={{0,4},{4,0},{8,12},{12,8},{1,5},{5,1},{9,13},{13,9},{2,6},{6,2},{1... | collective-permute-start | bytes 24584 | tf_op jit(solution)/shard_map/ppermute | solution.py:309
  13.2 30.6 %collective-permute-start.1 = (bf16[2,2,1024]{2,1,0:T(2,128)(2,1)}, bf16[2,2,1024]{2,1,0:T(2,128)(2,1)}, u32[]{:S(2)}, u32[]{:S(2)}) collective-permute-start(bf16[2,2,1024]{2,1,0:T(2,128)(2,1)} %get-tuple-element.39), channel_id=1, source_target_pairs={{0,8},{4,12},{8,0},{12,4},{1,9},{5,13},{9,1},{13,5},{2,10},{6,14},... | collective-permute-start | bytes 24584 | tf_op jit(solution)/shard_map/ppermute | solution.py:309
  15.8 28.0 %collective-permute-start.2 = (bf16[2,2,1024]{2,1,0:T(2,128)(2,1)S(1)}, bf16[2,2,1024]{2,1,0:T(2,128)(2,1)}, u32[]{:S(2)}, u32[]{:S(2)}) collective-permute-start(bf16[2,2,1024]{2,1,0:T(2,128)(2,1)S(1)} %get-tuple-element.36), channel_id=1, source_target_pairs={{0,12},{4,8},{8,4},{12,0},{1,13},{5,9},{9,5},{13,1},{2,14},{6,10},... | collective-permute-start | bytes 24584 | tf_op jit(solution)/shard_map/ppermute | solution.py:309
  40.6 22.1 %collective-permute-start.5 = (bf16[32,128,128]{2,1,0:T(8,128)(2,1)S(1)}, bf16[32,128,128]{2,1,0:T(8,128)(2,1)S(1)}, u32[]{:S(2)}, u32[]{:S(2)}) collective-permute-start(bf16[32,128,128]{2,1,0:T(8,128)(2,1)S(1)} %collective-permute-done.4.refs_2_.refs_6_), channel_id=1, source_target_pairs={{0,1},{1,0},{2,3},{3,2},{4,5},{5,4},{6,7},{7,6},{8,9},{9,8},{10,11... | collective-permute-start | bytes 3145736 | tf_op jit(solution)/shard_map/ppermute | solution.py:309
  46.9 27.8 %collective-permute-start.6 = (bf16[2,2,128,512]{3,2,1,0:T(8,128)(2,1)}, bf16[2,2,128,512]{3,2,1,0:T(8,128)(2,1)}, u32[]{:S(2)}, u32[]{:S(2)}) collective-permute-start(bf16[2,2,128,512]{3,2,1,0:T(8,128)(2,1)} %get-tuple-element.30), channel_id=1, source_target_pairs={{0,4},{4,0},{8,12},{12,8},{1,5},{5,1},{9,13},{13,9},{2,6},{6,2},{1... | collective-permute-start | bytes 1572872 | tf_op jit(solution)/shard_map/ppermute | solution.py:309
  48.7 38.5 %collective-permute-start.7 = (bf16[2,2,128,512]{3,2,1,0:T(8,128)(2,1)}, bf16[2,2,128,512]{3,2,1,0:T(8,128)(2,1)}, u32[]{:S(2)}, u32[]{:S(2)}) collective-permute-start(bf16[2,2,128,512]{3,2,1,0:T(8,128)(2,1)} %get-tuple-element.29), channel_id=1, source_target_pairs={{0,8},{4,12},{8,0},{12,4},{1,9},{5,13},{9,1},{13,5},{2,10},{6,14},... | collective-permute-start | bytes 1572872 | tf_op jit(solution)/shard_map/ppermute | solution.py:309
  51.3 35.9 %collective-permute-start.8 = (bf16[2,2,128,512]{3,2,1,0:T(8,128)(2,1)}, bf16[2,2,128,512]{3,2,1,0:T(8,128)(2,1)}, u32[]{:S(2)}, u32[]{:S(2)}) collective-permute-start(bf16[2,2,128,512]{3,2,1,0:T(8,128)(2,1)} %get-tuple-element.28), channel_id=1, source_target_pairs={{0,12},{4,8},{8,4},{12,0},{1,13},{5,9},{9,5},{13,1},{2,14},{6,10},... | collective-permute-start | bytes 1572872 | tf_op jit(solution)/shard_map/ppermute | solution.py:309
  92.4 124.8 %all-gather.6.cloned.1.call-start = ((), (), s32[]{:S(2)}) async-start(), calls=%async_computation.1 | async-start | bytes 2621440 | tf_op jit(solution)/shard_map/all_gather | solution.py:374
  103.6 6.0 %collective-permute-start.11 = (bf16[32,16,128]{2,1,0:T(8,128)(2,1)}, bf16[32,16,128]{2,1,0:T(8,128)(2,1)S(1)}, u32[]{:S(2)}, u32[]{:S(2)}) collective-permute-start(bf16[32,16,128]{2,1,0:T(8,128)(2,1)} %shard_map.79.refs_0_), channel_id=1, source_target_pairs={{0,3},{1,2},{2,1},{3,0},{4,7},{5,6},{6,5},{7,4},{8,11},{9,10},{10,... | collective-permute-start | bytes 393224 | tf_op jit(solution)/shard_map/ppermute | solution.py:309
  103.6 6.0 %collective-permute-start.9 = (bf16[32,16,128]{2,1,0:T(8,128)(2,1)}, bf16[32,16,128]{2,1,0:T(8,128)(2,1)S(1)}, u32[]{:S(2)}, u32[]{:S(2)}) collective-permute-start(bf16[32,16,128]{2,1,0:T(8,128)(2,1)} %shard_map.79.refs_0_), channel_id=1, source_target_pairs={{0,1},{1,0},{2,3},{3,2},{4,5},{5,4},{6,7},{7,6},{8,9},{9,8},{10,11... | collective-permute-start | bytes 393224 | tf_op jit(solution)/shard_map/ppermute | solution.py:309
  104.2 7.1 %collective-permute-start.12 = (f32[8,128]{1,0:T(8,128)S(1)}, f32[8,128]{1,0:T(8,128)S(1)}, u32[]{:S(2)}, u32[]{:S(2)}) collective-permute-start(f32[8,128]{1,0:T(8,128)S(1)} %copy-done.19), channel_id=1, source_target_pairs={{0,1},{1,0},{2,3},{3,2},{4,5},{5,4},{6,7},{7,6},{8,9},{9,8},{10,11... | collective-permute-start | bytes 12296 | tf_op jit(solution)/shard_map/ppermute | solution.py:309
  104.3 7.0 %collective-permute-start.13 = (f32[8,128]{1,0:T(8,128)S(1)}, f32[8,128]{1,0:T(8,128)S(1)}, u32[]{:S(2)}, u32[]{:S(2)}) collective-permute-start(f32[8,128]{1,0:T(8,128)S(1)} %copy-done.19), channel_id=1, source_target_pairs={{0,2},{1,3},{2,0},{3,1},{4,6},{5,7},{6,4},{7,5},{8,10},{9,11},{10,... | collective-permute-start | bytes 12296 | tf_op jit(solution)/shard_map/ppermute | solution.py:309
  112.0 24.7 %collective-permute-start.15 = (f32[8,128]{1,0:T(8,128)S(1)}, f32[8,128]{1,0:T(8,128)S(1)}, u32[]{:S(2)}, u32[]{:S(2)}) collective-permute-start(f32[8,128]{1,0:T(8,128)S(1)} %add_select_fusion.4), channel_id=1, source_target_pairs={{0,4},{4,0},{8,12},{12,8},{1,5},{5,1},{9,13},{13,9},{2,6},{6,2},{1... | collective-permute-start | bytes 12296 | tf_op jit(solution)/shard_map/ppermute | solution.py:309
  122.9 13.8 %collective-permute-start.16 = (f32[8,128]{1,0:T(8,128)S(1)}, f32[8,128]{1,0:T(8,128)S(1)}, u32[]{:S(2)}, u32[]{:S(2)}) collective-permute-start(f32[8,128]{1,0:T(8,128)S(1)} %add_select_fusion.4), channel_id=1, source_target_pairs={{0,8},{4,12},{8,0},{12,4},{1,9},{5,13},{9,1},{13,5},{2,10},{6,14},... | collective-permute-start | bytes 12296 | tf_op jit(solution)/shard_map/ppermute | solution.py:309
  124.0 12.7 %collective-permute-start.17 = (f32[8,128]{1,0:T(8,128)S(1)}, f32[8,128]{1,0:T(8,128)S(1)}, u32[]{:S(2)}, u32[]{:S(2)}) collective-permute-start(f32[8,128]{1,0:T(8,128)S(1)} %add_select_fusion.4), channel_id=1, source_target_pairs={{0,12},{4,8},{8,4},{12,0},{1,13},{5,9},{9,5},{13,1},{2,14},{6,10},... | collective-permute-start | bytes 12296 | tf_op jit(solution)/shard_map/ppermute | solution.py:309
  149.4 6.5 %collective-permute-start.19 = (bf16[32,16,128]{2,1,0:T(8,128)(2,1)}, bf16[32,16,128]{2,1,0:T(8,128)(2,1)S(1)}, u32[]{:S(2)}, u32[]{:S(2)}) collective-permute-start(bf16[32,16,128]{2,1,0:T(8,128)(2,1)} %shard_map.81.refs_0_), channel_id=1, source_target_pairs={{0,2},{1,3},{2,0},{3,1},{4,6},{5,7},{6,4},{7,5},{8,10},{9,11},{10,... | collective-permute-start | bytes 393224 | tf_op jit(solution)/shard_map/ppermute | solution.py:309
  151.2 6.7 %collective-permute-start.20 = (bf16[32,16,128]{2,1,0:T(8,128)(2,1)}, bf16[32,16,128]{2,1,0:T(8,128)(2,1)S(1)}, u32[]{:S(2)}, u32[]{:S(2)}) collective-permute-start(bf16[32,16,128]{2,1,0:T(8,128)(2,1)} %shard_map.81.refs_0_), channel_id=1, source_target_pairs={{0,3},{1,2},{2,1},{3,0},{4,7},{5,6},{6,5},{7,4},{8,11},{9,10},{10,... | collective-permute-start | bytes 393224 | tf_op jit(solution)/shard_map/ppermute | solution.py:309
  174.0 5.7 %collective-permute-start.23 = (f32[8,128]{1,0:T(8,128)}, f32[8,128]{1,0:T(8,128)S(1)}, u32[]{:S(2)}, u32[]{:S(2)}) collective-permute-start(f32[8,128]{1,0:T(8,128)} %get-tuple-element.19), channel_id=1, source_target_pairs={{0,12},{4,8},{8,4},{12,0},{1,13},{5,9},{9,5},{13,1},{2,14},{6,10},... | collective-permute-start | bytes 12296 | tf_op jit(solution)/shard_map/ppermute | solution.py:309
  175.4 41.8 %collective-permute-start.28 = (bf16[2,2,128,512]{3,2,1,0:T(8,128)(2,1)}, bf16[2,2,128,512]{3,2,1,0:T(8,128)(2,1)S(1)}, u32[]{:S(2)}, u32[]{:S(2)}) collective-permute-start(bf16[2,2,128,512]{3,2,1,0:T(8,128)(2,1)} %get-tuple-element.21), channel_id=1, source_target_pairs={{0,8},{4,12},{8,0},{12,4},{1,9},{5,13},{9,1},{13,5},{2,10},{6,14},... | collective-permute-start | bytes 1572872 | tf_op jit(solution)/shard_map/ppermute | solution.py:309
  182.3 40.5 %collective-permute-start.27 = (bf16[2,2,128,512]{3,2,1,0:T(8,128)(2,1)}, bf16[2,2,128,512]{3,2,1,0:T(8,128)(2,1)S(1)}, u32[]{:S(2)}, u32[]{:S(2)}) collective-permute-start(bf16[2,2,128,512]{3,2,1,0:T(8,128)(2,1)} %get-tuple-element.21), channel_id=1, source_target_pairs={{0,4},{4,0},{8,12},{12,8},{1,5},{5,1},{9,13},{13,9},{2,6},{6,2},{1... | collective-permute-start | bytes 1572872 | tf_op jit(solution)/shard_map/ppermute | solution.py:309
  217.2 13.9 %collective-permute-start.29 = (bf16[2,2,128,512]{3,2,1,0:T(8,128)(2,1)S(1)}, bf16[2,2,128,512]{3,2,1,0:T(8,128)(2,1)S(1)}, u32[]{:S(2)}, u32[]{:S(2)}) collective-permute-start(bf16[2,2,128,512]{3,2,1,0:T(8,128)(2,1)S(1)} %collective-permute-done.28), channel_id=1, source_target_pairs={{0,4},{4,0},{8,12},{12,8},{1,5},{5,1},{9,13},{13,9},{2,6},{6,2},{1... | collective-permute-start | bytes 1572872 | tf_op jit(solution)/shard_map/ppermute | solution.py:309
  (28 other events, 258.5 us)
Sparse Core Ops, SparseCore 0:
  92.5 55.8 all-gather.3
  150.0 64.4 all-gather.5

commit v3 on v2

--- a/solution.py
+++ b/solution.py
@@ -65,8 +65,8 @@
     tiles = turn_ref.shape[1]
     rows = turn_ref.shape[2]
     channels = grid_ref.shape[0] // tiles
-    sens_real = sens_ref[0, 0].astype(f32)
-    sens_imag = sens_ref[0, 1].astype(f32)
+    sens_real = sens_ref[0, 0, 0].astype(f32)
+    sens_imag = sens_ref[0, 0, 1].astype(f32)
     coil = jnp.concatenate(
         [sens_real * real - sens_imag * imag, sens_real * imag + sens_imag * real], 0
     )
@@ -174,8 +174,8 @@
 def combine(images, sens):
     total_real = total_imag = 0.0
     for (real, imag), sens_ref in zip(images, sens):
-        sens_real = sens_ref[0, 0].astype(f32)
-        sens_imag = sens_ref[0, 1].astype(f32)
+        sens_real = sens_ref[0, 0, 0].astype(f32)
+        sens_imag = sens_ref[0, 0, 1].astype(f32)
         total_real += sens_real * real + sens_imag * imag
         total_imag += sens_real * imag - sens_imag * real
     return total_real, total_imag
@@ -319,6 +319,18 @@
                 pieces[k ^ bit] = swapped(pieces[k], axis, bit)
         return [pieces[k] for k in sorted(pieces)]
 
+    first_bits = [1 << bit for bit in range(coil_count.bit_length() - 1)]
+
+    def completed(own, sent):
+        pieces = {0: own}
+        for bit, piece in zip(first_bits, sent):
+            pieces[bit] = piece
+        for bit in first_bits:
+            for k in range(coil_count):
+                if k not in pieces and (k ^ bit) in pieces:
+                    pieces[k] = swapped(pieces[k ^ bit], "coil", bit)
+        return [pieces[k] for k in range(coil_count)]
+
     def to_planes(array):
         pieces = []
         for k in range(coil_count):
@@ -326,27 +338,30 @@
             pieces.append(swapped(part, "coil", k) if k > 0 else part)
         return pieces
 
-    measured = to_planes(kspace[0])
-    sens_source, *measured = lax.optimization_barrier((sens_maps[0], *measured))
-    sens = to_planes(sens_source)
+    sens = lax.all_to_all(sens_maps[0], "coil", split_axis=0, concat_axis=0, tiled=True)
+    sens = sens.reshape(coil_count, own_planes, 2, rows, columns)
+    measured = jnp.stack(to_planes(kspace[0]))
+    by_coil = jnp.arange(coil_count, dtype=jnp.int32) ^ coil_index
+    measured = jnp.take(measured, by_coil, axis=0)
     all_weights = everywhere(weights, "pencil")
 
     packed = jnp.concatenate([tile_slot, tile_block, send_list.reshape(-1)])
-    places = lax.all_gather(packed, "pencil")
-    lists = places[:, 2 * tile_count :].reshape(peers, peers, cap)
+    places = jnp.stack(everywhere(packed, "pencil"))
     holder = (jnp.arange(peers, dtype=jnp.int32) ^ lax.axis_index("pencil"))[:, None]
-    own_places = jnp.take(places, holder[:, 0], axis=0)
-    slots = own_places[:, :tile_count]
-    block_of = (own_places[:, tile_count : 2 * tile_count] + blocks_dev * holder).reshape(-1)
+    by_owner = jnp.take(places, holder[:, 0], axis=0)
+    lists = by_owner[:, 2 * tile_count :].reshape(peers, peers, cap)
+    slots = places[:, :tile_count]
+    block_of = (places[:, tile_count : 2 * tile_count] + blocks_dev * holder).reshape(-1)
     brick = (slots // cap * brick_dev + lists[slots // cap, holder, slots % cap]).reshape(-1)
     line = brick // runs
     run = brick % runs
 
-    measured = jnp.stack(measured)
-    measured = lax.all_gather(
-        measured.reshape(channels, blocks_dev, size), "pencil", axis=1, tiled=True
-    )
-    measured = jnp.swapaxes(measured, 0, 1)
+    measured = measured.reshape(channels, blocks_dev, size)
+    measured = jnp.concatenate(everywhere(jnp.swapaxes(measured, 0, 1), "pencil"), 0)
+    measured_block = (
+        places[:, tile_count : 2 * tile_count]
+        + blocks_dev * jnp.arange(peers, dtype=jnp.int32)[:, None]
+    ).reshape(-1)
 
     cos_y, sin_y = wave(
         line - columns // 2, jnp.arange(columns, dtype=jnp.int32) - columns // 2, columns
@@ -369,9 +384,6 @@
 
     def added(samples):
         return tree_sum([part.astype(f32) for part in samples])
-
-    def gathered(own):
-        return lax.all_gather(own, "coil", axis=0, tiled=True).astype(f32)
 
     picture_shape = (own_planes, 2, rows, columns)
 
@@ -387,6 +399,10 @@
         mx, mx_back = mx.astype(bf16), table_parts(mx, 1)
         places_spec = pl.BlockSpec(memory_space=pltpu.SMEM)
         plane_spec = pl.BlockSpec((1, 2, rows, columns), lambda p: (p, 0, 0, 0))
+        sens_specs = [
+            pl.BlockSpec((1, 1, 2, rows, columns), functools.partial(lambda c, p: (c, p, 0, 0, 0), c))
+            for c in range(coil_count)
+        ]
         all_coils = pl.BlockSpec(
             (coil_count, 1, 2, rows, columns), lambda p: (0, p, 0, 0, 0)
         )
@@ -417,7 +433,7 @@
         grid = (own_planes,)
 
         def measured_images():
-            inputs = [block_of, measured, *all_weights, mx_back, eb, turn_back]
+            inputs = [measured_block, measured, *all_weights, mx_back, eb, turn_back]
             return call(
                 measured_kernel,
                 grid,
@@ -438,8 +454,15 @@
             return call(
                 start_kernel,
                 (own_planes, rows // chunk),
-                [images, *sens],
-                [coils_spec] + [spec] * coil_count,
+                [images] + [sens] * coil_count,
+                [coils_spec]
+                + [
+                    pl.BlockSpec(
+                        (1, 1, 2, chunk, columns),
+                        functools.partial(lambda c, p, r: (c, p, 0, r, 0), c),
+                    )
+                    for c in range(coil_count)
+                ],
                 [shaped(picture_shape), shaped(picture_shape, bf16), shaped((8, 128))],
                 [spec, spec, whole_block(shaped((8, 128)))],
                 [],
@@ -451,8 +474,8 @@
             return call(
                 functools.partial(forward_kernel, coil_count),
                 grid,
-                [block_of, picture, *sens, *tail],
-                [places_spec] + [plane_spec] * (1 + coil_count) + [whole_block(i) for i in tail],
+                [block_of, picture] + [sens] * coil_count + tail,
+                [places_spec, plane_spec] + sens_specs + [whole_block(i) for i in tail],
                 shaped(sums_shape, bf16),
                 whole_block(shaped(sums_shape)),
                 [grid_scratch, pltpu.VMEM(sums_shape, f32)],
@@ -467,10 +490,10 @@
             return call(
                 functools.partial(kernel, peers, coil_count),
                 grid,
-                [block_of, *inputs, *sens, *tables, *vectors],
+                [block_of, *inputs] + [sens] * coil_count + tables + vectors,
                 [places_spec]
                 + [whole_block(i) for i in inputs]
-                + [plane_spec] * coil_count
+                + sens_specs
                 + [whole_block(i) for i in tables]
                 + [plane_spec] * len(vectors),
                 outs,
@@ -496,7 +519,7 @@
 
     else:
         ein = functools.partial(jnp.einsum, precision=lax.Precision.HIGH)
-        all_sens = jnp.stack(sens).astype(f32)
+        all_sens = sens.astype(f32)
         map_real, map_imag = all_sens[:, :, 0], all_sens[:, :, 1]
         shape = (coil_count, own_planes)
         block_map = (block_of[:, None] == jnp.arange(blocks, dtype=jnp.int32)).astype(f32)
@@ -524,8 +547,8 @@
             product = ein("tgi,tis->tgs", grid, wide_weights)
             return ein("tb,tgs->bgs", block_map, product).astype(bf16)
 
-        def images_of(samples):
-            spread = ein("tgs,tis->tgi", jnp.take(samples, block_of, axis=0), wide_weights)
+        def images_of(samples, blocks_of=block_of):
+            spread = ein("tgs,tis->tgi", jnp.take(samples, blocks_of, axis=0), wide_weights)
             spread = spread.reshape(tiles, *shape, 2, size)
             back_real = ein("tcpi,xi->tcpx", spread[:, :, :, 0], cos_x) - ein(
                 "tcpi,xi->tcpx", spread[:, :, :, 1], sin_x
@@ -556,7 +579,7 @@
             return jnp.broadcast_to(jnp.stack(values)[:, None], (8, 128))
 
         def measured_images():
-            return images_of(measured.astype(f32))
+            return images_of(measured.astype(f32), measured_block)
 
         def start(images):
             right_side = combined(images)
@@ -580,8 +603,10 @@
             return (residual - scale * again).astype(bf16), dots
 
     right_side, rounded, dots = start(measured_images())
-    start_all = gathered(rounded)
+    start_own = rounded
+    start_sent = [swapped(start_own, "coil", k) for k in first_bits]
     samples = exchanged(forward(right_side))
+    samples, start_sent = lax.optimization_barrier((samples, start_sent))
     dots = summed_over(["pencil"], dots)
     energy = jnp.sum(jnp.square(added(samples)))
     place = lax.broadcasted_iota(jnp.int32, dots.shape, 0)
@@ -589,23 +614,35 @@
     start_norm = first_totals[0, 0]
     start_curve = first_totals[1, 0] + damping * start_norm
     first_step = start_norm / start_curve
-    applied = first(samples, right_side)
+    applied, start_pieces = lax.optimization_barrier(
+        (first(samples, right_side), completed(start_own, start_sent))
+    )
     residual = right_side - first_step * applied
-    residual_all = gathered(residual.astype(bf16))
+    residual_own = residual.astype(bf16)
+    residual_sent = [swapped(residual_own, "coil", k) for k in first_bits]
     samples = exchanged(forward(residual))
+    samples, residual_sent = lax.optimization_barrier((samples, residual_sent))
     rounded, dots = second(samples, first_totals, right_side, applied, residual)
+    rounded, dots, residual_pieces = lax.optimization_barrier(
+        (rounded, dots, completed(residual_own, residual_sent))
+    )
     mixed = everywhere(rounded, "coil")
     totals = summed_over(["coil", "pencil"], dots)
     ratio = totals[0, 0] / start_norm
     curve = totals[1, 0] + ratio * (totals[2, 0] + totals[3, 0]) + ratio * ratio * start_curve
     second_step = totals[0, 0] / curve
     share = second_step / first_step
-    picture = (first_step + second_step * ratio) * start_all + second_step * residual_all
-    out = (1.0 - share + share * ratio) * residual_all - share * ratio * start_all
-    for k, piece in enumerate(mixed):
+
+    picture = jnp.zeros((planes, 2, rows, columns), f32)
+    out = jnp.zeros((planes, 2, rows, columns), f32)
+    for k in range(coil_count):
         place = ((coil_index ^ k) * own_planes, 0, 0, 0)
-        known = lax.dynamic_slice(out, place, piece.shape)
-        out = lax.dynamic_update_slice(out, known + share * piece.astype(f32), place)
+        vector, known = start_pieces[k].astype(f32), residual_pieces[k].astype(f32)
+        piece = (first_step + second_step * ratio) * vector + second_step * known
+        picture = lax.dynamic_update_slice(picture, piece, place)
+        piece = (1.0 - share + share * ratio) * known - share * ratio * vector
+        piece += share * mixed[k].astype(f32)
+        out = lax.dynamic_update_slice(out, piece, place)
     return picture, out
 
 

time: 241 us -> 236 us (0.979)
  waiting for transfers between devices: 61.8 us -> 85.8 us
  blocking collectives: 20 us -> 0 us
  between operations: 21.6 us -> 7.66 us
  other arithmetic: 24.3 us -> 26.8 us
    ppermute x30 -> x39, waiting for transfers between devices: 61.8 us -> 85.8 us  [swapped(): lax.ppermute(array, axis, [(i, i ^ k) for i in range(lax.axis_size(axis))])]
    unnamed x1 -> x0, blocking collectives: 14.1 us -> none
    all_gather x1 -> x0, blocking collectives: 5.86 us -> none  [on_device(): lax.all_gather(measured.reshape(channels, blocks_dev, size), 'pencil', ax...]
    sub x1 -> x0, other arithmetic: 5.35 us -> none  [on_device(): (1.0 - share + share * ratio) * residual_all - share * ratio * start_all]
    all_to_all x0 -> x1, starting transfers between devices: none -> 3.86 us  [on_device(): lax.all_to_all(sens_maps[0], 'coil', split_axis=0, concat_axis=0, tiled=T...]
    gather x1 -> x3, local copies, waits for them, and re-layouts: 0.56 us -> 3.94 us  [the longest x2 3.38 us: on_device(): measured = jnp.take(measured, by_coil, axis=0)]
    ppermute x30 -> x39, starting transfers between devices: 40.3 us -> 37.2 us  [swapped(): lax.ppermute(array, axis, [(i, i ^ k) for i in range(lax.axis_size(axis))])]
    dynamic_update_slice x4 -> x5, other arithmetic: 0.93 us -> 4 us  [the longest x4 3.79 us: on_device(): out = lax.dynamic_update_slice(out, piece, place)]
  transfers between devices with their start and end apart: 32 -> 40, of which waited for: 11 -> 16; matrix products, arithmetic and copies ran while one was open for 16% -> 15% of each run, Pallas kernels for 20% -> 21%
where the time goes in v3:
time: 236 us; the launch traced here: 234 us
  waiting for transfers between devices  85.8 us (36%)
  Pallas kernels  54.4 us (23%)
  starting transfers between devices  41 us (17%)
  other arithmetic  26.8 us (11%)
  local copies, waits for them, and re-layouts  18.2 us (8%)
  between operations  7.66 us (3%)
    ppermute x39, waiting for transfers between devices, swapped(): lax.ppermute(array, axis, [(i, i ^ k) for i in range(lax.axis_size(axis))])  85.8 us
    pallas_call x6, Pallas kernels, call(): pl.pallas_call(kernel, grid=grid, in_specs=specs, out_specs=out_specs, ou...  54.4 us
    ppermute x39, starting transfers between devices, swapped(): lax.ppermute(array, axis, [(i, i ^ k) for i in range(lax.axis_size(axis))])  37.2 us
    unnamed x44, local copies, waits for them, and re-layouts  5.83 us
  transfers between devices with their start and end apart: 40, of which 16 were waited for; matrix products, arithmetic and copies ran while one was open for 15% of the time, Pallas kernels for 21%

profile of v3, /device:TPU:0, one launch (start us, length us, event | category | flops | bytes accessed | tf_op | source)
XLA Modules:
  0.0 233.9 jit_solution(9485664424209869419)
XLA Ops:
  2.1 3.0 %collective-permute-start.1 = (s32[96]{0:T(128)S(1)}, s32[96]{0:T(128)S(1)}, u32[]{:S(2)}, u32[]{:S(2)}) collective-permute-start(s32[96]{0:T(128)S(1)} %pad_add_fusion.1), channel_id=1, source_target_pairs={{0,2},{1,3},{2,0},{3,1},{4,6},{5,7},{6,4},{7,5},{8,10},{9,11},{10,... | collective-permute-start | bytes 1160 | tf_op jit(solution)/shard_map/ppermute | solution.py:309
  8.8 3.9 %all-to-all-start = ((bf16[8,2,128,512]{3,2,1,0:T(8,128)(2,1)}), bf16[8,2,128,512]{3,2,1,0:T(8,128)(2,1)S(1)}, u32[]{:S(2)}, u32[]{:S(2)}) async-start(bf16[8,2,128,512]{3,2,1,0:T(8,128)(2,1)} %bitcast.58), calls=%async_computation | async-start | bytes 4194304 | tf_op jit(solution)/shard_map/all_to_all | solution.py:341
  14.7 2.9 %collective-permute-start.4 = (bf16[2,2,1024]{2,1,0:T(2,128)(2,1)}, bf16[2,2,1024]{2,1,0:T(2,128)(2,1)}, u32[]{:S(2)}, u32[]{:S(2)}) collective-permute-start(bf16[2,2,1024]{2,1,0:T(2,128)(2,1)} %get-tuple-element.75), channel_id=1, source_target_pairs={{0,8},{4,12},{8,0},{12,4},{1,9},{5,13},{9,1},{13,5},{2,10},{6,14},... | collective-permute-start | bytes 24584 | tf_op jit(solution)/shard_map/ppermute | solution.py:309
  23.9 7.0 %collective-permute-done.10.refs_2_.refs_6_ = bf16[32,128,128]{2,1,0:T(8,128)(2,1)S(1)} collective-permute-done((bf16[32,128,128]{2,1,0:T(8,128)(2,1)}, bf16[32,128,128]{2,1,0:T(8,128)(2,1)S(1)}, u32[]{:S(2)}, u32[]{:S(2)}) %collective-permute-start.10) | collective-permute-done | bytes 1048608 | tf_op jit(solution)/shard_map/ppermute | solution.py:309
  33.6 28.1 %collective-permute-done.4 = bf16[2,2,1024]{2,1,0:T(2,128)(2,1)} collective-permute-done((bf16[2,2,1024]{2,1,0:T(2,128)(2,1)}, bf16[2,2,1024]{2,1,0:T(2,128)(2,1)}, u32[]{:S(2)}, u32[]{:S(2)}) %collective-permute-start.4) | collective-permute-done | bytes 8224 | tf_op jit(solution)/shard_map/ppermute | solution.py:309
  69.5 2.6 %pad_maximum_fusion.refs_5_.refs_13_ = bf16[768,1024]{1,0:T(8,128)(2,1)} fusion(bf16[256,1024]{1,0:T(8,128)(2,1)} %get-tuple-element.69, bf16[256,1024]{1,0:T(8,128)(2,1)} %get-tuple-element.68), kind=kLoop, calls=%fused_computation.3 | loop fusion | flops 4718592 | bytes 2621440 | tf_op jit(solution)/shard_map/concatenate | solution.py:42
  76.3 10.7 %shard_map.77.images = f32[4,2,2,128,512]{4,3,2,1,0:T(8,128)} custom-call(s32[128]{0:T(128)} %reshape.473.block, bf16[32,16,128]{2,1,0:T(8,128)(2,1)} %pad_maximum_fusion.3.samples, bf16[32,128,128]{2,1,0:T(8,128)(2,1)} %refs_4_.7, bf16[32,128,128]{2,1,0:T(8,128)(2,1)} %collective-permute-done.9.refs_1_.refs_5_, bf16[32,128,128]{2,1,0:T(8,128)(2,1)} %copy-done.1, ...), custom_call_target="tpu_custom_call" | custom-call | flops 1476395008 | bytes 6423040 | tf_op jit(solution)/shard_map/pallas_call | solution.py:415
  88.3 5.2 %shard_map.78 = (f32[2,2,128,512]{3,2,1,0:T(8,128)}, bf16[2,2,128,512]{3,2,1,0:T(8,128)(2,1)}, f32[8,128]{1,0:T(8,128)}) custom-call(f32[4,2,2,128,512]{4,3,2,1,0:T(8,128)} %shard_map.77.images, bf16[4,2,2,128,512]{4,3,2,1,0:T(8,128)(2,1)} %bitcast.38, bf16[4,2,2,128,512]{4,3,2,1,0:T(8,128)(2,1)} %bitcast.39, bf16[4,2,2,128,512]{4,3,2,1,0:T(8,128)(2,1)} %bitcast.40, ...), custom_call_target="tpu_custom_call" | custom-call | flops 4194304 | bytes 12582912 | tf_op jit(solution)/shard_map/pallas_call | solution.py:415
  98.3 7.5 %shard_map.79.refs_0_ = bf16[32,16,128]{2,1,0:T(8,128)(2,1)} custom-call(s32[128]{0:T(128)} %reshape.472.block, f32[2,2,128,512]{3,2,1,0:T(8,128)} %get-tuple-element.30.picture.refs_15_.refs_16_, bf16[4,2,2,128,512]{4,3,2,1,0:T(8,128)(2,1)} %bitcast.42, bf16[4,2,2,128,512]{4,3,2,1,0:T(8,128)(2,1)} %bitcast.43, bf16[4,2,2,128,512]{4,3,2,1,0:T(8,128)(2,1)} %bitcast.44, ...), custom_call_target="tpu_custom_call" | custom-call | flops 1476395008 | bytes 14156288 | tf_op jit(solution)/shard_map/pallas_call | solution.py:415
  108.1 4.3 %collective-permute-done.13.refs_2_ = bf16[32,16,128]{2,1,0:T(8,128)(2,1)S(1)} collective-permute-done((bf16[32,16,128]{2,1,0:T(8,128)(2,1)}, bf16[32,16,128]{2,1,0:T(8,128)(2,1)S(1)}, u32[]{:S(2)}, u32[]{:S(2)}) %collective-permute-start.13) | collective-permute-done | bytes 131104 | tf_op jit(solution)/shard_map/ppermute | solution.py:309
  115.6 2.2 collective-permute-done.15
  117.8 2.5 %collective-permute-done.16 = bf16[2,2,128,512]{3,2,1,0:T(8,128)(2,1)S(1)} collective-permute-done((bf16[2,2,128,512]{3,2,1,0:T(8,128)(2,1)}, bf16[2,2,128,512]{3,2,1,0:T(8,128)(2,1)S(1)}, u32[]{:S(2)}, u32[]{:S(2)}) %collective-permute-start.16) | collective-permute-done | bytes 524320 | tf_op jit(solution)/shard_map/ppermute | solution.py:309
  122.7 2.0 collective-permute-start.20
  125.0 2.2 collective-permute-start.22
  127.1 11.5 %shard_map.80.refs_17_ = f32[2,2,128,512]{3,2,1,0:T(8,128)} custom-call(s32[128]{0:T(128)} %reshape.472.block, bf16[32,16,128]{2,1,0:T(8,128)(2,1)} %shard_map.79.refs_0_, bf16[32,16,128]{2,1,0:T(8,128)(2,1)} %copy-done.6, bf16[32,16,128]{2,1,0:T(8,128)(2,1)} %copy-done.7, bf16[32,16,128]{2,1,0:T(8,128)(2,1)} %copy-done.8, bf16[32,128,128]{2,1,0:T(8,128)(2,1)} %refs_4_.7, ...), custom_call_target="tpu_custom_call" | custom-call | flops 1476395008 | bytes 16253440 | tf_op jit(solution)/shard_map/pallas_call | solution.py:415
  141.0 2.5 %fusion.49 = (bf16[2,2,128,512]{3,2,1,0:T(8,128)(2,1)S(1)}, f32[2,2,128,512]{3,2,1,0:T(8,128)}) fusion(f32[2,2,128,512]{3,2,1,0:T(8,128)S(1)} %copy-done.2, f32[2,2,128,512]{3,2,1,0:T(8,128)} %shard_map.80.refs_17_, f32[]{:T(128)S(6)} %div.62), kind=kLoop, calls=%fused_computation.156 | loop fusion | flops 786432 | bytes 3670020 | tf_op jit(solution)/shard_map/convert_element_type | solution.py:621
  145.7 7.4 %shard_map.81.refs_0_ = bf16[32,16,128]{2,1,0:T(8,128)(2,1)} custom-call(s32[128]{0:T(128)} %reshape.472.block, f32[2,2,128,512]{3,2,1,0:T(8,128)} %get-tuple-element.59.picture.refs_18_, bf16[4,2,2,128,512]{4,3,2,1,0:T(8,128)(2,1)} %bitcast.50, bf16[4,2,2,128,512]{4,3,2,1,0:T(8,128)(2,1)} %bitcast.51, bf16[4,2,2,128,512]{4,3,2,1,0:T(8,128)(2,1)} %bitcast.52, ...), custom_call_target="tpu_custom_call" | custom-call | flops 1476395008 | bytes 14156288 | tf_op jit(solution)/shard_map/pallas_call | solution.py:415
  155.1 4.7 %collective-permute-done.25.refs_2_ = bf16[32,16,128]{2,1,0:T(8,128)(2,1)S(1)} collective-permute-done((bf16[32,16,128]{2,1,0:T(8,128)(2,1)}, bf16[32,16,128]{2,1,0:T(8,128)(2,1)S(1)}, u32[]{:S(2)}, u32[]{:S(2)}) %collective-permute-start.25) | collective-permute-done | bytes 131104 | tf_op jit(solution)/shard_map/ppermute | solution.py:309
  161.7 4.0 %collective-permute-done.27 = bf16[2,2,128,512]{3,2,1,0:T(8,128)(2,1)S(1)} collective-permute-done((bf16[2,2,128,512]{3,2,1,0:T(8,128)(2,1)S(1)}, bf16[2,2,128,512]{3,2,1,0:T(8,128)(2,1)S(1)}, u32[]{:S(2)}, u32[]{:S(2)}) %collective-permute-start.27) | collective-permute-done | bytes 524320 | tf_op jit(solution)/shard_map/ppermute | solution.py:309
  167.2 12.2 %shard_map.82 = (bf16[2,2,128,512]{3,2,1,0:T(8,128)(2,1)}, f32[8,128]{1,0:T(8,128)}) custom-call(s32[128]{0:T(128)} %reshape.472.block, bf16[32,16,128]{2,1,0:T(8,128)(2,1)} %shard_map.81.refs_0_, bf16[32,16,128]{2,1,0:T(8,128)(2,1)} %copy-done.16, bf16[32,16,128]{2,1,0:T(8,128)(2,1)} %copy-done.17, bf16[32,16,128]{2,1,0:T(8,128)(2,1)} %copy-done.18, ...), custom_call_target="tpu_custom_call" | custom-call | flops 1476395008 | bytes 18354688 | tf_op jit(solution)/shard_map/pallas_call | solution.py:415
  189.2 2.9 %collective-permute-start.34 = (f32[8,128]{1,0:T(8,128)S(1)}, f32[8,128]{1,0:T(8,128)S(1)}, u32[]{:S(2)}, u32[]{:S(2)}) collective-permute-start(f32[8,128]{1,0:T(8,128)S(1)} %add_add_fusion.1), channel_id=1, source_target_pairs={{0,2},{1,3},{2,0},{3,1},{4,6},{5,7},{6,4},{7,5},{8,10},{9,11},{10,... | collective-permute-start | bytes 12296 | tf_op jit(solution)/shard_map/ppermute | solution.py:309
  192.2 2.4 %collective-permute-start.37 = (bf16[2,2,128,512]{3,2,1,0:T(8,128)(2,1)}, bf16[2,2,128,512]{3,2,1,0:T(8,128)(2,1)}, u32[]{:S(2)}, u32[]{:S(2)}) collective-permute-start(bf16[2,2,128,512]{3,2,1,0:T(8,128)(2,1)} %get-tuple-element.57), channel_id=1, source_target_pairs={{0,8},{4,12},{8,0},{12,4},{1,9},{5,13},{9,1},{13,5},{2,10},{6,14},... | collective-permute-start | bytes 1572872 | tf_op jit(solution)/shard_map/ppermute | solution.py:309
  202.5 16.1 %collective-permute-done.37 = bf16[2,2,128,512]{3,2,1,0:T(8,128)(2,1)} collective-permute-done((bf16[2,2,128,512]{3,2,1,0:T(8,128)(2,1)}, bf16[2,2,128,512]{3,2,1,0:T(8,128)(2,1)}, u32[]{:S(2)}, u32[]{:S(2)}) %collective-permute-start.37) | collective-permute-done | bytes 524320 | tf_op jit(solution)/shard_map/ppermute | solution.py:309
  221.7 8.3 %collective-permute-done.38 = bf16[2,2,128,512]{3,2,1,0:T(8,128)(2,1)S(1)} collective-permute-done((bf16[2,2,128,512]{3,2,1,0:T(8,128)(2,1)}, bf16[2,2,128,512]{3,2,1,0:T(8,128)(2,1)S(1)}, u32[]{:S(2)}, u32[]{:S(2)}) %collective-permute-start.38) | collective-permute-done | bytes 524320 | tf_op jit(solution)/shard_map/ppermute | solution.py:309
  (166 shorter events, 70.2 us)
Async XLA Ops:
  2.1 11.8 %collective-permute-start.1 = (s32[96]{0:T(128)S(1)}, s32[96]{0:T(128)S(1)}, u32[]{:S(2)}, u32[]{:S(2)}) collective-permute-start(s32[96]{0:T(128)S(1)} %pad_add_fusion.1), channel_id=1, source_target_pairs={{0,2},{1,3},{2,0},{3,1},{4,6},{5,7},{6,4},{7,5},{8,10},{9,11},{10,... | collective-permute-start | bytes 1160 | tf_op jit(solution)/shard_map/ppermute | solution.py:309
  5.1 9.6 %collective-permute-start = (s32[96]{0:T(128)S(1)}, s32[96]{0:T(128)S(1)}, u32[]{:S(2)}, u32[]{:S(2)}) collective-permute-start(s32[96]{0:T(128)S(1)} %pad_add_fusion.1), channel_id=1, source_target_pairs={{0,1},{1,0},{2,3},{3,2},{4,5},{5,4},{6,7},{7,6},{8,9},{9,8},{10,11... | collective-permute-start | bytes 1160 | tf_op jit(solution)/shard_map/ppermute | solution.py:309
  5.1 25.8 %collective-permute-start.10 = (bf16[32,128,128]{2,1,0:T(8,128)(2,1)}, bf16[32,128,128]{2,1,0:T(8,128)(2,1)S(1)}, u32[]{:S(2)}, u32[]{:S(2)}) collective-permute-start(bf16[32,128,128]{2,1,0:T(8,128)(2,1)} %refs_4_.7), channel_id=1, source_target_pairs={{0,2},{1,3},{2,0},{3,1},{4,6},{5,7},{6,4},{7,5},{8,10},{9,11},{10,... | collective-permute-start | bytes 3145736 | tf_op jit(solution)/shard_map/ppermute | solution.py:309
  5.3 71.1 %collective-permute-start.9 = (bf16[32,128,128]{2,1,0:T(8,128)(2,1)}, bf16[32,128,128]{2,1,0:T(8,128)(2,1)}, u32[]{:S(2)}, u32[]{:S(2)}) collective-permute-start(bf16[32,128,128]{2,1,0:T(8,128)(2,1)} %refs_4_.7), channel_id=1, source_target_pairs={{0,1},{1,0},{2,3},{3,2},{4,5},{5,4},{6,7},{7,6},{8,9},{9,8},{10,11... | collective-permute-start | bytes 3145736 | tf_op jit(solution)/shard_map/ppermute | solution.py:309
  7.0 26.6 %collective-permute-start.3 = (bf16[2,2,1024]{2,1,0:T(2,128)(2,1)}, bf16[2,2,1024]{2,1,0:T(2,128)(2,1)}, u32[]{:S(2)}, u32[]{:S(2)}) collective-permute-start(bf16[2,2,1024]{2,1,0:T(2,128)(2,1)} %get-tuple-element.73), channel_id=1, source_target_pairs={{0,4},{4,0},{8,12},{12,8},{1,5},{5,1},{9,13},{13,9},{2,6},{6,2},{1... | collective-permute-start | bytes 24584 | tf_op jit(solution)/shard_map/ppermute | solution.py:309
  8.8 78.2 %all-to-all-start = ((bf16[8,2,128,512]{3,2,1,0:T(8,128)(2,1)}), bf16[8,2,128,512]{3,2,1,0:T(8,128)(2,1)S(1)}, u32[]{:S(2)}, u32[]{:S(2)}) async-start(bf16[8,2,128,512]{3,2,1,0:T(8,128)(2,1)} %bitcast.58), calls=%async_computation | async-start | bytes 4194304 | tf_op jit(solution)/shard_map/all_to_all | solution.py:341
  14.7 47.0 %collective-permute-start.4 = (bf16[2,2,1024]{2,1,0:T(2,128)(2,1)}, bf16[2,2,1024]{2,1,0:T(2,128)(2,1)}, u32[]{:S(2)}, u32[]{:S(2)}) collective-permute-start(bf16[2,2,1024]{2,1,0:T(2,128)(2,1)} %get-tuple-element.75), channel_id=1, source_target_pairs={{0,8},{4,12},{8,0},{12,4},{1,9},{5,13},{9,1},{13,5},{2,10},{6,14},... | collective-permute-start | bytes 24584 | tf_op jit(solution)/shard_map/ppermute | solution.py:309
  17.7 44.1 %collective-permute-start.5 = (bf16[2,2,1024]{2,1,0:T(2,128)(2,1)}, bf16[2,2,1024]{2,1,0:T(2,128)(2,1)}, u32[]{:S(2)}, u32[]{:S(2)}) collective-permute-start(bf16[2,2,1024]{2,1,0:T(2,128)(2,1)} %get-tuple-element.74), channel_id=1, source_target_pairs={{0,12},{4,8},{8,4},{12,0},{1,13},{5,9},{9,5},{13,1},{2,14},{6,10},... | collective-permute-start | bytes 24584 | tf_op jit(solution)/shard_map/ppermute | solution.py:309
  30.9 45.4 %collective-permute-start.11 = (bf16[32,128,128]{2,1,0:T(8,128)(2,1)S(1)}, bf16[32,128,128]{2,1,0:T(8,128)(2,1)}, u32[]{:S(2)}, u32[]{:S(2)}) collective-permute-start(bf16[32,128,128]{2,1,0:T(8,128)(2,1)S(1)} %collective-permute-done.10.refs_2_.refs_6_), channel_id=1, source_target_pairs={{0,1},{1,0},{2,3},{3,2},{4,5},{5,4},{6,7},{7,6},{8,9},{9,8},{10,11... | collective-permute-start | bytes 3145736 | tf_op jit(solution)/shard_map/ppermute | solution.py:309
  93.6 24.2 %collective-permute-start.15 = (bf16[2,2,128,512]{3,2,1,0:T(8,128)(2,1)}, bf16[2,2,128,512]{3,2,1,0:T(8,128)(2,1)S(1)}, u32[]{:S(2)}, u32[]{:S(2)}) collective-permute-start(bf16[2,2,128,512]{3,2,1,0:T(8,128)(2,1)} %get-tuple-element.49), channel_id=1, source_target_pairs={{0,4},{4,0},{8,12},{12,8},{1,5},{5,1},{9,13},{13,9},{2,6},{6,2},{1... | collective-permute-start | bytes 1572872 | tf_op jit(solution)/shard_map/ppermute | solution.py:309
  94.2 26.1 %collective-permute-start.16 = (bf16[2,2,128,512]{3,2,1,0:T(8,128)(2,1)}, bf16[2,2,128,512]{3,2,1,0:T(8,128)(2,1)S(1)}, u32[]{:S(2)}, u32[]{:S(2)}) collective-permute-start(bf16[2,2,128,512]{3,2,1,0:T(8,128)(2,1)} %get-tuple-element.49), channel_id=1, source_target_pairs={{0,8},{4,12},{8,0},{12,4},{1,9},{5,13},{9,1},{13,5},{2,10},{6,14},... | collective-permute-start | bytes 1572872 | tf_op jit(solution)/shard_map/ppermute | solution.py:309
  107.7 14.2 %collective-permute-start.17 = (f32[8,128]{1,0:T(8,128)S(1)}, f32[8,128]{1,0:T(8,128)S(1)}, u32[]{:S(2)}, u32[]{:S(2)}) collective-permute-start(f32[8,128]{1,0:T(8,128)S(1)} %copy-done.21), channel_id=1, source_target_pairs={{0,1},{1,0},{2,3},{3,2},{4,5},{5,4},{6,7},{7,6},{8,9},{9,8},{10,11... | collective-permute-start | bytes 12296 | tf_op jit(solution)/shard_map/ppermute | solution.py:309
  112.4 9.5 %collective-permute-start.18 = (f32[8,128]{1,0:T(8,128)S(1)}, f32[8,128]{1,0:T(8,128)S(1)}, u32[]{:S(2)}, u32[]{:S(2)}) collective-permute-start(f32[8,128]{1,0:T(8,128)S(1)} %copy-done.21), channel_id=1, source_target_pairs={{0,2},{1,3},{2,0},{3,1},{4,6},{5,7},{6,4},{7,5},{8,10},{9,11},{10,... | collective-permute-start | bytes 12296 | tf_op jit(solution)/shard_map/ppermute | solution.py:309
  114.3 7.7 %collective-permute-start.19 = (f32[8,128]{1,0:T(8,128)S(1)}, f32[8,128]{1,0:T(8,128)S(1)}, u32[]{:S(2)}, u32[]{:S(2)}) collective-permute-start(f32[8,128]{1,0:T(8,128)S(1)} %copy-done.21), channel_id=1, source_target_pairs={{0,3},{1,2},{2,1},{3,0},{4,7},{5,6},{6,5},{7,4},{8,11},{9,10},{10,... | collective-permute-start | bytes 12296 | tf_op jit(solution)/shard_map/ppermute | solution.py:309
  120.3 20.7 %collective-permute-start.23 = (bf16[2,2,128,512]{3,2,1,0:T(8,128)(2,1)S(1)}, bf16[2,2,128,512]{3,2,1,0:T(8,128)(2,1)S(1)}, u32[]{:S(2)}, u32[]{:S(2)}) collective-permute-start(bf16[2,2,128,512]{3,2,1,0:T(8,128)(2,1)S(1)} %collective-permute-done.16), channel_id=1, source_target_pairs={{0,4},{4,0},{8,12},{12,8},{1,5},{5,1},{9,13},{13,9},{2,6},{6,2},{1... | collective-permute-start | bytes 1572872 | tf_op jit(solution)/shard_map/ppermute | solution.py:309
  122.7 16.0 %collective-permute-start.20 = (f32[8,128]{1,0:T(8,128)S(1)}, f32[8,128]{1,0:T(8,128)S(1)}, u32[]{:S(2)}, u32[]{:S(2)}) collective-permute-start(f32[8,128]{1,0:T(8,128)S(1)} %add_select_fusion.4), channel_id=1, source_target_pairs={{0,4},{4,0},{8,12},{12,8},{1,5},{5,1},{9,13},{13,9},{2,6},{6,2},{1... | collective-permute-start | bytes 12296 | tf_op jit(solution)/shard_map/ppermute | solution.py:309
  124.7 14.0 %collective-permute-start.21 = (f32[8,128]{1,0:T(8,128)S(1)}, f32[8,128]{1,0:T(8,128)S(1)}, u32[]{:S(2)}, u32[]{:S(2)}) collective-permute-start(f32[8,128]{1,0:T(8,128)S(1)} %add_select_fusion.4), channel_id=1, source_target_pairs={{0,8},{4,12},{8,0},{12,4},{1,9},{5,13},{9,1},{13,5},{2,10},{6,14},... | collective-permute-start | bytes 12296 | tf_op jit(solution)/shard_map/ppermute | solution.py:309
  125.0 13.7 %collective-permute-start.22 = (f32[8,128]{1,0:T(8,128)S(1)}, f32[8,128]{1,0:T(8,128)S(1)}, u32[]{:S(2)}, u32[]{:S(2)}) collective-permute-start(f32[8,128]{1,0:T(8,128)S(1)} %add_select_fusion.4), channel_id=1, source_target_pairs={{0,12},{4,8},{8,4},{12,0},{1,13},{5,9},{9,5},{13,1},{2,14},{6,10},... | collective-permute-start | bytes 12296 | tf_op jit(solution)/shard_map/ppermute | solution.py:309
  143.5 22.2 %collective-permute-start.27 = (bf16[2,2,128,512]{3,2,1,0:T(8,128)(2,1)S(1)}, bf16[2,2,128,512]{3,2,1,0:T(8,128)(2,1)S(1)}, u32[]{:S(2)}, u32[]{:S(2)}) collective-permute-start(bf16[2,2,128,512]{3,2,1,0:T(8,128)(2,1)S(1)} %get-tuple-element.50), channel_id=1, source_target_pairs={{0,4},{4,0},{8,12},{12,8},{1,5},{5,1},{9,13},{13,9},{2,6},{6,2},{1... | collective-permute-start | bytes 1572872 | tf_op jit(solution)/shard_map/ppermute | solution.py:309
  144.5 22.4 %collective-permute-start.28 = (bf16[2,2,128,512]{3,2,1,0:T(8,128)(2,1)S(1)}, bf16[2,2,128,512]{3,2,1,0:T(8,128)(2,1)S(1)}, u32[]{:S(2)}, u32[]{:S(2)}) collective-permute-start(bf16[2,2,128,512]{3,2,1,0:T(8,128)(2,1)S(1)} %get-tuple-element.50), channel_id=1, source_target_pairs={{0,8},{4,12},{8,0},{12,4},{1,9},{5,13},{9,1},{13,5},{2,10},{6,14},... | collective-permute-start | bytes 1572872 | tf_op jit(solution)/shard_map/ppermute | solution.py:309
  166.9 12.6 %collective-permute-start.29 = (bf16[2,2,128,512]{3,2,1,0:T(8,128)(2,1)S(1)}, bf16[2,2,128,512]{3,2,1,0:T(8,128)(2,1)S(1)}, u32[]{:S(2)}, u32[]{:S(2)}) collective-permute-start(bf16[2,2,128,512]{3,2,1,0:T(8,128)(2,1)S(1)} %collective-permute-done.28), channel_id=1, source_target_pairs={{0,4},{4,0},{8,12},{12,8},{1,5},{5,1},{9,13},{13,9},{2,6},{6,2},{1... | collective-permute-start | bytes 1572872 | tf_op jit(solution)/shard_map/ppermute | solution.py:309
  192.2 26.4 %collective-permute-start.36 = (bf16[2,2,128,512]{3,2,1,0:T(8,128)(2,1)}, bf16[2,2,128,512]{3,2,1,0:T(8,128)(2,1)}, u32[]{:S(2)}, u32[]{:S(2)}) collective-permute-start(bf16[2,2,128,512]{3,2,1,0:T(8,128)(2,1)} %get-tuple-element.57), channel_id=1, source_target_pairs={{0,4},{4,0},{8,12},{12,8},{1,5},{5,1},{9,13},{13,9},{2,6},{6,2},{1... | collective-permute-start | bytes 1572872 | tf_op jit(solution)/shard_map/ppermute | solution.py:309
  192.2 26.4 %collective-permute-start.37 = (bf16[2,2,128,512]{3,2,1,0:T(8,128)(2,1)}, bf16[2,2,128,512]{3,2,1,0:T(8,128)(2,1)}, u32[]{:S(2)}, u32[]{:S(2)}) collective-permute-start(bf16[2,2,128,512]{3,2,1,0:T(8,128)(2,1)} %get-tuple-element.57), channel_id=1, source_target_pairs={{0,8},{4,12},{8,0},{12,4},{1,9},{5,13},{9,1},{13,5},{2,10},{6,14},... | collective-permute-start | bytes 1572872 | tf_op jit(solution)/shard_map/ppermute | solution.py:309
  218.7 11.4 %collective-permute-start.38 = (bf16[2,2,128,512]{3,2,1,0:T(8,128)(2,1)}, bf16[2,2,128,512]{3,2,1,0:T(8,128)(2,1)S(1)}, u32[]{:S(2)}, u32[]{:S(2)}) collective-permute-start(bf16[2,2,128,512]{3,2,1,0:T(8,128)(2,1)} %collective-permute-done.37), channel_id=1, source_target_pairs={{0,4},{4,0},{8,12},{12,8},{1,5},{5,1},{9,13},{13,9},{2,6},{6,2},{1... | collective-permute-start | bytes 1572872 | tf_op jit(solution)/shard_map/ppermute | solution.py:309
  (38 other events, 328.9 us)

commit v4 on v3

--- a/solution.py
+++ b/solution.py
@@ -96,13 +96,15 @@
         def one(place, carry):
             tile = group * count + place
             start = pl.multiple_of(tile * channels, channels)
-            high, low = split(grid_ref[pl.ds(start, channels), :])
-            product = nn(jnp.concatenate([high, low], 0), weights_ref[place])
+            value = grid_ref[pl.ds(start, channels), :]
+            high = value.astype(bf16).astype(f32)
+            both = jnp.concatenate([high, value - high], 0).astype(bf16)
+            product = nn(both, weights_ref[place])
             sums_ref[block_ref[tile]] += product[:channels] + product[channels:]
             return carry
 
         lax.fori_loop(0, count, one, 0, unroll=True)
-    out_ref[...] = sums_ref[...].astype(bf16)
+    out_ref[...] = sums_ref[...].reshape(out_ref.shape).astype(bf16)
 
 
 def spread_tiles(block_ref, weights, parts_ref, grid_ref):
@@ -216,13 +218,13 @@
         sample_tiles(block, weights, grid, sums, samples)
 
 
-def spread_sum(block, samples, weights, grid, parts):
+def summed_parts(samples, parts):
     summed = tree_sum([part[...].astype(f32) for part in samples])
-    channels = summed.shape[1]
-    high, low = split(summed)
-    parts[:, :channels] = high
-    parts[:, channels:] = low
-    spread_tiles(block, weights, parts, grid)
+    blocks, channels, size = parts.shape[0], parts.shape[1] // 2, parts.shape[2]
+    value = summed.reshape(blocks, channels, size)
+    high = value.astype(bf16).astype(f32)
+    parts[...] = jnp.concatenate([high, value - high], 1).astype(bf16)
+    return summed
 
 
 def back_images(coils, plane, tiles, eb, mx, turn, grid):
@@ -232,51 +234,58 @@
     ]
 
 
+def step_of(norm, energy):
+    return jnp.where(norm > 0.0, norm / (energy + damping * norm), 1.0)
+
+
 def first_kernel(peers, coils, block, *refs):
     samples, weights, sens = refs[:peers], refs[peers : 2 * peers], refs[2 * peers :][:coils]
-    mx, eb, turn, right_side, applied, grid, parts = refs[2 * peers + coils :]
+    mx, eb, turn, *norms = refs[2 * peers + coils :][: 3 + peers]
+    right_side, residual, rounded, facts, dots, total_samples, grid, parts = refs[-8:]
     plane = pl.program_id(0)
 
     @pl.when(plane == 0)
     def _():
-        spread_sum(block, samples, weights, grid, parts)
+        summed = summed_parts(samples, parts)
+        total_samples[...] = summed
+        rows = lax.broadcasted_iota(jnp.int32, facts.shape, 0)
+        norm = tree_sum([part[...] for part in norms])
+        facts[...] = jnp.where(rows == 1, jnp.sum(summed * summed), norm)
+        dots[...] = jnp.zeros_like(dots)
+        spread_tiles(block, weights, parts, grid)
 
     images = back_images(len(sens), plane, turn.shape[2], eb, mx, turn, grid)
     total = combine(images, sens)
+    scale = step_of(facts[0:1, 0:1], facts[1:2, 0:1])
     for part in range(2):
-        applied[0, part] = total[part] + damping * right_side[0, part]
-
-
-def first_step_of(totals):
-    return totals[0:1, 0:1] / (totals[1:2, 0:1] + damping * totals[0:1, 0:1])
+        vector = right_side[0, part]
+        value = vector - scale * (total[part] + damping * vector)
+        residual[0, part] = value
+        rounded[0, part] = value.astype(bf16)
+        add_dots(dots, [(value, value), (value, vector)])
 
 
 def second_kernel(peers, coils, block, *refs):
     samples, weights, sens = refs[:peers], refs[peers : 2 * peers], refs[2 * peers :][:coils]
-    mx, eb, turn, totals, right_side, applied, residual = refs[2 * peers + coils :][:7]
-    rounded, dots, grid, parts = refs[-4:]
+    mx, eb, turn, facts, residual, rounded, grid, parts = refs[2 * peers + coils :]
     plane = pl.program_id(0)
 
     @pl.when(plane == 0)
     def _():
-        dots[...] = jnp.zeros_like(dots)
-        spread_sum(block, samples, weights, grid, parts)
+        summed_parts(samples, parts)
+        spread_tiles(block, weights, parts, grid)
 
     images = back_images(len(sens), plane, turn.shape[2], eb, mx, turn, grid)
     total = combine(images, sens)
+    scale = step_of(facts[0:1, 0:1], facts[1:2, 0:1])
     for part in range(2):
         vector = residual[0, part]
         again = total[part] + damping * vector
-        rounded[0, part] = (vector - first_step_of(totals) * again).astype(bf16)
-        add_dots(
-            dots,
-            [
-                (vector, vector),
-                (vector, again),
-                (vector, applied[0, part]),
-                (right_side[0, part], again),
-            ],
-        )
+        rounded[0, part] = (vector - scale * again).astype(bf16)
+
+
+def group_count_of(own_planes):
+    return 1
 
 
 def whole_block(array):
@@ -338,14 +347,27 @@
             pieces.append(swapped(part, "coil", k) if k > 0 else part)
         return pieces
 
-    sens = lax.all_to_all(sens_maps[0], "coil", split_axis=0, concat_axis=0, tiled=True)
-    sens = sens.reshape(coil_count, own_planes, 2, rows, columns)
-    measured = jnp.stack(to_planes(kspace[0]))
+    group_planes = own_planes // group_count_of(own_planes)
+    groups = range(own_planes // group_planes)
+    measured = to_planes(kspace[0])
+    packed = jnp.concatenate([tile_slot, tile_block, send_list.reshape(-1)])
+    sens_source, packed, measured = lax.optimization_barrier((sens_maps[0], packed, measured))
+    sens_source = sens_source.reshape(coil_count, own_planes, 2, rows, columns)
+    sens = [
+        lax.all_to_all(
+            sens_source[:, g * group_planes : (g + 1) * group_planes],
+            "coil",
+            split_axis=0,
+            concat_axis=0,
+            tiled=True,
+        )
+        for g in groups
+    ]
+    measured = jnp.stack(measured)
     by_coil = jnp.arange(coil_count, dtype=jnp.int32) ^ coil_index
     measured = jnp.take(measured, by_coil, axis=0)
     all_weights = everywhere(weights, "pencil")
 
-    packed = jnp.concatenate([tile_slot, tile_block, send_list.reshape(-1)])
     places = jnp.stack(everywhere(packed, "pencil"))
     holder = (jnp.arange(peers, dtype=jnp.int32) ^ lax.axis_index("pencil"))[:, None]
     by_owner = jnp.take(places, holder[:, 0], axis=0)
@@ -377,17 +399,17 @@
         count = lax.axis_size(axis)
         return [partial] + [swapped(partial, axis, k) for k in range(1, count)]
 
-    def summed_over(axes, dots):
-        for axis in axes:
-            dots = tree_sum(exchanged(dots, axis))
-        return dots
-
-    def added(samples):
-        return tree_sum([part.astype(f32) for part in samples])
-
-    picture_shape = (own_planes, 2, rows, columns)
-
-    if rows % 128 == 0 and columns % 128 == 0 and size % 128 == 0 and channels % 16 == 0:
+    group_shape = (group_planes, 2, rows, columns)
+    group_images = coil_count * group_planes
+    group_channels = 2 * group_images
+
+    if (
+        rows % 128 == 0
+        and columns % 128 == 0
+        and size % 128 == 0
+        and channels % 16 == 0
+        and group_channels % 8 == 0
+    ):
         ey = jnp.concatenate([cos_y, sin_y], 0).astype(bf16)
         eb = jnp.concatenate(
             [jnp.concatenate([cos_y, sin_y], 1), jnp.concatenate([-sin_y, cos_y], 1)], 0
@@ -403,15 +425,15 @@
             pl.BlockSpec((1, 1, 2, rows, columns), functools.partial(lambda c, p: (c, p, 0, 0, 0), c))
             for c in range(coil_count)
         ]
-        all_coils = pl.BlockSpec(
-            (coil_count, 1, 2, rows, columns), lambda p: (0, p, 0, 0, 0)
-        )
-        grid_scratch = pltpu.VMEM((tiles * channels, size), f32)
-        sums_shape = (blocks, channels, size)
+        grid_scratch = pltpu.VMEM((tiles * group_channels, size), f32)
         params = pltpu.CompilerParams(vmem_limit_bytes=vmem_limit)
-
-        def call(kernel, grid, inputs, specs, outs, out_specs, scratch, flops):
-            read = sum(math.prod(i.shape) * i.dtype.itemsize for i in inputs)
+        tail_tables = [mx_back, eb, turn_back]
+
+        def shaped(shape, dtype=f32):
+            return jax.ShapeDtypeStruct(shape, dtype)
+
+        def call(kernel, grid, inputs, specs, outs, out_specs, scratch, images):
+            flops = 2 * images * 8 * tiles * rows * (columns + size)
             return pl.pallas_call(
                 kernel,
                 grid=grid,
@@ -421,41 +443,39 @@
                 scratch_shapes=scratch,
                 compiler_params=params,
                 cost_estimate=pl.CostEstimate(
-                    flops=flops, bytes_accessed=read, transcendentals=0
+                    flops=flops,
+                    bytes_accessed=sum(math.prod(i.shape) * i.dtype.itemsize for i in inputs),
+                    transcendentals=0,
                 ),
             )(*inputs)
 
-        def shaped(shape, dtype=f32):
-            return jax.ShapeDtypeStruct(shape, dtype)
-
-        image_flops = 2 * images_count * 8 * tiles * rows * (columns + size)
-        tile_flops = 4 * tiles * channels * size * size
-        grid = (own_planes,)
-
         def measured_images():
-            inputs = [measured_block, measured, *all_weights, mx_back, eb, turn_back]
+            inputs = [measured_block, measured, *all_weights, *tail_tables]
+            shape = (coil_count, own_planes, 2, rows, columns)
             return call(
                 measured_kernel,
-                grid,
+                (own_planes,),
                 inputs,
                 [places_spec] + [whole_block(i) for i in inputs[1:]],
-                shaped((coil_count,) + picture_shape),
-                all_coils,
-                [grid_scratch],
-                image_flops + tile_flops,
-            )
-
-        def start(images):
+                shaped(shape),
+                pl.BlockSpec((coil_count, 1, 2, rows, columns), lambda p: (0, p, 0, 0, 0)),
+                [pltpu.VMEM((tiles * channels, size), f32)],
+                images_count,
+            )
+
+        def start(images, g):
             chunk = 64
             spec = pl.BlockSpec((1, 2, chunk, columns), lambda p, r: (p, 0, r, 0))
-            coils_spec = pl.BlockSpec(
-                (coil_count, 1, 2, chunk, columns), lambda p, r: (0, p, 0, r, 0)
-            )
+            images_spec = pl.BlockSpec(
+                (coil_count, 1, 2, chunk, columns),
+                lambda p, r: (0, p + g * group_planes, 0, r, 0),
+            )
+            dots_shape = shaped((8, 128))
             return call(
                 start_kernel,
-                (own_planes, rows // chunk),
-                [images] + [sens] * coil_count,
-                [coils_spec]
+                (group_planes, rows // chunk),
+                [images] + [sens[g]] * coil_count,
+                [images_spec]
                 + [
                     pl.BlockSpec(
                         (1, 1, 2, chunk, columns),
@@ -463,34 +483,33 @@
                     )
                     for c in range(coil_count)
                 ],
-                [shaped(picture_shape), shaped(picture_shape, bf16), shaped((8, 128))],
-                [spec, spec, whole_block(shaped((8, 128)))],
+                [shaped(group_shape), shaped(group_shape, bf16), dots_shape],
+                [spec, spec, whole_block(dots_shape)],
                 [],
-                8 * images_count * rows * columns,
-            )
-
-        def forward(picture):
+                0,
+            )
+
+        def forward(picture, g):
             tail = [*all_weights, ey, mx, turn]
+            out = shaped((blocks * group_channels, size), bf16)
             return call(
                 functools.partial(forward_kernel, coil_count),
-                grid,
-                [block_of, picture] + [sens] * coil_count + tail,
+                (group_planes,),
+                [block_of, picture] + [sens[g]] * coil_count + tail,
                 [places_spec, plane_spec] + sens_specs + [whole_block(i) for i in tail],
-                shaped(sums_shape, bf16),
-                whole_block(shaped(sums_shape)),
-                [grid_scratch, pltpu.VMEM(sums_shape, f32)],
-                image_flops + tile_flops,
-            )
-
-        parts_scratch = pltpu.VMEM((blocks, 2 * channels, size), bf16)
-
-        def back(kernel, samples, tables, vectors, outs, out_specs):
+                out,
+                whole_block(out),
+                [grid_scratch, pltpu.VMEM((blocks, group_channels, size), f32)],
+                group_images,
+            )
+
+        def back(kernel, samples, tables, vectors, g, outs, out_specs):
             inputs = [*samples, *all_weights]
-            tables = [mx_back, eb, turn_back, *tables]
+            tables = tail_tables + tables
             return call(
                 functools.partial(kernel, peers, coil_count),
-                grid,
-                [block_of, *inputs] + [sens] * coil_count + tables + vectors,
+                (group_planes,),
+                [block_of, *inputs] + [sens[g]] * coil_count + tables + vectors,
                 [places_spec]
                 + [whole_block(i) for i in inputs]
                 + sens_specs
@@ -498,35 +517,42 @@
                 + [plane_spec] * len(vectors),
                 outs,
                 out_specs,
-                [grid_scratch, parts_scratch],
-                image_flops + tile_flops,
-            )
-
-        def first(samples, right_side):
+                [grid_scratch, pltpu.VMEM((blocks, 2 * group_channels, size), bf16)],
+                group_images,
+            )
+
+        def first(samples, norms, right_side, g):
+            small, large = shaped((8, 128)), shaped(samples[0].shape)
             return back(
-                first_kernel, samples, [], [right_side], shaped(picture_shape), plane_spec
-            )
-
-        def second(samples, totals, right_side, applied, residual):
+                first_kernel,
+                samples,
+                norms,
+                [right_side],
+                g,
+                [shaped(group_shape), shaped(group_shape, bf16), small, small, large],
+                [plane_spec, plane_spec] + [whole_block(i) for i in (small, small, large)],
+            )
+
+        def second(samples, facts, residual, g):
             return back(
                 second_kernel,
                 samples,
-                [totals],
-                [right_side, applied, residual],
-                [shaped(picture_shape, bf16), shaped((8, 128))],
-                [plane_spec, whole_block(shaped((8, 128)))],
+                [facts],
+                [residual],
+                g,
+                shaped(group_shape, bf16),
+                plane_spec,
             )
 
     else:
         ein = functools.partial(jnp.einsum, precision=lax.Precision.HIGH)
-        all_sens = sens.astype(f32)
-        map_real, map_imag = all_sens[:, :, 0], all_sens[:, :, 1]
-        shape = (coil_count, own_planes)
+        maps = [array.astype(f32) for array in sens]
         block_map = (block_of[:, None] == jnp.arange(blocks, dtype=jnp.int32)).astype(f32)
         tc, ts = turn[0][:, None, None], turn[1][:, None, None]
         wide_weights = jnp.concatenate(all_weights, 0).astype(f32)
 
-        def forward(picture):
+        def forward(picture, g):
+            map_real, map_imag = maps[g][:, :, 0], maps[g][:, :, 1]
             coil_real = map_real * picture[None, :, 0] - map_imag * picture[None, :, 1]
             coil_imag = map_real * picture[None, :, 1] + map_imag * picture[None, :, 0]
             half_real = ein("ty,cpxy->tcpx", cos_y, coil_real) + ein(
@@ -543,13 +569,13 @@
                     ein("tcpx,xi->tcpi", imag, cos_x) - ein("tcpx,xi->tcpi", real, sin_x),
                 ],
                 3,
-            ).reshape(tiles, channels, size)
+            ).reshape(tiles, group_channels, size)
             product = ein("tgi,tis->tgs", grid, wide_weights)
-            return ein("tb,tgs->bgs", block_map, product).astype(bf16)
-
-        def images_of(samples, blocks_of=block_of):
+            return ein("tb,tgs->bgs", block_map, product).astype(bf16).reshape(-1, size)
+
+        def images_of(samples, blocks_of):
             spread = ein("tgs,tis->tgi", jnp.take(samples, blocks_of, axis=0), wide_weights)
-            spread = spread.reshape(tiles, *shape, 2, size)
+            spread = spread.reshape(tiles, coil_count, -1, 2, size)
             back_real = ein("tcpi,xi->tcpx", spread[:, :, :, 0], cos_x) - ein(
                 "tcpi,xi->tcpx", spread[:, :, :, 1], sin_x
             )
@@ -558,13 +584,17 @@
             )
             real = back_real * tc - back_imag * ts
             imag = back_imag * tc + back_real * ts
-            return (
-                ein("tcpx,ty->cpxy", real, cos_y) - ein("tcpx,ty->cpxy", imag, sin_y),
-                ein("tcpx,ty->cpxy", imag, cos_y) + ein("tcpx,ty->cpxy", real, sin_y),
-            )
-
-        def combined(images):
-            real, imag = images
+            return jnp.stack(
+                [
+                    ein("tcpx,ty->cpxy", real, cos_y) - ein("tcpx,ty->cpxy", imag, sin_y),
+                    ein("tcpx,ty->cpxy", imag, cos_y) + ein("tcpx,ty->cpxy", real, sin_y),
+                ],
+                2,
+            )
+
+        def combined(images, g):
+            map_real, map_imag = maps[g][:, :, 0], maps[g][:, :, 1]
+            real, imag = images[:, :, 0], images[:, :, 1]
             return jnp.stack(
                 [
                     jnp.sum(map_real * real + map_imag * imag, 0),
@@ -573,76 +603,107 @@
                 1,
             )
 
-        def stacked_dots(products):
-            values = [jnp.sum(left * right) for left, right in products]
-            values += [jnp.zeros((), f32)] * (8 - len(values))
+        def stacked_dots(values):
+            values = values + [jnp.zeros((), f32)] * (8 - len(values))
             return jnp.broadcast_to(jnp.stack(values)[:, None], (8, 128))
+
+        def applied_to(samples, vector, g):
+            samples = added(samples).reshape(blocks, group_channels, size)
+            return combined(images_of(samples, block_of), g) + damping * vector
 
         def measured_images():
             return images_of(measured.astype(f32), measured_block)
 
-        def start(images):
-            right_side = combined(images)
-            dots = stacked_dots([(right_side, right_side)])
+        def start(images, g):
+            right_side = combined(images[:, g * group_planes : (g + 1) * group_planes], g)
+            dots = stacked_dots([jnp.sum(right_side * right_side)])
             return right_side, right_side.astype(bf16), dots
 
-        def first(samples, right_side):
-            return combined(images_of(added(samples))) + damping * right_side
-
-        def second(samples, totals, right_side, applied, residual):
-            scale = totals[0, 0] / (totals[1, 0] + damping * totals[0, 0])
-            again = combined(images_of(added(samples))) + damping * residual
-            dots = stacked_dots(
-                [
-                    (residual, residual),
-                    (residual, again),
-                    (residual, applied),
-                    (right_side, again),
-                ]
-            )
-            return (residual - scale * again).astype(bf16), dots
-
-    right_side, rounded, dots = start(measured_images())
-    start_own = rounded
-    start_sent = [swapped(start_own, "coil", k) for k in first_bits]
-    samples = exchanged(forward(right_side))
-    samples, start_sent = lax.optimization_barrier((samples, start_sent))
-    dots = summed_over(["pencil"], dots)
-    energy = jnp.sum(jnp.square(added(samples)))
-    place = lax.broadcasted_iota(jnp.int32, dots.shape, 0)
-    first_totals = summed_over(["coil"], jnp.where(place == 1, energy, dots))
-    start_norm = first_totals[0, 0]
-    start_curve = first_totals[1, 0] + damping * start_norm
-    first_step = start_norm / start_curve
-    applied, start_pieces = lax.optimization_barrier(
-        (first(samples, right_side), completed(start_own, start_sent))
-    )
-    residual = right_side - first_step * applied
-    residual_own = residual.astype(bf16)
-    residual_sent = [swapped(residual_own, "coil", k) for k in first_bits]
-    samples = exchanged(forward(residual))
-    samples, residual_sent = lax.optimization_barrier((samples, residual_sent))
-    rounded, dots = second(samples, first_totals, right_side, applied, residual)
-    rounded, dots, residual_pieces = lax.optimization_barrier(
-        (rounded, dots, completed(residual_own, residual_sent))
-    )
-    mixed = everywhere(rounded, "coil")
-    totals = summed_over(["coil", "pencil"], dots)
-    ratio = totals[0, 0] / start_norm
-    curve = totals[1, 0] + ratio * (totals[2, 0] + totals[3, 0]) + ratio * ratio * start_curve
-    second_step = totals[0, 0] / curve
-    share = second_step / first_step
-
+        def first(samples, norms, right_side, g):
+            norm = tree_sum(norms)[0, 0]
+            total = added(samples)
+            energy = jnp.sum(jnp.square(total))
+            residual = right_side - step_of(norm, energy) * applied_to(samples, right_side, g)
+            dots = [jnp.sum(residual * residual), jnp.sum(residual * right_side)]
+            facts = stacked_dots([norm, energy])
+            return residual, residual.astype(bf16), facts, stacked_dots(dots), total
+
+        def second(samples, facts, residual, g):
+            again = applied_to(samples, residual, g)
+            return (residual - step_of(facts[0, 0], facts[1, 0]) * again).astype(bf16)
+
+    def added(samples):
+        return tree_sum([part.astype(f32) for part in samples])
+
+    def sent_by_bits(own):
+        return [swapped(own, "coil", k) for k in first_bits]
+
+    images = measured_images()
+    start_pieces, residual_pieces, mixed_own, mixed_sent, values = [], [], [], [], []
+    for g in groups:
+        right_side, start_own, norm = start(images, g)
+        start_sent = sent_by_bits(start_own)
+        samples = exchanged(forward(right_side, g))
+        norms = exchanged(norm)
+        samples, norms, start_sent = lax.optimization_barrier((samples, norms, start_sent))
+        residual, residual_own, facts, dots, start_total = first(samples, norms, right_side, g)
+        residual, residual_own, pieces = lax.optimization_barrier(
+            (residual, residual_own, completed(start_own, start_sent))
+        )
+        start_pieces.append(pieces)
+        residual_sent = sent_by_bits(residual_own)
+        samples = exchanged(forward(residual, g))
+        dots = exchanged(dots)
+        samples, dots, residual_sent = lax.optimization_barrier((samples, dots, residual_sent))
+        total = added(samples)
+        square, cross = tree_sum(dots)[:2, 0]
+        value = [facts[0, 0], facts[1, 0], square, cross]
+        value += [jnp.sum(total * total), jnp.sum(total * start_total)]
+        values.append(jnp.stack(value))
+        rounded = second(samples, facts, residual, g)
+        rounded, pieces = lax.optimization_barrier(
+            (rounded, completed(residual_own, residual_sent))
+        )
+        residual_pieces.append(pieces)
+        mixed_own.append(rounded)
+        mixed_sent.append(sent_by_bits(rounded))
+
+    values = jnp.stack(exchanged(jnp.stack(values), "coil"))
+    values, mixed_sent[-1][0] = lax.optimization_barrier((values, mixed_sent[-1][0]))
+    mixed_pieces = [completed(mixed_own[g], mixed_sent[g]) for g in groups]
+    norm, energy, square, cross, again, mixed = [values[:, :, i] for i in range(6)]
+    curve, mixed_curve = again + damping * square, mixed + damping * cross
+
+    def over_all(value):
+        return tree_sum([jnp.sum(value[k]) for k in range(coil_count)])
+
+    sigma = step_of(norm, energy)
+    start_norm = over_all(norm)
+    first_step = start_norm / over_all(energy + damping * norm)
+    part = first_step / sigma
+    rest = 1.0 - part
+    next_norm = over_all(part * part * square + 2.0 * part * rest * cross + rest * rest * norm)
+    more = rest + next_norm / start_norm
+    second_step = next_norm / over_all(
+        part * part * curve
+        + part * more * ((cross - square) / sigma + mixed_curve)
+        + more * more * (energy + damping * norm)
+    )
+    share = second_step / sigma
     picture = jnp.zeros((planes, 2, rows, columns), f32)
     out = jnp.zeros((planes, 2, rows, columns), f32)
     for k in range(coil_count):
-        place = ((coil_index ^ k) * own_planes, 0, 0, 0)
-        vector, known = start_pieces[k].astype(f32), residual_pieces[k].astype(f32)
-        piece = (first_step + second_step * ratio) * vector + second_step * known
-        picture = lax.dynamic_update_slice(picture, piece, place)
-        piece = (1.0 - share + share * ratio) * known - share * ratio * vector
-        piece += share * mixed[k].astype(f32)
-        out = lax.dynamic_update_slice(out, piece, place)
+        for g in groups:
+            place = ((coil_index ^ k) * own_planes + g * group_planes, 0, 0, 0)
+            vector = start_pieces[g][k].astype(f32)
+            known = residual_pieces[g][k].astype(f32)
+            weight, ratio, length = part[k, g], more[k, g], share[k, g]
+            piece = (first_step + second_step * ratio) * vector + second_step * weight * known
+            picture = lax.dynamic_update_slice(picture, piece, place)
+            piece = (weight - length * weight + length * ratio) * known
+            piece += (rest[k, g] - length * ratio) * vector
+            piece += length * weight * mixed_pieces[g][k].astype(f32)
+            out = lax.dynamic_update_slice(out, piece, place)
     return picture, out
 
 

time: 236 us -> 219 us (0.928)
  waiting for transfers between devices: 85.8 us -> 56 us
  between operations: 7.66 us -> 31.8 us
  other arithmetic: 26.8 us -> 17.3 us
  local copies, waits for them, and re-layouts: 18.2 us -> 24.4 us
  starting transfers between devices: 41 us -> 34.9 us
    ppermute x39 -> x36, waiting for transfers between devices: 85.8 us -> 43.7 us  [swapped(): lax.ppermute(array, axis, [(i, i ^ k) for i in range(lax.axis_size(axis))])]
    all_to_all x1, waiting for transfers between devices: 0.01 us -> 12.3 us  [on_device(): lax.all_to_all(sens_source[:, g * group_planes:(g + 1) * group_planes], '...]
    ppermute x39 -> x36, starting transfers between devices: 37.2 us -> 31.3 us  [swapped(): lax.ppermute(array, axis, [(i, i ^ k) for i in range(lax.axis_size(axis))])]
    slice x2 -> x10, local copies, waits for them, and re-layouts: 1.13 us -> 6.66 us  [the longest x4 2.56 us: over_all(): return tree_sum([jnp.sum(value[k]) for k in range(coil_count)])]
    another operation x2 -> x4, local copies, waits for them, and re-layouts: 1.04 us -> 5.36 us  [the longest x1 3.8 us: on_device(): values.append(jnp.stack(value))]
    gather x2, local copies, waits for them, and re-layouts: 3.38 us -> 0.65 us  [on_device(): measured = jnp.take(measured, by_coil, axis=0)]
    convert_element_type x1 -> x0, other arithmetic: 2.46 us -> none  [on_device(): residual_own = residual.astype(bf16)]
    unnamed x44 -> x50, local copies, waits for them, and re-layouts: 5.83 us -> 6.07 us
  transfers between devices with their start and end apart: 40 -> 37, of which waited for: 16 -> 14; matrix products, arithmetic and copies ran while one was open for 15% -> 16% of each run, Pallas kernels for 21% -> 22%
where the time goes in v4:
time: 219 us; the launch traced here: 218 us
  waiting for transfers between devices  56 us (26%)
  Pallas kernels  54.2 us (25%)
  starting transfers between devices  34.9 us (16%)
  between operations  31.8 us (15%)
  local copies, waits for them, and re-layouts  24.4 us (11%)
  other arithmetic  17.3 us (8%)
    pallas_call x6, Pallas kernels, call(): pl.pallas_call(kernel, grid=grid, in_specs=specs, out_specs=out_specs, ou...  54.2 us
    ppermute x36, waiting for transfers between devices, swapped(): lax.ppermute(array, axis, [(i, i ^ k) for i in range(lax.axis_size(axis))])  43.7 us
    ppermute x36, starting transfers between devices, swapped(): lax.ppermute(array, axis, [(i, i ^ k) for i in range(lax.axis_size(axis))])  31.3 us
    all_to_all x1, waiting for transfers between devices, on_device(): lax.all_to_all(sens_source[:, g * group_planes:(g + 1) * group_planes], '...  12.3 us
    unnamed x50, local copies, waits for them, and re-layouts  6.07 us
  transfers between devices with their start and end apart: 37, of which 14 were waited for; matrix products, arithmetic and copies ran while one was open for 16% of the time, Pallas kernels for 22%

profile of v4, /device:TPU:0, one launch (start us, length us, event | category | flops | bytes accessed | tf_op | source)
XLA Modules:
  0.0 218.4 jit_solution(10141615219083050251)
XLA Ops:
  1.1 2.6 %collective-permute-start.10 = (bf16[32,128,128]{2,1,0:T(8,128)(2,1)}, bf16[32,128,128]{2,1,0:T(8,128)(2,1)}, u32[]{:S(2)}, u32[]{:S(2)}) collective-permute-start(bf16[32,128,128]{2,1,0:T(8,128)(2,1)} %refs_4_.7), channel_id=1, source_target_pairs={{0,2},{1,3},{2,0},{3,1},{4,6},{5,7},{6,4},{7,5},{8,10},{9,11},{10,... | collective-permute-start | bytes 3145736 | tf_op jit(solution)/shard_map/ppermute | solution.py:318
  6.2 2.6 %collective-permute-start.1 = (bf16[2,2,1024]{2,1,0:T(2,128)(2,1)S(1)}, bf16[2,2,1024]{2,1,0:T(2,128)(2,1)S(1)}, u32[]{:S(2)}, u32[]{:S(2)}) collective-permute-start(bf16[2,2,1024]{2,1,0:T(2,128)(2,1)S(1)} %get-tuple-element.122), channel_id=1, source_target_pairs={{0,8},{4,12},{8,0},{12,4},{1,9},{5,13},{9,1},{13,5},{2,10},{6,14},... | collective-permute-start | bytes 24584 | tf_op jit(solution)/shard_map/ppermute | solution.py:318
  10.7 3.5 %collective-permute-done.2 = bf16[2,2,1024]{2,1,0:T(2,128)(2,1)S(1)} collective-permute-done((bf16[2,2,1024]{2,1,0:T(2,128)(2,1)S(1)}, bf16[2,2,1024]{2,1,0:T(2,128)(2,1)S(1)}, u32[]{:S(2)}, u32[]{:S(2)}) %collective-permute-start.2) | collective-permute-done | bytes 8224 | tf_op jit(solution)/shard_map/ppermute | solution.py:318
  14.2 3.6 %all-to-all-start = ((bf16[4,2,2,128,512]{4,3,2,1,0:T(8,128)(2,1)}), bf16[4,2,2,128,512]{4,3,2,1,0:T(8,128)(2,1)S(1)}, u32[]{:S(2)}, u32[]{:S(2)}) async-start(bf16[4,2,2,128,512]{4,3,2,1,0:T(8,128)(2,1)} %bitcast.125), calls=%async_computation | async-start | bytes 4194304 | tf_op jit(solution)/shard_map/all_to_all | solution.py:357
  20.3 7.6 %collective-permute-done.4 = s32[96]{0:T(128)S(1)} collective-permute-done((s32[96]{0:T(128)S(1)}, s32[96]{0:T(128)S(1)}, u32[]{:S(2)}, u32[]{:S(2)}) %collective-permute-start.4) | collective-permute-done | bytes 416 | tf_op jit(solution)/shard_map/ppermute | solution.py:318
  42.0 10.6 %shard_map.77.images = f32[4,2,2,128,512]{4,3,2,1,0:T(8,128)} custom-call(s32[128]{0:T(128)} %reshape.845.block, bf16[32,16,128]{2,1,0:T(8,128)(2,1)} %pad_maximum_fusion.3.samples, bf16[32,128,128]{2,1,0:T(8,128)(2,1)} %refs_4_.7, bf16[32,128,128]{2,1,0:T(8,128)(2,1)} %copy-done.1, bf16[32,128,128]{2,1,0:T(8,128)(2,1)} %collective-permute-done.10.refs_2_.refs_6_, ...), custom_call_target="tpu_custom_call" | custom-call | flops 1342177280 | bytes 6423040 | tf_op jit(solution)/shard_map/pallas_call | solution.py:437
  52.6 12.3 %all-to-all-done.refs_0_.refs_1_.refs_2_.refs_3_.refs_8_.refs_9_.refs_10_.refs_11_ = bf16[4,2,2,128,512]{4,3,2,1,0:T(8,128)(2,1)S(1)} async-done(((bf16[4,2,2,128,512]{4,3,2,1,0:T(8,128)(2,1)}), bf16[4,2,2,128,512]{4,3,2,1,0:T(8,128)(2,1)S(1)}, u32[]{:S(2)}, u32[]{:S(2)}) %all-to-all-start) | async-done | bytes 2097184 | tf_op jit(solution)/shard_map/all_to_all | solution.py:357
  66.2 5.2 %shard_map.78 = (f32[2,2,128,512]{3,2,1,0:T(8,128)}, bf16[2,2,128,512]{3,2,1,0:T(8,128)(2,1)}, f32[8,128]{1,0:T(8,128)}) custom-call(f32[4,2,2,128,512]{4,3,2,1,0:T(8,128)} %shard_map.77.images, bf16[4,2,2,128,512]{4,3,2,1,0:T(8,128)(2,1)} %copy-done, bf16[4,2,2,128,512]{4,3,2,1,0:T(8,128)(2,1)} %copy-done, bf16[4,2,2,128,512]{4,3,2,1,0:T(8,128)(2,1)} %copy-done, ...), custom_call_target="tpu_custom_call" | custom-call | bytes 12582912 | tf_op jit(solution)/shard_map/pallas_call | solution.py:437
  71.4 2.0 collective-permute-start.19
  78.1 7.4 %shard_map.79.refs_0_ = bf16[512,128]{1,0:T(8,128)(2,1)} custom-call(s32[128]{0:T(128)} %reshape.844.block, f32[2,2,128,512]{3,2,1,0:T(8,128)} %get-tuple-element.55.picture.refs_19_, bf16[4,2,2,128,512]{4,3,2,1,0:T(8,128)(2,1)} %copy-done, bf16[4,2,2,128,512]{4,3,2,1,0:T(8,128)(2,1)} %copy-done, bf16[4,2,2,128,512]{4,3,2,1,0:T(8,128)(2,1)} %copy-done, ...), custom_call_target="tpu_custom_call" | custom-call | flops 1342177280 | bytes 14156288 | tf_op jit(solution)/shard_map/pallas_call | solution.py:437
  87.4 5.0 %collective-permute-done.13.refs_2_ = bf16[512,128]{1,0:T(8,128)(2,1)S(1)} collective-permute-done((bf16[512,128]{1,0:T(8,128)(2,1)}, bf16[512,128]{1,0:T(8,128)(2,1)S(1)}, u32[]{:S(2)}, u32[]{:S(2)}) %collective-permute-start.13) | collective-permute-done | bytes 131104 | tf_op jit(solution)/shard_map/ppermute | solution.py:318
  93.9 2.9 %collective-permute-done.19 = bf16[2,2,128,512]{3,2,1,0:T(8,128)(2,1)S(1)} collective-permute-done((bf16[2,2,128,512]{3,2,1,0:T(8,128)(2,1)}, bf16[2,2,128,512]{3,2,1,0:T(8,128)(2,1)S(1)}, u32[]{:S(2)}, u32[]{:S(2)}) %collective-permute-start.19) | collective-permute-done | bytes 524320 | tf_op jit(solution)/shard_map/ppermute | solution.py:318
  96.8 12.0 %shard_map.80 = (f32[2,2,128,512]{3,2,1,0:T(8,128)}, bf16[2,2,128,512]{3,2,1,0:T(8,128)(2,1)}, f32[8,128]{1,0:T(8,128)}, f32[8,128]{1,0:T(8,128)}, f32[512,128]{1,0:T(8,128)}) custom-call(s32[128]{0:T(128)} %reshape.844.block, bf16[512,128]{1,0:T(8,128)(2,1)} %shard_map.79.refs_0_, bf16[512,128]{1,0:T(8,128)(2,1)} %copy-done.18, ...), custom_call_target="tpu_custom_call" | custom-call | flops 1342177280 | bytes 16269824 | tf_op jit(solution)/shard_map/pallas_call | solution.py:437
  108.9 2.1 collective-permute-start.27
  113.3 7.4 %shard_map.81.refs_0_ = bf16[512,128]{1,0:T(8,128)(2,1)} custom-call(s32[128]{0:T(128)} %reshape.844.block, f32[2,2,128,512]{3,2,1,0:T(8,128)} %get-tuple-element.71.picture.refs_16_, bf16[4,2,2,128,512]{4,3,2,1,0:T(8,128)(2,1)} %copy-done, bf16[4,2,2,128,512]{4,3,2,1,0:T(8,128)(2,1)} %copy-done, bf16[4,2,2,128,512]{4,3,2,1,0:T(8,128)(2,1)} %copy-done, ...), custom_call_target="tpu_custom_call" | custom-call | flops 1342177280 | bytes 14156288 | tf_op jit(solution)/shard_map/pallas_call | solution.py:437
  122.6 5.0 %collective-permute-done.22.refs_2_ = bf16[512,128]{1,0:T(8,128)(2,1)S(1)} collective-permute-done((bf16[512,128]{1,0:T(8,128)(2,1)}, bf16[512,128]{1,0:T(8,128)(2,1)S(1)}, u32[]{:S(2)}, u32[]{:S(2)}) %collective-permute-start.22) | collective-permute-done | bytes 131104 | tf_op jit(solution)/shard_map/ppermute | solution.py:318
  129.0 3.4 %collective-permute-done.27 = bf16[2,2,128,512]{3,2,1,0:T(8,128)(2,1)S(1)} collective-permute-done((bf16[2,2,128,512]{3,2,1,0:T(8,128)(2,1)}, bf16[2,2,128,512]{3,2,1,0:T(8,128)(2,1)S(1)}, u32[]{:S(2)}, u32[]{:S(2)}) %collective-permute-start.27) | collective-permute-done | bytes 524320 | tf_op jit(solution)/shard_map/ppermute | solution.py:318
  132.4 2.2 %collective-permute-done.28 = bf16[2,2,128,512]{3,2,1,0:T(8,128)(2,1)S(1)} collective-permute-done((bf16[2,2,128,512]{3,2,1,0:T(8,128)(2,1)}, bf16[2,2,128,512]{3,2,1,0:T(8,128)(2,1)S(1)}, u32[]{:S(2)}, u32[]{:S(2)}) %collective-permute-start.28) | collective-permute-done | bytes 524320 | tf_op jit(solution)/shard_map/ppermute | solution.py:318
  136.2 11.6 %shard_map.82 = bf16[2,2,128,512]{3,2,1,0:T(8,128)(2,1)} custom-call(s32[128]{0:T(128)} %reshape.844.block, bf16[512,128]{1,0:T(8,128)(2,1)} %shard_map.81.refs_0_, bf16[512,128]{1,0:T(8,128)(2,1)} %copy-done.8, bf16[512,128]{1,0:T(8,128)(2,1)} %copy-done.9, bf16[512,128]{1,0:T(8,128)(2,1)} %copy-done.10, bf16[32,128,128]{2,1,0:T(8,128)(2,1)} %refs_4_.7, ...), custom_call_target="tpu_custom_call" | custom-call | flops 1342177280 | bytes 16257536 | tf_op jit(solution)/shard_map/pallas_call | solution.py:437
  152.0 3.8 %stack.78 = f32[6]{0:T(128)S(1)} concatenate(f32[1]{0:T(128)} %bitcast.19, f32[1]{0:T(128)} %bitcast.20, f32[1]{0:T(128)} %bitcast.21, f32[1]{0:T(128)} %bitcast.22, f32[1]{0:T(128)} %bitcast.23, f32[1]{0:T(128)} %bitcast.24), dimensions={0} | concatenate | bytes 48 | tf_op jit(solution)/shard_map/stack | solution.py:662
  155.8 2.4 %collective-permute-start.31 = (f32[1,6]{1,0:T(1,128)S(1)}, f32[1,6]{1,0:T(1,128)S(1)}, u32[]{:S(2)}, u32[]{:S(2)}) collective-permute-start(f32[1,6]{1,0:T(1,128)S(1)} %bitcast.130), channel_id=1, source_target_pairs={{0,12},{4,8},{8,4},{12,0},{1,13},{5,9},{9,5},{13,1},{2,14},{6,10},... | collective-permute-start | bytes 80 | tf_op jit(solution)/shard_map/ppermute | solution.py:318
  158.2 2.0 collective-permute-start.29
  161.2 5.8 %collective-permute-done.30 = f32[1,6]{1,0:T(1,128)S(1)} collective-permute-done((f32[1,6]{1,0:T(1,128)S(1)}, f32[1,6]{1,0:T(1,128)S(1)}, u32[]{:S(2)}, u32[]{:S(2)}) %collective-permute-start.30) | collective-permute-done | bytes 56 | tf_op jit(solution)/shard_map/ppermute | solution.py:318
  210.1 4.5 %collective-permute-done.35 = bf16[2,2,128,512]{3,2,1,0:T(8,128)(2,1)S(1)} collective-permute-done((bf16[2,2,128,512]{3,2,1,0:T(8,128)(2,1)}, bf16[2,2,128,512]{3,2,1,0:T(8,128)(2,1)S(1)}, u32[]{:S(2)}, u32[]{:S(2)}) %collective-permute-start.35) | collective-permute-done | bytes 524320 | tf_op jit(solution)/shard_map/ppermute | solution.py:318
  (177 shorter events, 59.4 us)
Async XLA Ops:
  0.6 40.3 %collective-permute-start.9 = (bf16[32,128,128]{2,1,0:T(8,128)(2,1)}, bf16[32,128,128]{2,1,0:T(8,128)(2,1)S(1)}, u32[]{:S(2)}, u32[]{:S(2)}) collective-permute-start(bf16[32,128,128]{2,1,0:T(8,128)(2,1)} %refs_4_.7), channel_id=1, source_target_pairs={{0,1},{1,0},{2,3},{3,2},{4,5},{5,4},{6,7},{7,6},{8,9},{9,8},{10,11... | collective-permute-start | bytes 3145736 | tf_op jit(solution)/shard_map/ppermute | solution.py:318
  1.1 32.2 %collective-permute-start.10 = (bf16[32,128,128]{2,1,0:T(8,128)(2,1)}, bf16[32,128,128]{2,1,0:T(8,128)(2,1)}, u32[]{:S(2)}, u32[]{:S(2)}) collective-permute-start(bf16[32,128,128]{2,1,0:T(8,128)(2,1)} %refs_4_.7), channel_id=1, source_target_pairs={{0,2},{1,3},{2,0},{3,1},{4,6},{5,7},{6,4},{7,5},{8,10},{9,11},{10,... | collective-permute-start | bytes 3145736 | tf_op jit(solution)/shard_map/ppermute | solution.py:318
  14.2 50.7 %all-to-all-start = ((bf16[4,2,2,128,512]{4,3,2,1,0:T(8,128)(2,1)}), bf16[4,2,2,128,512]{4,3,2,1,0:T(8,128)(2,1)S(1)}, u32[]{:S(2)}, u32[]{:S(2)}) async-start(bf16[4,2,2,128,512]{4,3,2,1,0:T(8,128)(2,1)} %bitcast.125), calls=%async_computation | async-start | bytes 4194304 | tf_op jit(solution)/shard_map/all_to_all | solution.py:357
  19.0 8.8 %collective-permute-start.4 = (s32[96]{0:T(128)S(1)}, s32[96]{0:T(128)S(1)}, u32[]{:S(2)}, u32[]{:S(2)}) collective-permute-start(s32[96]{0:T(128)S(1)} %pad_add_fusion.1), channel_id=1, source_target_pairs={{0,2},{1,3},{2,0},{3,1},{4,6},{5,7},{6,4},{7,5},{8,10},{9,11},{10,... | collective-permute-start | bytes 1160 | tf_op jit(solution)/shard_map/ppermute | solution.py:318
  19.5 10.7 %collective-permute-start.3 = (s32[96]{0:T(128)S(1)}, s32[96]{0:T(128)S(1)}, u32[]{:S(2)}, u32[]{:S(2)}) collective-permute-start(s32[96]{0:T(128)S(1)} %pad_add_fusion.1), channel_id=1, source_target_pairs={{0,1},{1,0},{2,3},{3,2},{4,5},{5,4},{6,7},{7,6},{8,9},{9,8},{10,11... | collective-permute-start | bytes 1160 | tf_op jit(solution)/shard_map/ppermute | solution.py:318
  28.5 9.4 %collective-permute-start.7 = (bf16[8,16,128]{2,1,0:T(8,128)(2,1)}, bf16[8,16,128]{2,1,0:T(8,128)(2,1)}, u32[]{:S(2)}, u32[]{:S(2)}) collective-permute-start(bf16[8,16,128]{2,1,0:T(8,128)(2,1)} %fusion.34), channel_id=1, source_target_pairs={{0,2},{1,3},{2,0},{3,1},{4,6},{5,7},{6,4},{7,5},{8,10},{9,11},{10,... | collective-permute-start | bytes 98312 | tf_op jit(solution)/shard_map/ppermute | solution.py:318
  30.3 9.2 %collective-permute-start.6 = (bf16[8,16,128]{2,1,0:T(8,128)(2,1)}, bf16[8,16,128]{2,1,0:T(8,128)(2,1)}, u32[]{:S(2)}, u32[]{:S(2)}) collective-permute-start(bf16[8,16,128]{2,1,0:T(8,128)(2,1)} %fusion.34), channel_id=1, source_target_pairs={{0,1},{1,0},{2,3},{3,2},{4,5},{5,4},{6,7},{7,6},{8,9},{9,8},{10,11... | collective-permute-start | bytes 98312 | tf_op jit(solution)/shard_map/ppermute | solution.py:318
  71.4 22.5 %collective-permute-start.18 = (bf16[2,2,128,512]{3,2,1,0:T(8,128)(2,1)}, bf16[2,2,128,512]{3,2,1,0:T(8,128)(2,1)S(1)}, u32[]{:S(2)}, u32[]{:S(2)}) collective-permute-start(bf16[2,2,128,512]{3,2,1,0:T(8,128)(2,1)} %get-tuple-element.87), channel_id=1, source_target_pairs={{0,4},{4,0},{8,12},{12,8},{1,5},{5,1},{9,13},{13,9},{2,6},{6,2},{1... | collective-permute-start | bytes 1572872 | tf_op jit(solution)/shard_map/ppermute | solution.py:318
  71.4 25.3 %collective-permute-start.19 = (bf16[2,2,128,512]{3,2,1,0:T(8,128)(2,1)}, bf16[2,2,128,512]{3,2,1,0:T(8,128)(2,1)S(1)}, u32[]{:S(2)}, u32[]{:S(2)}) collective-permute-start(bf16[2,2,128,512]{3,2,1,0:T(8,128)(2,1)} %get-tuple-element.87), channel_id=1, source_target_pairs={{0,8},{4,12},{8,0},{12,4},{1,9},{5,13},{9,1},{13,5},{2,10},{6,14},... | collective-permute-start | bytes 1572872 | tf_op jit(solution)/shard_map/ppermute | solution.py:318
  76.2 9.3 %collective-permute-start.15 = (f32[8,128]{1,0:T(8,128)}, f32[8,128]{1,0:T(8,128)S(1)}, u32[]{:S(2)}, u32[]{:S(2)}) collective-permute-start(f32[8,128]{1,0:T(8,128)} %get-tuple-element.62.refs_15_), channel_id=1, source_target_pairs={{0,1},{1,0},{2,3},{3,2},{4,5},{5,4},{6,7},{7,6},{8,9},{9,8},{10,11... | collective-permute-start | bytes 12296 | tf_op jit(solution)/shard_map/ppermute | solution.py:318
  76.2 9.6 %collective-permute-start.16 = (f32[8,128]{1,0:T(8,128)}, f32[8,128]{1,0:T(8,128)S(1)}, u32[]{:S(2)}, u32[]{:S(2)}) collective-permute-start(f32[8,128]{1,0:T(8,128)} %get-tuple-element.62.refs_15_), channel_id=1, source_target_pairs={{0,2},{1,3},{2,0},{3,1},{4,6},{5,7},{6,4},{7,5},{8,10},{9,11},{10,... | collective-permute-start | bytes 12296 | tf_op jit(solution)/shard_map/ppermute | solution.py:318
  76.7 9.6 %collective-permute-start.17 = (f32[8,128]{1,0:T(8,128)}, f32[8,128]{1,0:T(8,128)S(1)}, u32[]{:S(2)}, u32[]{:S(2)}) collective-permute-start(f32[8,128]{1,0:T(8,128)} %get-tuple-element.62.refs_15_), channel_id=1, source_target_pairs={{0,3},{1,2},{2,1},{3,0},{4,7},{5,6},{6,5},{7,4},{8,11},{9,10},{10,... | collective-permute-start | bytes 12296 | tf_op jit(solution)/shard_map/ppermute | solution.py:318
  96.7 12.1 %collective-permute-start.20 = (bf16[2,2,128,512]{3,2,1,0:T(8,128)(2,1)S(1)}, bf16[2,2,128,512]{3,2,1,0:T(8,128)(2,1)S(1)}, u32[]{:S(2)}, u32[]{:S(2)}) collective-permute-start(bf16[2,2,128,512]{3,2,1,0:T(8,128)(2,1)S(1)} %collective-permute-done.19), channel_id=1, source_target_pairs={{0,4},{4,0},{8,12},{12,8},{1,5},{5,1},{9,13},{13,9},{2,6},{6,2},{1... | collective-permute-start | bytes 1572872 | tf_op jit(solution)/shard_map/ppermute | solution.py:318
  108.9 23.5 %collective-permute-start.27 = (bf16[2,2,128,512]{3,2,1,0:T(8,128)(2,1)}, bf16[2,2,128,512]{3,2,1,0:T(8,128)(2,1)S(1)}, u32[]{:S(2)}, u32[]{:S(2)}) collective-permute-start(bf16[2,2,128,512]{3,2,1,0:T(8,128)(2,1)} %get-tuple-element.88), channel_id=1, source_target_pairs={{0,4},{4,0},{8,12},{12,8},{1,5},{5,1},{9,13},{13,9},{2,6},{6,2},{1... | collective-permute-start | bytes 1572872 | tf_op jit(solution)/shard_map/ppermute | solution.py:318
  110.9 23.7 %collective-permute-start.28 = (bf16[2,2,128,512]{3,2,1,0:T(8,128)(2,1)}, bf16[2,2,128,512]{3,2,1,0:T(8,128)(2,1)S(1)}, u32[]{:S(2)}, u32[]{:S(2)}) collective-permute-start(bf16[2,2,128,512]{3,2,1,0:T(8,128)(2,1)} %get-tuple-element.88), channel_id=1, source_target_pairs={{0,8},{4,12},{8,0},{12,4},{1,9},{5,13},{9,1},{13,5},{2,10},{6,14},... | collective-permute-start | bytes 1572872 | tf_op jit(solution)/shard_map/ppermute | solution.py:318
  111.4 9.2 %collective-permute-start.24 = (f32[8,128]{1,0:T(8,128)}, f32[8,128]{1,0:T(8,128)S(1)}, u32[]{:S(2)}, u32[]{:S(2)}) collective-permute-start(f32[8,128]{1,0:T(8,128)} %get-tuple-element.74), channel_id=1, source_target_pairs={{0,1},{1,0},{2,3},{3,2},{4,5},{5,4},{6,7},{7,6},{8,9},{9,8},{10,11... | collective-permute-start | bytes 12296 | tf_op jit(solution)/shard_map/ppermute | solution.py:318
  111.4 9.6 %collective-permute-start.25 = (f32[8,128]{1,0:T(8,128)}, f32[8,128]{1,0:T(8,128)S(1)}, u32[]{:S(2)}, u32[]{:S(2)}) collective-permute-start(f32[8,128]{1,0:T(8,128)} %get-tuple-element.74), channel_id=1, source_target_pairs={{0,2},{1,3},{2,0},{3,1},{4,6},{5,7},{6,4},{7,5},{8,10},{9,11},{10,... | collective-permute-start | bytes 12296 | tf_op jit(solution)/shard_map/ppermute | solution.py:318
  111.9 9.6 %collective-permute-start.26 = (f32[8,128]{1,0:T(8,128)}, f32[8,128]{1,0:T(8,128)S(1)}, u32[]{:S(2)}, u32[]{:S(2)}) collective-permute-start(f32[8,128]{1,0:T(8,128)} %get-tuple-element.74), channel_id=1, source_target_pairs={{0,3},{1,2},{2,1},{3,0},{4,7},{5,6},{6,5},{7,4},{8,11},{9,10},{10,... | collective-permute-start | bytes 12296 | tf_op jit(solution)/shard_map/ppermute | solution.py:318
  134.6 13.2 %collective-permute-start.32 = (bf16[2,2,128,512]{3,2,1,0:T(8,128)(2,1)S(1)}, bf16[2,2,128,512]{3,2,1,0:T(8,128)(2,1)S(1)}, u32[]{:S(2)}, u32[]{:S(2)}) collective-permute-start(bf16[2,2,128,512]{3,2,1,0:T(8,128)(2,1)S(1)} %collective-permute-done.28), channel_id=1, source_target_pairs={{0,4},{4,0},{8,12},{12,8},{1,5},{5,1},{9,13},{13,9},{2,6},{6,2},{1... | collective-permute-start | bytes 1572872 | tf_op jit(solution)/shard_map/ppermute | solution.py:318
  147.8 19.2 %collective-permute-start.33 = (bf16[2,2,128,512]{3,2,1,0:T(8,128)(2,1)}, bf16[2,2,128,512]{3,2,1,0:T(8,128)(2,1)}, u32[]{:S(2)}, u32[]{:S(2)}) collective-permute-start(bf16[2,2,128,512]{3,2,1,0:T(8,128)(2,1)} %shard_map.82), channel_id=1, source_target_pairs={{0,4},{4,0},{8,12},{12,8},{1,5},{5,1},{9,13},{13,9},{2,6},{6,2},{1... | collective-permute-start | bytes 1572872 | tf_op jit(solution)/shard_map/ppermute | solution.py:318
  158.2 8.8 %collective-permute-start.30 = (f32[1,6]{1,0:T(1,128)S(1)}, f32[1,6]{1,0:T(1,128)S(1)}, u32[]{:S(2)}, u32[]{:S(2)}) collective-permute-start(f32[1,6]{1,0:T(1,128)S(1)} %bitcast.131), channel_id=1, source_target_pairs={{0,8},{4,12},{8,0},{12,4},{1,9},{5,13},{9,1},{13,5},{2,10},{6,14},... | collective-permute-start | bytes 80 | tf_op jit(solution)/shard_map/ppermute | solution.py:318
  158.2 8.8 %collective-permute-start.29 = (f32[1,6]{1,0:T(1,128)S(1)}, f32[1,6]{1,0:T(1,128)S(1)}, u32[]{:S(2)}, u32[]{:S(2)}) collective-permute-start(f32[1,6]{1,0:T(1,128)S(1)} %bitcast.132), channel_id=1, source_target_pairs={{0,4},{4,0},{8,12},{12,8},{1,5},{5,1},{9,13},{13,9},{2,6},{6,2},{1... | collective-permute-start | bytes 80 | tf_op jit(solution)/shard_map/ppermute | solution.py:318
  167.0 38.1 %collective-permute-start.34 = (bf16[2,2,128,512]{3,2,1,0:T(8,128)(2,1)}, bf16[2,2,128,512]{3,2,1,0:T(8,128)(2,1)}, u32[]{:S(2)}, u32[]{:S(2)}) collective-permute-start(bf16[2,2,128,512]{3,2,1,0:T(8,128)(2,1)} %shard_map.82), channel_id=1, source_target_pairs={{0,8},{4,12},{8,0},{12,4},{1,9},{5,13},{9,1},{13,5},{2,10},{6,14},... | collective-permute-start | bytes 1572872 | tf_op jit(solution)/shard_map/ppermute | solution.py:318
  205.1 9.5 %collective-permute-start.35 = (bf16[2,2,128,512]{3,2,1,0:T(8,128)(2,1)}, bf16[2,2,128,512]{3,2,1,0:T(8,128)(2,1)S(1)}, u32[]{:S(2)}, u32[]{:S(2)}) collective-permute-start(bf16[2,2,128,512]{3,2,1,0:T(8,128)(2,1)} %collective-permute-done.34), channel_id=1, source_target_pairs={{0,4},{4,0},{8,12},{12,8},{1,5},{5,1},{9,13},{13,9},{2,6},{6,2},{1... | collective-permute-start | bytes 1572872 | tf_op jit(solution)/shard_map/ppermute | solution.py:318
  (38 other events, 383.7 us)

commit v5 on v4

--- a/solution.py
+++ b/solution.py
@@ -61,29 +61,37 @@
     return values[0]
 
 
-def forward_image(step, real, imag, sens_ref, ey, mx, turn_ref, grid_ref):
+def forward_images(plane, planes, picture, sens, ey, mx, turn_ref, grid_ref):
     tiles = turn_ref.shape[1]
     rows = turn_ref.shape[2]
     channels = grid_ref.shape[0] // tiles
-    sens_real = sens_ref[0, 0, 0].astype(f32)
-    sens_imag = sens_ref[0, 0, 1].astype(f32)
-    coil = jnp.concatenate(
-        [sens_real * real - sens_imag * imag, sens_real * imag + sens_imag * real], 0
-    )
-    both = nt(ey[...], coil.astype(bf16))
-    half_real = both[:tiles, :rows] + both[tiles:, rows:]
-    half_imag = both[:tiles, rows:] - both[tiles:, :rows]
-    turned = jnp.concatenate(
-        [
-            half_real * turn_ref[0] + half_imag * turn_ref[1],
-            half_imag * turn_ref[0] - half_real * turn_ref[1],
-        ],
-        1,
-    )
-    grid = nn(turned.astype(bf16), mx[...])
+    real, imag = picture[0, 0], picture[0, 1]
+    turned = []
+    for sens_ref in sens:
+        sens_real = sens_ref[0, 0, 0].astype(f32)
+        sens_imag = sens_ref[0, 0, 1].astype(f32)
+        coil = jnp.concatenate(
+            [sens_real * real - sens_imag * imag, sens_real * imag + sens_imag * real], 0
+        )
+        both = nt(ey[...], coil.astype(bf16))
+        half_real = both[:tiles, :rows] + both[tiles:, rows:]
+        half_imag = both[:tiles, rows:] - both[tiles:, :rows]
+        turned.append(
+            jnp.concatenate(
+                [
+                    half_real * turn_ref[0] + half_imag * turn_ref[1],
+                    half_imag * turn_ref[0] - half_real * turn_ref[1],
+                ],
+                1,
+            ).astype(bf16)
+        )
+    grid = nn(jnp.concatenate(turned, 0), mx[...])
     size = grid.shape[1] // 2
-    grid_ref[pl.ds(2 * step, tiles, stride=channels), :] = grid[:, :size]
-    grid_ref[pl.ds(2 * step + 1, tiles, stride=channels), :] = grid[:, size:]
+    for coil in range(len(sens)):
+        step = coil * planes + plane
+        part = grid[coil * tiles : (coil + 1) * tiles]
+        grid_ref[pl.ds(2 * step, tiles, stride=channels), :] = part[:, :size]
+        grid_ref[pl.ds(2 * step + 1, tiles, stride=channels), :] = part[:, size:]
 
 
 def sample_tiles(block_ref, weights, grid_ref, sums_ref, out_ref):
@@ -125,27 +133,38 @@
         lax.fori_loop(0, count, one, 0, unroll=True)
 
 
-def adjoint_image(step, tiles, ey_back, mx_back, turn_ref, grid_ref):
+def adjoint_images(coils, plane, planes, ey_back, mx_back, turn_ref, grid_ref):
+    rows, tiles = turn_ref.shape[1], turn_ref.shape[2]
     channels = grid_ref.shape[0] // tiles
-    rows = turn_ref.shape[1]
-    grid = jnp.concatenate(
-        [
-            grid_ref[pl.ds(2 * step, tiles, stride=channels), :],
-            grid_ref[pl.ds(2 * step + 1, tiles, stride=channels), :],
-        ],
-        1,
-    )
-    back = nt(mx_back[...], data_parts(grid))
-    turned = jnp.concatenate(
-        [
-            back[:rows] * turn_ref[0] - back[rows:] * turn_ref[1],
-            back[rows:] * turn_ref[0] + back[:rows] * turn_ref[1],
-        ],
-        1,
-    )
-    image = nn(data_parts(turned), ey_back[...])
+    grids = []
+    for coil in range(coils):
+        step = coil * planes + plane
+        grid = jnp.concatenate(
+            [
+                grid_ref[pl.ds(2 * step, tiles, stride=channels), :],
+                grid_ref[pl.ds(2 * step + 1, tiles, stride=channels), :],
+            ],
+            1,
+        )
+        grids.append(data_parts(grid))
+    back = nt(mx_back[...], jnp.concatenate(grids, 0))
+    turned = []
+    for coil in range(coils):
+        part = back[:, coil * tiles : (coil + 1) * tiles]
+        both = jnp.concatenate(
+            [
+                part[:rows] * turn_ref[0] - part[rows:] * turn_ref[1],
+                part[rows:] * turn_ref[0] + part[:rows] * turn_ref[1],
+            ],
+            1,
+        )
+        turned.append(data_parts(both))
+    image = nn(jnp.concatenate(turned, 0), ey_back[...])
     columns = image.shape[1] // 2
-    return image[:, :columns], image[:, columns:]
+    return [
+        (image[c * rows : (c + 1) * rows, :columns], image[c * rows : (c + 1) * rows, columns:])
+        for c in range(coils)
+    ]
 
 
 def add_dots(dots_ref, products):
@@ -165,10 +184,8 @@
     def _():
         spread_tiles(block, weights, samples, grid)
 
-    for coil in range(coils):
-        real, imag = adjoint_image(
-            coil * pl.num_programs(0) + plane, turn.shape[2], eb, mx, turn, grid
-        )
+    found = adjoint_images(coils, plane, pl.num_programs(0), eb, mx, turn, grid)
+    for coil, (real, imag) in enumerate(found):
         images[coil, 0, 0] = real
         images[coil, 0, 1] = imag
 
@@ -201,17 +218,7 @@
     sens = refs[:coils]
     *weights, ey, mx, turn, samples, grid, sums = refs[coils:]
     plane = pl.program_id(0)
-    for coil, sens_ref in enumerate(sens):
-        forward_image(
-            coil * pl.num_programs(0) + plane,
-            picture[0, 0],
-            picture[0, 1],
-            sens_ref,
-            ey,
-            mx,
-            turn,
-            grid,
-        )
+    forward_images(plane, pl.num_programs(0), picture, sens, ey, mx, turn, grid)
 
     @pl.when(plane == pl.num_programs(0) - 1)
     def _():
@@ -225,13 +232,6 @@
     high = value.astype(bf16).astype(f32)
     parts[...] = jnp.concatenate([high, value - high], 1).astype(bf16)
     return summed
-
-
-def back_images(coils, plane, tiles, eb, mx, turn, grid):
-    return [
-        adjoint_image(coil * pl.num_programs(0) + plane, tiles, eb, mx, turn, grid)
-        for coil in range(coils)
-    ]
 
 
 def step_of(norm, energy):
@@ -254,7 +254,7 @@
         dots[...] = jnp.zeros_like(dots)
         spread_tiles(block, weights, parts, grid)
 
-    images = back_images(len(sens), plane, turn.shape[2], eb, mx, turn, grid)
+    images = adjoint_images(coils, plane, pl.num_programs(0), eb, mx, turn, grid)
     total = combine(images, sens)
     scale = step_of(facts[0:1, 0:1], facts[1:2, 0:1])
     for part in range(2):
@@ -275,13 +275,93 @@
         summed_parts(samples, parts)
         spread_tiles(block, weights, parts, grid)
 
-    images = back_images(len(sens), plane, turn.shape[2], eb, mx, turn, grid)
+    images = adjoint_images(coils, plane, pl.num_programs(0), eb, mx, turn, grid)
     total = combine(images, sens)
     scale = step_of(facts[0:1, 0:1], facts[1:2, 0:1])
     for part in range(2):
         vector = residual[0, part]
         again = total[part] + damping * vector
         rounded[0, part] = (vector - scale * again).astype(bf16)
+
+
+def facts_kernel(peers, *refs):
+    samples, dots = refs[:peers], refs[peers : 2 * peers]
+    start_total, facts, out = refs[2 * peers :]
+    summed = tree_sum([part[...].astype(f32) for part in samples])
+    both = tree_sum([part[...] for part in dots])
+    rows = lax.broadcasted_iota(jnp.int32, out.shape, 0)
+    values = [facts[0:1], facts[1:2], both[0:1], both[1:2]]
+    values += [jnp.sum(summed * summed), jnp.sum(summed * start_total[...])]
+    total = jnp.zeros(out.shape, f32)
+    for row, value in enumerate(values):
+        total = jnp.where(rows == row, value, total)
+    out[...] = total
+
+
+def coefficients(norm, energy, square, cross, again, mixed):
+    def over_all(values):
+        return tree_sum([sum(of_coil) for of_coil in values])
+
+    def each(function, *lists):
+        return [[function(*items) for items in zip(*of_coil)] for of_coil in zip(*lists)]
+
+    start_curve = each(lambda e, n: e + damping * n, energy, norm)
+    curve = each(lambda e, n: e + damping * n, again, square)
+    mixed_curve = each(lambda e, n: e + damping * n, mixed, cross)
+    sigma = each(step_of, norm, energy)
+    start_norm = over_all(norm)
+    first_step = start_norm / over_all(start_curve)
+    part = each(lambda s: first_step / s, sigma)
+    next_norm = over_all(
+        each(
+            lambda w, n, c, s: w * w * s + 2.0 * w * (1.0 - w) * c + (1.0 - w) * (1.0 - w) * n,
+            part,
+            norm,
+            cross,
+            square,
+        )
+    )
+    more = each(lambda w: 1.0 - w + next_norm / start_norm, part)
+    second_step = next_norm / over_all(
+        each(
+            lambda w, m, q, c, s, z, qm, qs: w * w * q
+            + w * m * ((c - s) / z + qm)
+            + m * m * qs,
+            part,
+            more,
+            curve,
+            cross,
+            square,
+            sigma,
+            mixed_curve,
+            start_curve,
+        )
+    )
+    share = each(lambda z: second_step / z, sigma)
+    picture = each(lambda w, m: (first_step + second_step * m, second_step * w), part, more)
+    residual = each(
+        lambda w, m, h: (1.0 - w - h * m, w - h * w + h * m, h * w), part, more, share
+    )
+    return picture, residual
+
+
+def assemble_kernel(coils, group_steps, combos, is_residual, order, *refs):
+    infos, pieces, out = refs[:coils], refs[coils:-1], refs[-1]
+    groups = infos[0].shape[0]
+    numbers = [
+        [[info[g, row : row + 1, 0:1] for g in range(groups)] for info in infos]
+        for row in range(6)
+    ]
+    factors = coefficients(*numbers)[is_residual]
+    count = 3 if is_residual else 2
+    for place, (k, g) in enumerate(combos):
+
+        @pl.when(pl.program_id(0) // group_steps == place)
+        def _():
+            total = 0.0
+            for factor, piece in zip(factors[k][g], pieces[place * count :][:count]):
+                total += factor.reshape(1, 1, 1, 1) * piece[...].astype(f32)
+            out[...] = total
 
 
 def group_count_of(own_planes):
@@ -419,6 +499,9 @@
             [jnp.concatenate([cos_x, -sin_x], 1), jnp.concatenate([sin_x, cos_x], 1)], 0
         )
         mx, mx_back = mx.astype(bf16), table_parts(mx, 1)
+        measured, ey, mx, turn, block_of = lax.optimization_barrier(
+            (measured, ey, mx, turn, block_of)
+        )
         places_spec = pl.BlockSpec(memory_space=pltpu.SMEM)
         plane_spec = pl.BlockSpec((1, 2, rows, columns), lambda p: (p, 0, 0, 0))
         sens_specs = [
@@ -533,6 +616,62 @@
                 [plane_spec, plane_spec] + [whole_block(i) for i in (small, small, large)],
             )
 
+        def facts_of(samples, dots, start_total, facts):
+            inputs = [*samples, *dots, start_total, facts]
+            return pl.pallas_call(
+                functools.partial(facts_kernel, peers),
+                in_specs=[pl.BlockSpec(memory_space=pltpu.VMEM)] * len(inputs),
+                out_specs=pl.BlockSpec(memory_space=pltpu.VMEM),
+                out_shape=shaped((8, 128)),
+                compiler_params=params,
+            )(*inputs)
+
+        def assembled(infos, vectors, ks, out=None):
+            combos = [(k, g) for k in ks for g in groups]
+            order = jnp.stack(
+                [
+                    (coil_index ^ k) * own_planes + g * group_planes + p
+                    for k, g in combos
+                    for p in range(group_planes)
+                ]
+            ).astype(jnp.int32)
+            inputs = [vector[g][k] for k, g in combos for vector in vectors]
+
+            def spec(place):
+                first_step = place // len(vectors) * group_planes
+                return pl.BlockSpec(
+                    (1, 2, rows, columns),
+                    lambda i, o: (jnp.clip(i - first_step, 0, group_planes - 1), 0, 0, 0),
+                )
+
+            specs = [pl.BlockSpec(infos[0].shape, lambda i, o: (0, 0, 0))] * len(infos)
+            specs += [spec(place) for place in range(len(inputs))]
+            aliases = {}
+            kernel = functools.partial(
+                assemble_kernel, coil_count, group_planes, combos, len(vectors) == 3
+            )
+            if out is not None:
+                aliases = {1 + len(infos) + len(inputs): 0}
+                inner = kernel
+                inputs = inputs + [out]
+                specs.append(pl.BlockSpec(memory_space=pl.ANY))
+
+                def kernel(*refs):
+                    inner(*refs[:-2], refs[-1])
+
+            return pl.pallas_call(
+                kernel,
+                grid_spec=pltpu.PrefetchScalarGridSpec(
+                    num_scalar_prefetch=1,
+                    grid=(len(combos) * group_planes,),
+                    in_specs=specs,
+                    out_specs=pl.BlockSpec((1, 2, rows, columns), lambda i, o: (o[i], 0, 0, 0)),
+                ),
+                out_shape=shaped((planes, 2, rows, columns)),
+                input_output_aliases=aliases,
+                compiler_params=params,
+            )(order, *infos, *inputs)
+
         def second(samples, facts, residual, g):
             return back(
                 second_kernel,
@@ -628,6 +767,30 @@
             facts = stacked_dots([norm, energy])
             return residual, residual.astype(bf16), facts, stacked_dots(dots), total
 
+        def facts_of(samples, dots, start_total, facts):
+            total = added(samples)
+            square, cross = tree_sum(dots)[:2, 0]
+            values = [facts[0, 0], facts[1, 0], square, cross]
+            values += [jnp.sum(total * total), jnp.sum(total * start_total)]
+            return stacked_dots(values)
+
+        def assembled(infos, vectors, ks, out=None):
+            numbers = [
+                [[info[g, row, 0] for g in groups] for info in infos] for row in range(6)
+            ]
+            factors = coefficients(*numbers)[len(vectors) == 3]
+            if out is None:
+                out = jnp.zeros((planes, 2, rows, columns), f32)
+            for k in ks:
+                for g in groups:
+                    place = ((coil_index ^ k) * own_planes + g * group_planes, 0, 0, 0)
+                    piece = sum(
+                        factor * vector[g][k].astype(f32)
+                        for factor, vector in zip(factors[k][g], vectors)
+                    )
+                    out = lax.dynamic_update_slice(out, piece, place)
+            return out
+
         def second(samples, facts, residual, g):
             again = applied_to(samples, residual, g)
             return (residual - step_of(facts[0, 0], facts[1, 0]) * again).astype(bf16)
@@ -639,7 +802,7 @@
         return [swapped(own, "coil", k) for k in first_bits]
 
     images = measured_images()
-    start_pieces, residual_pieces, mixed_own, mixed_sent, values = [], [], [], [], []
+    start_pieces, residual_pieces, mixed_pieces, infos = [], [], [], []
     for g in groups:
         right_side, start_own, norm = start(images, g)
         start_sent = sent_by_bits(start_own)
@@ -655,55 +818,21 @@
         samples = exchanged(forward(residual, g))
         dots = exchanged(dots)
         samples, dots, residual_sent = lax.optimization_barrier((samples, dots, residual_sent))
-        total = added(samples)
-        square, cross = tree_sum(dots)[:2, 0]
-        value = [facts[0, 0], facts[1, 0], square, cross]
-        value += [jnp.sum(total * total), jnp.sum(total * start_total)]
-        values.append(jnp.stack(value))
-        rounded = second(samples, facts, residual, g)
-        rounded, pieces = lax.optimization_barrier(
-            (rounded, completed(residual_own, residual_sent))
+        info = facts_of(samples, dots, start_total, facts)
+        infos.append(info)
+        rounded = second(samples, info, residual, g)
+        last = g == groups[-1]
+        others = exchanged(jnp.stack(infos), "coil") if last else []
+        rounded, others, pieces = lax.optimization_barrier(
+            (rounded, others, completed(residual_own, residual_sent))
         )
         residual_pieces.append(pieces)
-        mixed_own.append(rounded)
-        mixed_sent.append(sent_by_bits(rounded))
-
-    values = jnp.stack(exchanged(jnp.stack(values), "coil"))
-    values, mixed_sent[-1][0] = lax.optimization_barrier((values, mixed_sent[-1][0]))
-    mixed_pieces = [completed(mixed_own[g], mixed_sent[g]) for g in groups]
-    norm, energy, square, cross, again, mixed = [values[:, :, i] for i in range(6)]
-    curve, mixed_curve = again + damping * square, mixed + damping * cross
-
-    def over_all(value):
-        return tree_sum([jnp.sum(value[k]) for k in range(coil_count)])
-
-    sigma = step_of(norm, energy)
-    start_norm = over_all(norm)
-    first_step = start_norm / over_all(energy + damping * norm)
-    part = first_step / sigma
-    rest = 1.0 - part
-    next_norm = over_all(part * part * square + 2.0 * part * rest * cross + rest * rest * norm)
-    more = rest + next_norm / start_norm
-    second_step = next_norm / over_all(
-        part * part * curve
-        + part * more * ((cross - square) / sigma + mixed_curve)
-        + more * more * (energy + damping * norm)
-    )
-    share = second_step / sigma
-    picture = jnp.zeros((planes, 2, rows, columns), f32)
-    out = jnp.zeros((planes, 2, rows, columns), f32)
-    for k in range(coil_count):
-        for g in groups:
-            place = ((coil_index ^ k) * own_planes + g * group_planes, 0, 0, 0)
-            vector = start_pieces[g][k].astype(f32)
-            known = residual_pieces[g][k].astype(f32)
-            weight, ratio, length = part[k, g], more[k, g], share[k, g]
-            piece = (first_step + second_step * ratio) * vector + second_step * weight * known
-            picture = lax.dynamic_update_slice(picture, piece, place)
-            piece = (weight - length * weight + length * ratio) * known
-            piece += (rest[k, g] - length * ratio) * vector
-            piece += length * weight * mixed_pieces[g][k].astype(f32)
-            out = lax.dynamic_update_slice(out, piece, place)
+        mixed_pieces.append(completed(rounded, sent_by_bits(rounded)))
+
+    picture = assembled(others, [start_pieces, residual_pieces], range(coil_count))
+    vectors = [start_pieces, residual_pieces, mixed_pieces]
+    out = assembled(others, vectors, range(coil_count - 1))
+    out = assembled(others, vectors, [coil_count - 1], out)
     return picture, out
 
 

time: 219 us -> 197 us (0.90)
  between operations: 31.8 us -> 1.03 us
  Pallas kernels: 54.2 us -> 70 us
  waiting for transfers between devices: 56 us -> 71.3 us
  local copies, waits for them, and re-layouts: 24.4 us -> 10.6 us
  other arithmetic: 17.3 us -> 9.21 us
    pallas_call x0 -> x4, Pallas kernels: none -> 20.9 us  [the longest x3 18.8 us: assembled(): pl.pallas_call(kernel, grid_spec=pltpu.PrefetchScalarGridSpec(num_scalar_...]
    ppermute x36, waiting for transfers between devices: 43.7 us -> 56.4 us  [swapped(): lax.ppermute(array, axis, [(i, i ^ k) for i in range(lax.axis_size(axis))])]
    slice x10 -> x0, local copies, waits for them, and re-layouts: 6.66 us -> none  [the longest x4 2.56 us: over_all(): return tree_sum([jnp.sum(value[k]) for k in range(coil_count)])]
    pallas_call x6, Pallas kernels: 54.2 us -> 49.1 us  [call(): pl.pallas_call(kernel, grid=grid, in_specs=specs, out_specs=out_specs, ou...]
    another operation x4 -> x2, local copies, waits for them, and re-layouts: 5.36 us -> 1.31 us  [assembled(): jnp.stack([(coil_index ^ k) * own_planes + g * group_planes + p for k, g...]
    dynamic_update_slice x5 -> x0, other arithmetic: 4 us -> none  [the longest x4 3.79 us: on_device(): out = lax.dynamic_update_slice(out, piece, place)]
    unnamed x50 -> x52, local copies, waits for them, and re-layouts: 6.07 us -> 3 us
    all_to_all x1, waiting for transfers between devices: 12.3 us -> 14.9 us  [on_device(): lax.all_to_all(sens_source[:, g * group_planes:(g + 1) * group_planes], '...]
  transfers between devices with their start and end apart: 37 -> 37, of which waited for: 14 -> 13; matrix products, arithmetic and copies ran while one was open for 16% -> 9% of each run, Pallas kernels for 22% -> 31%
where the time goes in v5:
time: 197 us; the launch traced here: 196 us
  waiting for transfers between devices  71.3 us (36%)
  Pallas kernels  70 us (36%)
  starting transfers between devices  34.3 us (17%)
  local copies, waits for them, and re-layouts  10.6 us (5%)
  other arithmetic  9.21 us (5%)
    ppermute x36, waiting for transfers between devices, swapped(): lax.ppermute(array, axis, [(i, i ^ k) for i in range(lax.axis_size(axis))])  56.4 us
    pallas_call x6, Pallas kernels, call(): pl.pallas_call(kernel, grid=grid, in_specs=specs, out_specs=out_specs, ou...  49.1 us
    ppermute x36, starting transfers between devices, swapped(): lax.ppermute(array, axis, [(i, i ^ k) for i in range(lax.axis_size(axis))])  30.6 us
    pallas_call x3, Pallas kernels, assembled(): pl.pallas_call(kernel, grid_spec=pltpu.PrefetchScalarGridSpec(num_scalar_...  18.8 us
    all_to_all x1, waiting for transfers between devices, on_device(): lax.all_to_all(sens_source[:, g * group_planes:(g + 1) * group_planes], '...  14.9 us
  transfers between devices with their start and end apart: 37, of which 13 were waited for; matrix products, arithmetic and copies ran while one was open for 9% of the time, Pallas kernels for 31%

profile of v5, /device:TPU:0, one launch (start us, length us, event | category | flops | bytes accessed | tf_op | source)
XLA Modules:
  0.0 196.4 jit_solution(3310445979311272176)
XLA Ops:
  0.6 3.0 %collective-permute-start.10 = (bf16[32,128,128]{2,1,0:T(8,128)(2,1)}, bf16[32,128,128]{2,1,0:T(8,128)(2,1)S(1)}, u32[]{:S(2)}, u32[]{:S(2)}) collective-permute-start(bf16[32,128,128]{2,1,0:T(8,128)(2,1)} %refs_4_.7), channel_id=1, source_target_pairs={{0,2},{1,3},{2,0},{3,1},{4,6},{5,7},{6,4},{7,5},{8,10},{9,11},{10,... | collective-permute-start | bytes 3145736 | tf_op jit(solution)/shard_map/ppermute | solution.py:398
  4.4 3.7 %collective-permute-start.2 = (bf16[2,2,1024]{2,1,0:T(2,128)(2,1)S(1)}, bf16[2,2,1024]{2,1,0:T(2,128)(2,1)S(1)}, u32[]{:S(2)}, u32[]{:S(2)}) collective-permute-start(bf16[2,2,1024]{2,1,0:T(2,128)(2,1)S(1)} %get-tuple-element.116), channel_id=1, source_target_pairs={{0,12},{4,8},{8,4},{12,0},{1,13},{5,9},{9,5},{13,1},{2,14},{6,10},... | collective-permute-start | bytes 24584 | tf_op jit(solution)/shard_map/ppermute | solution.py:398
  12.7 3.6 %all-to-all-start = ((bf16[4,2,2,128,512]{4,3,2,1,0:T(8,128)(2,1)}), bf16[4,2,2,128,512]{4,3,2,1,0:T(8,128)(2,1)S(1)}, u32[]{:S(2)}, u32[]{:S(2)}) async-start(bf16[4,2,2,128,512]{4,3,2,1,0:T(8,128)(2,1)} %bitcast.45), calls=%async_computation | async-start | bytes 4194304 | tf_op jit(solution)/shard_map/all_to_all | solution.py:437
  19.0 8.1 %collective-permute-done.7 = s32[96]{0:T(128)S(1)} collective-permute-done((s32[96]{0:T(128)S(1)}, s32[96]{0:T(128)S(1)}, u32[]{:S(2)}, u32[]{:S(2)}) %collective-permute-start.7) | collective-permute-done | bytes 416 | tf_op jit(solution)/shard_map/ppermute | solution.py:398
  39.6 9.5 %shard_map.77.images = f32[4,2,2,128,512]{4,3,2,1,0:T(8,128)} custom-call(s32[128]{0:T(128)} %reshape.473.block, bf16[32,16,128]{2,1,0:T(8,128)(2,1)} %pad_maximum_fusion.3.samples, bf16[32,128,128]{2,1,0:T(8,128)(2,1)} %refs_4_.7, bf16[32,128,128]{2,1,0:T(8,128)(2,1)} %collective-permute-done.9.refs_1_.refs_5_, bf16[32,128,128]{2,1,0:T(8,128)(2,1)} %copy-done.1, ...), custom_call_target="tpu_custom_call" | custom-call | flops 1342177280 | bytes 6423040 | tf_op jit(solution)/shard_map/pallas_call | solution.py:520
  49.0 14.9 %all-to-all-done.refs_0_.refs_1_.refs_2_.refs_3_.refs_8_.refs_9_.refs_10_.refs_11_ = bf16[4,2,2,128,512]{4,3,2,1,0:T(8,128)(2,1)S(1)} async-done(((bf16[4,2,2,128,512]{4,3,2,1,0:T(8,128)(2,1)}), bf16[4,2,2,128,512]{4,3,2,1,0:T(8,128)(2,1)S(1)}, u32[]{:S(2)}, u32[]{:S(2)}) %all-to-all-start) | async-done | bytes 2097184 | tf_op jit(solution)/shard_map/all_to_all | solution.py:437
  65.3 5.1 %shard_map.78 = (f32[2,2,128,512]{3,2,1,0:T(8,128)}, bf16[2,2,128,512]{3,2,1,0:T(8,128)(2,1)}, f32[8,128]{1,0:T(8,128)}) custom-call(f32[4,2,2,128,512]{4,3,2,1,0:T(8,128)} %shard_map.77.images, bf16[4,2,2,128,512]{4,3,2,1,0:T(8,128)(2,1)} %copy-done, bf16[4,2,2,128,512]{4,3,2,1,0:T(8,128)(2,1)} %copy-done, bf16[4,2,2,128,512]{4,3,2,1,0:T(8,128)(2,1)} %copy-done, ...), custom_call_target="tpu_custom_call" | custom-call | bytes 12582912 | tf_op jit(solution)/shard_map/pallas_call | solution.py:520
  70.5 2.0 %collective-permute-start.18 = (bf16[2,2,128,512]{3,2,1,0:T(8,128)(2,1)}, bf16[2,2,128,512]{3,2,1,0:T(8,128)(2,1)S(1)}, u32[]{:S(2)}, u32[]{:S(2)}) collective-permute-start(bf16[2,2,128,512]{3,2,1,0:T(8,128)(2,1)} %get-tuple-element.101.refs_4_), channel_id=1, source_target_pairs={{0,4},{4,0},{8,12},{12,8},{1,5},{5,1},{9,13},{13,9},{2,6},{6,2},{1... | collective-permute-start | bytes 1572872 | tf_op jit(solution)/shard_map/ppermute | solution.py:398
  74.4 6.6 %shard_map.79.refs_0_ = bf16[512,128]{1,0:T(8,128)(2,1)} custom-call(s32[128]{0:T(128)} %reshape.472.block, f32[2,2,128,512]{3,2,1,0:T(8,128)} %get-tuple-element.64.picture.refs_19_, bf16[4,2,2,128,512]{4,3,2,1,0:T(8,128)(2,1)} %copy-done, bf16[4,2,2,128,512]{4,3,2,1,0:T(8,128)(2,1)} %copy-done, bf16[4,2,2,128,512]{4,3,2,1,0:T(8,128)(2,1)} %copy-done, ...), custom_call_target="tpu_custom_call" | custom-call | flops 1342177280 | bytes 14156288 | tf_op jit(solution)/shard_map/pallas_call | solution.py:520
  82.9 3.9 %collective-permute-done.14.refs_3_ = bf16[512,128]{1,0:T(8,128)(2,1)S(1)} collective-permute-done((bf16[512,128]{1,0:T(8,128)(2,1)}, bf16[512,128]{1,0:T(8,128)(2,1)S(1)}, u32[]{:S(2)}, u32[]{:S(2)}) %collective-permute-start.14) | collective-permute-done | bytes 131104 | tf_op jit(solution)/shard_map/ppermute | solution.py:398
  86.8 3.0 %collective-permute-done.13.refs_2_ = bf16[512,128]{1,0:T(8,128)(2,1)S(1)} collective-permute-done((bf16[512,128]{1,0:T(8,128)(2,1)}, bf16[512,128]{1,0:T(8,128)(2,1)S(1)}, u32[]{:S(2)}, u32[]{:S(2)}) %collective-permute-start.13) | collective-permute-done | bytes 131104 | tf_op jit(solution)/shard_map/ppermute | solution.py:398
  89.8 3.9 %collective-permute-done.19.refs_8_.refs_10_ = bf16[2,2,128,512]{3,2,1,0:T(8,128)(2,1)S(1)} collective-permute-done((bf16[2,2,128,512]{3,2,1,0:T(8,128)(2,1)}, bf16[2,2,128,512]{3,2,1,0:T(8,128)(2,1)S(1)}, u32[]{:S(2)}, u32[]{:S(2)}) %collective-permute-start.19) | collective-permute-done | bytes 524320 | tf_op jit(solution)/shard_map/ppermute | solution.py:398
  95.2 11.0 %shard_map.80 = (f32[2,2,128,512]{3,2,1,0:T(8,128)}, bf16[2,2,128,512]{3,2,1,0:T(8,128)(2,1)}, f32[8,128]{1,0:T(8,128)}, f32[8,128]{1,0:T(8,128)}, f32[512,128]{1,0:T(8,128)}) custom-call(s32[128]{0:T(128)} %reshape.472.block, bf16[512,128]{1,0:T(8,128)(2,1)} %shard_map.79.refs_0_, bf16[512,128]{1,0:T(8,128)(2,1)} %copy-done.16, ...), custom_call_target="tpu_custom_call" | custom-call | flops 1342177280 | bytes 16269824 | tf_op jit(solution)/shard_map/pallas_call | solution.py:520
  112.0 6.5 %shard_map.81.refs_0_ = bf16[512,128]{1,0:T(8,128)(2,1)} custom-call(s32[128]{0:T(128)} %reshape.472.block, f32[2,2,128,512]{3,2,1,0:T(8,128)} %get-tuple-element.82.picture.refs_16_, bf16[4,2,2,128,512]{4,3,2,1,0:T(8,128)(2,1)} %copy-done, bf16[4,2,2,128,512]{4,3,2,1,0:T(8,128)(2,1)} %copy-done, bf16[4,2,2,128,512]{4,3,2,1,0:T(8,128)(2,1)} %copy-done, ...), custom_call_target="tpu_custom_call" | custom-call | flops 1342177280 | bytes 14156288 | tf_op jit(solution)/shard_map/pallas_call | solution.py:520
  120.5 3.8 %collective-permute-done.23.refs_3_ = bf16[512,128]{1,0:T(8,128)(2,1)S(1)} collective-permute-done((bf16[512,128]{1,0:T(8,128)(2,1)}, bf16[512,128]{1,0:T(8,128)(2,1)S(1)}, u32[]{:S(2)}, u32[]{:S(2)}) %collective-permute-start.23) | collective-permute-done | bytes 131104 | tf_op jit(solution)/shard_map/ppermute | solution.py:398
  124.3 3.1 %collective-permute-done.22.refs_2_ = bf16[512,128]{1,0:T(8,128)(2,1)S(1)} collective-permute-done((bf16[512,128]{1,0:T(8,128)(2,1)}, bf16[512,128]{1,0:T(8,128)(2,1)S(1)}, u32[]{:S(2)}, u32[]{:S(2)}) %collective-permute-start.22) | collective-permute-done | bytes 131104 | tf_op jit(solution)/shard_map/ppermute | solution.py:398
  127.4 4.3 %collective-permute-done.28.refs_9_.refs_11_ = bf16[2,2,128,512]{3,2,1,0:T(8,128)(2,1)S(1)} collective-permute-done((bf16[2,2,128,512]{3,2,1,0:T(8,128)(2,1)}, bf16[2,2,128,512]{3,2,1,0:T(8,128)(2,1)S(1)}, u32[]{:S(2)}, u32[]{:S(2)}) %collective-permute-start.28) | collective-permute-done | bytes 524320 | tf_op jit(solution)/shard_map/ppermute | solution.py:398
  132.5 2.1 %shard_map.82.refs_15_ = f32[8,128]{1,0:T(8,128)} custom-call(bf16[512,128]{1,0:T(8,128)(2,1)} %shard_map.81.refs_0_, bf16[512,128]{1,0:T(8,128)(2,1)} %copy-done.10, bf16[512,128]{1,0:T(8,128)(2,1)} %copy-done.9, bf16[512,128]{1,0:T(8,128)(2,1)} %copy-done.8, f32[8,128]{1,0:T(8,128)} %get-tuple-element.89.refs_4_, f32[8,128]{1,0:T(8,128)} %copy-done.22, ...), custom_call_target="tpu_custom_call" | custom-call | tf_op jit(solution)/shard_map/pallas_call | solution.py:621
  134.6 1.9 collective-permute-start.31
  139.0 10.4 %shard_map.83.refs_6_ = bf16[2,2,128,512]{3,2,1,0:T(8,128)(2,1)} custom-call(s32[128]{0:T(128)} %reshape.472.block, bf16[512,128]{1,0:T(8,128)(2,1)} %shard_map.81.refs_0_, bf16[512,128]{1,0:T(8,128)(2,1)} %copy-done.10, bf16[512,128]{1,0:T(8,128)(2,1)} %copy-done.9, bf16[512,128]{1,0:T(8,128)(2,1)} %copy-done.8, bf16[32,128,128]{2,1,0:T(8,128)(2,1)} %refs_4_.7, ...), custom_call_target="tpu_custom_call" | custom-call | flops 1342177280 | bytes 16257536 | tf_op jit(solution)/shard_map/pallas_call | solution.py:520
  152.0 22.0 %collective-permute-done.33.refs_12_ = bf16[2,2,128,512]{3,2,1,0:T(8,128)(2,1)S(1)} collective-permute-done((bf16[2,2,128,512]{3,2,1,0:T(8,128)(2,1)}, bf16[2,2,128,512]{3,2,1,0:T(8,128)(2,1)S(1)}, u32[]{:S(2)}, u32[]{:S(2)}) %collective-permute-start.33) | collective-permute-done | bytes 524320 | tf_op jit(solution)/shard_map/ppermute | solution.py:398
  175.9 8.2 %shard_map.84 = f32[8,2,128,512]{3,2,1,0:T(8,128)} custom-call(s32[8]{0:T(128)} %stack.92.order, f32[1,8,128]{2,1,0:T(8,128)} %bitcast.49, f32[1,8,128]{2,1,0:T(8,128)} %copy-done.19, f32[1,8,128]{2,1,0:T(8,128)} %copy-done.18, f32[1,8,128]{2,1,0:T(8,128)} %copy-done.17, bf16[2,2,128,512]{3,2,1,0:T(8,128)(2,1)} %get-tuple-element.101.refs_4_, ...), custom_call_target="tpu_custom_call" | custom-call | tf_op jit(solution)/shard_map/pallas_call | solution.py:662
  184.9 7.3 %shard_map.85.refs_8_ = f32[8,2,128,512]{3,2,1,0:T(8,128)} custom-call(s32[6]{0:T(128)} %stack.107.order, f32[1,8,128]{2,1,0:T(8,128)} %bitcast.50, f32[1,8,128]{2,1,0:T(8,128)} %copy-done.19, f32[1,8,128]{2,1,0:T(8,128)} %copy-done.18, f32[1,8,128]{2,1,0:T(8,128)} %copy-done.17, bf16[2,2,128,512]{3,2,1,0:T(8,128)(2,1)} %get-tuple-element.101.refs_4_, ...), custom_call_target="tpu_custom_call" | custom-call | tf_op jit(solution)/shard_map/pallas_call | solution.py:662
  193.1 3.3 %shard_map.86 = f32[8,2,128,512]{3,2,1,0:T(8,128)} custom-call(s32[2]{0:T(128)} %pad_add_fusion.2.refs_0_, f32[1,8,128]{2,1,0:T(8,128)} %bitcast.51, f32[1,8,128]{2,1,0:T(8,128)} %copy-done.19, f32[1,8,128]{2,1,0:T(8,128)} %copy-done.18, f32[1,8,128]{2,1,0:T(8,128)} %copy-done.17, ...), custom_call_target="tpu_custom_call", output_to_operand_aliasing={{}: (8, {})} | custom-call | tf_op jit(solution)/shard_map/pallas_call | solution.py:662
  (159 shorter events, 44.1 us)
Async XLA Ops:
  0.6 31.4 %collective-permute-start.10 = (bf16[32,128,128]{2,1,0:T(8,128)(2,1)}, bf16[32,128,128]{2,1,0:T(8,128)(2,1)S(1)}, u32[]{:S(2)}, u32[]{:S(2)}) collective-permute-start(bf16[32,128,128]{2,1,0:T(8,128)(2,1)} %refs_4_.7), channel_id=1, source_target_pairs={{0,2},{1,3},{2,0},{3,1},{4,6},{5,7},{6,4},{7,5},{8,10},{9,11},{10,... | collective-permute-start | bytes 3145736 | tf_op jit(solution)/shard_map/ppermute | solution.py:398
  3.7 35.9 %collective-permute-start.9 = (bf16[32,128,128]{2,1,0:T(8,128)(2,1)}, bf16[32,128,128]{2,1,0:T(8,128)(2,1)}, u32[]{:S(2)}, u32[]{:S(2)}) collective-permute-start(bf16[32,128,128]{2,1,0:T(8,128)(2,1)} %refs_4_.7), channel_id=1, source_target_pairs={{0,1},{1,0},{2,3},{3,2},{4,5},{5,4},{6,7},{7,6},{8,9},{9,8},{10,11... | collective-permute-start | bytes 3145736 | tf_op jit(solution)/shard_map/ppermute | solution.py:398
  12.7 51.3 %all-to-all-start = ((bf16[4,2,2,128,512]{4,3,2,1,0:T(8,128)(2,1)}), bf16[4,2,2,128,512]{4,3,2,1,0:T(8,128)(2,1)S(1)}, u32[]{:S(2)}, u32[]{:S(2)}) async-start(bf16[4,2,2,128,512]{4,3,2,1,0:T(8,128)(2,1)} %bitcast.45), calls=%async_computation | async-start | bytes 4194304 | tf_op jit(solution)/shard_map/all_to_all | solution.py:437
  17.7 9.3 %collective-permute-start.7 = (s32[96]{0:T(128)S(1)}, s32[96]{0:T(128)S(1)}, u32[]{:S(2)}, u32[]{:S(2)}) collective-permute-start(s32[96]{0:T(128)S(1)} %pad_add_fusion.1), channel_id=1, source_target_pairs={{0,2},{1,3},{2,0},{3,1},{4,6},{5,7},{6,4},{7,5},{8,10},{9,11},{10,... | collective-permute-start | bytes 1160 | tf_op jit(solution)/shard_map/ppermute | solution.py:398
  18.3 10.7 %collective-permute-start.6 = (s32[96]{0:T(128)S(1)}, s32[96]{0:T(128)S(1)}, u32[]{:S(2)}, u32[]{:S(2)}) collective-permute-start(s32[96]{0:T(128)S(1)} %pad_add_fusion.1), channel_id=1, source_target_pairs={{0,1},{1,0},{2,3},{3,2},{4,5},{5,4},{6,7},{7,6},{8,9},{9,8},{10,11... | collective-permute-start | bytes 1160 | tf_op jit(solution)/shard_map/ppermute | solution.py:398
  27.2 9.5 %collective-permute-start.4 = (bf16[8,16,128]{2,1,0:T(8,128)(2,1)S(1)}, bf16[8,16,128]{2,1,0:T(8,128)(2,1)S(1)}, u32[]{:S(2)}, u32[]{:S(2)}) collective-permute-start(bf16[8,16,128]{2,1,0:T(8,128)(2,1)S(1)} %fusion.14), channel_id=1, source_target_pairs={{0,2},{1,3},{2,0},{3,1},{4,6},{5,7},{6,4},{7,5},{8,10},{9,11},{10,... | collective-permute-start | bytes 98312 | tf_op jit(solution)/shard_map/ppermute | solution.py:398
  28.9 10.0 %collective-permute-start.3 = (bf16[8,16,128]{2,1,0:T(8,128)(2,1)S(1)}, bf16[8,16,128]{2,1,0:T(8,128)(2,1)S(1)}, u32[]{:S(2)}, u32[]{:S(2)}) collective-permute-start(bf16[8,16,128]{2,1,0:T(8,128)(2,1)S(1)} %fusion.14), channel_id=1, source_target_pairs={{0,1},{1,0},{2,3},{3,2},{4,5},{5,4},{6,7},{7,6},{8,9},{9,8},{10,11... | collective-permute-start | bytes 98312 | tf_op jit(solution)/shard_map/ppermute | solution.py:398
  70.4 23.3 %collective-permute-start.19 = (bf16[2,2,128,512]{3,2,1,0:T(8,128)(2,1)}, bf16[2,2,128,512]{3,2,1,0:T(8,128)(2,1)S(1)}, u32[]{:S(2)}, u32[]{:S(2)}) collective-permute-start(bf16[2,2,128,512]{3,2,1,0:T(8,128)(2,1)} %get-tuple-element.101.refs_4_), channel_id=1, source_target_pairs={{0,8},{4,12},{8,0},{12,4},{1,9},{5,13},{9,1},{13,5},{2,10},{6,14},... | collective-permute-start | bytes 1572872 | tf_op jit(solution)/shard_map/ppermute | solution.py:398
  70.5 24.4 %collective-permute-start.18 = (bf16[2,2,128,512]{3,2,1,0:T(8,128)(2,1)}, bf16[2,2,128,512]{3,2,1,0:T(8,128)(2,1)S(1)}, u32[]{:S(2)}, u32[]{:S(2)}) collective-permute-start(bf16[2,2,128,512]{3,2,1,0:T(8,128)(2,1)} %get-tuple-element.101.refs_4_), channel_id=1, source_target_pairs={{0,4},{4,0},{8,12},{12,8},{1,5},{5,1},{9,13},{13,9},{2,6},{6,2},{1... | collective-permute-start | bytes 1572872 | tf_op jit(solution)/shard_map/ppermute | solution.py:398
  72.5 8.8 %collective-permute-start.16 = (f32[8,128]{1,0:T(8,128)}, f32[8,128]{1,0:T(8,128)S(1)}, u32[]{:S(2)}, u32[]{:S(2)}) collective-permute-start(f32[8,128]{1,0:T(8,128)} %get-tuple-element.74.refs_15_), channel_id=1, source_target_pairs={{0,2},{1,3},{2,0},{3,1},{4,6},{5,7},{6,4},{7,5},{8,10},{9,11},{10,... | collective-permute-start | bytes 12296 | tf_op jit(solution)/shard_map/ppermute | solution.py:398
  73.0 9.6 %collective-permute-start.15 = (f32[8,128]{1,0:T(8,128)}, f32[8,128]{1,0:T(8,128)S(1)}, u32[]{:S(2)}, u32[]{:S(2)}) collective-permute-start(f32[8,128]{1,0:T(8,128)} %get-tuple-element.74.refs_15_), channel_id=1, source_target_pairs={{0,1},{1,0},{2,3},{3,2},{4,5},{5,4},{6,7},{7,6},{8,9},{9,8},{10,11... | collective-permute-start | bytes 12296 | tf_op jit(solution)/shard_map/ppermute | solution.py:398
  81.3 8.5 %collective-permute-start.13 = (bf16[512,128]{1,0:T(8,128)(2,1)}, bf16[512,128]{1,0:T(8,128)(2,1)S(1)}, u32[]{:S(2)}, u32[]{:S(2)}) collective-permute-start(bf16[512,128]{1,0:T(8,128)(2,1)} %shard_map.79.refs_0_), channel_id=1, source_target_pairs={{0,2},{1,3},{2,0},{3,1},{4,6},{5,7},{6,4},{7,5},{8,10},{9,11},{10,... | collective-permute-start | bytes 393224 | tf_op jit(solution)/shard_map/ppermute | solution.py:398
  94.9 12.7 %collective-permute-start.20 = (bf16[2,2,128,512]{3,2,1,0:T(8,128)(2,1)S(1)}, bf16[2,2,128,512]{3,2,1,0:T(8,128)(2,1)S(1)}, u32[]{:S(2)}, u32[]{:S(2)}) collective-permute-start(bf16[2,2,128,512]{3,2,1,0:T(8,128)(2,1)S(1)} %collective-permute-done.19.refs_8_.refs_10_), channel_id=1, source_target_pairs={{0,4},{4,0},{8,12},{12,8},{1,5},{5,1},{9,13},{13,9},{2,6},{6,2},{1... | collective-permute-start | bytes 1572872 | tf_op jit(solution)/shard_map/ppermute | solution.py:398
  107.6 24.1 %collective-permute-start.28 = (bf16[2,2,128,512]{3,2,1,0:T(8,128)(2,1)}, bf16[2,2,128,512]{3,2,1,0:T(8,128)(2,1)S(1)}, u32[]{:S(2)}, u32[]{:S(2)}) collective-permute-start(bf16[2,2,128,512]{3,2,1,0:T(8,128)(2,1)} %get-tuple-element.102.refs_5_), channel_id=1, source_target_pairs={{0,8},{4,12},{8,0},{12,4},{1,9},{5,13},{9,1},{13,5},{2,10},{6,14},... | collective-permute-start | bytes 1572872 | tf_op jit(solution)/shard_map/ppermute | solution.py:398
  108.4 23.4 %collective-permute-start.27 = (bf16[2,2,128,512]{3,2,1,0:T(8,128)(2,1)}, bf16[2,2,128,512]{3,2,1,0:T(8,128)(2,1)S(1)}, u32[]{:S(2)}, u32[]{:S(2)}) collective-permute-start(bf16[2,2,128,512]{3,2,1,0:T(8,128)(2,1)} %get-tuple-element.102.refs_5_), channel_id=1, source_target_pairs={{0,4},{4,0},{8,12},{12,8},{1,5},{5,1},{9,13},{13,9},{2,6},{6,2},{1... | collective-permute-start | bytes 1572872 | tf_op jit(solution)/shard_map/ppermute | solution.py:398
  110.1 8.8 %collective-permute-start.25 = (f32[8,128]{1,0:T(8,128)}, f32[8,128]{1,0:T(8,128)S(1)}, u32[]{:S(2)}, u32[]{:S(2)}) collective-permute-start(f32[8,128]{1,0:T(8,128)} %get-tuple-element.89.refs_4_), channel_id=1, source_target_pairs={{0,2},{1,3},{2,0},{3,1},{4,6},{5,7},{6,4},{7,5},{8,10},{9,11},{10,... | collective-permute-start | bytes 12296 | tf_op jit(solution)/shard_map/ppermute | solution.py:398
  110.7 9.8 %collective-permute-start.24 = (f32[8,128]{1,0:T(8,128)}, f32[8,128]{1,0:T(8,128)S(1)}, u32[]{:S(2)}, u32[]{:S(2)}) collective-permute-start(f32[8,128]{1,0:T(8,128)} %get-tuple-element.89.refs_4_), channel_id=1, source_target_pairs={{0,1},{1,0},{2,3},{3,2},{4,5},{5,4},{6,7},{7,6},{8,9},{9,8},{10,11... | collective-permute-start | bytes 12296 | tf_op jit(solution)/shard_map/ppermute | solution.py:398
  131.7 17.7 %collective-permute-start.32 = (bf16[2,2,128,512]{3,2,1,0:T(8,128)(2,1)S(1)}, bf16[2,2,128,512]{3,2,1,0:T(8,128)(2,1)S(1)}, u32[]{:S(2)}, u32[]{:S(2)}) collective-permute-start(bf16[2,2,128,512]{3,2,1,0:T(8,128)(2,1)S(1)} %collective-permute-done.28.refs_9_.refs_11_), channel_id=1, source_target_pairs={{0,4},{4,0},{8,12},{12,8},{1,5},{5,1},{9,13},{13,9},{2,6},{6,2},{1... | collective-permute-start | bytes 1572872 | tf_op jit(solution)/shard_map/ppermute | solution.py:398
  134.6 14.8 %collective-permute-start.31 = (f32[1,8,128]{2,1,0:T(8,128)}, f32[1,8,128]{2,1,0:T(8,128)S(1)}, u32[]{:S(2)}, u32[]{:S(2)}) collective-permute-start(f32[1,8,128]{2,1,0:T(8,128)} %bitcast.46), channel_id=1, source_target_pairs={{0,12},{4,8},{8,4},{12,0},{1,13},{5,9},{9,5},{13,1},{2,14},{6,10},... | collective-permute-start | bytes 12296 | tf_op jit(solution)/shard_map/ppermute | solution.py:398
  136.5 12.9 %collective-permute-start.30 = (f32[1,8,128]{2,1,0:T(8,128)}, f32[1,8,128]{2,1,0:T(8,128)S(1)}, u32[]{:S(2)}, u32[]{:S(2)}) collective-permute-start(f32[1,8,128]{2,1,0:T(8,128)} %bitcast.47), channel_id=1, source_target_pairs={{0,8},{4,12},{8,0},{12,4},{1,9},{5,13},{9,1},{13,5},{2,10},{6,14},... | collective-permute-start | bytes 12296 | tf_op jit(solution)/shard_map/ppermute | solution.py:398
  137.4 12.0 %collective-permute-start.29 = (f32[1,8,128]{2,1,0:T(8,128)}, f32[1,8,128]{2,1,0:T(8,128)S(1)}, u32[]{:S(2)}, u32[]{:S(2)}) collective-permute-start(f32[1,8,128]{2,1,0:T(8,128)} %bitcast.48), channel_id=1, source_target_pairs={{0,4},{4,0},{8,12},{12,8},{1,5},{5,1},{9,13},{13,9},{2,6},{6,2},{1... | collective-permute-start | bytes 12296 | tf_op jit(solution)/shard_map/ppermute | solution.py:398
  149.5 24.5 %collective-permute-start.33 = (bf16[2,2,128,512]{3,2,1,0:T(8,128)(2,1)}, bf16[2,2,128,512]{3,2,1,0:T(8,128)(2,1)S(1)}, u32[]{:S(2)}, u32[]{:S(2)}) collective-permute-start(bf16[2,2,128,512]{3,2,1,0:T(8,128)(2,1)} %shard_map.83.refs_6_), channel_id=1, source_target_pairs={{0,8},{4,12},{8,0},{12,4},{1,9},{5,13},{9,1},{13,5},{2,10},{6,14},... | collective-permute-start | bytes 1572872 | tf_op jit(solution)/shard_map/ppermute | solution.py:398
  150.8 33.3 %collective-permute-start.35 = (bf16[2,2,128,512]{3,2,1,0:T(8,128)(2,1)}, bf16[2,2,128,512]{3,2,1,0:T(8,128)(2,1)S(1)}, u32[]{:S(2)}, u32[]{:S(2)}) collective-permute-start(bf16[2,2,128,512]{3,2,1,0:T(8,128)(2,1)} %shard_map.83.refs_6_), channel_id=1, source_target_pairs={{0,4},{4,0},{8,12},{12,8},{1,5},{5,1},{9,13},{13,9},{2,6},{6,2},{1... | collective-permute-start | bytes 1572872 | tf_op jit(solution)/shard_map/ppermute | solution.py:398
  173.9 18.3 %collective-permute-start.34 = (bf16[2,2,128,512]{3,2,1,0:T(8,128)(2,1)S(1)}, bf16[2,2,128,512]{3,2,1,0:T(8,128)(2,1)S(1)}, u32[]{:S(2)}, u32[]{:S(2)}) collective-permute-start(bf16[2,2,128,512]{3,2,1,0:T(8,128)(2,1)S(1)} %collective-permute-done.33.refs_12_), channel_id=1, source_target_pairs={{0,4},{4,0},{8,12},{12,8},{1,5},{5,1},{9,13},{13,9},{2,6},{6,2},{1... | collective-permute-start | bytes 1572872 | tf_op jit(solution)/shard_map/ppermute | solution.py:398
  (39 other events, 388.0 us)

commit v6 on v5

--- a/solution.py
+++ b/solution.py
@@ -285,12 +285,11 @@
 
 
 def facts_kernel(peers, *refs):
-    samples, dots = refs[:peers], refs[peers : 2 * peers]
-    start_total, facts, out = refs[2 * peers :]
+    samples = refs[:peers]
+    dots, start_total, facts, out = refs[peers:]
     summed = tree_sum([part[...].astype(f32) for part in samples])
-    both = tree_sum([part[...] for part in dots])
     rows = lax.broadcasted_iota(jnp.int32, out.shape, 0)
-    values = [facts[0:1], facts[1:2], both[0:1], both[1:2]]
+    values = [facts[0:1], facts[1:2], dots[0:1], dots[1:2]]
     values += [jnp.sum(summed * summed), jnp.sum(summed * start_total[...])]
     total = jnp.zeros(out.shape, f32)
     for row, value in enumerate(values):
@@ -345,22 +344,33 @@
     return picture, residual
 
 
-def assemble_kernel(coils, group_steps, combos, is_residual, order, *refs):
-    infos, pieces, out = refs[:coils], refs[coils:-1], refs[-1]
+def assemble_kernel(coils, group_steps, combos, is_residual, has_out, order, *refs):
+    infos, pieces, (out, kept) = refs[:coils], refs[coils:-2], refs[-2:]
     groups = infos[0].shape[0]
-    numbers = [
-        [[info[g, row : row + 1, 0:1] for g in range(groups)] for info in infos]
-        for row in range(6)
-    ]
-    factors = coefficients(*numbers)[is_residual]
     count = 3 if is_residual else 2
-    for place, (k, g) in enumerate(combos):
+
+    @pl.when(pl.program_id(0) == 0)
+    def _():
+        numbers = [
+            [[info[g, row : row + 1, 0:1] for g in range(groups)] for info in infos]
+            for row in range(6)
+        ]
+        factors = coefficients(*numbers)[is_residual]
+        rows = lax.broadcasted_iota(jnp.int32, kept.shape[1:], 0)
+        for place, (k, g) in enumerate(combos):
+            total = jnp.zeros(kept.shape[1:], f32)
+            for row, factor in enumerate(factors[k][g]):
+                total = jnp.where(rows == row, factor, total)
+            kept[place] = total
+
+    for place in range(len(combos)):
 
         @pl.when(pl.program_id(0) // group_steps == place)
         def _():
             total = 0.0
-            for factor, piece in zip(factors[k][g], pieces[place * count :][:count]):
-                total += factor.reshape(1, 1, 1, 1) * piece[...].astype(f32)
+            for row, piece in enumerate(pieces[place * count :][:count]):
+                factor = kept[place, row : row + 1, 0:1].reshape(1, 1, 1, 1)
+                total += factor * piece[...].astype(f32)
             out[...] = total
 
 
@@ -617,7 +627,7 @@
             )
 
         def facts_of(samples, dots, start_total, facts):
-            inputs = [*samples, *dots, start_total, facts]
+            inputs = [*samples, dots, start_total, facts]
             return pl.pallas_call(
                 functools.partial(facts_kernel, peers),
                 in_specs=[pl.BlockSpec(memory_space=pltpu.VMEM)] * len(inputs),
@@ -648,16 +658,17 @@
             specs += [spec(place) for place in range(len(inputs))]
             aliases = {}
             kernel = functools.partial(
-                assemble_kernel, coil_count, group_planes, combos, len(vectors) == 3
+                assemble_kernel,
+                coil_count,
+                group_planes,
+                combos,
+                len(vectors) == 3,
+                out is not None,
             )
             if out is not None:
                 aliases = {1 + len(infos) + len(inputs): 0}
-                inner = kernel
                 inputs = inputs + [out]
                 specs.append(pl.BlockSpec(memory_space=pl.ANY))
-
-                def kernel(*refs):
-                    inner(*refs[:-2], refs[-1])
 
             return pl.pallas_call(
                 kernel,
@@ -666,6 +677,7 @@
                     grid=(len(combos) * group_planes,),
                     in_specs=specs,
                     out_specs=pl.BlockSpec((1, 2, rows, columns), lambda i, o: (o[i], 0, 0, 0)),
+                    scratch_shapes=[pltpu.VMEM((len(combos), 8, 128), f32)],
                 ),
                 out_shape=shaped((planes, 2, rows, columns)),
                 input_output_aliases=aliases,
@@ -769,8 +781,7 @@
 
         def facts_of(samples, dots, start_total, facts):
             total = added(samples)
-            square, cross = tree_sum(dots)[:2, 0]
-            values = [facts[0, 0], facts[1, 0], square, cross]
+            values = [facts[0, 0], facts[1, 0], dots[0, 0], dots[1, 0]]
             values += [jnp.sum(total * total), jnp.sum(total * start_total)]
             return stacked_dots(values)
 
@@ -802,37 +813,52 @@
         return [swapped(own, "coil", k) for k in first_bits]
 
     images = measured_images()
-    start_pieces, residual_pieces, mixed_pieces, infos = [], [], [], []
+    start_pieces, residual_pieces, mixed_own, mixed_sent, infos = [], [], [], [], []
     for g in groups:
         right_side, start_own, norm = start(images, g)
         start_sent = sent_by_bits(start_own)
         samples = exchanged(forward(right_side, g))
         norms = exchanged(norm)
-        samples, norms, start_sent = lax.optimization_barrier((samples, norms, start_sent))
         residual, residual_own, facts, dots, start_total = first(samples, norms, right_side, g)
-        residual, residual_own, pieces = lax.optimization_barrier(
-            (residual, residual_own, completed(start_own, start_sent))
-        )
-        start_pieces.append(pieces)
+        residual, residual_own, start_sent = lax.optimization_barrier(
+            (residual, residual_own, start_sent)
+        )
         residual_sent = sent_by_bits(residual_own)
         samples = exchanged(forward(residual, g))
-        dots = exchanged(dots)
-        samples, dots, residual_sent = lax.optimization_barrier((samples, dots, residual_sent))
+        samples, pieces = lax.optimization_barrier(
+            (samples, completed(start_own, start_sent))
+        )
+        start_pieces.append(pieces)
         info = facts_of(samples, dots, start_total, facts)
         infos.append(info)
         rounded = second(samples, info, residual, g)
         last = g == groups[-1]
         others = exchanged(jnp.stack(infos), "coil") if last else []
-        rounded, others, pieces = lax.optimization_barrier(
-            (rounded, others, completed(residual_own, residual_sent))
-        )
-        residual_pieces.append(pieces)
-        mixed_pieces.append(completed(rounded, sent_by_bits(rounded)))
+        rounded, others, residual_sent = lax.optimization_barrier(
+            (rounded, others, residual_sent)
+        )
+        residual_pieces.append(completed(residual_own, residual_sent))
+        mixed_own.append(rounded)
+        mixed_sent.append(sent_by_bits(rounded))
+
+    others, mixed_sent[-1][0] = lax.optimization_barrier((jnp.stack(others), mixed_sent[-1][0]))
+    rows_of = lax.broadcasted_iota(jnp.int32, others.shape, 2)
+    shared = (rows_of == 2) | (rows_of == 3)
+    others = jnp.where(shared, tree_sum(exchanged(others)), others)
+    others = [others[k] for k in range(coil_count)]
 
     picture = assembled(others, [start_pieces, residual_pieces], range(coil_count))
+    early = [
+        [own, sent[0]] + [None] * (coil_count - 2)
+        for own, sent in zip(mixed_own, mixed_sent)
+    ]
+    out = assembled(others, [start_pieces, residual_pieces, early], range(2))
+    out, mixed_sent = lax.optimization_barrier((out, mixed_sent))
+    mixed_pieces = [completed(own, sent) for own, sent in zip(mixed_own, mixed_sent)]
     vectors = [start_pieces, residual_pieces, mixed_pieces]
-    out = assembled(others, vectors, range(coil_count - 1))
-    out = assembled(others, vectors, [coil_count - 1], out)
+    late = coil_count - 1
+    out = assembled(others, vectors, range(2, late), out)
+    out = assembled(others, vectors, [late], out)
     return picture, out
 
 

time: 197 us -> 202 us (1.025)
    pallas_call x3 -> x4, Pallas kernels: 18.8 us -> 20.3 us  [assembled(): pl.pallas_call(kernel, grid_spec=pltpu.PrefetchScalarGridSpec(num_scalar_...]
where the time goes in v6:
time: 202 us; the launch traced here: 201 us
  waiting for transfers between devices  73 us (36%)
  Pallas kernels  71.5 us (35%)
  starting transfers between devices  34.2 us (17%)
  local copies, waits for them, and re-layouts  11 us (5%)
  other arithmetic  10.5 us (5%)
    ppermute x36, waiting for transfers between devices, swapped(): lax.ppermute(array, axis, [(i, i ^ k) for i in range(lax.axis_size(axis))])  56.8 us
    pallas_call x6, Pallas kernels, call(): pl.pallas_call(kernel, grid=grid, in_specs=specs, out_specs=out_specs, ou...  49 us
    ppermute x36, starting transfers between devices, swapped(): lax.ppermute(array, axis, [(i, i ^ k) for i in range(lax.axis_size(axis))])  30.6 us
    pallas_call x4, Pallas kernels, assembled(): pl.pallas_call(kernel, grid_spec=pltpu.PrefetchScalarGridSpec(num_scalar_...  20.3 us
    all_to_all x1, waiting for transfers between devices, on_device(): lax.all_to_all(sens_source[:, g * group_planes:(g + 1) * group_planes], '...  16.2 us
  transfers between devices with their start and end apart: 37, of which 13 were waited for; matrix products, arithmetic and copies ran while one was open for 9% of the time, Pallas kernels for 31%

profile of v6, /device:TPU:0, one launch (start us, length us, event | category | flops | bytes accessed | tf_op | source)
XLA Modules:
  0.0 201.2 jit_solution(3515666763007345687)
XLA Ops:
  0.6 3.0 %collective-permute-start.10 = (bf16[32,128,128]{2,1,0:T(8,128)(2,1)}, bf16[32,128,128]{2,1,0:T(8,128)(2,1)S(1)}, u32[]{:S(2)}, u32[]{:S(2)}) collective-permute-start(bf16[32,128,128]{2,1,0:T(8,128)(2,1)} %refs_4_.7), channel_id=1, source_target_pairs={{0,2},{1,3},{2,0},{3,1},{4,6},{5,7},{6,4},{7,5},{8,10},{9,11},{10,... | collective-permute-start | bytes 3145736 | tf_op jit(solution)/shard_map/ppermute | solution.py:408
  6.1 2.6 %collective-permute-start.1 = (bf16[2,2,1024]{2,1,0:T(2,128)(2,1)S(1)}, bf16[2,2,1024]{2,1,0:T(2,128)(2,1)S(1)}, u32[]{:S(2)}, u32[]{:S(2)}) collective-permute-start(bf16[2,2,1024]{2,1,0:T(2,128)(2,1)S(1)} %get-tuple-element.95), channel_id=1, source_target_pairs={{0,8},{4,12},{8,0},{12,4},{1,9},{5,13},{9,1},{13,5},{2,10},{6,14},... | collective-permute-start | bytes 24584 | tf_op jit(solution)/shard_map/ppermute | solution.py:408
  11.0 3.1 %collective-permute-done.2 = bf16[2,2,1024]{2,1,0:T(2,128)(2,1)S(1)} collective-permute-done((bf16[2,2,1024]{2,1,0:T(2,128)(2,1)S(1)}, bf16[2,2,1024]{2,1,0:T(2,128)(2,1)S(1)}, u32[]{:S(2)}, u32[]{:S(2)}) %collective-permute-start.2) | collective-permute-done | bytes 8224 | tf_op jit(solution)/shard_map/ppermute | solution.py:408
  14.1 3.6 %all-to-all-start = ((bf16[4,2,2,128,512]{4,3,2,1,0:T(8,128)(2,1)}), bf16[4,2,2,128,512]{4,3,2,1,0:T(8,128)(2,1)S(1)}, u32[]{:S(2)}, u32[]{:S(2)}) async-start(bf16[4,2,2,128,512]{4,3,2,1,0:T(8,128)(2,1)} %bitcast.57), calls=%async_computation | async-start | bytes 4194304 | tf_op jit(solution)/shard_map/all_to_all | solution.py:447
  20.4 6.6 %collective-permute-done.7 = s32[96]{0:T(128)S(1)} collective-permute-done((s32[96]{0:T(128)S(1)}, s32[96]{0:T(128)S(1)}, u32[]{:S(2)}, u32[]{:S(2)}) %collective-permute-start.7) | collective-permute-done | bytes 416 | tf_op jit(solution)/shard_map/ppermute | solution.py:408
  39.5 9.5 %shard_map.77.images = f32[4,2,2,128,512]{4,3,2,1,0:T(8,128)} custom-call(s32[128]{0:T(128)} %reshape.474.block, bf16[32,16,128]{2,1,0:T(8,128)(2,1)} %pad_maximum_fusion.3.samples, bf16[32,128,128]{2,1,0:T(8,128)(2,1)} %refs_4_.7, bf16[32,128,128]{2,1,0:T(8,128)(2,1)} %collective-permute-done.9.refs_1_.refs_5_, bf16[32,128,128]{2,1,0:T(8,128)(2,1)} %copy-done.1, ...), custom_call_target="tpu_custom_call" | custom-call | flops 1342177280 | bytes 6423040 | tf_op jit(solution)/shard_map/pallas_call | solution.py:530
  48.9 16.2 %all-to-all-done.refs_0_.refs_1_.refs_2_.refs_3_.refs_8_.refs_9_.refs_10_.refs_11_ = bf16[4,2,2,128,512]{4,3,2,1,0:T(8,128)(2,1)S(1)} async-done(((bf16[4,2,2,128,512]{4,3,2,1,0:T(8,128)(2,1)}), bf16[4,2,2,128,512]{4,3,2,1,0:T(8,128)(2,1)S(1)}, u32[]{:S(2)}, u32[]{:S(2)}) %all-to-all-start) | async-done | bytes 2097184 | tf_op jit(solution)/shard_map/all_to_all | solution.py:447
  66.5 5.1 %shard_map.78 = (f32[2,2,128,512]{3,2,1,0:T(8,128)}, bf16[2,2,128,512]{3,2,1,0:T(8,128)(2,1)}, f32[8,128]{1,0:T(8,128)}) custom-call(f32[4,2,2,128,512]{4,3,2,1,0:T(8,128)} %shard_map.77.images, bf16[4,2,2,128,512]{4,3,2,1,0:T(8,128)(2,1)} %copy-done, bf16[4,2,2,128,512]{4,3,2,1,0:T(8,128)(2,1)} %copy-done, bf16[4,2,2,128,512]{4,3,2,1,0:T(8,128)(2,1)} %copy-done, ...), custom_call_target="tpu_custom_call" | custom-call | bytes 12582912 | tf_op jit(solution)/shard_map/pallas_call | solution.py:530
  71.7 2.0 collective-permute-start.19
  75.5 6.5 %shard_map.79.refs_0_ = bf16[512,128]{1,0:T(8,128)(2,1)} custom-call(s32[128]{0:T(128)} %reshape.473.block, f32[2,2,128,512]{3,2,1,0:T(8,128)} %get-tuple-element.52.picture.refs_19_, bf16[4,2,2,128,512]{4,3,2,1,0:T(8,128)(2,1)} %copy-done, bf16[4,2,2,128,512]{4,3,2,1,0:T(8,128)(2,1)} %copy-done, bf16[4,2,2,128,512]{4,3,2,1,0:T(8,128)(2,1)} %copy-done, ...), custom_call_target="tpu_custom_call" | custom-call | flops 1342177280 | bytes 14156288 | tf_op jit(solution)/shard_map/pallas_call | solution.py:530
  84.0 4.9 %collective-permute-done.13.refs_2_ = bf16[512,128]{1,0:T(8,128)(2,1)S(1)} collective-permute-done((bf16[512,128]{1,0:T(8,128)(2,1)}, bf16[512,128]{1,0:T(8,128)(2,1)S(1)}, u32[]{:S(2)}, u32[]{:S(2)}) %collective-permute-start.13) | collective-permute-done | bytes 131104 | tf_op jit(solution)/shard_map/ppermute | solution.py:408
  91.1 11.0 %shard_map.80 = (f32[2,2,128,512]{3,2,1,0:T(8,128)}, bf16[2,2,128,512]{3,2,1,0:T(8,128)(2,1)}, f32[8,128]{1,0:T(8,128)}, f32[8,128]{1,0:T(8,128)}, f32[512,128]{1,0:T(8,128)}) custom-call(s32[128]{0:T(128)} %reshape.473.block, bf16[512,128]{1,0:T(8,128)(2,1)} %shard_map.79.refs_0_, bf16[512,128]{1,0:T(8,128)(2,1)} %copy-done.14, ...), custom_call_target="tpu_custom_call" | custom-call | flops 1342177280 | bytes 16269824 | tf_op jit(solution)/shard_map/pallas_call | solution.py:530
  105.2 6.5 %shard_map.81.refs_0_ = bf16[512,128]{1,0:T(8,128)(2,1)} custom-call(s32[128]{0:T(128)} %reshape.473.block, f32[2,2,128,512]{3,2,1,0:T(8,128)} %get-tuple-element.60.picture.refs_16_, bf16[4,2,2,128,512]{4,3,2,1,0:T(8,128)(2,1)} %copy-done, bf16[4,2,2,128,512]{4,3,2,1,0:T(8,128)(2,1)} %copy-done, bf16[4,2,2,128,512]{4,3,2,1,0:T(8,128)(2,1)} %copy-done, ...), custom_call_target="tpu_custom_call" | custom-call | flops 1342177280 | bytes 14156288 | tf_op jit(solution)/shard_map/pallas_call | solution.py:530
  113.7 4.9 %collective-permute-done.21.refs_2_ = bf16[512,128]{1,0:T(8,128)(2,1)S(1)} collective-permute-done((bf16[512,128]{1,0:T(8,128)(2,1)}, bf16[512,128]{1,0:T(8,128)(2,1)S(1)}, u32[]{:S(2)}, u32[]{:S(2)}) %collective-permute-start.21) | collective-permute-done | bytes 131104 | tf_op jit(solution)/shard_map/ppermute | solution.py:408
  120.1 8.2 %collective-permute-done.23.refs_10_.refs_4_ = bf16[2,2,128,512]{3,2,1,0:T(8,128)(2,1)S(1)} collective-permute-done((bf16[2,2,128,512]{3,2,1,0:T(8,128)(2,1)S(1)}, bf16[2,2,128,512]{3,2,1,0:T(8,128)(2,1)S(1)}, u32[]{:S(2)}, u32[]{:S(2)}) %collective-permute-start.23) | collective-permute-done | bytes 524320 | tf_op jit(solution)/shard_map/ppermute | solution.py:408
  128.2 2.2 %shard_map.82.refs_15_ = f32[8,128]{1,0:T(8,128)} custom-call(bf16[512,128]{1,0:T(8,128)(2,1)} %shard_map.81.refs_0_, bf16[512,128]{1,0:T(8,128)(2,1)} %copy-done.8, bf16[512,128]{1,0:T(8,128)(2,1)} %copy-done.9, bf16[512,128]{1,0:T(8,128)(2,1)} %copy-done.10, f32[8,128]{1,0:T(8,128)} %get-tuple-element.67.refs_4_, f32[512,128]{1,0:T(8,128)} %get-tuple-element.68.refs_5_, ...), custom_call_target="tpu_custom_call" | custom-call | tf_op jit(solution)/shard_map/pallas_call | solution.py:631
  130.4 2.9 %collective-permute-start.25 = (f32[1,8,128]{2,1,0:T(8,128)}, f32[1,8,128]{2,1,0:T(8,128)S(1)}, u32[]{:S(2)}, u32[]{:S(2)}) collective-permute-start(f32[1,8,128]{2,1,0:T(8,128)} %bitcast.59), channel_id=1, source_target_pairs={{0,8},{4,12},{8,0},{12,4},{1,9},{5,13},{9,1},{13,5},{2,10},{6,14},... | collective-permute-start | bytes 12296 | tf_op jit(solution)/shard_map/ppermute | solution.py:408
  134.8 10.4 %shard_map.83.refs_6_ = bf16[2,2,128,512]{3,2,1,0:T(8,128)(2,1)} custom-call(s32[128]{0:T(128)} %reshape.473.block, bf16[512,128]{1,0:T(8,128)(2,1)} %shard_map.81.refs_0_, bf16[512,128]{1,0:T(8,128)(2,1)} %copy-done.8, bf16[512,128]{1,0:T(8,128)(2,1)} %copy-done.9, bf16[512,128]{1,0:T(8,128)(2,1)} %copy-done.10, bf16[32,128,128]{2,1,0:T(8,128)(2,1)} %refs_4_.7, ...), custom_call_target="tpu_custom_call" | custom-call | flops 1342177280 | bytes 16257536 | tf_op jit(solution)/shard_map/pallas_call | solution.py:530
  145.3 2.9 %collective-permute-start.34 = (bf16[2,2,128,512]{3,2,1,0:T(8,128)(2,1)}, bf16[2,2,128,512]{3,2,1,0:T(8,128)(2,1)S(1)}, u32[]{:S(2)}, u32[]{:S(2)}) collective-permute-start(bf16[2,2,128,512]{3,2,1,0:T(8,128)(2,1)} %shard_map.83.refs_6_), channel_id=1, source_target_pairs={{0,8},{4,12},{8,0},{12,4},{1,9},{5,13},{9,1},{13,5},{2,10},{6,14},... | collective-permute-start | bytes 1572872 | tf_op jit(solution)/shard_map/ppermute | solution.py:408
  148.3 21.0 %collective-permute-done.29.refs_9_ = bf16[2,2,128,512]{3,2,1,0:T(8,128)(2,1)S(1)} collective-permute-done((bf16[2,2,128,512]{3,2,1,0:T(8,128)(2,1)}, bf16[2,2,128,512]{3,2,1,0:T(8,128)(2,1)S(1)}, u32[]{:S(2)}, u32[]{:S(2)}) %collective-permute-start.29) | collective-permute-done | bytes 524320 | tf_op jit(solution)/shard_map/ppermute | solution.py:408
  173.8 5.4 %shard_map.85.refs_7_ = f32[8,2,128,512]{3,2,1,0:T(8,128)} custom-call(s32[4]{0:T(128)} %pad_add_fusion.3.order, f32[1,8,128]{2,1,0:T(8,128)} %get-tuple-element.99.refs_0_, f32[1,8,128]{2,1,0:T(8,128)} %get-tuple-element.98.refs_1_, f32[1,8,128]{2,1,0:T(8,128)} %get-tuple-element.97.refs_2_, f32[1,8,128]{2,1,0:T(8,128)} %get-tuple-element.96.refs_3_, ...), custom_call_target="tpu_custom_call" | custom-call | tf_op jit(solution)/shard_map/pallas_call | solution.py:673
  181.7 3.3 %shard_map.86.refs_7_ = f32[8,2,128,512]{3,2,1,0:T(8,128)} custom-call(s32[2]{0:T(128)} %pad_add_fusion.4.order, f32[1,8,128]{2,1,0:T(8,128)} %get-tuple-element.99.refs_0_, f32[1,8,128]{2,1,0:T(8,128)} %get-tuple-element.98.refs_1_, f32[1,8,128]{2,1,0:T(8,128)} %get-tuple-element.97.refs_2_, ...), custom_call_target="tpu_custom_call", output_to_operand_aliasing={{}: (8, {})} | custom-call | tf_op jit(solution)/shard_map/pallas_call | solution.py:673
  187.3 8.2 %shard_map.84 = f32[8,2,128,512]{3,2,1,0:T(8,128)} custom-call(s32[8]{0:T(128)} %stack.110.order, f32[1,8,128]{2,1,0:T(8,128)} %get-tuple-element.99.refs_0_, f32[1,8,128]{2,1,0:T(8,128)} %get-tuple-element.98.refs_1_, f32[1,8,128]{2,1,0:T(8,128)} %get-tuple-element.97.refs_2_, f32[1,8,128]{2,1,0:T(8,128)} %get-tuple-element.96.refs_3_, ...), custom_call_target="tpu_custom_call" | custom-call | tf_op jit(solution)/shard_map/pallas_call | solution.py:673
  197.9 3.3 %shard_map.87 = f32[8,2,128,512]{3,2,1,0:T(8,128)} custom-call(s32[2]{0:T(128)} %pad_add_fusion.2.order, f32[1,8,128]{2,1,0:T(8,128)} %get-tuple-element.99.refs_0_, f32[1,8,128]{2,1,0:T(8,128)} %get-tuple-element.98.refs_1_, f32[1,8,128]{2,1,0:T(8,128)} %get-tuple-element.97.refs_2_, ...), custom_call_target="tpu_custom_call", output_to_operand_aliasing={{}: (8, {})} | custom-call | tf_op jit(solution)/shard_map/pallas_call | solution.py:673
  (155 shorter events, 46.7 us)
Async XLA Ops:
  0.6 31.4 %collective-permute-start.10 = (bf16[32,128,128]{2,1,0:T(8,128)(2,1)}, bf16[32,128,128]{2,1,0:T(8,128)(2,1)S(1)}, u32[]{:S(2)}, u32[]{:S(2)}) collective-permute-start(bf16[32,128,128]{2,1,0:T(8,128)(2,1)} %refs_4_.7), channel_id=1, source_target_pairs={{0,2},{1,3},{2,0},{3,1},{4,6},{5,7},{6,4},{7,5},{8,10},{9,11},{10,... | collective-permute-start | bytes 3145736 | tf_op jit(solution)/shard_map/ppermute | solution.py:408
  3.7 35.8 %collective-permute-start.9 = (bf16[32,128,128]{2,1,0:T(8,128)(2,1)}, bf16[32,128,128]{2,1,0:T(8,128)(2,1)}, u32[]{:S(2)}, u32[]{:S(2)}) collective-permute-start(bf16[32,128,128]{2,1,0:T(8,128)(2,1)} %refs_4_.7), channel_id=1, source_target_pairs={{0,1},{1,0},{2,3},{3,2},{4,5},{5,4},{6,7},{7,6},{8,9},{9,8},{10,11... | collective-permute-start | bytes 3145736 | tf_op jit(solution)/shard_map/ppermute | solution.py:408
  14.1 51.0 %all-to-all-start = ((bf16[4,2,2,128,512]{4,3,2,1,0:T(8,128)(2,1)}), bf16[4,2,2,128,512]{4,3,2,1,0:T(8,128)(2,1)S(1)}, u32[]{:S(2)}, u32[]{:S(2)}) async-start(bf16[4,2,2,128,512]{4,3,2,1,0:T(8,128)(2,1)} %bitcast.57), calls=%async_computation | async-start | bytes 4194304 | tf_op jit(solution)/shard_map/all_to_all | solution.py:447
  19.2 7.9 %collective-permute-start.7 = (s32[96]{0:T(128)S(1)}, s32[96]{0:T(128)S(1)}, u32[]{:S(2)}, u32[]{:S(2)}) collective-permute-start(s32[96]{0:T(128)S(1)} %pad_add_fusion.1), channel_id=1, source_target_pairs={{0,2},{1,3},{2,0},{3,1},{4,6},{5,7},{6,4},{7,5},{8,10},{9,11},{10,... | collective-permute-start | bytes 1160 | tf_op jit(solution)/shard_map/ppermute | solution.py:408
  19.7 9.2 %collective-permute-start.6 = (s32[96]{0:T(128)S(1)}, s32[96]{0:T(128)S(1)}, u32[]{:S(2)}, u32[]{:S(2)}) collective-permute-start(s32[96]{0:T(128)S(1)} %pad_add_fusion.1), channel_id=1, source_target_pairs={{0,1},{1,0},{2,3},{3,2},{4,5},{5,4},{6,7},{7,6},{8,9},{9,8},{10,11... | collective-permute-start | bytes 1160 | tf_op jit(solution)/shard_map/ppermute | solution.py:408
  27.2 9.6 %collective-permute-start.4 = (bf16[8,16,128]{2,1,0:T(8,128)(2,1)S(1)}, bf16[8,16,128]{2,1,0:T(8,128)(2,1)S(1)}, u32[]{:S(2)}, u32[]{:S(2)}) collective-permute-start(bf16[8,16,128]{2,1,0:T(8,128)(2,1)S(1)} %fusion.14), channel_id=1, source_target_pairs={{0,2},{1,3},{2,0},{3,1},{4,6},{5,7},{6,4},{7,5},{8,10},{9,11},{10,... | collective-permute-start | bytes 98312 | tf_op jit(solution)/shard_map/ppermute | solution.py:408
  28.9 9.9 %collective-permute-start.3 = (bf16[8,16,128]{2,1,0:T(8,128)(2,1)S(1)}, bf16[8,16,128]{2,1,0:T(8,128)(2,1)S(1)}, u32[]{:S(2)}, u32[]{:S(2)}) collective-permute-start(bf16[8,16,128]{2,1,0:T(8,128)(2,1)S(1)} %fusion.14), channel_id=1, source_target_pairs={{0,1},{1,0},{2,3},{3,2},{4,5},{5,4},{6,7},{7,6},{8,9},{9,8},{10,11... | collective-permute-start | bytes 98312 | tf_op jit(solution)/shard_map/ppermute | solution.py:408
  32.1 7.4 %collective-permute-start.11 = (bf16[32,128,128]{2,1,0:T(8,128)(2,1)S(1)}, bf16[32,128,128]{2,1,0:T(8,128)(2,1)}, u32[]{:S(2)}, u32[]{:S(2)}) collective-permute-start(bf16[32,128,128]{2,1,0:T(8,128)(2,1)S(1)} %collective-permute-done.10.refs_2_.refs_6_), channel_id=1, source_target_pairs={{0,1},{1,0},{2,3},{3,2},{4,5},{5,4},{6,7},{7,6},{8,9},{9,8},{10,11... | collective-permute-start | bytes 3145736 | tf_op jit(solution)/shard_map/ppermute | solution.py:408
  71.6 30.5 %collective-permute-start.18 = (bf16[2,2,128,512]{3,2,1,0:T(8,128)(2,1)}, bf16[2,2,128,512]{3,2,1,0:T(8,128)(2,1)S(1)}, u32[]{:S(2)}, u32[]{:S(2)}) collective-permute-start(bf16[2,2,128,512]{3,2,1,0:T(8,128)(2,1)} %get-tuple-element.77.refs_4_), channel_id=1, source_target_pairs={{0,4},{4,0},{8,12},{12,8},{1,5},{5,1},{9,13},{13,9},{2,6},{6,2},{1... | collective-permute-start | bytes 1572872 | tf_op jit(solution)/shard_map/ppermute | solution.py:408
  71.7 30.5 %collective-permute-start.19 = (bf16[2,2,128,512]{3,2,1,0:T(8,128)(2,1)}, bf16[2,2,128,512]{3,2,1,0:T(8,128)(2,1)S(1)}, u32[]{:S(2)}, u32[]{:S(2)}) collective-permute-start(bf16[2,2,128,512]{3,2,1,0:T(8,128)(2,1)} %get-tuple-element.77.refs_4_), channel_id=1, source_target_pairs={{0,8},{4,12},{8,0},{12,4},{1,9},{5,13},{9,1},{13,5},{2,10},{6,14},... | collective-permute-start | bytes 1572872 | tf_op jit(solution)/shard_map/ppermute | solution.py:408
  73.7 8.4 %collective-permute-start.15 = (f32[8,128]{1,0:T(8,128)}, f32[8,128]{1,0:T(8,128)S(1)}, u32[]{:S(2)}, u32[]{:S(2)}) collective-permute-start(f32[8,128]{1,0:T(8,128)} %get-tuple-element.56.refs_15_), channel_id=1, source_target_pairs={{0,1},{1,0},{2,3},{3,2},{4,5},{5,4},{6,7},{7,6},{8,9},{9,8},{10,11... | collective-permute-start | bytes 12296 | tf_op jit(solution)/shard_map/ppermute | solution.py:408
  73.7 8.8 %collective-permute-start.16 = (f32[8,128]{1,0:T(8,128)}, f32[8,128]{1,0:T(8,128)S(1)}, u32[]{:S(2)}, u32[]{:S(2)}) collective-permute-start(f32[8,128]{1,0:T(8,128)} %get-tuple-element.56.refs_15_), channel_id=1, source_target_pairs={{0,2},{1,3},{2,0},{3,1},{4,6},{5,7},{6,4},{7,5},{8,10},{9,11},{10,... | collective-permute-start | bytes 12296 | tf_op jit(solution)/shard_map/ppermute | solution.py:408
  74.2 8.8 %collective-permute-start.17 = (f32[8,128]{1,0:T(8,128)}, f32[8,128]{1,0:T(8,128)S(1)}, u32[]{:S(2)}, u32[]{:S(2)}) collective-permute-start(f32[8,128]{1,0:T(8,128)} %get-tuple-element.56.refs_15_), channel_id=1, source_target_pairs={{0,3},{1,2},{2,1},{3,0},{4,7},{5,6},{6,5},{7,4},{8,11},{9,10},{10,... | collective-permute-start | bytes 12296 | tf_op jit(solution)/shard_map/ppermute | solution.py:408
  82.9 7.4 %collective-permute-start.14 = (bf16[512,128]{1,0:T(8,128)(2,1)}, bf16[512,128]{1,0:T(8,128)(2,1)S(1)}, u32[]{:S(2)}, u32[]{:S(2)}) collective-permute-start(bf16[512,128]{1,0:T(8,128)(2,1)} %shard_map.79.refs_0_), channel_id=1, source_target_pairs={{0,3},{1,2},{2,1},{3,0},{4,7},{5,6},{6,5},{7,4},{8,11},{9,10},{10,... | collective-permute-start | bytes 393224 | tf_op jit(solution)/shard_map/ppermute | solution.py:408
  102.1 26.1 %collective-permute-start.23 = (bf16[2,2,128,512]{3,2,1,0:T(8,128)(2,1)S(1)}, bf16[2,2,128,512]{3,2,1,0:T(8,128)(2,1)S(1)}, u32[]{:S(2)}, u32[]{:S(2)}) collective-permute-start(bf16[2,2,128,512]{3,2,1,0:T(8,128)(2,1)S(1)} %collective-permute-done.19.refs_8_.refs_4_), channel_id=1, source_target_pairs={{0,4},{4,0},{8,12},{12,8},{1,5},{5,1},{9,13},{13,9},{2,6},{6,2},{1... | collective-permute-start | bytes 1572872 | tf_op jit(solution)/shard_map/ppermute | solution.py:408
  102.3 42.9 %collective-permute-start.27 = (bf16[2,2,128,512]{3,2,1,0:T(8,128)(2,1)}, bf16[2,2,128,512]{3,2,1,0:T(8,128)(2,1)S(1)}, u32[]{:S(2)}, u32[]{:S(2)}) collective-permute-start(bf16[2,2,128,512]{3,2,1,0:T(8,128)(2,1)} %get-tuple-element.70.refs_5_), channel_id=1, source_target_pairs={{0,4},{4,0},{8,12},{12,8},{1,5},{5,1},{9,13},{13,9},{2,6},{6,2},{1... | collective-permute-start | bytes 1572872 | tf_op jit(solution)/shard_map/ppermute | solution.py:408
  104.2 41.0 %collective-permute-start.28 = (bf16[2,2,128,512]{3,2,1,0:T(8,128)(2,1)}, bf16[2,2,128,512]{3,2,1,0:T(8,128)(2,1)S(1)}, u32[]{:S(2)}, u32[]{:S(2)}) collective-permute-start(bf16[2,2,128,512]{3,2,1,0:T(8,128)(2,1)} %get-tuple-element.70.refs_5_), channel_id=1, source_target_pairs={{0,8},{4,12},{8,0},{12,4},{1,9},{5,13},{9,1},{13,5},{2,10},{6,14},... | collective-permute-start | bytes 1572872 | tf_op jit(solution)/shard_map/ppermute | solution.py:408
  130.4 14.8 %collective-permute-start.24 = (f32[1,8,128]{2,1,0:T(8,128)}, f32[1,8,128]{2,1,0:T(8,128)S(1)}, u32[]{:S(2)}, u32[]{:S(2)}) collective-permute-start(f32[1,8,128]{2,1,0:T(8,128)} %bitcast.58), channel_id=1, source_target_pairs={{0,4},{4,0},{8,12},{12,8},{1,5},{5,1},{9,13},{13,9},{2,6},{6,2},{1... | collective-permute-start | bytes 12296 | tf_op jit(solution)/shard_map/ppermute | solution.py:408
  130.4 14.8 %collective-permute-start.25 = (f32[1,8,128]{2,1,0:T(8,128)}, f32[1,8,128]{2,1,0:T(8,128)S(1)}, u32[]{:S(2)}, u32[]{:S(2)}) collective-permute-start(f32[1,8,128]{2,1,0:T(8,128)} %bitcast.59), channel_id=1, source_target_pairs={{0,8},{4,12},{8,0},{12,4},{1,9},{5,13},{9,1},{13,5},{2,10},{6,14},... | collective-permute-start | bytes 12296 | tf_op jit(solution)/shard_map/ppermute | solution.py:408
  133.3 11.9 %collective-permute-start.26 = (f32[1,8,128]{2,1,0:T(8,128)}, f32[1,8,128]{2,1,0:T(8,128)S(1)}, u32[]{:S(2)}, u32[]{:S(2)}) collective-permute-start(f32[1,8,128]{2,1,0:T(8,128)} %bitcast.60), channel_id=1, source_target_pairs={{0,12},{4,8},{8,4},{12,0},{1,13},{5,9},{9,5},{13,1},{2,14},{6,10},... | collective-permute-start | bytes 12296 | tf_op jit(solution)/shard_map/ppermute | solution.py:408
  145.3 24.0 %collective-permute-start.29 = (bf16[2,2,128,512]{3,2,1,0:T(8,128)(2,1)}, bf16[2,2,128,512]{3,2,1,0:T(8,128)(2,1)S(1)}, u32[]{:S(2)}, u32[]{:S(2)}) collective-permute-start(bf16[2,2,128,512]{3,2,1,0:T(8,128)(2,1)} %shard_map.83.refs_6_), channel_id=1, source_target_pairs={{0,4},{4,0},{8,12},{12,8},{1,5},{5,1},{9,13},{13,9},{2,6},{6,2},{1... | collective-permute-start | bytes 1572872 | tf_op jit(solution)/shard_map/ppermute | solution.py:408
  145.3 33.9 %collective-permute-start.34 = (bf16[2,2,128,512]{3,2,1,0:T(8,128)(2,1)}, bf16[2,2,128,512]{3,2,1,0:T(8,128)(2,1)S(1)}, u32[]{:S(2)}, u32[]{:S(2)}) collective-permute-start(bf16[2,2,128,512]{3,2,1,0:T(8,128)(2,1)} %shard_map.83.refs_6_), channel_id=1, source_target_pairs={{0,8},{4,12},{8,0},{12,4},{1,9},{5,13},{9,1},{13,5},{2,10},{6,14},... | collective-permute-start | bytes 1572872 | tf_op jit(solution)/shard_map/ppermute | solution.py:408
  171.7 14.8 %collective-permute-start.33 = (bf16[2,2,128,512]{3,2,1,0:T(8,128)(2,1)S(1)}, bf16[2,2,128,512]{3,2,1,0:T(8,128)(2,1)S(1)}, u32[]{:S(2)}, u32[]{:S(2)}) collective-permute-start(bf16[2,2,128,512]{3,2,1,0:T(8,128)(2,1)S(1)} %collective-permute-done.28.refs_9_.refs_5_), channel_id=1, source_target_pairs={{0,4},{4,0},{8,12},{12,8},{1,5},{5,1},{9,13},{13,9},{2,6},{6,2},{1... | collective-permute-start | bytes 1572872 | tf_op jit(solution)/shard_map/ppermute | solution.py:408
  179.2 17.8 %collective-permute-start.35 = (bf16[2,2,128,512]{3,2,1,0:T(8,128)(2,1)S(1)}, bf16[2,2,128,512]{3,2,1,0:T(8,128)(2,1)S(1)}, u32[]{:S(2)}, u32[]{:S(2)}) collective-permute-start(bf16[2,2,128,512]{3,2,1,0:T(8,128)(2,1)S(1)} %collective-permute-done.34.refs_6_), channel_id=1, source_target_pairs={{0,4},{4,0},{8,12},{12,8},{1,5},{5,1},{9,13},{13,9},{2,6},{6,2},{1... | collective-permute-start | bytes 1572872 | tf_op jit(solution)/shard_map/ppermute | solution.py:408
  (34 other events, 249.6 us)

commit v7 on v5

--- a/solution.py
+++ b/solution.py
@@ -281,7 +281,7 @@
     for part in range(2):
         vector = residual[0, part]
         again = total[part] + damping * vector
-        rounded[0, part] = (vector - scale * again).astype(bf16)
+        rounded[0, part] = (vector - scale * again).astype(rounded.dtype)
 
 
 def facts_kernel(peers, *refs):
@@ -345,27 +345,67 @@
     return picture, residual
 
 
-def assemble_kernel(coils, group_steps, combos, is_residual, order, *refs):
-    infos, pieces, out = refs[:coils], refs[coils:-1], refs[-1]
+def kept_coefficients(infos, kept, first, combos, is_residual):
     groups = infos[0].shape[0]
     numbers = [
         [[info[g, row : row + 1, 0:1] for g in range(groups)] for info in infos]
         for row in range(6)
     ]
     factors = coefficients(*numbers)[is_residual]
-    count = 3 if is_residual else 2
+    rows = lax.broadcasted_iota(jnp.int32, kept.shape[1:], 0)
     for place, (k, g) in enumerate(combos):
-
+        total = jnp.zeros(kept.shape[1:], f32)
+        for row, factor in enumerate(factors[k][g]):
+            total = jnp.where(rows == row, factor, total)
+        kept[first + place] = total
+
+
+def assemble_kernel(coils, group_steps, combos, counts, is_residual, order, *refs):
+    infos, pieces, (out, kept) = refs[:coils], refs[coils:-2], refs[-2:]
+
+    @pl.when(pl.program_id(0) == 0)
+    def _():
+        kept_coefficients(infos, kept, 0, combos, is_residual)
+
+    def write(place, used):
         @pl.when(pl.program_id(0) // group_steps == place)
         def _():
-            total = 0.0
-            for factor, piece in zip(factors[k][g], pieces[place * count :][:count]):
-                total += factor.reshape(1, 1, 1, 1) * piece[...].astype(f32)
-            out[...] = total
+            if len(used) == 1:
+                out[...] = used[0][...].astype(f32)
+            else:
+                total = 0.0
+                for row, piece in enumerate(used):
+                    factor = kept[place, row : row + 1, 0:1].reshape(1, 1, 1, 1)
+                    total += factor * piece[...].astype(f32)
+                out[...] = total
+
+    first = 0
+    for place, count in enumerate(counts):
+        write(place, pieces[first : first + count])
+        first += count
+
+
+def finish_kernel(coils, g, *refs):
+    infos, (start, residual, mixed, picture, out, kept) = refs[:coils], refs[coils:]
+
+    @pl.when((pl.program_id(0) == 0) & (pl.program_id(1) == 0))
+    def _():
+        kept_coefficients(infos, kept, 0, [(0, g)], False)
+        kept_coefficients(infos, kept, 1, [(0, g)], True)
+
+    def mixture(place, vectors):
+        total = 0.0
+        for row, vector in enumerate(vectors):
+            factor = kept[place, row : row + 1, 0:1].reshape(1, 1, 1, 1)
+            total += factor * vector[...]
+        return total.astype(bf16)
+
+    picture[...] = mixture(0, [start, residual])
+    out[...] = mixture(1, [start, residual, mixed])
 
 
 def group_count_of(own_planes):
-    return 1
+    return 2 if own_planes % 2 == 0 else 1
 
 
 def whole_block(array):
@@ -433,16 +473,12 @@
     packed = jnp.concatenate([tile_slot, tile_block, send_list.reshape(-1)])
     sens_source, packed, measured = lax.optimization_barrier((sens_maps[0], packed, measured))
     sens_source = sens_source.reshape(coil_count, own_planes, 2, rows, columns)
-    sens = [
-        lax.all_to_all(
-            sens_source[:, g * group_planes : (g + 1) * group_planes],
-            "coil",
-            split_axis=0,
-            concat_axis=0,
-            tiled=True,
-        )
-        for g in groups
-    ]
+    sens = []
+    for g in groups:
+        part = sens_source[:, g * group_planes : (g + 1) * group_planes]
+        if g > 0:
+            part, sens[-1] = lax.optimization_barrier((part, sens[-1]))
+        sens.append(lax.all_to_all(part, "coil", split_axis=0, concat_axis=0, tiled=True))
     measured = jnp.stack(measured)
     by_coil = jnp.arange(coil_count, dtype=jnp.int32) ^ coil_index
     measured = jnp.take(measured, by_coil, axis=0)
@@ -626,8 +662,9 @@
                 compiler_params=params,
             )(*inputs)
 
-        def assembled(infos, vectors, ks, out=None):
+        def assembled(infos, vectors, ks, is_residual, out=None):
             combos = [(k, g) for k in ks for g in groups]
+            counts = [len(vectors[g]) for k, g in combos]
             order = jnp.stack(
                 [
                     (coil_index ^ k) * own_planes + g * group_planes + p
@@ -635,30 +672,23 @@
                     for p in range(group_planes)
                 ]
             ).astype(jnp.int32)
-            inputs = [vector[g][k] for k, g in combos for vector in vectors]
-
-            def spec(place):
-                first_step = place // len(vectors) * group_planes
-                return pl.BlockSpec(
-                    (1, 2, rows, columns),
-                    lambda i, o: (jnp.clip(i - first_step, 0, group_planes - 1), 0, 0, 0),
-                )
-
-            specs = [pl.BlockSpec(infos[0].shape, lambda i, o: (0, 0, 0))] * len(infos)
-            specs += [spec(place) for place in range(len(inputs))]
+            inputs, specs = [], [pl.BlockSpec(infos[0].shape, lambda i, o: (0, 0, 0))] * len(infos)
+            for place, (k, g) in enumerate(combos):
+
+                def plane_of(i, o, first=place * group_planes):
+                    return jnp.clip(i - first, 0, group_planes - 1), 0, 0, 0
+
+                for vector in vectors[g]:
+                    inputs.append(vector[k])
+                    specs.append(pl.BlockSpec((1, 2, rows, columns), plane_of))
             aliases = {}
             kernel = functools.partial(
-                assemble_kernel, coil_count, group_planes, combos, len(vectors) == 3
+                assemble_kernel, coil_count, group_planes, combos, counts, is_residual
             )
             if out is not None:
                 aliases = {1 + len(infos) + len(inputs): 0}
-                inner = kernel
-                inputs = inputs + [out]
+                inputs.append(out)
                 specs.append(pl.BlockSpec(memory_space=pl.ANY))
-
-                def kernel(*refs):
-                    inner(*refs[:-2], refs[-1])
-
             return pl.pallas_call(
                 kernel,
                 grid_spec=pltpu.PrefetchScalarGridSpec(
@@ -666,20 +696,34 @@
                     grid=(len(combos) * group_planes,),
                     in_specs=specs,
                     out_specs=pl.BlockSpec((1, 2, rows, columns), lambda i, o: (o[i], 0, 0, 0)),
+                    scratch_shapes=[pltpu.VMEM((len(combos), 8, 128), f32)],
                 ),
                 out_shape=shaped((planes, 2, rows, columns)),
                 input_output_aliases=aliases,
                 compiler_params=params,
             )(order, *infos, *inputs)
 
-        def second(samples, facts, residual, g):
+        def finished(infos, vectors, g):
+            spec = pl.BlockSpec((1, 2, rows // 2, columns), lambda p, r: (p, 0, r, 0))
+            small = pl.BlockSpec(infos[0].shape, lambda p, r: (0, 0, 0))
+            return pl.pallas_call(
+                functools.partial(finish_kernel, coil_count, g),
+                grid=(group_planes, 2),
+                in_specs=[small] * len(infos) + [spec] * 3,
+                out_specs=[spec] * 2,
+                out_shape=[shaped(group_shape, bf16)] * 2,
+                scratch_shapes=[pltpu.VMEM((2, 8, 128), f32)],
+                compiler_params=params,
+            )(*infos, *vectors)
+
+        def second(samples, facts, residual, g, dtype):
             return back(
                 second_kernel,
                 samples,
                 [facts],
                 [residual],
                 g,
-                shaped(group_shape, bf16),
+                shaped(group_shape, dtype),
                 plane_spec,
             )
 
@@ -774,26 +818,38 @@
             values += [jnp.sum(total * total), jnp.sum(total * start_total)]
             return stacked_dots(values)
 
-        def assembled(infos, vectors, ks, out=None):
+        def factors_of(infos, is_residual):
             numbers = [
                 [[info[g, row, 0] for g in groups] for info in infos] for row in range(6)
             ]
-            factors = coefficients(*numbers)[len(vectors) == 3]
+            return coefficients(*numbers)[is_residual]
+
+        def mixture(factors, vectors):
+            return sum(factor * vector.astype(f32) for factor, vector in zip(factors, vectors))
+
+        def assembled(infos, vectors, ks, is_residual, out=None):
+            factors = factors_of(infos, is_residual)
             if out is None:
                 out = jnp.zeros((planes, 2, rows, columns), f32)
             for k in ks:
                 for g in groups:
                     place = ((coil_index ^ k) * own_planes + g * group_planes, 0, 0, 0)
-                    piece = sum(
-                        factor * vector[g][k].astype(f32)
-                        for factor, vector in zip(factors[k][g], vectors)
-                    )
+                    pieces = [vector[k] for vector in vectors[g]]
+                    if len(pieces) == 1:
+                        piece = pieces[0].astype(f32)
+                    else:
+                        piece = mixture(factors[k][g], pieces)
                     out = lax.dynamic_update_slice(out, piece, place)
             return out
 
-        def second(samples, facts, residual, g):
+        def finished(infos, vectors, g):
+            return [
+                mixture(factors_of(infos, i)[0][g], vectors).astype(bf16) for i in (False, True)
+            ]
+
+        def second(samples, facts, residual, g, dtype):
             again = applied_to(samples, residual, g)
-            return (residual - step_of(facts[0, 0], facts[1, 0]) * again).astype(bf16)
+            return (residual - step_of(facts[0, 0], facts[1, 0]) * again).astype(dtype)
 
     def added(samples):
         return tree_sum([part.astype(f32) for part in samples])
@@ -802,37 +858,55 @@
         return [swapped(own, "coil", k) for k in first_bits]
 
     images = measured_images()
-    start_pieces, residual_pieces, mixed_pieces, infos = [], [], [], []
+    last = len(groups) - 1
+    starts, residuals, mixeds, start_owns, residual_owns, infos = [], [], [], [], [], []
     for g in groups:
         right_side, start_own, norm = start(images, g)
-        start_sent = sent_by_bits(start_own)
         samples = exchanged(forward(right_side, g))
         norms = exchanged(norm)
-        samples, norms, start_sent = lax.optimization_barrier((samples, norms, start_sent))
         residual, residual_own, facts, dots, start_total = first(samples, norms, right_side, g)
-        residual, residual_own, pieces = lax.optimization_barrier(
-            (residual, residual_own, completed(start_own, start_sent))
+        if g == last and last > 0:
+            owns = [start_owns[0], residual_owns[0]]
+            *owns, _ = lax.optimization_barrier((*owns, sens[last]))
+            sent = [sent_by_bits(own) for own in owns]
+            residual, residual_own, sent = lax.optimization_barrier((residual, residual_own, sent))
+            early = [completed(own, pieces) for own, pieces in zip(owns, sent)]
+            mixed_sent = sent_by_bits(mixeds[0])
+        dots = exchanged(dots)
+        samples = exchanged(forward(residual, g))
+        samples, dots = lax.optimization_barrier((samples, dots))
+        info = facts_of(samples, dots, start_total, facts)
+        mixed = second(samples, info, residual, g, bf16 if g < last else f32)
+        infos.append(info)
+        starts.append(right_side)
+        residuals.append(residual)
+        mixeds.append(mixed)
+        start_owns.append(start_own)
+        residual_owns.append(residual_own)
+
+    others = exchanged(jnp.stack(infos), "coil")
+    if last > 0:
+        mixeds[last], others, early, mixed_sent = lax.optimization_barrier(
+            (mixeds[last], others, early, mixed_sent)
         )
-        start_pieces.append(pieces)
-        residual_sent = sent_by_bits(residual_own)
-        samples = exchanged(forward(residual, g))
-        dots = exchanged(dots)
-        samples, dots, residual_sent = lax.optimization_barrier((samples, dots, residual_sent))
-        info = facts_of(samples, dots, start_total, facts)
-        infos.append(info)
-        rounded = second(samples, info, residual, g)
-        last = g == groups[-1]
-        others = exchanged(jnp.stack(infos), "coil") if last else []
-        rounded, others, pieces = lax.optimization_barrier(
-            (rounded, others, completed(residual_own, residual_sent))
-        )
-        residual_pieces.append(pieces)
-        mixed_pieces.append(completed(rounded, sent_by_bits(rounded)))
-
-    picture = assembled(others, [start_pieces, residual_pieces], range(coil_count))
-    vectors = [start_pieces, residual_pieces, mixed_pieces]
-    out = assembled(others, vectors, range(coil_count - 1))
-    out = assembled(others, vectors, [coil_count - 1], out)
+    final = finished(others, [starts[last], residuals[last], mixeds[last]], last)
+    final_sent = [sent_by_bits(own) for own in final]
+    first_vectors = []
+    if last > 0:
+        early.append(completed(mixeds[0], mixed_sent))
+        first_vectors = [early]
+    final_pieces = [completed(own, sent) for own, sent in zip(final, final_sent)]
+    late = coil_count - 1
+    near = [[own] + sent[:1] + [None] * (coil_count - 2) for own, sent in zip(final, final_sent)]
+    vectors = [v[:2] for v in first_vectors]
+    picture = assembled(others, vectors + [near[:1]], range(2), False)
+    out = assembled(others, first_vectors + [near[1:]], range(2), True)
+    vectors = vectors + [final_pieces[:1]]
+    first_vectors = first_vectors + [final_pieces[1:]]
+    picture = assembled(others, vectors, range(2, late), False, picture)
+    out = assembled(others, first_vectors, range(2, late), True, out)
+    picture = assembled(others, vectors, [late], False, picture)
+    out = assembled(others, first_vectors, [late], True, out)
     return picture, out
 
 

time: 197 us -> 243 us (1.23)
  Pallas kernels: 70 us -> 98.4 us
  starting transfers between devices: 34.3 us -> 51.9 us
  waiting for transfers between devices: 71.3 us -> 62.9 us
  local copies, waits for them, and re-layouts: 10.6 us -> 17 us
    pallas_call x6 -> x11, Pallas kernels: 49.1 us -> 70.9 us  [call(): pl.pallas_call(kernel, grid=grid, in_specs=specs, out_specs=out_specs, ou...]
    ppermute x36 -> x54, starting transfers between devices: 30.6 us -> 44.7 us  [swapped(): lax.ppermute(array, axis, [(i, i ^ k) for i in range(lax.axis_size(axis))])]
    ppermute x36 -> x54, waiting for transfers between devices: 56.4 us -> 49.7 us  [swapped(): lax.ppermute(array, axis, [(i, i ^ k) for i in range(lax.axis_size(axis))])]
    unnamed x52 -> x106, local copies, waits for them, and re-layouts: 3 us -> 7.75 us
    all_to_all x1 -> x2, starting transfers between devices: 3.61 us -> 7.21 us  [on_device(): lax.all_to_all(part, 'coil', split_axis=0, concat_axis=0, tiled=True)]
    slice x0 -> x1, local copies, waits for them, and re-layouts: none -> 3.07 us  [on_device(): part = sens_source[:, g * group_planes:(g + 1) * group_planes]]
    pallas_call x3 -> x6, Pallas kernels: 18.8 us -> 21.3 us  [assembled(): pl.pallas_call(kernel, grid_spec=pltpu.PrefetchScalarGridSpec(num_scalar_...]
    pallas_call x0 -> x1, Pallas kernels: none -> 2.45 us  [finished(): pl.pallas_call(functools.partial(finish_kernel, coil_count, g), grid=(gro...]
  transfers between devices with their start and end apart: 37 -> 56, of which waited for: 13 -> 16; matrix products, arithmetic and copies ran while one was open for 9% -> 8% of each run, Pallas kernels for 31% -> 36%
where the time goes in v7:
time: 243 us
  Pallas kernels  98.4 us (40%)
  waiting for transfers between devices  62.9 us (26%)
  starting transfers between devices  51.9 us (21%)
  local copies, waits for them, and re-layouts  17 us (7%)
  other arithmetic  11.3 us (5%)
    pallas_call x11, Pallas kernels, call(): pl.pallas_call(kernel, grid=grid, in_specs=specs, out_specs=out_specs, ou...  70.9 us
    ppermute x54, waiting for transfers between devices, swapped(): lax.ppermute(array, axis, [(i, i ^ k) for i in range(lax.axis_size(axis))])  49.7 us
    ppermute x54, starting transfers between devices, swapped(): lax.ppermute(array, axis, [(i, i ^ k) for i in range(lax.axis_size(axis))])  44.7 us
    pallas_call x6, Pallas kernels, assembled(): pl.pallas_call(kernel, grid_spec=pltpu.PrefetchScalarGridSpec(num_scalar_...  21.3 us
    all_to_all x2, waiting for transfers between devices, on_device(): lax.all_to_all(part, 'coil', split_axis=0, concat_axis=0, tiled=True)  13.2 us
    unnamed x106, local copies, waits for them, and re-layouts  7.75 us
    all_to_all x2, starting transfers between devices, on_device(): lax.all_to_all(part, 'coil', split_axis=0, concat_axis=0, tiled=True)  7.21 us
  transfers between devices with their start and end apart: 56, of which 16 were waited for; matrix products, arithmetic and copies ran while one was open for 8% of the time, Pallas kernels for 36%

profile of v7, /device:TPU:0, one launch (start us, length us, event | category | flops | bytes accessed | tf_op | source)
XLA Modules:
  0.0 242.7 jit_solution(11765122362712311324)
XLA Ops:
  0.6 3.0 %collective-permute-start.10 = (bf16[32,128,128]{2,1,0:T(8,128)(2,1)}, bf16[32,128,128]{2,1,0:T(8,128)(2,1)S(1)}, u32[]{:S(2)}, u32[]{:S(2)}) collective-permute-start(bf16[32,128,128]{2,1,0:T(8,128)(2,1)} %refs_4_.15), channel_id=1, source_target_pairs={{0,2},{1,3},{2,0},{3,1},{4,6},{5,7},{6,4},{7,5},{8,10},{9,11},{10,... | collective-permute-start | bytes 3145736 | tf_op jit(solution)/shard_map/ppermute | solution.py:438
  14.1 3.1 %fusion.29 = (bf16[4,1,2,128,512]{4,3,2,1,0:T(8,128)(2,1)}, bf16[4,1,2,128,512]{4,3,2,1,0:T(8,128)(2,1)}) fusion(bf16[4,2,2,128,512]{4,3,2,1,0:T(8,128)(2,1)} %bitcast.46), kind=kLoop, calls=%fused_computation.117 | loop fusion | bytes 4194304 | tf_op jit(solution)/shard_map/slice | solution.py:478
  17.2 3.5 %all-to-all-start = ((bf16[4,1,2,128,512]{4,3,2,1,0:T(8,128)(2,1)}), bf16[4,1,2,128,512]{4,3,2,1,0:T(8,128)(2,1)S(1)}, u32[]{:S(2)}, u32[]{:S(2)}) async-start(bf16[4,1,2,128,512]{4,3,2,1,0:T(8,128)(2,1)} %get-tuple-element.138), calls=%async_computation | async-start | bytes 2097152 | tf_op jit(solution)/shard_map/all_to_all | solution.py:481
  22.8 4.3 %collective-permute-done.7 = s32[96]{0:T(128)S(1)} collective-permute-done((s32[96]{0:T(128)S(1)}, s32[96]{0:T(128)S(1)}, u32[]{:S(2)}, u32[]{:S(2)}) %collective-permute-start.7) | collective-permute-done | bytes 416 | tf_op jit(solution)/shard_map/ppermute | solution.py:438
  32.4 13.2 %all-to-all-done.refs_0_.refs_1_.refs_2_.refs_3_.refs_8_.refs_9_.refs_10_.refs_11_ = bf16[4,1,2,128,512]{4,3,2,1,0:T(8,128)(2,1)S(1)} async-done(((bf16[4,1,2,128,512]{4,3,2,1,0:T(8,128)(2,1)}), bf16[4,1,2,128,512]{4,3,2,1,0:T(8,128)(2,1)S(1)}, u32[]{:S(2)}, u32[]{:S(2)}) %all-to-all-start) | async-done | bytes 1048608 | tf_op jit(solution)/shard_map/all_to_all | solution.py:481
  45.7 3.7 %all-to-all-start.1 = ((bf16[4,1,2,128,512]{4,3,2,1,0:T(8,128)(2,1)}), bf16[4,1,2,128,512]{4,3,2,1,0:T(8,128)(2,1)S(1)}, u32[]{:S(2)}, u32[]{:S(2)}) async-start(bf16[4,1,2,128,512]{4,3,2,1,0:T(8,128)(2,1)} %get-tuple-element.77), calls=%async_computation.1 | async-start | bytes 2097152 | tf_op jit(solution)/shard_map/all_to_all | solution.py:481
  56.2 9.5 %shard_map.77.images = f32[4,2,2,128,512]{4,3,2,1,0:T(8,128)} custom-call(s32[128]{0:T(128)} %reshape.473.block, bf16[32,16,128]{2,1,0:T(8,128)(2,1)} %pad_maximum_fusion.3.samples, bf16[32,128,128]{2,1,0:T(8,128)(2,1)} %refs_4_.15, bf16[32,128,128]{2,1,0:T(8,128)(2,1)} %collective-permute-done.9.refs_1_.refs_5_, bf16[32,128,128]{2,1,0:T(8,128)(2,1)} %copy-done.2, ...), custom_call_target="tpu_custom_call" | custom-call | flops 1342177280 | bytes 6423040 | tf_op jit(solution)/shard_map/pallas_call | solution.py:556
  68.6 5.4 %shard_map.82.refs_0_ = bf16[256,128]{1,0:T(8,128)(2,1)} custom-call(s32[128]{0:T(128)} %reshape.472.block, f32[1,2,128,512]{3,2,1,0:T(8,128)} %get-tuple-element.86.picture.refs_19_, bf16[4,1,2,128,512]{4,3,2,1,0:T(8,128)(2,1)} %copy-done, bf16[4,1,2,128,512]{4,3,2,1,0:T(8,128)(2,1)} %copy-done, bf16[4,1,2,128,512]{4,3,2,1,0:T(8,128)(2,1)} %copy-done, ...), custom_call_target="tpu_custom_call" | custom-call | flops 671088640 | bytes 9437696 | tf_op jit(solution)/shard_map/pallas_call | solution.py:556
  81.9 8.5 %shard_map.83 = (f32[1,2,128,512]{3,2,1,0:T(8,128)}, bf16[1,2,128,512]{3,2,1,0:T(8,128)(2,1)}, f32[8,128]{1,0:T(8,128)}, f32[8,128]{1,0:T(8,128)}, f32[256,128]{1,0:T(8,128)}) custom-call(s32[128]{0:T(128)} %reshape.472.block, bf16[256,128]{1,0:T(8,128)(2,1)} %shard_map.82.refs_0_, bf16[256,128]{1,0:T(8,128)(2,1)} %copy-done.31, ...), custom_call_target="tpu_custom_call" | custom-call | flops 671088640 | bytes 11289088 | tf_op jit(solution)/shard_map/pallas_call | solution.py:556
  90.3 5.4 %shard_map.87.refs_0_ = bf16[256,128]{1,0:T(8,128)(2,1)} custom-call(s32[128]{0:T(128)} %reshape.472.block, f32[1,2,128,512]{3,2,1,0:T(8,128)} %get-tuple-element.103.picture.refs_16_, bf16[4,1,2,128,512]{4,3,2,1,0:T(8,128)(2,1)} %copy-done, bf16[4,1,2,128,512]{4,3,2,1,0:T(8,128)(2,1)} %copy-done, bf16[4,1,2,128,512]{4,3,2,1,0:T(8,128)(2,1)} %copy-done, ...), custom_call_target="tpu_custom_call" | custom-call | flops 671088640 | bytes 9437696 | tf_op jit(solution)/shard_map/pallas_call | solution.py:556
  110.5 5.4 %shard_map.79.refs_0_ = bf16[256,128]{1,0:T(8,128)(2,1)} custom-call(s32[128]{0:T(128)} %reshape.472.block, f32[1,2,128,512]{3,2,1,0:T(8,128)} %get-tuple-element.78.picture.refs_19_.refs_4_, bf16[4,1,2,128,512]{4,3,2,1,0:T(8,128)(2,1)} %copy-done.1, bf16[4,1,2,128,512]{4,3,2,1,0:T(8,128)(2,1)} %copy-done.1, bf16[4,1,2,128,512]{4,3,2,1,0:T(8,128)(2,1)} %copy-done.1, ...), custom_call_target="tpu_custom_call" | custom-call | flops 671088640 | bytes 9437696 | tf_op jit(solution)/shard_map/pallas_call | solution.py:556
  119.3 3.7 %collective-permute-done.13.refs_2_ = bf16[256,128]{1,0:T(8,128)(2,1)S(1)} collective-permute-done((bf16[256,128]{1,0:T(8,128)(2,1)}, bf16[256,128]{1,0:T(8,128)(2,1)S(1)}, u32[]{:S(2)}, u32[]{:S(2)}) %collective-permute-start.13) | collective-permute-done | bytes 65568 | tf_op jit(solution)/shard_map/ppermute | solution.py:438
  128.0 8.4 %shard_map.80 = (f32[1,2,128,512]{3,2,1,0:T(8,128)}, bf16[1,2,128,512]{3,2,1,0:T(8,128)(2,1)}, f32[8,128]{1,0:T(8,128)}, f32[8,128]{1,0:T(8,128)}, f32[256,128]{1,0:T(8,128)}) custom-call(s32[128]{0:T(128)} %reshape.472.block, bf16[256,128]{1,0:T(8,128)(2,1)} %shard_map.79.refs_0_, bf16[256,128]{1,0:T(8,128)(2,1)} %copy-done.34, ...), custom_call_target="tpu_custom_call" | custom-call | flops 671088640 | bytes 11289088 | tf_op jit(solution)/shard_map/pallas_call | solution.py:556
  136.4 5.8 %shard_map.84.refs_0_ = bf16[256,128]{1,0:T(8,128)(2,1)} custom-call(s32[128]{0:T(128)} %reshape.472.block, f32[1,2,128,512]{3,2,1,0:T(8,128)} %get-tuple-element.91.picture.refs_16_.refs_5_, bf16[4,1,2,128,512]{4,3,2,1,0:T(8,128)(2,1)} %copy-done.1, bf16[4,1,2,128,512]{4,3,2,1,0:T(8,128)(2,1)} %copy-done.1, bf16[4,1,2,128,512]{4,3,2,1,0:T(8,128)(2,1)} %copy-done.1, ...), custom_call_target="tpu_custom_call" | custom-call | flops 671088640 | bytes 9437696 | tf_op jit(solution)/shard_map/pallas_call | solution.py:556
  142.3 8.1 %shard_map.89.refs_6_ = bf16[1,2,128,512]{3,2,1,0:T(8,128)(2,1)} custom-call(s32[128]{0:T(128)} %reshape.472.block, bf16[256,128]{1,0:T(8,128)(2,1)} %shard_map.87.refs_0_, bf16[256,128]{1,0:T(8,128)(2,1)} %copy-done.16, bf16[256,128]{1,0:T(8,128)(2,1)} %copy-done.17, bf16[256,128]{1,0:T(8,128)(2,1)} %copy-done.18, bf16[32,128,128]{2,1,0:T(8,128)(2,1)} %refs_4_.15, ...), custom_call_target="tpu_custom_call" | custom-call | flops 671088640 | bytes 11276800 | tf_op jit(solution)/shard_map/pallas_call | solution.py:556
  165.4 4.1 %collective-permute-done.30.refs_3_ = bf16[256,128]{1,0:T(8,128)(2,1)S(1)} collective-permute-done((bf16[256,128]{1,0:T(8,128)(2,1)S(1)}, bf16[256,128]{1,0:T(8,128)(2,1)S(1)}, u32[]{:S(2)}, u32[]{:S(2)}) %collective-permute-start.30) | collective-permute-done | bytes 65568 | tf_op jit(solution)/shard_map/ppermute | solution.py:438
  173.4 3.6 %collective-permute-start.42 = (f32[2,8,128]{2,1,0:T(8,128)S(1)}, f32[2,8,128]{2,1,0:T(8,128)S(1)}, u32[]{:S(2)}, u32[]{:S(2)}) collective-permute-start(f32[2,8,128]{2,1,0:T(8,128)S(1)} %pad_maximum_fusion.7.refs_0_), channel_id=1, source_target_pairs={{0,12},{4,8},{8,4},{12,0},{1,13},{5,9},{9,5},{13,1},{2,14},{6,10},... | collective-permute-start | bytes 24584 | tf_op jit(solution)/shard_map/ppermute | solution.py:438
  177.0 8.4 %shard_map.86.refs_6_ = f32[1,2,128,512]{3,2,1,0:T(8,128)} custom-call(s32[128]{0:T(128)} %reshape.472.block, bf16[256,128]{1,0:T(8,128)(2,1)} %shard_map.84.refs_0_, bf16[256,128]{1,0:T(8,128)(2,1)} %copy-done.19, bf16[256,128]{1,0:T(8,128)(2,1)} %copy-done.20, bf16[256,128]{1,0:T(8,128)(2,1)} %copy-done.21, bf16[32,128,128]{2,1,0:T(8,128)(2,1)} %refs_4_.15, ...), custom_call_target="tpu_custom_call" | custom-call | flops 671088640 | bytes 11276800 | tf_op jit(solution)/shard_map/pallas_call | solution.py:556
  193.5 13.8 %collective-permute-done.51.refs_7_ = bf16[1,2,128,512]{3,2,1,0:T(8,128)(2,1)S(1)} collective-permute-done((bf16[1,2,128,512]{3,2,1,0:T(8,128)(2,1)}, bf16[1,2,128,512]{3,2,1,0:T(8,128)(2,1)S(1)}, u32[]{:S(2)}, u32[]{:S(2)}) %collective-permute-start.51) | collective-permute-done | bytes 262176 | tf_op jit(solution)/shard_map/ppermute | solution.py:438
  207.3 5.5 %collective-permute-done.47.refs_6_ = bf16[1,2,128,512]{3,2,1,0:T(8,128)(2,1)S(1)} collective-permute-done((bf16[1,2,128,512]{3,2,1,0:T(8,128)(2,1)}, bf16[1,2,128,512]{3,2,1,0:T(8,128)(2,1)S(1)}, u32[]{:S(2)}, u32[]{:S(2)}) %collective-permute-start.47) | collective-permute-done | bytes 262176 | tf_op jit(solution)/shard_map/ppermute | solution.py:438
  218.4 4.2 %shard_map.91.refs_7_ = f32[8,2,128,512]{3,2,1,0:T(8,128)} custom-call(s32[4]{0:T(128)} %pad_add_fusion.4.order, f32[2,8,128]{2,1,0:T(8,128)} %copy-done.12, f32[2,8,128]{2,1,0:T(8,128)} %copy-done.13, f32[2,8,128]{2,1,0:T(8,128)} %copy-done.14, f32[2,8,128]{2,1,0:T(8,128)} %copy-done.15, bf16[1,2,128,512]{3,2,1,0:T(8,128)(2,1)} %get-tuple-element.129.refs_4_, ...), custom_call_target="tpu_custom_call" | custom-call | tf_op jit(solution)/shard_map/pallas_call | solution.py:692
  223.4 4.6 %shard_map.94.refs_8_ = f32[8,2,128,512]{3,2,1,0:T(8,128)} custom-call(s32[4]{0:T(128)} %pad_add_fusion.4.order, f32[2,8,128]{2,1,0:T(8,128)} %copy-done.12, f32[2,8,128]{2,1,0:T(8,128)} %copy-done.13, f32[2,8,128]{2,1,0:T(8,128)} %copy-done.14, f32[2,8,128]{2,1,0:T(8,128)} %copy-done.15, bf16[1,2,128,512]{3,2,1,0:T(8,128)(2,1)} %get-tuple-element.129.refs_4_, ...), custom_call_target="tpu_custom_call" | custom-call | tf_op jit(solution)/shard_map/pallas_call | solution.py:692
  228.0 3.2 %shard_map.95.refs_8_ = f32[8,2,128,512]{3,2,1,0:T(8,128)} custom-call(s32[2]{0:T(128)} %pad_add_fusion.3.order, f32[2,8,128]{2,1,0:T(8,128)} %copy-done.12, f32[2,8,128]{2,1,0:T(8,128)} %copy-done.13, f32[2,8,128]{2,1,0:T(8,128)} %copy-done.14, f32[2,8,128]{2,1,0:T(8,128)} %copy-done.15, ...), custom_call_target="tpu_custom_call", output_to_operand_aliasing={{}: (9, {})} | custom-call | tf_op jit(solution)/shard_map/pallas_call | solution.py:692
  239.5 3.2 %shard_map.96 = f32[8,2,128,512]{3,2,1,0:T(8,128)} custom-call(s32[2]{0:T(128)} %pad_add_fusion.1.order, f32[2,8,128]{2,1,0:T(8,128)} %copy-done.12, f32[2,8,128]{2,1,0:T(8,128)} %copy-done.13, f32[2,8,128]{2,1,0:T(8,128)} %copy-done.14, f32[2,8,128]{2,1,0:T(8,128)} %copy-done.15, ...), custom_call_target="tpu_custom_call", output_to_operand_aliasing={{}: (9, {})} | custom-call | tf_op jit(solution)/shard_map/pallas_call | solution.py:692
  (263 shorter events, 99.7 us)
Async XLA Ops:
  0.6 31.4 %collective-permute-start.10 = (bf16[32,128,128]{2,1,0:T(8,128)(2,1)}, bf16[32,128,128]{2,1,0:T(8,128)(2,1)S(1)}, u32[]{:S(2)}, u32[]{:S(2)}) collective-permute-start(bf16[32,128,128]{2,1,0:T(8,128)(2,1)} %refs_4_.15), channel_id=1, source_target_pairs={{0,2},{1,3},{2,0},{3,1},{4,6},{5,7},{6,4},{7,5},{8,10},{9,11},{10,... | collective-permute-start | bytes 3145736 | tf_op jit(solution)/shard_map/ppermute | solution.py:438
  3.7 52.5 %collective-permute-start.9 = (bf16[32,128,128]{2,1,0:T(8,128)(2,1)}, bf16[32,128,128]{2,1,0:T(8,128)(2,1)}, u32[]{:S(2)}, u32[]{:S(2)}) collective-permute-start(bf16[32,128,128]{2,1,0:T(8,128)(2,1)} %refs_4_.15), channel_id=1, source_target_pairs={{0,1},{1,0},{2,3},{3,2},{4,5},{5,4},{6,7},{7,6},{8,9},{9,8},{10,11... | collective-permute-start | bytes 3145736 | tf_op jit(solution)/shard_map/ppermute | solution.py:438
  17.2 28.5 %all-to-all-start = ((bf16[4,1,2,128,512]{4,3,2,1,0:T(8,128)(2,1)}), bf16[4,1,2,128,512]{4,3,2,1,0:T(8,128)(2,1)S(1)}, u32[]{:S(2)}, u32[]{:S(2)}) async-start(bf16[4,1,2,128,512]{4,3,2,1,0:T(8,128)(2,1)} %get-tuple-element.138), calls=%async_computation | async-start | bytes 2097152 | tf_op jit(solution)/shard_map/all_to_all | solution.py:481
  27.2 26.4 %collective-permute-start.4 = (bf16[8,16,128]{2,1,0:T(8,128)(2,1)S(1)}, bf16[8,16,128]{2,1,0:T(8,128)(2,1)S(1)}, u32[]{:S(2)}, u32[]{:S(2)}) collective-permute-start(bf16[8,16,128]{2,1,0:T(8,128)(2,1)S(1)} %fusion.14), channel_id=1, source_target_pairs={{0,2},{1,3},{2,0},{3,1},{4,6},{5,7},{6,4},{7,5},{8,10},{9,11},{10,... | collective-permute-start | bytes 98312 | tf_op jit(solution)/shard_map/ppermute | solution.py:438
  28.9 26.5 %collective-permute-start.3 = (bf16[8,16,128]{2,1,0:T(8,128)(2,1)S(1)}, bf16[8,16,128]{2,1,0:T(8,128)(2,1)S(1)}, u32[]{:S(2)}, u32[]{:S(2)}) collective-permute-start(bf16[8,16,128]{2,1,0:T(8,128)(2,1)S(1)} %fusion.14), channel_id=1, source_target_pairs={{0,1},{1,0},{2,3},{3,2},{4,5},{5,4},{6,7},{7,6},{8,9},{9,8},{10,11... | collective-permute-start | bytes 98312 | tf_op jit(solution)/shard_map/ppermute | solution.py:438
  32.1 24.1 %collective-permute-start.11 = (bf16[32,128,128]{2,1,0:T(8,128)(2,1)S(1)}, bf16[32,128,128]{2,1,0:T(8,128)(2,1)}, u32[]{:S(2)}, u32[]{:S(2)}) collective-permute-start(bf16[32,128,128]{2,1,0:T(8,128)(2,1)S(1)} %collective-permute-done.10.refs_2_.refs_6_), channel_id=1, source_target_pairs={{0,1},{1,0},{2,3},{3,2},{4,5},{5,4},{6,7},{7,6},{8,9},{9,8},{10,11... | collective-permute-start | bytes 3145736 | tf_op jit(solution)/shard_map/ppermute | solution.py:438
  45.7 54.3 %all-to-all-start.1 = ((bf16[4,1,2,128,512]{4,3,2,1,0:T(8,128)(2,1)}), bf16[4,1,2,128,512]{4,3,2,1,0:T(8,128)(2,1)S(1)}, u32[]{:S(2)}, u32[]{:S(2)}) async-start(bf16[4,1,2,128,512]{4,3,2,1,0:T(8,128)(2,1)} %get-tuple-element.77), calls=%async_computation.1 | async-start | bytes 2097152 | tf_op jit(solution)/shard_map/all_to_all | solution.py:481
  105.4 31.0 %collective-permute-start.24 = (bf16[1,2,128,512]{3,2,1,0:T(8,128)(2,1)S(1)}, bf16[1,2,128,512]{3,2,1,0:T(8,128)(2,1)S(1)}, u32[]{:S(2)}, u32[]{:S(2)}) collective-permute-start(bf16[1,2,128,512]{3,2,1,0:T(8,128)(2,1)S(1)} %copy-done.3), channel_id=1, source_target_pairs={{0,4},{4,0},{8,12},{12,8},{1,5},{5,1},{9,13},{13,9},{2,6},{6,2},{1... | collective-permute-start | bytes 786440 | tf_op jit(solution)/shard_map/ppermute | solution.py:438
  107.3 29.1 %collective-permute-start.25 = (bf16[1,2,128,512]{3,2,1,0:T(8,128)(2,1)S(1)}, bf16[1,2,128,512]{3,2,1,0:T(8,128)(2,1)S(1)}, u32[]{:S(2)}, u32[]{:S(2)}) collective-permute-start(bf16[1,2,128,512]{3,2,1,0:T(8,128)(2,1)S(1)} %copy-done.3), channel_id=1, source_target_pairs={{0,8},{4,12},{8,0},{12,4},{1,9},{5,13},{9,1},{13,5},{2,10},{6,14},... | collective-permute-start | bytes 786440 | tf_op jit(solution)/shard_map/ppermute | solution.py:438
  109.6 26.8 %collective-permute-start.26 = (bf16[1,2,128,512]{3,2,1,0:T(8,128)(2,1)S(1)}, bf16[1,2,128,512]{3,2,1,0:T(8,128)(2,1)S(1)}, u32[]{:S(2)}, u32[]{:S(2)}) collective-permute-start(bf16[1,2,128,512]{3,2,1,0:T(8,128)(2,1)S(1)} %copy-done.4), channel_id=1, source_target_pairs={{0,4},{4,0},{8,12},{12,8},{1,5},{5,1},{9,13},{13,9},{2,6},{6,2},{1... | collective-permute-start | bytes 786440 | tf_op jit(solution)/shard_map/ppermute | solution.py:438
  110.3 26.2 %collective-permute-start.27 = (bf16[1,2,128,512]{3,2,1,0:T(8,128)(2,1)S(1)}, bf16[1,2,128,512]{3,2,1,0:T(8,128)(2,1)S(1)}, u32[]{:S(2)}, u32[]{:S(2)}) collective-permute-start(bf16[1,2,128,512]{3,2,1,0:T(8,128)(2,1)S(1)} %copy-done.4), channel_id=1, source_target_pairs={{0,8},{4,12},{8,0},{12,4},{1,9},{5,13},{9,1},{13,5},{2,10},{6,14},... | collective-permute-start | bytes 786440 | tf_op jit(solution)/shard_map/ppermute | solution.py:438
  142.2 21.6 %collective-permute-start.28 = (bf16[256,128]{1,0:T(8,128)(2,1)}, bf16[256,128]{1,0:T(8,128)(2,1)S(1)}, u32[]{:S(2)}, u32[]{:S(2)}) collective-permute-start(bf16[256,128]{1,0:T(8,128)(2,1)} %shard_map.84.refs_0_), channel_id=1, source_target_pairs={{0,1},{1,0},{2,3},{3,2},{4,5},{5,4},{6,7},{7,6},{8,9},{9,8},{10,11... | collective-permute-start | bytes 196616 | tf_op jit(solution)/shard_map/ppermute | solution.py:438
  150.4 22.7 %collective-permute-start.45 = (bf16[1,2,128,512]{3,2,1,0:T(8,128)(2,1)}, bf16[1,2,128,512]{3,2,1,0:T(8,128)(2,1)S(1)}, u32[]{:S(2)}, u32[]{:S(2)}) collective-permute-start(bf16[1,2,128,512]{3,2,1,0:T(8,128)(2,1)} %shard_map.89.refs_6_), channel_id=1, source_target_pairs={{0,4},{4,0},{8,12},{12,8},{1,5},{5,1},{9,13},{13,9},{2,6},{6,2},{1... | collective-permute-start | bytes 786440 | tf_op jit(solution)/shard_map/ppermute | solution.py:438
  152.2 21.2 %collective-permute-start.46 = (bf16[1,2,128,512]{3,2,1,0:T(8,128)(2,1)}, bf16[1,2,128,512]{3,2,1,0:T(8,128)(2,1)S(1)}, u32[]{:S(2)}, u32[]{:S(2)}) collective-permute-start(bf16[1,2,128,512]{3,2,1,0:T(8,128)(2,1)} %shard_map.89.refs_6_), channel_id=1, source_target_pairs={{0,8},{4,12},{8,0},{12,4},{1,9},{5,13},{9,1},{13,5},{2,10},{6,14},... | collective-permute-start | bytes 786440 | tf_op jit(solution)/shard_map/ppermute | solution.py:438
  163.3 22.2 %collective-permute-start.43 = (bf16[1,2,128,512]{3,2,1,0:T(8,128)(2,1)S(1)}, bf16[1,2,128,512]{3,2,1,0:T(8,128)(2,1)S(1)}, u32[]{:S(2)}, u32[]{:S(2)}) collective-permute-start(bf16[1,2,128,512]{3,2,1,0:T(8,128)(2,1)S(1)} %collective-permute-done.25.refs_4_), channel_id=1, source_target_pairs={{0,4},{4,0},{8,12},{12,8},{1,5},{5,1},{9,13},{13,9},{2,6},{6,2},{1... | collective-permute-start | bytes 786440 | tf_op jit(solution)/shard_map/ppermute | solution.py:438
  163.9 21.7 %collective-permute-start.44 = (bf16[1,2,128,512]{3,2,1,0:T(8,128)(2,1)S(1)}, bf16[1,2,128,512]{3,2,1,0:T(8,128)(2,1)S(1)}, u32[]{:S(2)}, u32[]{:S(2)}) collective-permute-start(bf16[1,2,128,512]{3,2,1,0:T(8,128)(2,1)S(1)} %collective-permute-done.27.refs_5_), channel_id=1, source_target_pairs={{0,4},{4,0},{8,12},{12,8},{1,5},{5,1},{9,13},{13,9},{2,6},{6,2},{1... | collective-permute-start | bytes 786440 | tf_op jit(solution)/shard_map/ppermute | solution.py:438
  172.6 12.8 %collective-permute-start.40 = (f32[2,8,128]{2,1,0:T(8,128)S(1)}, f32[2,8,128]{2,1,0:T(8,128)S(1)}, u32[]{:S(2)}, u32[]{:S(2)}) collective-permute-start(f32[2,8,128]{2,1,0:T(8,128)S(1)} %pad_maximum_fusion.7.refs_0_), channel_id=1, source_target_pairs={{0,4},{4,0},{8,12},{12,8},{1,5},{5,1},{9,13},{13,9},{2,6},{6,2},{1... | collective-permute-start | bytes 24584 | tf_op jit(solution)/shard_map/ppermute | solution.py:438
  188.5 18.8 %collective-permute-start.51 = (bf16[1,2,128,512]{3,2,1,0:T(8,128)(2,1)}, bf16[1,2,128,512]{3,2,1,0:T(8,128)(2,1)S(1)}, u32[]{:S(2)}, u32[]{:S(2)}) collective-permute-start(bf16[1,2,128,512]{3,2,1,0:T(8,128)(2,1)} %get-tuple-element.134.refs_7_), channel_id=1, source_target_pairs={{0,8},{4,12},{8,0},{12,4},{1,9},{5,13},{9,1},{13,5},{2,10},{6,14},... | collective-permute-start | bytes 786440 | tf_op jit(solution)/shard_map/ppermute | solution.py:438
  188.5 24.3 %collective-permute-start.47 = (bf16[1,2,128,512]{3,2,1,0:T(8,128)(2,1)}, bf16[1,2,128,512]{3,2,1,0:T(8,128)(2,1)S(1)}, u32[]{:S(2)}, u32[]{:S(2)}) collective-permute-start(bf16[1,2,128,512]{3,2,1,0:T(8,128)(2,1)} %get-tuple-element.126.refs_6_), channel_id=1, source_target_pairs={{0,8},{4,12},{8,0},{12,4},{1,9},{5,13},{9,1},{13,5},{2,10},{6,14},... | collective-permute-start | bytes 786440 | tf_op jit(solution)/shard_map/ppermute | solution.py:438
  191.5 31.2 %collective-permute-start.53 = (bf16[1,2,128,512]{3,2,1,0:T(8,128)(2,1)}, bf16[1,2,128,512]{3,2,1,0:T(8,128)(2,1)S(1)}, u32[]{:S(2)}, u32[]{:S(2)}) collective-permute-start(bf16[1,2,128,512]{3,2,1,0:T(8,128)(2,1)} %get-tuple-element.134.refs_7_), channel_id=1, source_target_pairs={{0,4},{4,0},{8,12},{12,8},{1,5},{5,1},{9,13},{13,9},{2,6},{6,2},{1... | collective-permute-start | bytes 786440 | tf_op jit(solution)/shard_map/ppermute | solution.py:438
  191.5 26.2 %collective-permute-start.49 = (bf16[1,2,128,512]{3,2,1,0:T(8,128)(2,1)}, bf16[1,2,128,512]{3,2,1,0:T(8,128)(2,1)S(1)}, u32[]{:S(2)}, u32[]{:S(2)}) collective-permute-start(bf16[1,2,128,512]{3,2,1,0:T(8,128)(2,1)} %get-tuple-element.126.refs_6_), channel_id=1, source_target_pairs={{0,4},{4,0},{8,12},{12,8},{1,5},{5,1},{9,13},{13,9},{2,6},{6,2},{1... | collective-permute-start | bytes 786440 | tf_op jit(solution)/shard_map/ppermute | solution.py:438
  193.5 44.5 %collective-permute-start.50 = (bf16[1,2,128,512]{3,2,1,0:T(8,128)(2,1)S(1)}, bf16[1,2,128,512]{3,2,1,0:T(8,128)(2,1)S(1)}, u32[]{:S(2)}, u32[]{:S(2)}) collective-permute-start(bf16[1,2,128,512]{3,2,1,0:T(8,128)(2,1)S(1)} %collective-permute-done.46.refs_6_), channel_id=1, source_target_pairs={{0,4},{4,0},{8,12},{12,8},{1,5},{5,1},{9,13},{13,9},{2,6},{6,2},{1... | collective-permute-start | bytes 786440 | tf_op jit(solution)/shard_map/ppermute | solution.py:438
  207.3 30.7 %collective-permute-start.52 = (bf16[1,2,128,512]{3,2,1,0:T(8,128)(2,1)S(1)}, bf16[1,2,128,512]{3,2,1,0:T(8,128)(2,1)S(1)}, u32[]{:S(2)}, u32[]{:S(2)}) collective-permute-start(bf16[1,2,128,512]{3,2,1,0:T(8,128)(2,1)S(1)} %collective-permute-done.51.refs_7_), channel_id=1, source_target_pairs={{0,4},{4,0},{8,12},{12,8},{1,5},{5,1},{9,13},{13,9},{2,6},{6,2},{1... | collective-permute-start | bytes 786440 | tf_op jit(solution)/shard_map/ppermute | solution.py:438
  212.9 21.4 %collective-permute-start.48 = (bf16[1,2,128,512]{3,2,1,0:T(8,128)(2,1)S(1)}, bf16[1,2,128,512]{3,2,1,0:T(8,128)(2,1)S(1)}, u32[]{:S(2)}, u32[]{:S(2)}) collective-permute-start(bf16[1,2,128,512]{3,2,1,0:T(8,128)(2,1)S(1)} %collective-permute-done.47.refs_6_), channel_id=1, source_target_pairs={{0,4},{4,0},{8,12},{12,8},{1,5},{5,1},{9,13},{13,9},{2,6},{6,2},{1... | collective-permute-start | bytes 786440 | tf_op jit(solution)/shard_map/ppermute | solution.py:438
  (85 other events, 681.7 us)

commit v8 on v6

--- a/solution.py
+++ b/solution.py
@@ -94,24 +94,55 @@
         grid_ref[pl.ds(2 * step + 1, tiles, stride=channels), :] = part[:, size:]
 
 
+def tile_products(lefts, rights):
+    rows, size = lefts[0].shape
+    empty = jnp.zeros((rows, size), bf16)
+    left = jnp.concatenate(
+        [
+            jnp.concatenate([value, empty] if place % 2 == 0 else [empty, value], 1)
+            for place, value in enumerate(lefts)
+        ],
+        0,
+    )
+    right = jnp.concatenate(
+        [jnp.concatenate(rights[:2], 0), jnp.concatenate(rights[2:], 0)], 1
+    )
+    product = nn(left, right)
+    return [
+        product[place * rows : (place + 1) * rows, place // 2 * size : (place // 2 + 1) * size]
+        for place in range(4)
+    ]
+
+
+def each_four(count, function):
+    def one(index, carry):
+        function([index * 4 + place for place in range(4)])
+        return carry
+
+    lax.fori_loop(0, count // 4, one, 0, unroll=True)
+
+
 def sample_tiles(block_ref, weights, grid_ref, sums_ref, out_ref):
     count = weights[0].shape[0]
     channels = sums_ref.shape[1]
     sums_ref[...] = jnp.zeros_like(sums_ref)
 
+    def left_of(tile):
+        value = grid_ref[pl.ds(pl.multiple_of(tile * channels, channels), channels), :]
+        high = value.astype(bf16).astype(f32)
+        return jnp.concatenate([high, value - high], 0).astype(bf16)
+
     for group, weights_ref in enumerate(weights):
 
-        def one(place, carry):
-            tile = group * count + place
-            start = pl.multiple_of(tile * channels, channels)
-            value = grid_ref[pl.ds(start, channels), :]
-            high = value.astype(bf16).astype(f32)
-            both = jnp.concatenate([high, value - high], 0).astype(bf16)
-            product = nn(both, weights_ref[place])
-            sums_ref[block_ref[tile]] += product[:channels] + product[channels:]
-            return carry
-
-        lax.fori_loop(0, count, one, 0, unroll=True)
+        def four(places):
+            tiles = [group * count + place for place in places]
+            products = tile_products(
+                [left_of(tile) for tile in tiles], [weights_ref[place] for place in places]
+            )
+            for tile, product in zip(tiles, products):
+                sums_ref[block_ref[tile]] += product[:channels] + product[channels:]
+
+        each_four(count, four)
     out_ref[...] = sums_ref[...].reshape(out_ref.shape).astype(bf16)
 
 
@@ -121,16 +152,19 @@
 
     for group, weights_ref in enumerate(weights):
 
-        def one(place, carry):
-            tile = group * count + place
-            start = pl.multiple_of(tile * channels, channels)
-            product = nt(parts_ref[block_ref[tile]], weights_ref[place])
-            if product.shape[0] > channels:
-                product = product[:channels] + product[channels:]
-            grid_ref[pl.ds(start, channels), :] = product
-            return carry
-
-        lax.fori_loop(0, count, one, 0, unroll=True)
+        def four(places):
+            tiles = [group * count + place for place in places]
+            products = tile_products(
+                [parts_ref[block_ref[tile]] for tile in tiles],
+                [weights_ref[place] for place in places],
+            )
+            for tile, product in zip(tiles, products):
+                if product.shape[0] > channels:
+                    product = product[:channels] + product[channels:]
+                start = pl.multiple_of(tile * channels, channels)
+                grid_ref[pl.ds(start, channels), :] = product
+
+        each_four(count, four)
 
 
 def adjoint_images(coils, plane, planes, ey_back, mx_back, turn_ref, grid_ref):
@@ -285,11 +319,12 @@
 
 
 def facts_kernel(peers, *refs):
-    samples = refs[:peers]
-    dots, start_total, facts, out = refs[peers:]
+    samples, dots = refs[:peers], refs[peers : 2 * peers]
+    start_total, facts, out = refs[2 * peers :]
+    both = tree_sum([part[...] for part in dots])
     summed = tree_sum([part[...].astype(f32) for part in samples])
     rows = lax.broadcasted_iota(jnp.int32, out.shape, 0)
-    values = [facts[0:1], facts[1:2], dots[0:1], dots[1:2]]
+    values = [facts[0:1], facts[1:2], both[0:1], both[1:2]]
     values += [jnp.sum(summed * summed), jnp.sum(summed * start_total[...])]
     total = jnp.zeros(out.shape, f32)
     for row, value in enumerate(values):
@@ -457,6 +492,7 @@
     by_coil = jnp.arange(coil_count, dtype=jnp.int32) ^ coil_index
     measured = jnp.take(measured, by_coil, axis=0)
     all_weights = everywhere(weights, "pencil")
+    turned_weights = [jnp.swapaxes(array, 1, 2) for array in all_weights]
 
     places = jnp.stack(everywhere(packed, "pencil"))
     holder = (jnp.arange(peers, dtype=jnp.int32) ^ lax.axis_index("pencil"))[:, None]
@@ -498,6 +534,7 @@
         and columns % 128 == 0
         and size % 128 == 0
         and channels % 16 == 0
+        and tile_count % 4 == 0
         and group_channels % 8 == 0
     ):
         ey = jnp.concatenate([cos_y, sin_y], 0).astype(bf16)
@@ -543,7 +580,7 @@
             )(*inputs)
 
         def measured_images():
-            inputs = [measured_block, measured, *all_weights, *tail_tables]
+            inputs = [measured_block, measured, *turned_weights, *tail_tables]
             shape = (coil_count, own_planes, 2, rows, columns)
             return call(
                 measured_kernel,
@@ -597,7 +634,7 @@
             )
 
         def back(kernel, samples, tables, vectors, g, outs, out_specs):
-            inputs = [*samples, *all_weights]
+            inputs = [*samples, *turned_weights]
             tables = tail_tables + tables
             return call(
                 functools.partial(kernel, peers, coil_count),
@@ -627,7 +664,7 @@
             )
 
         def facts_of(samples, dots, start_total, facts):
-            inputs = [*samples, dots, start_total, facts]
+            inputs = [*samples, *dots, start_total, facts]
             return pl.pallas_call(
                 functools.partial(facts_kernel, peers),
                 in_specs=[pl.BlockSpec(memory_space=pltpu.VMEM)] * len(inputs),
@@ -781,7 +818,8 @@
 
         def facts_of(samples, dots, start_total, facts):
             total = added(samples)
-            values = [facts[0, 0], facts[1, 0], dots[0, 0], dots[1, 0]]
+            square, cross = tree_sum(dots)[:2, 0]
+            values = [facts[0, 0], facts[1, 0], square, cross]
             values += [jnp.sum(total * total), jnp.sum(total * start_total)]
             return stacked_dots(values)
 
@@ -819,33 +857,27 @@
         start_sent = sent_by_bits(start_own)
         samples = exchanged(forward(right_side, g))
         norms = exchanged(norm)
+        samples, norms, start_sent = lax.optimization_barrier((samples, norms, start_sent))
         residual, residual_own, facts, dots, start_total = first(samples, norms, right_side, g)
-        residual, residual_own, start_sent = lax.optimization_barrier(
-            (residual, residual_own, start_sent)
-        )
+        residual, residual_own, pieces = lax.optimization_barrier(
+            (residual, residual_own, completed(start_own, start_sent))
+        )
+        start_pieces.append(pieces)
         residual_sent = sent_by_bits(residual_own)
+        dots = exchanged(dots)
         samples = exchanged(forward(residual, g))
-        samples, pieces = lax.optimization_barrier(
-            (samples, completed(start_own, start_sent))
-        )
-        start_pieces.append(pieces)
+        samples, dots, residual_sent = lax.optimization_barrier((samples, dots, residual_sent))
         info = facts_of(samples, dots, start_total, facts)
         infos.append(info)
         rounded = second(samples, info, residual, g)
         last = g == groups[-1]
         others = exchanged(jnp.stack(infos), "coil") if last else []
-        rounded, others, residual_sent = lax.optimization_barrier(
-            (rounded, others, residual_sent)
-        )
-        residual_pieces.append(completed(residual_own, residual_sent))
+        rounded, others, pieces = lax.optimization_barrier(
+            (rounded, others, completed(residual_own, residual_sent))
+        )
+        residual_pieces.append(pieces)
         mixed_own.append(rounded)
         mixed_sent.append(sent_by_bits(rounded))
-
-    others, mixed_sent[-1][0] = lax.optimization_barrier((jnp.stack(others), mixed_sent[-1][0]))
-    rows_of = lax.broadcasted_iota(jnp.int32, others.shape, 2)
-    shared = (rows_of == 2) | (rows_of == 3)
-    others = jnp.where(shared, tree_sum(exchanged(others)), others)
-    others = [others[k] for k in range(coil_count)]
 
     picture = assembled(others, [start_pieces, residual_pieces], range(coil_count))
     early = [
@@ -853,7 +885,7 @@
         for own, sent in zip(mixed_own, mixed_sent)
     ]
     out = assembled(others, [start_pieces, residual_pieces, early], range(2))
-    out, mixed_sent = lax.optimization_barrier((out, mixed_sent))
+    picture, out, mixed_sent = lax.optimization_barrier((picture, out, mixed_sent))
     mixed_pieces = [completed(own, sent) for own, sent in zip(mixed_own, mixed_sent)]
     vectors = [start_pieces, residual_pieces, mixed_pieces]
     late = coil_count - 1

time: 202 us -> 201 us (level)
  local copies, waits for them, and re-layouts: 11 us -> 18.8 us
  Pallas kernels: 71.5 us -> 66.4 us
  waiting for transfers between devices: 73 us -> 68.6 us
    ppermute x0 -> x3, local copies, waits for them, and re-layouts: none -> 6.82 us  [swapped(): lax.ppermute(array, axis, [(i, i ^ k) for i in range(lax.axis_size(axis))])]
    ppermute x36, waiting for transfers between devices: 56.8 us -> 51.7 us  [swapped(): lax.ppermute(array, axis, [(i, i ^ k) for i in range(lax.axis_size(axis))])]
    pallas_call x6, Pallas kernels: 49 us -> 44 us  [call(): pl.pallas_call(kernel, grid=grid, in_specs=specs, out_specs=out_specs, ou...]
    unnamed x42 -> x55, local copies, waits for them, and re-layouts: 3.66 us -> 5.03 us
  transfers between devices with their start and end apart: 37 -> 37, of which waited for: 13 -> 13; matrix products, arithmetic and copies ran while one was open for 9% -> 12% of each run, Pallas kernels for 31% -> 29%
where the time goes in v8:
time: 201 us; the launch traced here: 200 us
  waiting for transfers between devices  68.6 us (34%)
  Pallas kernels  66.4 us (33%)
  starting transfers between devices  34.5 us (17%)
  local copies, waits for them, and re-layouts  18.8 us (9%)
  other arithmetic  10.5 us (5%)
    ppermute x36, waiting for transfers between devices, swapped(): lax.ppermute(array, axis, [(i, i ^ k) for i in range(lax.axis_size(axis))])  51.7 us
    pallas_call x6, Pallas kernels, call(): pl.pallas_call(kernel, grid=grid, in_specs=specs, out_specs=out_specs, ou...  44 us
    ppermute x36, starting transfers between devices, swapped(): lax.ppermute(array, axis, [(i, i ^ k) for i in range(lax.axis_size(axis))])  30.9 us
    pallas_call x4, Pallas kernels, assembled(): pl.pallas_call(kernel, grid_spec=pltpu.PrefetchScalarGridSpec(num_scalar_...  20.3 us
    all_to_all x1, waiting for transfers between devices, on_device(): lax.all_to_all(sens_source[:, g * group_planes:(g + 1) * group_planes], '...  16.9 us
    ppermute x3, local copies, waits for them, and re-layouts, swapped(): lax.ppermute(array, axis, [(i, i ^ k) for i in range(lax.axis_size(axis))])  6.82 us
    unnamed x55, local copies, waits for them, and re-layouts  5.03 us
  transfers between devices with their start and end apart: 37, of which 13 were waited for; matrix products, arithmetic and copies ran while one was open for 12% of the time, Pallas kernels for 29%

profile of v8, /device:TPU:0, one launch (start us, length us, event | category | flops | bytes accessed | tf_op | source)
XLA Modules:
  0.0 199.8 jit_solution(18276901657516323284)
XLA Ops:
  2.8 2.6 %collective-permute-start.10 = (bf16[32,128,128]{1,2,0:T(8,128)(2,1)S(1)}, bf16[32,128,128]{1,2,0:T(8,128)(2,1)}, u32[]{:S(2)}, u32[]{:S(2)}) collective-permute-start(bf16[32,128,128]{1,2,0:T(8,128)(2,1)S(1)} %copy.20), channel_id=1, source_target_pairs={{0,2},{1,3},{2,0},{3,1},{4,6},{5,7},{6,4},{7,5},{8,10},{9,11},{10,... | collective-permute-start | bytes 3145736 | tf_op jit(solution)/shard_map/ppermute | solution.py:443
  7.8 2.6 %collective-permute-start.1 = (bf16[2,2,1024]{2,1,0:T(2,128)(2,1)S(1)}, bf16[2,2,1024]{2,1,0:T(2,128)(2,1)S(1)}, u32[]{:S(2)}, u32[]{:S(2)}) collective-permute-start(bf16[2,2,1024]{2,1,0:T(2,128)(2,1)S(1)} %get-tuple-element.125), channel_id=1, source_target_pairs={{0,8},{4,12},{8,0},{12,4},{1,9},{5,13},{9,1},{13,5},{2,10},{6,14},... | collective-permute-start | bytes 24584 | tf_op jit(solution)/shard_map/ppermute | solution.py:443
  12.7 3.1 %collective-permute-done.2 = bf16[2,2,1024]{2,1,0:T(2,128)(2,1)S(1)} collective-permute-done((bf16[2,2,1024]{2,1,0:T(2,128)(2,1)S(1)}, bf16[2,2,1024]{2,1,0:T(2,128)(2,1)S(1)}, u32[]{:S(2)}, u32[]{:S(2)}) %collective-permute-start.2) | collective-permute-done | bytes 8224 | tf_op jit(solution)/shard_map/ppermute | solution.py:443
  15.8 3.6 %all-to-all-start = ((bf16[4,2,2,128,512]{4,3,2,1,0:T(8,128)(2,1)}), bf16[4,2,2,128,512]{4,3,2,1,0:T(8,128)(2,1)S(1)}, u32[]{:S(2)}, u32[]{:S(2)}) async-start(bf16[4,2,2,128,512]{4,3,2,1,0:T(8,128)(2,1)} %bitcast.52), calls=%async_computation | async-start | bytes 4194304 | tf_op jit(solution)/shard_map/all_to_all | solution.py:482
  22.2 7.1 %collective-permute-done.7 = s32[96]{0:T(128)S(1)} collective-permute-done((s32[96]{0:T(128)S(1)}, s32[96]{0:T(128)S(1)}, u32[]{:S(2)}, u32[]{:S(2)}) %collective-permute-start.7) | collective-permute-done | bytes 416 | tf_op jit(solution)/shard_map/ppermute | solution.py:443
  41.7 8.0 %shard_map.77.images = f32[4,2,2,128,512]{4,3,2,1,0:T(8,128)} custom-call(s32[128]{0:T(128)} %reshape.473.block, bf16[32,16,128]{2,1,0:T(8,128)(2,1)} %pad_maximum_fusion.3.samples, bf16[32,128,128]{2,1,0:T(8,128)(2,1)} %bitcast.49, bf16[32,128,128]{2,1,0:T(8,128)(2,1)} %bitcast.27.refs_1_.refs_5_, bf16[32,128,128]{2,1,0:T(8,128)(2,1)} %bitcast.28.refs_2_.refs_6_, ...), custom_call_target="tpu_custom_call" | custom-call | flops 1342177280 | bytes 6423040 | tf_op jit(solution)/shard_map/pallas_call | solution.py:567
  49.7 16.9 %all-to-all-done.refs_0_.refs_1_.refs_2_.refs_3_.refs_8_.refs_9_.refs_10_.refs_11_ = bf16[4,2,2,128,512]{4,3,2,1,0:T(8,128)(2,1)S(1)} async-done(((bf16[4,2,2,128,512]{4,3,2,1,0:T(8,128)(2,1)}), bf16[4,2,2,128,512]{4,3,2,1,0:T(8,128)(2,1)S(1)}, u32[]{:S(2)}, u32[]{:S(2)}) %all-to-all-start) | async-done | bytes 2097184 | tf_op jit(solution)/shard_map/all_to_all | solution.py:482
  67.8 5.1 %shard_map.78 = (f32[2,2,128,512]{3,2,1,0:T(8,128)}, bf16[2,2,128,512]{3,2,1,0:T(8,128)(2,1)}, f32[8,128]{1,0:T(8,128)}) custom-call(f32[4,2,2,128,512]{4,3,2,1,0:T(8,128)} %shard_map.77.images, bf16[4,2,2,128,512]{4,3,2,1,0:T(8,128)(2,1)} %copy-done, bf16[4,2,2,128,512]{4,3,2,1,0:T(8,128)(2,1)} %copy-done, bf16[4,2,2,128,512]{4,3,2,1,0:T(8,128)(2,1)} %copy-done, ...), custom_call_target="tpu_custom_call" | custom-call | bytes 12582912 | tf_op jit(solution)/shard_map/pallas_call | solution.py:567
  77.3 2.3 %copy.24.refs_6_ = bf16[32,128,128]{2,1,0:T(8,128)(2,1)} copy(bf16[32,128,128]{1,2,0:T(8,128)(2,1)} %collective-permute-done.10) | data formatting | bytes 2097152 | tf_op jit(solution)/shard_map/ppermute | solution.py:443
  83.7 6.1 %shard_map.79.refs_0_ = bf16[512,128]{1,0:T(8,128)(2,1)} custom-call(s32[128]{0:T(128)} %reshape.472.block, f32[2,2,128,512]{3,2,1,0:T(8,128)} %get-tuple-element.67.picture.refs_19_, bf16[4,2,2,128,512]{4,3,2,1,0:T(8,128)(2,1)} %copy-done, bf16[4,2,2,128,512]{4,3,2,1,0:T(8,128)(2,1)} %copy-done, bf16[4,2,2,128,512]{4,3,2,1,0:T(8,128)(2,1)} %copy-done, ...), custom_call_target="tpu_custom_call" | custom-call | flops 1342177280 | bytes 14156288 | tf_op jit(solution)/shard_map/pallas_call | solution.py:567
  91.8 5.0 %collective-permute-done.13.refs_2_ = bf16[512,128]{1,0:T(8,128)(2,1)S(1)} collective-permute-done((bf16[512,128]{1,0:T(8,128)(2,1)}, bf16[512,128]{1,0:T(8,128)(2,1)S(1)}, u32[]{:S(2)}, u32[]{:S(2)}) %collective-permute-start.13) | collective-permute-done | bytes 131104 | tf_op jit(solution)/shard_map/ppermute | solution.py:443
  98.8 9.7 %shard_map.80 = (f32[2,2,128,512]{3,2,1,0:T(8,128)}, bf16[2,2,128,512]{3,2,1,0:T(8,128)(2,1)}, f32[8,128]{1,0:T(8,128)}, f32[8,128]{1,0:T(8,128)}, f32[512,128]{1,0:T(8,128)}) custom-call(s32[128]{0:T(128)} %reshape.472.block, bf16[512,128]{1,0:T(8,128)(2,1)} %shard_map.79.refs_0_, bf16[512,128]{1,0:T(8,128)(2,1)} %copy-done.14, ...), custom_call_target="tpu_custom_call" | custom-call | flops 1342177280 | bytes 16269824 | tf_op jit(solution)/shard_map/pallas_call | solution.py:567
  108.5 4.1 %collective-permute-done.20.refs_10_.refs_4_ = bf16[2,2,128,512]{3,2,1,0:T(8,128)(2,1)S(1)} collective-permute-done((bf16[2,2,128,512]{3,2,1,0:T(8,128)(2,1)S(1)}, bf16[2,2,128,512]{3,2,1,0:T(8,128)(2,1)S(1)}, u32[]{:S(2)}, u32[]{:S(2)}) %collective-permute-start.20) | collective-permute-done | bytes 524320 | tf_op jit(solution)/shard_map/ppermute | solution.py:443
  112.9 2.7 %collective-permute-start.28 = (bf16[2,2,128,512]{3,2,1,0:T(8,128)(2,1)}, bf16[2,2,128,512]{3,2,1,0:T(8,128)(2,1)S(1)}, u32[]{:S(2)}, u32[]{:S(2)}) collective-permute-start(bf16[2,2,128,512]{3,2,1,0:T(8,128)(2,1)} %get-tuple-element.105.refs_5_), channel_id=1, source_target_pairs={{0,8},{4,12},{8,0},{12,4},{1,9},{5,13},{9,1},{13,5},{2,10},{6,14},... | collective-permute-start | bytes 1572872 | tf_op jit(solution)/shard_map/ppermute | solution.py:443
  117.4 6.1 %shard_map.81.refs_0_ = bf16[512,128]{1,0:T(8,128)(2,1)} custom-call(s32[128]{0:T(128)} %reshape.472.block, f32[2,2,128,512]{3,2,1,0:T(8,128)} %get-tuple-element.85.picture.refs_16_, bf16[4,2,2,128,512]{4,3,2,1,0:T(8,128)(2,1)} %copy-done, bf16[4,2,2,128,512]{4,3,2,1,0:T(8,128)(2,1)} %copy-done, bf16[4,2,2,128,512]{4,3,2,1,0:T(8,128)(2,1)} %copy-done, ...), custom_call_target="tpu_custom_call" | custom-call | flops 1342177280 | bytes 14156288 | tf_op jit(solution)/shard_map/pallas_call | solution.py:567
  125.5 5.0 %collective-permute-done.22.refs_2_ = bf16[512,128]{1,0:T(8,128)(2,1)S(1)} collective-permute-done((bf16[512,128]{1,0:T(8,128)(2,1)}, bf16[512,128]{1,0:T(8,128)(2,1)S(1)}, u32[]{:S(2)}, u32[]{:S(2)}) %collective-permute-start.22) | collective-permute-done | bytes 131104 | tf_op jit(solution)/shard_map/ppermute | solution.py:443
  131.8 5.5 %collective-permute-done.27.refs_7_.refs_8_ = bf16[2,2,128,512]{3,2,1,0:T(8,128)(2,1)S(1)} collective-permute-done((bf16[2,2,128,512]{3,2,1,0:T(8,128)(2,1)}, bf16[2,2,128,512]{3,2,1,0:T(8,128)(2,1)S(1)}, u32[]{:S(2)}, u32[]{:S(2)}) %collective-permute-start.27) | collective-permute-done | bytes 524320 | tf_op jit(solution)/shard_map/ppermute | solution.py:443
  145.6 9.0 %shard_map.83.refs_6_ = bf16[2,2,128,512]{3,2,1,0:T(8,128)(2,1)} custom-call(s32[128]{0:T(128)} %reshape.472.block, bf16[512,128]{1,0:T(8,128)(2,1)} %shard_map.81.refs_0_, bf16[512,128]{1,0:T(8,128)(2,1)} %copy-done.8, bf16[512,128]{1,0:T(8,128)(2,1)} %copy-done.9, bf16[512,128]{1,0:T(8,128)(2,1)} %copy-done.10, bf16[32,128,128]{2,1,0:T(8,128)(2,1)} %bitcast.51, ...), custom_call_target="tpu_custom_call" | custom-call | flops 1342177280 | bytes 16257536 | tf_op jit(solution)/shard_map/pallas_call | solution.py:567
  158.9 8.2 %shard_map.84 = f32[8,2,128,512]{3,2,1,0:T(8,128)} custom-call(s32[8]{0:T(128)} %stack.95.order, f32[1,8,128]{2,1,0:T(8,128)} %bitcast.56, f32[1,8,128]{2,1,0:T(8,128)} %copy-done.17, f32[1,8,128]{2,1,0:T(8,128)} %copy-done.18, f32[1,8,128]{2,1,0:T(8,128)} %copy-done.19, bf16[2,2,128,512]{3,2,1,0:T(8,128)(2,1)} %get-tuple-element.104.refs_4_, ...), custom_call_target="tpu_custom_call" | custom-call | tf_op jit(solution)/shard_map/pallas_call | solution.py:710
  167.1 9.4 %collective-permute-done.33.refs_9_ = bf16[2,2,128,512]{3,2,1,0:T(8,128)(2,1)S(1)} collective-permute-done((bf16[2,2,128,512]{3,2,1,0:T(8,128)(2,1)}, bf16[2,2,128,512]{3,2,1,0:T(8,128)(2,1)S(1)}, u32[]{:S(2)}, u32[]{:S(2)}) %collective-permute-start.33) | collective-permute-done | bytes 524320 | tf_op jit(solution)/shard_map/ppermute | solution.py:443
  177.3 5.4 %shard_map.85.refs_7_ = f32[8,2,128,512]{3,2,1,0:T(8,128)} custom-call(s32[4]{0:T(128)} %pad_add_fusion.2.order, f32[1,8,128]{2,1,0:T(8,128)} %bitcast.57, f32[1,8,128]{2,1,0:T(8,128)} %copy-done.17, f32[1,8,128]{2,1,0:T(8,128)} %copy-done.18, f32[1,8,128]{2,1,0:T(8,128)} %copy-done.19, bf16[2,2,128,512]{3,2,1,0:T(8,128)(2,1)} %get-tuple-element.104.refs_4_, ...), custom_call_target="tpu_custom_call" | custom-call | tf_op jit(solution)/shard_map/pallas_call | solution.py:710
  184.2 3.3 %shard_map.86.refs_7_ = f32[8,2,128,512]{3,2,1,0:T(8,128)} custom-call(s32[2]{0:T(128)} %pad_add_fusion.4.order, f32[1,8,128]{2,1,0:T(8,128)} %bitcast.58, f32[1,8,128]{2,1,0:T(8,128)} %copy-done.17, f32[1,8,128]{2,1,0:T(8,128)} %copy-done.18, f32[1,8,128]{2,1,0:T(8,128)} %copy-done.19, ...), custom_call_target="tpu_custom_call", output_to_operand_aliasing={{}: (8, {})} | custom-call | tf_op jit(solution)/shard_map/pallas_call | solution.py:710
  187.5 8.2 %collective-permute-done.35.refs_6_ = bf16[2,2,128,512]{3,2,1,0:T(8,128)(2,1)S(1)} collective-permute-done((bf16[2,2,128,512]{3,2,1,0:T(8,128)(2,1)S(1)}, bf16[2,2,128,512]{3,2,1,0:T(8,128)(2,1)S(1)}, u32[]{:S(2)}, u32[]{:S(2)}) %collective-permute-start.35) | collective-permute-done | bytes 524320 | tf_op jit(solution)/shard_map/ppermute | solution.py:443
  196.5 3.3 %shard_map.87 = f32[8,2,128,512]{3,2,1,0:T(8,128)} custom-call(s32[2]{0:T(128)} %pad_add_fusion.3.order, f32[1,8,128]{2,1,0:T(8,128)} %bitcast.59, f32[1,8,128]{2,1,0:T(8,128)} %copy-done.17, f32[1,8,128]{2,1,0:T(8,128)} %copy-done.18, f32[1,8,128]{2,1,0:T(8,128)} %copy-done.19, bf16[2,2,128,512]{3,2,1,0:T(8,128)(2,1)} %copy-done.3, ...), custom_call_target="tpu_custom_call", output_to_operand_aliasing={{}: (8, {})} | custom-call | tf_op jit(solution)/shard_map/pallas_call | solution.py:710
  (167 shorter events, 56.5 us)
Async XLA Ops:
  2.3 39.4 %collective-permute-start.9 = (bf16[32,128,128]{1,2,0:T(8,128)(2,1)S(1)}, bf16[32,128,128]{1,2,0:T(8,128)(2,1)}, u32[]{:S(2)}, u32[]{:S(2)}) collective-permute-start(bf16[32,128,128]{1,2,0:T(8,128)(2,1)S(1)} %copy.20), channel_id=1, source_target_pairs={{0,1},{1,0},{2,3},{3,2},{4,5},{5,4},{6,7},{7,6},{8,9},{9,8},{10,11... | collective-permute-start | bytes 3145736 | tf_op jit(solution)/shard_map/ppermute | solution.py:443
  2.8 31.4 %collective-permute-start.10 = (bf16[32,128,128]{1,2,0:T(8,128)(2,1)S(1)}, bf16[32,128,128]{1,2,0:T(8,128)(2,1)}, u32[]{:S(2)}, u32[]{:S(2)}) collective-permute-start(bf16[32,128,128]{1,2,0:T(8,128)(2,1)S(1)} %copy.20), channel_id=1, source_target_pairs={{0,2},{1,3},{2,0},{3,1},{4,6},{5,7},{6,4},{7,5},{8,10},{9,11},{10,... | collective-permute-start | bytes 3145736 | tf_op jit(solution)/shard_map/ppermute | solution.py:443
  15.8 50.7 %all-to-all-start = ((bf16[4,2,2,128,512]{4,3,2,1,0:T(8,128)(2,1)}), bf16[4,2,2,128,512]{4,3,2,1,0:T(8,128)(2,1)S(1)}, u32[]{:S(2)}, u32[]{:S(2)}) async-start(bf16[4,2,2,128,512]{4,3,2,1,0:T(8,128)(2,1)} %bitcast.52), calls=%async_computation | async-start | bytes 4194304 | tf_op jit(solution)/shard_map/all_to_all | solution.py:482
  20.9 8.3 %collective-permute-start.7 = (s32[96]{0:T(128)S(1)}, s32[96]{0:T(128)S(1)}, u32[]{:S(2)}, u32[]{:S(2)}) collective-permute-start(s32[96]{0:T(128)S(1)} %pad_add_fusion.1), channel_id=1, source_target_pairs={{0,2},{1,3},{2,0},{3,1},{4,6},{5,7},{6,4},{7,5},{8,10},{9,11},{10,... | collective-permute-start | bytes 1160 | tf_op jit(solution)/shard_map/ppermute | solution.py:443
  21.4 9.6 %collective-permute-start.6 = (s32[96]{0:T(128)S(1)}, s32[96]{0:T(128)S(1)}, u32[]{:S(2)}, u32[]{:S(2)}) collective-permute-start(s32[96]{0:T(128)S(1)} %pad_add_fusion.1), channel_id=1, source_target_pairs={{0,1},{1,0},{2,3},{3,2},{4,5},{5,4},{6,7},{7,6},{8,9},{9,8},{10,11... | collective-permute-start | bytes 1160 | tf_op jit(solution)/shard_map/ppermute | solution.py:443
  29.3 9.5 %collective-permute-start.4 = (bf16[8,16,128]{2,1,0:T(8,128)(2,1)S(1)}, bf16[8,16,128]{2,1,0:T(8,128)(2,1)S(1)}, u32[]{:S(2)}, u32[]{:S(2)}) collective-permute-start(bf16[8,16,128]{2,1,0:T(8,128)(2,1)S(1)} %fusion.14), channel_id=1, source_target_pairs={{0,2},{1,3},{2,0},{3,1},{4,6},{5,7},{6,4},{7,5},{8,10},{9,11},{10,... | collective-permute-start | bytes 98312 | tf_op jit(solution)/shard_map/ppermute | solution.py:443
  31.1 9.9 %collective-permute-start.3 = (bf16[8,16,128]{2,1,0:T(8,128)(2,1)S(1)}, bf16[8,16,128]{2,1,0:T(8,128)(2,1)S(1)}, u32[]{:S(2)}, u32[]{:S(2)}) collective-permute-start(bf16[8,16,128]{2,1,0:T(8,128)(2,1)S(1)} %fusion.14), channel_id=1, source_target_pairs={{0,1},{1,0},{2,3},{3,2},{4,5},{5,4},{6,7},{7,6},{8,9},{9,8},{10,11... | collective-permute-start | bytes 98312 | tf_op jit(solution)/shard_map/ppermute | solution.py:443
  73.0 25.2 %collective-permute-start.18 = (bf16[2,2,128,512]{3,2,1,0:T(8,128)(2,1)}, bf16[2,2,128,512]{3,2,1,0:T(8,128)(2,1)S(1)}, u32[]{:S(2)}, u32[]{:S(2)}) collective-permute-start(bf16[2,2,128,512]{3,2,1,0:T(8,128)(2,1)} %get-tuple-element.104.refs_4_), channel_id=1, source_target_pairs={{0,4},{4,0},{8,12},{12,8},{1,5},{5,1},{9,13},{13,9},{2,6},{6,2},{1... | collective-permute-start | bytes 1572872 | tf_op jit(solution)/shard_map/ppermute | solution.py:443
  73.0 25.3 %collective-permute-start.19 = (bf16[2,2,128,512]{3,2,1,0:T(8,128)(2,1)}, bf16[2,2,128,512]{3,2,1,0:T(8,128)(2,1)S(1)}, u32[]{:S(2)}, u32[]{:S(2)}) collective-permute-start(bf16[2,2,128,512]{3,2,1,0:T(8,128)(2,1)} %get-tuple-element.104.refs_4_), channel_id=1, source_target_pairs={{0,8},{4,12},{8,0},{12,4},{1,9},{5,13},{9,1},{13,5},{2,10},{6,14},... | collective-permute-start | bytes 1572872 | tf_op jit(solution)/shard_map/ppermute | solution.py:443
  81.9 8.4 %collective-permute-start.16 = (f32[8,128]{1,0:T(8,128)S(1)}, f32[8,128]{1,0:T(8,128)S(1)}, u32[]{:S(2)}, u32[]{:S(2)}) collective-permute-start(f32[8,128]{1,0:T(8,128)S(1)} %copy-done.23), channel_id=1, source_target_pairs={{0,2},{1,3},{2,0},{3,1},{4,6},{5,7},{6,4},{7,5},{8,10},{9,11},{10,... | collective-permute-start | bytes 12296 | tf_op jit(solution)/shard_map/ppermute | solution.py:443
  82.4 8.4 %collective-permute-start.17 = (f32[8,128]{1,0:T(8,128)S(1)}, f32[8,128]{1,0:T(8,128)S(1)}, u32[]{:S(2)}, u32[]{:S(2)}) collective-permute-start(f32[8,128]{1,0:T(8,128)S(1)} %copy-done.23), channel_id=1, source_target_pairs={{0,3},{1,2},{2,1},{3,0},{4,7},{5,6},{6,5},{7,4},{8,11},{9,10},{10,... | collective-permute-start | bytes 12296 | tf_op jit(solution)/shard_map/ppermute | solution.py:443
  98.4 14.3 %collective-permute-start.20 = (bf16[2,2,128,512]{3,2,1,0:T(8,128)(2,1)S(1)}, bf16[2,2,128,512]{3,2,1,0:T(8,128)(2,1)S(1)}, u32[]{:S(2)}, u32[]{:S(2)}) collective-permute-start(bf16[2,2,128,512]{3,2,1,0:T(8,128)(2,1)S(1)} %collective-permute-done.19.refs_8_.refs_4_), channel_id=1, source_target_pairs={{0,4},{4,0},{8,12},{12,8},{1,5},{5,1},{9,13},{13,9},{2,6},{6,2},{1... | collective-permute-start | bytes 1572872 | tf_op jit(solution)/shard_map/ppermute | solution.py:443
  112.6 24.7 %collective-permute-start.27 = (bf16[2,2,128,512]{3,2,1,0:T(8,128)(2,1)}, bf16[2,2,128,512]{3,2,1,0:T(8,128)(2,1)S(1)}, u32[]{:S(2)}, u32[]{:S(2)}) collective-permute-start(bf16[2,2,128,512]{3,2,1,0:T(8,128)(2,1)} %get-tuple-element.105.refs_5_), channel_id=1, source_target_pairs={{0,4},{4,0},{8,12},{12,8},{1,5},{5,1},{9,13},{13,9},{2,6},{6,2},{1... | collective-permute-start | bytes 1572872 | tf_op jit(solution)/shard_map/ppermute | solution.py:443
  112.9 25.8 %collective-permute-start.28 = (bf16[2,2,128,512]{3,2,1,0:T(8,128)(2,1)}, bf16[2,2,128,512]{3,2,1,0:T(8,128)(2,1)S(1)}, u32[]{:S(2)}, u32[]{:S(2)}) collective-permute-start(bf16[2,2,128,512]{3,2,1,0:T(8,128)(2,1)} %get-tuple-element.105.refs_5_), channel_id=1, source_target_pairs={{0,8},{4,12},{8,0},{12,4},{1,9},{5,13},{9,1},{13,5},{2,10},{6,14},... | collective-permute-start | bytes 1572872 | tf_op jit(solution)/shard_map/ppermute | solution.py:443
  115.5 8.0 %collective-permute-start.24 = (f32[8,128]{1,0:T(8,128)}, f32[8,128]{1,0:T(8,128)S(1)}, u32[]{:S(2)}, u32[]{:S(2)}) collective-permute-start(f32[8,128]{1,0:T(8,128)} %get-tuple-element.92.refs_4_), channel_id=1, source_target_pairs={{0,1},{1,0},{2,3},{3,2},{4,5},{5,4},{6,7},{7,6},{8,9},{9,8},{10,11... | collective-permute-start | bytes 12296 | tf_op jit(solution)/shard_map/ppermute | solution.py:443
  115.5 8.4 %collective-permute-start.25 = (f32[8,128]{1,0:T(8,128)}, f32[8,128]{1,0:T(8,128)S(1)}, u32[]{:S(2)}, u32[]{:S(2)}) collective-permute-start(f32[8,128]{1,0:T(8,128)} %get-tuple-element.92.refs_4_), channel_id=1, source_target_pairs={{0,2},{1,3},{2,0},{3,1},{4,6},{5,7},{6,4},{7,5},{8,10},{9,11},{10,... | collective-permute-start | bytes 12296 | tf_op jit(solution)/shard_map/ppermute | solution.py:443
  116.1 8.4 %collective-permute-start.26 = (f32[8,128]{1,0:T(8,128)}, f32[8,128]{1,0:T(8,128)S(1)}, u32[]{:S(2)}, u32[]{:S(2)}) collective-permute-start(f32[8,128]{1,0:T(8,128)} %get-tuple-element.92.refs_4_), channel_id=1, source_target_pairs={{0,3},{1,2},{2,1},{3,0},{4,7},{5,6},{6,5},{7,4},{8,11},{9,10},{10,... | collective-permute-start | bytes 12296 | tf_op jit(solution)/shard_map/ppermute | solution.py:443
  138.7 16.0 %collective-permute-start.32 = (bf16[2,2,128,512]{3,2,1,0:T(8,128)(2,1)S(1)}, bf16[2,2,128,512]{3,2,1,0:T(8,128)(2,1)S(1)}, u32[]{:S(2)}, u32[]{:S(2)}) collective-permute-start(bf16[2,2,128,512]{3,2,1,0:T(8,128)(2,1)S(1)} %collective-permute-done.28.refs_9_.refs_5_), channel_id=1, source_target_pairs={{0,4},{4,0},{8,12},{12,8},{1,5},{5,1},{9,13},{13,9},{2,6},{6,2},{1... | collective-permute-start | bytes 1572872 | tf_op jit(solution)/shard_map/ppermute | solution.py:443
  141.2 13.4 %collective-permute-start.29 = (f32[1,8,128]{2,1,0:T(8,128)}, f32[1,8,128]{2,1,0:T(8,128)S(1)}, u32[]{:S(2)}, u32[]{:S(2)}) collective-permute-start(f32[1,8,128]{2,1,0:T(8,128)} %bitcast.53), channel_id=1, source_target_pairs={{0,4},{4,0},{8,12},{12,8},{1,5},{5,1},{9,13},{13,9},{2,6},{6,2},{1... | collective-permute-start | bytes 12296 | tf_op jit(solution)/shard_map/ppermute | solution.py:443
  142.8 11.8 %collective-permute-start.30 = (f32[1,8,128]{2,1,0:T(8,128)}, f32[1,8,128]{2,1,0:T(8,128)S(1)}, u32[]{:S(2)}, u32[]{:S(2)}) collective-permute-start(f32[1,8,128]{2,1,0:T(8,128)} %bitcast.54), channel_id=1, source_target_pairs={{0,8},{4,12},{8,0},{12,4},{1,9},{5,13},{9,1},{13,5},{2,10},{6,14},... | collective-permute-start | bytes 12296 | tf_op jit(solution)/shard_map/ppermute | solution.py:443
  144.0 10.7 %collective-permute-start.31 = (f32[1,8,128]{2,1,0:T(8,128)}, f32[1,8,128]{2,1,0:T(8,128)S(1)}, u32[]{:S(2)}, u32[]{:S(2)}) collective-permute-start(f32[1,8,128]{2,1,0:T(8,128)} %bitcast.55), channel_id=1, source_target_pairs={{0,12},{4,8},{8,4},{12,0},{1,13},{5,9},{9,5},{13,1},{2,14},{6,10},... | collective-permute-start | bytes 12296 | tf_op jit(solution)/shard_map/ppermute | solution.py:443
  154.7 21.9 %collective-permute-start.33 = (bf16[2,2,128,512]{3,2,1,0:T(8,128)(2,1)}, bf16[2,2,128,512]{3,2,1,0:T(8,128)(2,1)S(1)}, u32[]{:S(2)}, u32[]{:S(2)}) collective-permute-start(bf16[2,2,128,512]{3,2,1,0:T(8,128)(2,1)} %shard_map.83.refs_6_), channel_id=1, source_target_pairs={{0,4},{4,0},{8,12},{12,8},{1,5},{5,1},{9,13},{13,9},{2,6},{6,2},{1... | collective-permute-start | bytes 1572872 | tf_op jit(solution)/shard_map/ppermute | solution.py:443
  155.5 27.3 %collective-permute-start.34 = (bf16[2,2,128,512]{3,2,1,0:T(8,128)(2,1)}, bf16[2,2,128,512]{3,2,1,0:T(8,128)(2,1)S(1)}, u32[]{:S(2)}, u32[]{:S(2)}) collective-permute-start(bf16[2,2,128,512]{3,2,1,0:T(8,128)(2,1)} %shard_map.83.refs_6_), channel_id=1, source_target_pairs={{0,8},{4,12},{8,0},{12,4},{1,9},{5,13},{9,1},{13,5},{2,10},{6,14},... | collective-permute-start | bytes 1572872 | tf_op jit(solution)/shard_map/ppermute | solution.py:443
  182.8 12.9 %collective-permute-start.35 = (bf16[2,2,128,512]{3,2,1,0:T(8,128)(2,1)S(1)}, bf16[2,2,128,512]{3,2,1,0:T(8,128)(2,1)S(1)}, u32[]{:S(2)}, u32[]{:S(2)}) collective-permute-start(bf16[2,2,128,512]{3,2,1,0:T(8,128)(2,1)S(1)} %collective-permute-done.34.refs_6_), channel_id=1, source_target_pairs={{0,4},{4,0},{8,12},{12,8},{1,5},{5,1},{9,13},{13,9},{2,6},{6,2},{1... | collective-permute-start | bytes 1572872 | tf_op jit(solution)/shard_map/ppermute | solution.py:443
  (40 other events, 300.1 us)

commit v9 on v8

--- a/solution.py
+++ b/solution.py
@@ -122,8 +122,20 @@
     lax.fori_loop(0, count // 4, one, 0, unroll=True)
 
 
-def sample_tiles(block_ref, weights, grid_ref, sums_ref, out_ref):
-    count = weights[0].shape[0]
+def weight_copies(weights, held, sems):
+    return [
+        pltpu.make_async_copy(ref, held.at[place], sems.at[place])
+        for place, ref in enumerate(weights)
+    ]
+
+
+def start_copies(copies):
+    for copy in copies:
+        copy.start()
+
+
+def sample_tiles(block_ref, copies, weights, grid_ref, sums_ref, out_ref):
+    count = weights.shape[1]
     channels = sums_ref.shape[1]
     sums_ref[...] = jnp.zeros_like(sums_ref)
 
@@ -132,12 +144,13 @@
         high = value.astype(bf16).astype(f32)
         return jnp.concatenate([high, value - high], 0).astype(bf16)
 
-    for group, weights_ref in enumerate(weights):
+    for group, copy in enumerate(copies):
+        copy.wait()
 
         def four(places):
             tiles = [group * count + place for place in places]
             products = tile_products(
-                [left_of(tile) for tile in tiles], [weights_ref[place] for place in places]
+                [left_of(tile) for tile in tiles], [weights[group, place] for place in places]
             )
             for tile, product in zip(tiles, products):
                 sums_ref[block_ref[tile]] += product[:channels] + product[channels:]
@@ -146,17 +159,18 @@
     out_ref[...] = sums_ref[...].reshape(out_ref.shape).astype(bf16)
 
 
-def spread_tiles(block_ref, weights, parts_ref, grid_ref):
-    count = weights[0].shape[0]
-    channels = grid_ref.shape[0] // (count * len(weights))
-
-    for group, weights_ref in enumerate(weights):
+def spread_tiles(block_ref, copies, weights, parts_ref, grid_ref):
+    count = weights.shape[1]
+    channels = grid_ref.shape[0] // (count * len(copies))
+
+    for group, copy in enumerate(copies):
+        copy.wait()
 
         def four(places):
             tiles = [group * count + place for place in places]
             products = tile_products(
                 [parts_ref[block_ref[tile]] for tile in tiles],
-                [weights_ref[place] for place in places],
+                [weights[group, place] for place in places],
             )
             for tile, product in zip(tiles, products):
                 if product.shape[0] > channels:
@@ -210,13 +224,15 @@
 
 
 def measured_kernel(block, samples, *refs):
-    *weights, mx, eb, turn, images, grid = refs
+    *weights, mx, eb, turn, images, grid, held, sems = refs
     plane = pl.program_id(0)
     coils = images.shape[0]
 
     @pl.when(plane == 0)
     def _():
-        spread_tiles(block, weights, samples, grid)
+        copies = weight_copies(weights, held, sems)
+        start_copies(copies)
+        spread_tiles(block, copies, held, samples, grid)
 
     found = adjoint_images(coils, plane, pl.num_programs(0), eb, mx, turn, grid)
     for coil, (real, imag) in enumerate(found):
@@ -250,13 +266,18 @@
 
 def forward_kernel(coils, block, picture, *refs):
     sens = refs[:coils]
-    *weights, ey, mx, turn, samples, grid, sums = refs[coils:]
+    *weights, ey, mx, turn, samples, grid, sums, held, sems = refs[coils:]
     plane = pl.program_id(0)
+
+    @pl.when(plane == 0)
+    def _():
+        start_copies(weight_copies(weights, held, sems))
+
     forward_images(plane, pl.num_programs(0), picture, sens, ey, mx, turn, grid)
 
     @pl.when(plane == pl.num_programs(0) - 1)
     def _():
-        sample_tiles(block, weights, grid, sums, samples)
+        sample_tiles(block, weight_copies(weights, held, sems), held, grid, sums, samples)
 
 
 def summed_parts(samples, parts):
@@ -275,18 +296,20 @@
 def first_kernel(peers, coils, block, *refs):
     samples, weights, sens = refs[:peers], refs[peers : 2 * peers], refs[2 * peers :][:coils]
     mx, eb, turn, *norms = refs[2 * peers + coils :][: 3 + peers]
-    right_side, residual, rounded, facts, dots, total_samples, grid, parts = refs[-8:]
+    right_side, residual, rounded, facts, dots, total_samples, grid, parts, held, sems = refs[-10:]
     plane = pl.program_id(0)
 
     @pl.when(plane == 0)
     def _():
+        copies = weight_copies(weights, held, sems)
+        start_copies(copies)
         summed = summed_parts(samples, parts)
         total_samples[...] = summed
         rows = lax.broadcasted_iota(jnp.int32, facts.shape, 0)
         norm = tree_sum([part[...] for part in norms])
         facts[...] = jnp.where(rows == 1, jnp.sum(summed * summed), norm)
         dots[...] = jnp.zeros_like(dots)
-        spread_tiles(block, weights, parts, grid)
+        spread_tiles(block, copies, held, parts, grid)
 
     images = adjoint_images(coils, plane, pl.num_programs(0), eb, mx, turn, grid)
     total = combine(images, sens)
@@ -301,13 +324,15 @@
 
 def second_kernel(peers, coils, block, *refs):
     samples, weights, sens = refs[:peers], refs[peers : 2 * peers], refs[2 * peers :][:coils]
-    mx, eb, turn, facts, residual, rounded, grid, parts = refs[2 * peers + coils :]
+    mx, eb, turn, facts, residual, rounded, grid, parts, held, sems = refs[2 * peers + coils :]
     plane = pl.program_id(0)
 
     @pl.when(plane == 0)
     def _():
+        copies = weight_copies(weights, held, sems)
+        start_copies(copies)
         summed_parts(samples, parts)
-        spread_tiles(block, weights, parts, grid)
+        spread_tiles(block, copies, held, parts, grid)
 
     images = adjoint_images(coils, plane, pl.num_programs(0), eb, mx, turn, grid)
     total = combine(images, sens)
@@ -546,8 +571,8 @@
             [jnp.concatenate([cos_x, -sin_x], 1), jnp.concatenate([sin_x, cos_x], 1)], 0
         )
         mx, mx_back = mx.astype(bf16), table_parts(mx, 1)
-        measured, ey, mx, turn, block_of = lax.optimization_barrier(
-            (measured, ey, mx, turn, block_of)
+        measured, ey, mx, turn, block_of, all_weights = lax.optimization_barrier(
+            (measured, ey, mx, turn, block_of, all_weights)
         )
         places_spec = pl.BlockSpec(memory_space=pltpu.SMEM)
         plane_spec = pl.BlockSpec((1, 2, rows, columns), lambda p: (p, 0, 0, 0))
@@ -558,6 +583,11 @@
         grid_scratch = pltpu.VMEM((tiles * group_channels, size), f32)
         params = pltpu.CompilerParams(vmem_limit_bytes=vmem_limit)
         tail_tables = [mx_back, eb, turn_back]
+        weights_specs = [pl.BlockSpec(memory_space=pl.ANY)] * peers
+        held_weights = [
+            pltpu.VMEM((peers,) + weights.shape, bf16),
+            pltpu.SemaphoreType.DMA((peers,)),
+        ]
 
         def shaped(shape, dtype=f32):
             return jax.ShapeDtypeStruct(shape, dtype)
@@ -586,10 +616,12 @@
                 measured_kernel,
                 (own_planes,),
                 inputs,
-                [places_spec] + [whole_block(i) for i in inputs[1:]],
+                [places_spec, whole_block(measured)]
+                + weights_specs
+                + [whole_block(i) for i in tail_tables],
                 shaped(shape),
                 pl.BlockSpec((coil_count, 1, 2, rows, columns), lambda p: (0, p, 0, 0, 0)),
-                [pltpu.VMEM((tiles * channels, size), f32)],
+                [pltpu.VMEM((tiles * channels, size), f32)] + held_weights,
                 images_count,
             )
 
@@ -620,34 +652,37 @@
             )
 
         def forward(picture, g):
-            tail = [*all_weights, ey, mx, turn]
+            tail = [ey, mx, turn]
             out = shaped((blocks * group_channels, size), bf16)
             return call(
                 functools.partial(forward_kernel, coil_count),
                 (group_planes,),
-                [block_of, picture] + [sens[g]] * coil_count + tail,
-                [places_spec, plane_spec] + sens_specs + [whole_block(i) for i in tail],
+                [block_of, picture] + [sens[g]] * coil_count + [*all_weights, *tail],
+                [places_spec, plane_spec]
+                + sens_specs
+                + weights_specs
+                + [whole_block(i) for i in tail],
                 out,
                 whole_block(out),
-                [grid_scratch, pltpu.VMEM((blocks, group_channels, size), f32)],
+                [grid_scratch, pltpu.VMEM((blocks, group_channels, size), f32)] + held_weights,
                 group_images,
             )
 
         def back(kernel, samples, tables, vectors, g, outs, out_specs):
-            inputs = [*samples, *turned_weights]
             tables = tail_tables + tables
             return call(
                 functools.partial(kernel, peers, coil_count),
                 (group_planes,),
-                [block_of, *inputs] + [sens[g]] * coil_count + tables + vectors,
+                [block_of, *samples, *turned_weights] + [sens[g]] * coil_count + tables + vectors,
                 [places_spec]
-                + [whole_block(i) for i in inputs]
+                + [whole_block(i) for i in samples]
+                + weights_specs
                 + sens_specs
                 + [whole_block(i) for i in tables]
                 + [plane_spec] * len(vectors),
                 outs,
                 out_specs,
-                [grid_scratch, pltpu.VMEM((blocks, 2 * group_channels, size), bf16)],
+                [grid_scratch, pltpu.VMEM((blocks, 2 * group_channels, size), bf16)] + held_weights,
                 group_images,
             )
 
@@ -855,7 +890,8 @@
     for g in groups:
         right_side, start_own, norm = start(images, g)
         start_sent = sent_by_bits(start_own)
-        samples = exchanged(forward(right_side, g))
+        samples, norm = lax.optimization_barrier((forward(right_side, g), norm))
+        samples = exchanged(samples)
         norms = exchanged(norm)
         samples, norms, start_sent = lax.optimization_barrier((samples, norms, start_sent))
         residual, residual_own, facts, dots, start_total = first(samples, norms, right_side, g)
@@ -885,7 +921,7 @@
         for own, sent in zip(mixed_own, mixed_sent)
     ]
     out = assembled(others, [start_pieces, residual_pieces, early], range(2))
-    picture, out, mixed_sent = lax.optimization_barrier((picture, out, mixed_sent))
+    picture, mixed_sent = lax.optimization_barrier((picture, mixed_sent))
     mixed_pieces = [completed(own, sent) for own, sent in zip(mixed_own, mixed_sent)]
     vectors = [start_pieces, residual_pieces, mixed_pieces]
     late = coil_count - 1

time: 201 us -> 196 us (0.975)
  waiting for transfers between devices: 68.6 us -> 66.1 us
    optimization_barrier x0 -> x3, local copies, waits for them, and re-layouts: none -> 6.82 us  [on_device(): lax.optimization_barrier((measured, ey, mx, turn, block_of, all_weights))]
    ppermute x3 -> x0, local copies, waits for them, and re-layouts: 6.82 us -> none  [swapped(): lax.ppermute(array, axis, [(i, i ^ k) for i in range(lax.axis_size(axis))])]
  transfers between devices with their start and end apart: 37 -> 37, of which waited for: 13 -> 14; matrix products, arithmetic and copies ran while one was open for 12% -> 12% of each run, Pallas kernels for 29% -> 30%
where the time goes in v9:
time: 196 us; the launch traced here: 195 us
  Pallas kernels  66.5 us (34%)
  waiting for transfers between devices  66.1 us (34%)
  starting transfers between devices  33.3 us (17%)
  local copies, waits for them, and re-layouts  17.6 us (9%)
  other arithmetic  10.6 us (5%)
    ppermute x36, waiting for transfers between devices, swapped(): lax.ppermute(array, axis, [(i, i ^ k) for i in range(lax.axis_size(axis))])  49.7 us
    pallas_call x6, Pallas kernels, call(): pl.pallas_call(kernel, grid=grid, in_specs=specs, out_specs=out_specs, ou...  44.1 us
    ppermute x36, starting transfers between devices, swapped(): lax.ppermute(array, axis, [(i, i ^ k) for i in range(lax.axis_size(axis))])  29.7 us
    pallas_call x4, Pallas kernels, assembled(): pl.pallas_call(kernel, grid_spec=pltpu.PrefetchScalarGridSpec(num_scalar_...  20.3 us
    all_to_all x1, waiting for transfers between devices, on_device(): lax.all_to_all(sens_source[:, g * group_planes:(g + 1) * group_planes], '...  16.4 us
    optimization_barrier x3, local copies, waits for them, and re-layouts, on_device(): lax.optimization_barrier((measured, ey, mx, turn, block_of, all_weights))  6.82 us
  transfers between devices with their start and end apart: 37, of which 14 were waited for; matrix products, arithmetic and copies ran while one was open for 12% of the time, Pallas kernels for 30%

profile of v9, /device:TPU:0, one launch (start us, length us, event | category | flops | bytes accessed | tf_op | source)
XLA Modules:
  0.0 195.3 jit_solution(12948419580501002762)
XLA Ops:
  2.8 2.6 %collective-permute-start.10 = (bf16[32,128,128]{1,2,0:T(8,128)(2,1)S(1)}, bf16[32,128,128]{1,2,0:T(8,128)(2,1)}, u32[]{:S(2)}, u32[]{:S(2)}) collective-permute-start(bf16[32,128,128]{1,2,0:T(8,128)(2,1)S(1)} %copy.20), channel_id=1, source_target_pairs={{0,2},{1,3},{2,0},{3,1},{4,6},{5,7},{6,4},{7,5},{8,10},{9,11},{10,... | collective-permute-start | bytes 3145736 | tf_op jit(solution)/shard_map/ppermute | solution.py:468
  7.8 2.6 %collective-permute-start.1 = (bf16[2,2,1024]{2,1,0:T(2,128)(2,1)S(1)}, bf16[2,2,1024]{2,1,0:T(2,128)(2,1)S(1)}, u32[]{:S(2)}, u32[]{:S(2)}) collective-permute-start(bf16[2,2,1024]{2,1,0:T(2,128)(2,1)S(1)} %get-tuple-element.135), channel_id=1, source_target_pairs={{0,8},{4,12},{8,0},{12,4},{1,9},{5,13},{9,1},{13,5},{2,10},{6,14},... | collective-permute-start | bytes 24584 | tf_op jit(solution)/shard_map/ppermute | solution.py:468
  12.7 3.1 %collective-permute-done.2 = bf16[2,2,1024]{2,1,0:T(2,128)(2,1)S(1)} collective-permute-done((bf16[2,2,1024]{2,1,0:T(2,128)(2,1)S(1)}, bf16[2,2,1024]{2,1,0:T(2,128)(2,1)S(1)}, u32[]{:S(2)}, u32[]{:S(2)}) %collective-permute-start.2) | collective-permute-done | bytes 8224 | tf_op jit(solution)/shard_map/ppermute | solution.py:468
  15.8 3.6 %all-to-all-start = ((bf16[4,2,2,128,512]{4,3,2,1,0:T(8,128)(2,1)}), bf16[4,2,2,128,512]{4,3,2,1,0:T(8,128)(2,1)S(1)}, u32[]{:S(2)}, u32[]{:S(2)}) async-start(bf16[4,2,2,128,512]{4,3,2,1,0:T(8,128)(2,1)} %bitcast.52), calls=%async_computation | async-start | bytes 4194304 | tf_op jit(solution)/shard_map/all_to_all | solution.py:507
  22.2 7.1 %collective-permute-done.7 = s32[96]{0:T(128)S(1)} collective-permute-done((s32[96]{0:T(128)S(1)}, s32[96]{0:T(128)S(1)}, u32[]{:S(2)}, u32[]{:S(2)}) %collective-permute-start.7) | collective-permute-done | bytes 416 | tf_op jit(solution)/shard_map/ppermute | solution.py:468
  41.7 8.4 %shard_map.77.images = f32[4,2,2,128,512]{4,3,2,1,0:T(8,128)} custom-call(s32[128]{0:T(128)} %reshape.473.block, bf16[32,16,128]{2,1,0:T(8,128)(2,1)} %pad_maximum_fusion.3.samples, bf16[32,128,128]{2,1,0:T(8,128)(2,1)} %bitcast.49, bf16[32,128,128]{2,1,0:T(8,128)(2,1)} %bitcast.27.refs_1_.refs_5_, bf16[32,128,128]{2,1,0:T(8,128)(2,1)} %bitcast.28.refs_2_.refs_6_, ...), custom_call_target="tpu_custom_call" | custom-call | flops 1342177280 | bytes 6423040 | tf_op jit(solution)/shard_map/pallas_call | solution.py:597
  50.1 16.4 %all-to-all-done.refs_0_.refs_1_.refs_2_.refs_3_.refs_8_.refs_9_.refs_10_.refs_11_ = bf16[4,2,2,128,512]{4,3,2,1,0:T(8,128)(2,1)S(1)} async-done(((bf16[4,2,2,128,512]{4,3,2,1,0:T(8,128)(2,1)}), bf16[4,2,2,128,512]{4,3,2,1,0:T(8,128)(2,1)S(1)}, u32[]{:S(2)}, u32[]{:S(2)}) %all-to-all-start) | async-done | bytes 2097184 | tf_op jit(solution)/shard_map/all_to_all | solution.py:507
  67.8 5.2 %shard_map.78 = (f32[2,2,128,512]{3,2,1,0:T(8,128)}, bf16[2,2,128,512]{3,2,1,0:T(8,128)(2,1)}, f32[8,128]{1,0:T(8,128)}) custom-call(f32[4,2,2,128,512]{4,3,2,1,0:T(8,128)} %shard_map.77.images, bf16[4,2,2,128,512]{4,3,2,1,0:T(8,128)(2,1)} %copy-done, bf16[4,2,2,128,512]{4,3,2,1,0:T(8,128)(2,1)} %copy-done, bf16[4,2,2,128,512]{4,3,2,1,0:T(8,128)(2,1)} %copy-done, ...), custom_call_target="tpu_custom_call" | custom-call | bytes 12582912 | tf_op jit(solution)/shard_map/pallas_call | solution.py:597
  75.1 2.3 %copy.23.refs_5_ = bf16[32,128,128]{2,1,0:T(8,128)(2,1)} copy(bf16[32,128,128]{1,2,0:T(8,128)(2,1)} %collective-permute-done.9) | data formatting | bytes 2097152 | tf_op jit(solution)/shard_map/optimization_barrier | solution.py:574
  77.3 2.3 %copy.24.refs_6_ = bf16[32,128,128]{2,1,0:T(8,128)(2,1)} copy(bf16[32,128,128]{1,2,0:T(8,128)(2,1)} %collective-permute-done.10) | data formatting | bytes 2097152 | tf_op jit(solution)/shard_map/optimization_barrier | solution.py:574
  79.6 2.3 %copy.25.refs_7_ = bf16[32,128,128]{2,1,0:T(8,128)(2,1)} copy(bf16[32,128,128]{1,2,0:T(8,128)(2,1)} %collective-permute-done.11) | data formatting | bytes 2097152 | tf_op jit(solution)/shard_map/optimization_barrier | solution.py:574
  81.9 5.5 %shard_map.79.refs_0_ = bf16[512,128]{1,0:T(8,128)(2,1)} custom-call(s32[128]{0:T(128)} %reshape.472.block, f32[2,2,128,512]{3,2,1,0:T(8,128)} %get-tuple-element.72.picture.refs_19_, bf16[4,2,2,128,512]{4,3,2,1,0:T(8,128)(2,1)} %copy-done, bf16[4,2,2,128,512]{4,3,2,1,0:T(8,128)(2,1)} %copy-done, bf16[4,2,2,128,512]{4,3,2,1,0:T(8,128)(2,1)} %copy-done, ...), custom_call_target="tpu_custom_call" | custom-call | flops 1342177280 | bytes 14156288 | tf_op jit(solution)/shard_map/pallas_call | solution.py:597
  92.7 5.1 %collective-permute-done.13.refs_2_ = bf16[512,128]{1,0:T(8,128)(2,1)S(1)} collective-permute-done((bf16[512,128]{1,0:T(8,128)(2,1)}, bf16[512,128]{1,0:T(8,128)(2,1)S(1)}, u32[]{:S(2)}, u32[]{:S(2)}) %collective-permute-start.13) | collective-permute-done | bytes 131104 | tf_op jit(solution)/shard_map/ppermute | solution.py:468
  98.5 10.2 %shard_map.80 = (f32[2,2,128,512]{3,2,1,0:T(8,128)}, bf16[2,2,128,512]{3,2,1,0:T(8,128)(2,1)}, f32[8,128]{1,0:T(8,128)}, f32[8,128]{1,0:T(8,128)}, f32[512,128]{1,0:T(8,128)}) custom-call(s32[128]{0:T(128)} %reshape.472.block, bf16[512,128]{1,0:T(8,128)(2,1)} %shard_map.79.refs_0_, bf16[512,128]{1,0:T(8,128)(2,1)} %copy-done.14, ...), custom_call_target="tpu_custom_call" | custom-call | flops 1342177280 | bytes 16269824 | tf_op jit(solution)/shard_map/pallas_call | solution.py:597
  108.6 4.2 %collective-permute-done.20.refs_10_.refs_4_ = bf16[2,2,128,512]{3,2,1,0:T(8,128)(2,1)S(1)} collective-permute-done((bf16[2,2,128,512]{3,2,1,0:T(8,128)(2,1)S(1)}, bf16[2,2,128,512]{3,2,1,0:T(8,128)(2,1)S(1)}, u32[]{:S(2)}, u32[]{:S(2)}) %collective-permute-start.20) | collective-permute-done | bytes 524320 | tf_op jit(solution)/shard_map/ppermute | solution.py:468
  117.2 5.4 %shard_map.81.refs_0_ = bf16[512,128]{1,0:T(8,128)(2,1)} custom-call(s32[128]{0:T(128)} %reshape.472.block, f32[2,2,128,512]{3,2,1,0:T(8,128)} %get-tuple-element.96.picture.refs_16_, bf16[4,2,2,128,512]{4,3,2,1,0:T(8,128)(2,1)} %copy-done, bf16[4,2,2,128,512]{4,3,2,1,0:T(8,128)(2,1)} %copy-done, bf16[4,2,2,128,512]{4,3,2,1,0:T(8,128)(2,1)} %copy-done, ...), custom_call_target="tpu_custom_call" | custom-call | flops 1342177280 | bytes 14156288 | tf_op jit(solution)/shard_map/pallas_call | solution.py:597
  124.6 5.0 %collective-permute-done.22.refs_2_ = bf16[512,128]{1,0:T(8,128)(2,1)S(1)} collective-permute-done((bf16[512,128]{1,0:T(8,128)(2,1)}, bf16[512,128]{1,0:T(8,128)(2,1)S(1)}, u32[]{:S(2)}, u32[]{:S(2)}) %collective-permute-start.22) | collective-permute-done | bytes 131104 | tf_op jit(solution)/shard_map/ppermute | solution.py:468
  131.0 6.3 %collective-permute-done.27.refs_7_.refs_8_ = bf16[2,2,128,512]{3,2,1,0:T(8,128)(2,1)S(1)} collective-permute-done((bf16[2,2,128,512]{3,2,1,0:T(8,128)(2,1)}, bf16[2,2,128,512]{3,2,1,0:T(8,128)(2,1)S(1)}, u32[]{:S(2)}, u32[]{:S(2)}) %collective-permute-start.27) | collective-permute-done | bytes 524320 | tf_op jit(solution)/shard_map/ppermute | solution.py:468
  145.8 9.5 %shard_map.83.refs_6_ = bf16[2,2,128,512]{3,2,1,0:T(8,128)(2,1)} custom-call(s32[128]{0:T(128)} %reshape.472.block, bf16[512,128]{1,0:T(8,128)(2,1)} %shard_map.81.refs_0_, bf16[512,128]{1,0:T(8,128)(2,1)} %copy-done.8, bf16[512,128]{1,0:T(8,128)(2,1)} %copy-done.9, bf16[512,128]{1,0:T(8,128)(2,1)} %copy-done.10, bf16[32,128,128]{2,1,0:T(8,128)(2,1)} %bitcast.51, ...), custom_call_target="tpu_custom_call" | custom-call | flops 1342177280 | bytes 16257536 | tf_op jit(solution)/shard_map/pallas_call | solution.py:597
  158.6 8.2 %shard_map.84 = f32[8,2,128,512]{3,2,1,0:T(8,128)} custom-call(s32[8]{0:T(128)} %stack.95.order, f32[1,8,128]{2,1,0:T(8,128)} %bitcast.56, f32[1,8,128]{2,1,0:T(8,128)} %copy-done.17, f32[1,8,128]{2,1,0:T(8,128)} %copy-done.18, f32[1,8,128]{2,1,0:T(8,128)} %copy-done.19, bf16[2,2,128,512]{3,2,1,0:T(8,128)(2,1)} %get-tuple-element.115.refs_4_, ...), custom_call_target="tpu_custom_call" | custom-call | tf_op jit(solution)/shard_map/pallas_call | solution.py:745
  166.9 10.9 %collective-permute-done.33.refs_9_ = bf16[2,2,128,512]{3,2,1,0:T(8,128)(2,1)S(1)} collective-permute-done((bf16[2,2,128,512]{3,2,1,0:T(8,128)(2,1)}, bf16[2,2,128,512]{3,2,1,0:T(8,128)(2,1)S(1)}, u32[]{:S(2)}, u32[]{:S(2)}) %collective-permute-start.33) | collective-permute-done | bytes 524320 | tf_op jit(solution)/shard_map/ppermute | solution.py:468
  182.0 5.4 %shard_map.85.refs_7_ = f32[8,2,128,512]{3,2,1,0:T(8,128)} custom-call(s32[4]{0:T(128)} %pad_add_fusion.4.order, f32[1,8,128]{2,1,0:T(8,128)} %bitcast.57, f32[1,8,128]{2,1,0:T(8,128)} %copy-done.17, f32[1,8,128]{2,1,0:T(8,128)} %copy-done.18, f32[1,8,128]{2,1,0:T(8,128)} %copy-done.19, bf16[2,2,128,512]{3,2,1,0:T(8,128)(2,1)} %get-tuple-element.115.refs_4_, ...), custom_call_target="tpu_custom_call" | custom-call | tf_op jit(solution)/shard_map/pallas_call | solution.py:745
  187.5 3.3 %shard_map.86.refs_7_ = f32[8,2,128,512]{3,2,1,0:T(8,128)} custom-call(s32[2]{0:T(128)} %pad_add_fusion.3.order, f32[1,8,128]{2,1,0:T(8,128)} %bitcast.58, f32[1,8,128]{2,1,0:T(8,128)} %copy-done.17, f32[1,8,128]{2,1,0:T(8,128)} %copy-done.18, f32[1,8,128]{2,1,0:T(8,128)} %copy-done.19, ...), custom_call_target="tpu_custom_call", output_to_operand_aliasing={{}: (8, {})} | custom-call | tf_op jit(solution)/shard_map/pallas_call | solution.py:745
  192.0 3.3 %shard_map.87 = f32[8,2,128,512]{3,2,1,0:T(8,128)} custom-call(s32[2]{0:T(128)} %pad_add_fusion.2.order, f32[1,8,128]{2,1,0:T(8,128)} %bitcast.59, f32[1,8,128]{2,1,0:T(8,128)} %copy-done.17, f32[1,8,128]{2,1,0:T(8,128)} %copy-done.18, f32[1,8,128]{2,1,0:T(8,128)} %copy-done.19, bf16[2,2,128,512]{3,2,1,0:T(8,128)(2,1)} %copy-done.3, ...), custom_call_target="tpu_custom_call", output_to_operand_aliasing={{}: (8, {})} | custom-call | tf_op jit(solution)/shard_map/pallas_call | solution.py:745
  (167 shorter events, 56.1 us)
Async XLA Ops:
  2.3 39.4 %collective-permute-start.9 = (bf16[32,128,128]{1,2,0:T(8,128)(2,1)S(1)}, bf16[32,128,128]{1,2,0:T(8,128)(2,1)}, u32[]{:S(2)}, u32[]{:S(2)}) collective-permute-start(bf16[32,128,128]{1,2,0:T(8,128)(2,1)S(1)} %copy.20), channel_id=1, source_target_pairs={{0,1},{1,0},{2,3},{3,2},{4,5},{5,4},{6,7},{7,6},{8,9},{9,8},{10,11... | collective-permute-start | bytes 3145736 | tf_op jit(solution)/shard_map/ppermute | solution.py:468
  2.8 31.4 %collective-permute-start.10 = (bf16[32,128,128]{1,2,0:T(8,128)(2,1)S(1)}, bf16[32,128,128]{1,2,0:T(8,128)(2,1)}, u32[]{:S(2)}, u32[]{:S(2)}) collective-permute-start(bf16[32,128,128]{1,2,0:T(8,128)(2,1)S(1)} %copy.20), channel_id=1, source_target_pairs={{0,2},{1,3},{2,0},{3,1},{4,6},{5,7},{6,4},{7,5},{8,10},{9,11},{10,... | collective-permute-start | bytes 3145736 | tf_op jit(solution)/shard_map/ppermute | solution.py:468
  15.8 50.7 %all-to-all-start = ((bf16[4,2,2,128,512]{4,3,2,1,0:T(8,128)(2,1)}), bf16[4,2,2,128,512]{4,3,2,1,0:T(8,128)(2,1)S(1)}, u32[]{:S(2)}, u32[]{:S(2)}) async-start(bf16[4,2,2,128,512]{4,3,2,1,0:T(8,128)(2,1)} %bitcast.52), calls=%async_computation | async-start | bytes 4194304 | tf_op jit(solution)/shard_map/all_to_all | solution.py:507
  20.9 8.3 %collective-permute-start.7 = (s32[96]{0:T(128)S(1)}, s32[96]{0:T(128)S(1)}, u32[]{:S(2)}, u32[]{:S(2)}) collective-permute-start(s32[96]{0:T(128)S(1)} %pad_add_fusion.1), channel_id=1, source_target_pairs={{0,2},{1,3},{2,0},{3,1},{4,6},{5,7},{6,4},{7,5},{8,10},{9,11},{10,... | collective-permute-start | bytes 1160 | tf_op jit(solution)/shard_map/ppermute | solution.py:468
  21.4 9.6 %collective-permute-start.6 = (s32[96]{0:T(128)S(1)}, s32[96]{0:T(128)S(1)}, u32[]{:S(2)}, u32[]{:S(2)}) collective-permute-start(s32[96]{0:T(128)S(1)} %pad_add_fusion.1), channel_id=1, source_target_pairs={{0,1},{1,0},{2,3},{3,2},{4,5},{5,4},{6,7},{7,6},{8,9},{9,8},{10,11... | collective-permute-start | bytes 1160 | tf_op jit(solution)/shard_map/ppermute | solution.py:468
  29.3 9.5 %collective-permute-start.4 = (bf16[8,16,128]{2,1,0:T(8,128)(2,1)S(1)}, bf16[8,16,128]{2,1,0:T(8,128)(2,1)S(1)}, u32[]{:S(2)}, u32[]{:S(2)}) collective-permute-start(bf16[8,16,128]{2,1,0:T(8,128)(2,1)S(1)} %fusion.14), channel_id=1, source_target_pairs={{0,2},{1,3},{2,0},{3,1},{4,6},{5,7},{6,4},{7,5},{8,10},{9,11},{10,... | collective-permute-start | bytes 98312 | tf_op jit(solution)/shard_map/ppermute | solution.py:468
  31.1 9.9 %collective-permute-start.3 = (bf16[8,16,128]{2,1,0:T(8,128)(2,1)S(1)}, bf16[8,16,128]{2,1,0:T(8,128)(2,1)S(1)}, u32[]{:S(2)}, u32[]{:S(2)}) collective-permute-start(bf16[8,16,128]{2,1,0:T(8,128)(2,1)S(1)} %fusion.14), channel_id=1, source_target_pairs={{0,1},{1,0},{2,3},{3,2},{4,5},{5,4},{6,7},{7,6},{8,9},{9,8},{10,11... | collective-permute-start | bytes 98312 | tf_op jit(solution)/shard_map/ppermute | solution.py:468
  34.2 7.5 %collective-permute-start.11 = (bf16[32,128,128]{1,2,0:T(8,128)(2,1)}, bf16[32,128,128]{1,2,0:T(8,128)(2,1)}, u32[]{:S(2)}, u32[]{:S(2)}) collective-permute-start(bf16[32,128,128]{1,2,0:T(8,128)(2,1)} %collective-permute-done.10), channel_id=1, source_target_pairs={{0,1},{1,0},{2,3},{3,2},{4,5},{5,4},{6,7},{7,6},{8,9},{9,8},{10,11... | collective-permute-start | bytes 3145736 | tf_op jit(solution)/shard_map/ppermute | solution.py:468
  73.0 24.8 %collective-permute-start.18 = (bf16[2,2,128,512]{3,2,1,0:T(8,128)(2,1)}, bf16[2,2,128,512]{3,2,1,0:T(8,128)(2,1)S(1)}, u32[]{:S(2)}, u32[]{:S(2)}) collective-permute-start(bf16[2,2,128,512]{3,2,1,0:T(8,128)(2,1)} %get-tuple-element.115.refs_4_), channel_id=1, source_target_pairs={{0,4},{4,0},{8,12},{12,8},{1,5},{5,1},{9,13},{13,9},{2,6},{6,2},{1... | collective-permute-start | bytes 1572872 | tf_op jit(solution)/shard_map/ppermute | solution.py:468
  73.1 25.3 %collective-permute-start.19 = (bf16[2,2,128,512]{3,2,1,0:T(8,128)(2,1)}, bf16[2,2,128,512]{3,2,1,0:T(8,128)(2,1)S(1)}, u32[]{:S(2)}, u32[]{:S(2)}) collective-permute-start(bf16[2,2,128,512]{3,2,1,0:T(8,128)(2,1)} %get-tuple-element.115.refs_4_), channel_id=1, source_target_pairs={{0,8},{4,12},{8,0},{12,4},{1,9},{5,13},{9,1},{13,5},{2,10},{6,14},... | collective-permute-start | bytes 1572872 | tf_op jit(solution)/shard_map/ppermute | solution.py:468
  98.4 14.5 %collective-permute-start.20 = (bf16[2,2,128,512]{3,2,1,0:T(8,128)(2,1)S(1)}, bf16[2,2,128,512]{3,2,1,0:T(8,128)(2,1)S(1)}, u32[]{:S(2)}, u32[]{:S(2)}) collective-permute-start(bf16[2,2,128,512]{3,2,1,0:T(8,128)(2,1)S(1)} %collective-permute-done.19.refs_8_.refs_4_), channel_id=1, source_target_pairs={{0,4},{4,0},{8,12},{12,8},{1,5},{5,1},{9,13},{13,9},{2,6},{6,2},{1... | collective-permute-start | bytes 1572872 | tf_op jit(solution)/shard_map/ppermute | solution.py:468
  112.9 24.4 %collective-permute-start.27 = (bf16[2,2,128,512]{3,2,1,0:T(8,128)(2,1)}, bf16[2,2,128,512]{3,2,1,0:T(8,128)(2,1)S(1)}, u32[]{:S(2)}, u32[]{:S(2)}) collective-permute-start(bf16[2,2,128,512]{3,2,1,0:T(8,128)(2,1)} %get-tuple-element.116.refs_5_), channel_id=1, source_target_pairs={{0,4},{4,0},{8,12},{12,8},{1,5},{5,1},{9,13},{13,9},{2,6},{6,2},{1... | collective-permute-start | bytes 1572872 | tf_op jit(solution)/shard_map/ppermute | solution.py:468
  113.2 26.0 %collective-permute-start.28 = (bf16[2,2,128,512]{3,2,1,0:T(8,128)(2,1)}, bf16[2,2,128,512]{3,2,1,0:T(8,128)(2,1)S(1)}, u32[]{:S(2)}, u32[]{:S(2)}) collective-permute-start(bf16[2,2,128,512]{3,2,1,0:T(8,128)(2,1)} %get-tuple-element.116.refs_5_), channel_id=1, source_target_pairs={{0,8},{4,12},{8,0},{12,4},{1,9},{5,13},{9,1},{13,5},{2,10},{6,14},... | collective-permute-start | bytes 1572872 | tf_op jit(solution)/shard_map/ppermute | solution.py:468
  115.3 7.3 %collective-permute-start.24 = (f32[8,128]{1,0:T(8,128)}, f32[8,128]{1,0:T(8,128)S(1)}, u32[]{:S(2)}, u32[]{:S(2)}) collective-permute-start(f32[8,128]{1,0:T(8,128)} %get-tuple-element.103.refs_4_), channel_id=1, source_target_pairs={{0,1},{1,0},{2,3},{3,2},{4,5},{5,4},{6,7},{7,6},{8,9},{9,8},{10,11... | collective-permute-start | bytes 12296 | tf_op jit(solution)/shard_map/ppermute | solution.py:468
  115.3 7.7 %collective-permute-start.25 = (f32[8,128]{1,0:T(8,128)}, f32[8,128]{1,0:T(8,128)S(1)}, u32[]{:S(2)}, u32[]{:S(2)}) collective-permute-start(f32[8,128]{1,0:T(8,128)} %get-tuple-element.103.refs_4_), channel_id=1, source_target_pairs={{0,2},{1,3},{2,0},{3,1},{4,6},{5,7},{6,4},{7,5},{8,10},{9,11},{10,... | collective-permute-start | bytes 12296 | tf_op jit(solution)/shard_map/ppermute | solution.py:468
  116.3 7.7 %collective-permute-start.26 = (f32[8,128]{1,0:T(8,128)}, f32[8,128]{1,0:T(8,128)S(1)}, u32[]{:S(2)}, u32[]{:S(2)}) collective-permute-start(f32[8,128]{1,0:T(8,128)} %get-tuple-element.103.refs_4_), channel_id=1, source_target_pairs={{0,3},{1,2},{2,1},{3,0},{4,7},{5,6},{6,5},{7,4},{8,11},{9,10},{10,... | collective-permute-start | bytes 12296 | tf_op jit(solution)/shard_map/ppermute | solution.py:468
  124.0 6.9 %collective-permute-start.23 = (bf16[512,128]{1,0:T(8,128)(2,1)}, bf16[512,128]{1,0:T(8,128)(2,1)S(1)}, u32[]{:S(2)}, u32[]{:S(2)}) collective-permute-start(bf16[512,128]{1,0:T(8,128)(2,1)} %shard_map.81.refs_0_), channel_id=1, source_target_pairs={{0,3},{1,2},{2,1},{3,0},{4,7},{5,6},{6,5},{7,4},{8,11},{9,10},{10,... | collective-permute-start | bytes 393224 | tf_op jit(solution)/shard_map/ppermute | solution.py:468
  139.2 16.2 %collective-permute-start.32 = (bf16[2,2,128,512]{3,2,1,0:T(8,128)(2,1)S(1)}, bf16[2,2,128,512]{3,2,1,0:T(8,128)(2,1)S(1)}, u32[]{:S(2)}, u32[]{:S(2)}) collective-permute-start(bf16[2,2,128,512]{3,2,1,0:T(8,128)(2,1)S(1)} %collective-permute-done.28.refs_9_.refs_5_), channel_id=1, source_target_pairs={{0,4},{4,0},{8,12},{12,8},{1,5},{5,1},{9,13},{13,9},{2,6},{6,2},{1... | collective-permute-start | bytes 1572872 | tf_op jit(solution)/shard_map/ppermute | solution.py:468
  141.4 13.9 %collective-permute-start.29 = (f32[1,8,128]{2,1,0:T(8,128)}, f32[1,8,128]{2,1,0:T(8,128)S(1)}, u32[]{:S(2)}, u32[]{:S(2)}) collective-permute-start(f32[1,8,128]{2,1,0:T(8,128)} %bitcast.53), channel_id=1, source_target_pairs={{0,4},{4,0},{8,12},{12,8},{1,5},{5,1},{9,13},{13,9},{2,6},{6,2},{1... | collective-permute-start | bytes 12296 | tf_op jit(solution)/shard_map/ppermute | solution.py:468
  143.3 12.0 %collective-permute-start.30 = (f32[1,8,128]{2,1,0:T(8,128)}, f32[1,8,128]{2,1,0:T(8,128)S(1)}, u32[]{:S(2)}, u32[]{:S(2)}) collective-permute-start(f32[1,8,128]{2,1,0:T(8,128)} %bitcast.54), channel_id=1, source_target_pairs={{0,8},{4,12},{8,0},{12,4},{1,9},{5,13},{9,1},{13,5},{2,10},{6,14},... | collective-permute-start | bytes 12296 | tf_op jit(solution)/shard_map/ppermute | solution.py:468
  143.9 11.5 %collective-permute-start.31 = (f32[1,8,128]{2,1,0:T(8,128)}, f32[1,8,128]{2,1,0:T(8,128)S(1)}, u32[]{:S(2)}, u32[]{:S(2)}) collective-permute-start(f32[1,8,128]{2,1,0:T(8,128)} %bitcast.55), channel_id=1, source_target_pairs={{0,12},{4,8},{8,4},{12,0},{1,13},{5,9},{9,5},{13,1},{2,14},{6,10},... | collective-permute-start | bytes 12296 | tf_op jit(solution)/shard_map/ppermute | solution.py:468
  155.4 22.4 %collective-permute-start.33 = (bf16[2,2,128,512]{3,2,1,0:T(8,128)(2,1)}, bf16[2,2,128,512]{3,2,1,0:T(8,128)(2,1)S(1)}, u32[]{:S(2)}, u32[]{:S(2)}) collective-permute-start(bf16[2,2,128,512]{3,2,1,0:T(8,128)(2,1)} %shard_map.83.refs_6_), channel_id=1, source_target_pairs={{0,4},{4,0},{8,12},{12,8},{1,5},{5,1},{9,13},{13,9},{2,6},{6,2},{1... | collective-permute-start | bytes 1572872 | tf_op jit(solution)/shard_map/ppermute | solution.py:468
  156.5 23.5 %collective-permute-start.34 = (bf16[2,2,128,512]{3,2,1,0:T(8,128)(2,1)}, bf16[2,2,128,512]{3,2,1,0:T(8,128)(2,1)S(1)}, u32[]{:S(2)}, u32[]{:S(2)}) collective-permute-start(bf16[2,2,128,512]{3,2,1,0:T(8,128)(2,1)} %shard_map.83.refs_6_), channel_id=1, source_target_pairs={{0,8},{4,12},{8,0},{12,4},{1,9},{5,13},{9,1},{13,5},{2,10},{6,14},... | collective-permute-start | bytes 1572872 | tf_op jit(solution)/shard_map/ppermute | solution.py:468
  180.0 11.2 %collective-permute-start.35 = (bf16[2,2,128,512]{3,2,1,0:T(8,128)(2,1)S(1)}, bf16[2,2,128,512]{3,2,1,0:T(8,128)(2,1)S(1)}, u32[]{:S(2)}, u32[]{:S(2)}) collective-permute-start(bf16[2,2,128,512]{3,2,1,0:T(8,128)(2,1)S(1)} %collective-permute-done.34.refs_6_), channel_id=1, source_target_pairs={{0,4},{4,0},{8,12},{12,8},{1,5},{5,1},{9,13},{13,9},{2,6},{6,2},{1... | collective-permute-start | bytes 1572872 | tf_op jit(solution)/shard_map/ppermute | solution.py:468
  (40 other events, 292.2 us)

commit v10 on v9

--- a/solution.py
+++ b/solution.py
@@ -159,19 +159,20 @@
     out_ref[...] = sums_ref[...].reshape(out_ref.shape).astype(bf16)
 
 
-def spread_tiles(block_ref, copies, weights, parts_ref, grid_ref):
-    count = weights.shape[1]
-    channels = grid_ref.shape[0] // (count * len(copies))
-
-    for group, copy in enumerate(copies):
-        copy.wait()
+def spread_tiles(block_ref, weights, parts_ref, grid_ref, turned_ref=None):
+    count = weights[0].shape[0]
+    channels = grid_ref.shape[0] // (count * len(weights))
+
+    for group, weights_ref in enumerate(weights):
 
         def four(places):
             tiles = [group * count + place for place in places]
-            products = tile_products(
-                [parts_ref[block_ref[tile]] for tile in tiles],
-                [weights[group, place] for place in places],
-            )
+            rights = [weights_ref[place] for place in places]
+            if turned_ref is not None:
+                rights = [right.astype(f32).T.astype(bf16) for right in rights]
+                for place, right in zip(places, rights):
+                    turned_ref[group, place] = right
+            products = tile_products([parts_ref[block_ref[tile]] for tile in tiles], rights)
             for tile, product in zip(tiles, products):
                 if product.shape[0] > channels:
                     product = product[:channels] + product[channels:]
@@ -224,15 +225,13 @@
 
 
 def measured_kernel(block, samples, *refs):
-    *weights, mx, eb, turn, images, grid, held, sems = refs
+    *weights, mx, eb, turn, images, turned, grid = refs
     plane = pl.program_id(0)
     coils = images.shape[0]
 
     @pl.when(plane == 0)
     def _():
-        copies = weight_copies(weights, held, sems)
-        start_copies(copies)
-        spread_tiles(block, copies, held, samples, grid)
+        spread_tiles(block, weights, samples, grid, turned)
 
     found = adjoint_images(coils, plane, pl.num_programs(0), eb, mx, turn, grid)
     for coil, (real, imag) in enumerate(found):
@@ -294,22 +293,20 @@
 
 
 def first_kernel(peers, coils, block, *refs):
-    samples, weights, sens = refs[:peers], refs[peers : 2 * peers], refs[2 * peers :][:coils]
-    mx, eb, turn, *norms = refs[2 * peers + coils :][: 3 + peers]
-    right_side, residual, rounded, facts, dots, total_samples, grid, parts, held, sems = refs[-10:]
+    samples, weights, sens = refs[:peers], refs[peers], refs[peers + 1 :][:coils]
+    mx, eb, turn, *norms = refs[peers + 1 + coils :][: 3 + peers]
+    right_side, residual, rounded, facts, dots, total_samples, grid, parts = refs[-8:]
     plane = pl.program_id(0)
 
     @pl.when(plane == 0)
     def _():
-        copies = weight_copies(weights, held, sems)
-        start_copies(copies)
         summed = summed_parts(samples, parts)
         total_samples[...] = summed
         rows = lax.broadcasted_iota(jnp.int32, facts.shape, 0)
         norm = tree_sum([part[...] for part in norms])
         facts[...] = jnp.where(rows == 1, jnp.sum(summed * summed), norm)
         dots[...] = jnp.zeros_like(dots)
-        spread_tiles(block, copies, held, parts, grid)
+        spread_tiles(block, [weights.at[k] for k in range(peers)], parts, grid)
 
     images = adjoint_images(coils, plane, pl.num_programs(0), eb, mx, turn, grid)
     total = combine(images, sens)
@@ -323,16 +320,14 @@
 
 
 def second_kernel(peers, coils, block, *refs):
-    samples, weights, sens = refs[:peers], refs[peers : 2 * peers], refs[2 * peers :][:coils]
-    mx, eb, turn, facts, residual, rounded, grid, parts, held, sems = refs[2 * peers + coils :]
+    samples, weights, sens = refs[:peers], refs[peers], refs[peers + 1 :][:coils]
+    mx, eb, turn, facts, residual, rounded, grid, parts = refs[peers + 1 + coils :]
     plane = pl.program_id(0)
 
     @pl.when(plane == 0)
     def _():
-        copies = weight_copies(weights, held, sems)
-        start_copies(copies)
         summed_parts(samples, parts)
-        spread_tiles(block, copies, held, parts, grid)
+        spread_tiles(block, [weights.at[k] for k in range(peers)], parts, grid)
 
     images = adjoint_images(coils, plane, pl.num_programs(0), eb, mx, turn, grid)
     total = combine(images, sens)
@@ -404,7 +399,7 @@
     return picture, residual
 
 
-def assemble_kernel(coils, group_steps, combos, is_residual, has_out, order, *refs):
+def assemble_kernel(coils, group_steps, combos, is_residual, order, *refs):
     infos, pieces, (out, kept) = refs[:coils], refs[coils:-2], refs[-2:]
     groups = infos[0].shape[0]
     count = 3 if is_residual else 2
@@ -501,7 +496,9 @@
     groups = range(own_planes // group_planes)
     measured = to_planes(kspace[0])
     packed = jnp.concatenate([tile_slot, tile_block, send_list.reshape(-1)])
-    sens_source, packed, measured = lax.optimization_barrier((sens_maps[0], packed, measured))
+    sens_source, packed, measured, own_weights = lax.optimization_barrier(
+        (sens_maps[0], packed, measured, weights)
+    )
     sens_source = sens_source.reshape(coil_count, own_planes, 2, rows, columns)
     sens = [
         lax.all_to_all(
@@ -516,8 +513,7 @@
     measured = jnp.stack(measured)
     by_coil = jnp.arange(coil_count, dtype=jnp.int32) ^ coil_index
     measured = jnp.take(measured, by_coil, axis=0)
-    all_weights = everywhere(weights, "pencil")
-    turned_weights = [jnp.swapaxes(array, 1, 2) for array in all_weights]
+    all_weights = everywhere(own_weights, "pencil")
 
     places = jnp.stack(everywhere(packed, "pencil"))
     holder = (jnp.arange(peers, dtype=jnp.int32) ^ lax.axis_index("pencil"))[:, None]
@@ -610,18 +606,20 @@
             )(*inputs)
 
         def measured_images():
-            inputs = [measured_block, measured, *turned_weights, *tail_tables]
+            inputs = [measured_block, measured, *all_weights, *tail_tables]
+            turned_shape = shaped((peers,) + weights.shape, bf16)
             shape = (coil_count, own_planes, 2, rows, columns)
             return call(
                 measured_kernel,
                 (own_planes,),
                 inputs,
-                [places_spec, whole_block(measured)]
-                + weights_specs
-                + [whole_block(i) for i in tail_tables],
-                shaped(shape),
-                pl.BlockSpec((coil_count, 1, 2, rows, columns), lambda p: (0, p, 0, 0, 0)),
-                [pltpu.VMEM((tiles * channels, size), f32)] + held_weights,
+                [places_spec] + [whole_block(i) for i in inputs[1:]],
+                [shaped(shape), turned_shape],
+                [
+                    pl.BlockSpec((coil_count, 1, 2, rows, columns), lambda p: (0, p, 0, 0, 0)),
+                    whole_block(turned_shape),
+                ],
+                [pltpu.VMEM((tiles * channels, size), f32)],
                 images_count,
             )
 
@@ -669,20 +667,20 @@
             )
 
         def back(kernel, samples, tables, vectors, g, outs, out_specs):
+            inputs = [*samples, turned_weights]
             tables = tail_tables + tables
             return call(
                 functools.partial(kernel, peers, coil_count),
                 (group_planes,),
-                [block_of, *samples, *turned_weights] + [sens[g]] * coil_count + tables + vectors,
+                [block_of, *inputs] + [sens[g]] * coil_count + tables + vectors,
                 [places_spec]
-                + [whole_block(i) for i in samples]
-                + weights_specs
+                + [whole_block(i) for i in inputs]
                 + sens_specs
                 + [whole_block(i) for i in tables]
                 + [plane_spec] * len(vectors),
                 outs,
                 out_specs,
-                [grid_scratch, pltpu.VMEM((blocks, 2 * group_channels, size), bf16)] + held_weights,
+                [grid_scratch, pltpu.VMEM((blocks, 2 * group_channels, size), bf16)],
                 group_images,
             )
 
@@ -717,38 +715,40 @@
                     for p in range(group_planes)
                 ]
             ).astype(jnp.int32)
+            chunks = rows // 64
             inputs = [vector[g][k] for k, g in combos for vector in vectors]
 
             def spec(place):
-                first_step = place // len(vectors) * group_planes
-                return pl.BlockSpec(
-                    (1, 2, rows, columns),
-                    lambda i, o: (jnp.clip(i - first_step, 0, group_planes - 1), 0, 0, 0),
-                )
+                first = place // len(vectors) * group_planes * chunks
+
+                def part_of(i, o):
+                    i = jnp.clip(i - first, 0, group_planes * chunks - 1)
+                    return i // chunks, 0, i % chunks, 0
+
+                return pl.BlockSpec((1, 2, 64, columns), part_of)
 
             specs = [pl.BlockSpec(infos[0].shape, lambda i, o: (0, 0, 0))] * len(infos)
             specs += [spec(place) for place in range(len(inputs))]
             aliases = {}
-            kernel = functools.partial(
-                assemble_kernel,
-                coil_count,
-                group_planes,
-                combos,
-                len(vectors) == 3,
-                out is not None,
-            )
             if out is not None:
                 aliases = {1 + len(infos) + len(inputs): 0}
                 inputs = inputs + [out]
                 specs.append(pl.BlockSpec(memory_space=pl.ANY))
-
             return pl.pallas_call(
-                kernel,
+                functools.partial(
+                    assemble_kernel,
+                    coil_count,
+                    group_planes * chunks,
+                    combos,
+                    len(vectors) == 3,
+                ),
                 grid_spec=pltpu.PrefetchScalarGridSpec(
                     num_scalar_prefetch=1,
-                    grid=(len(combos) * group_planes,),
+                    grid=(len(combos) * group_planes * chunks,),
                     in_specs=specs,
-                    out_specs=pl.BlockSpec((1, 2, rows, columns), lambda i, o: (o[i], 0, 0, 0)),
+                    out_specs=pl.BlockSpec(
+                        (1, 2, 64, columns), lambda i, o: (o[i // chunks], 0, i % chunks, 0)
+                    ),
                     scratch_shapes=[pltpu.VMEM((len(combos), 8, 128), f32)],
                 ),
                 out_shape=shaped((planes, 2, rows, columns)),
@@ -835,7 +835,7 @@
             return combined(images_of(samples, block_of), g) + damping * vector
 
         def measured_images():
-            return images_of(measured.astype(f32), measured_block)
+            return images_of(measured.astype(f32), measured_block), None
 
         def start(images, g):
             right_side = combined(images[:, g * group_planes : (g + 1) * group_planes], g)
@@ -885,7 +885,7 @@
     def sent_by_bits(own):
         return [swapped(own, "coil", k) for k in first_bits]
 
-    images = measured_images()
+    images, turned_weights = measured_images()
     start_pieces, residual_pieces, mixed_own, mixed_sent, infos = [], [], [], [], []
     for g in groups:
         right_side, start_own, norm = start(images, g)
@@ -895,21 +895,23 @@
         norms = exchanged(norm)
         samples, norms, start_sent = lax.optimization_barrier((samples, norms, start_sent))
         residual, residual_own, facts, dots, start_total = first(samples, norms, right_side, g)
-        residual, residual_own, pieces = lax.optimization_barrier(
-            (residual, residual_own, completed(start_own, start_sent))
+        dots = exchanged(dots)
+        residual, residual_own, dots, pieces = lax.optimization_barrier(
+            (residual, residual_own, dots, completed(start_own, start_sent))
         )
         start_pieces.append(pieces)
         residual_sent = sent_by_bits(residual_own)
-        dots = exchanged(dots)
         samples = exchanged(forward(residual, g))
-        samples, dots, residual_sent = lax.optimization_barrier((samples, dots, residual_sent))
+        samples, dots = lax.optimization_barrier((samples, dots))
         info = facts_of(samples, dots, start_total, facts)
         infos.append(info)
+        others = exchanged(jnp.stack(infos), "coil") if g == groups[-1] else []
+        samples, info, others, residual_sent = lax.optimization_barrier(
+            (samples, info, others, residual_sent)
+        )
         rounded = second(samples, info, residual, g)
-        last = g == groups[-1]
-        others = exchanged(jnp.stack(infos), "coil") if last else []
-        rounded, others, pieces = lax.optimization_barrier(
-            (rounded, others, completed(residual_own, residual_sent))
+        rounded, pieces = lax.optimization_barrier(
+            (rounded, completed(residual_own, residual_sent))
         )
         residual_pieces.append(pieces)
         mixed_own.append(rounded)

time: 196 us -> 195 us (level)
  Pallas kernels: 66.5 us -> 75.6 us
  local copies, waits for them, and re-layouts: 17.6 us -> 9.86 us
  waiting for transfers between devices: 66.1 us -> 59.5 us
  starting transfers between devices: 33.3 us -> 37.4 us
    all_to_all x1, waiting for transfers between devices: 16.4 us -> 0.01 us  [on_device(): lax.all_to_all(sens_source[:, g * group_planes:(g + 1) * group_planes], '...]
    ppermute x36, waiting for transfers between devices: 49.7 us -> 59.5 us  [swapped(): lax.ppermute(array, axis, [(i, i ^ k) for i in range(lax.axis_size(axis))])]
    pallas_call x4, Pallas kernels: 20.3 us -> 28.6 us  [assembled(): pl.pallas_call(functools.partial(assemble_kernel, coil_count, group_plane...]
    optimization_barrier x3 -> x0, local copies, waits for them, and re-layouts: 6.82 us -> none  [on_device(): lax.optimization_barrier((measured, ey, mx, turn, block_of, all_weights))]
    ppermute x36, starting transfers between devices: 29.7 us -> 33.8 us  [swapped(): lax.ppermute(array, axis, [(i, i ^ k) for i in range(lax.axis_size(axis))])]
  transfers between devices with their start and end apart: 37 -> 37, of which waited for: 14 -> 18; matrix products, arithmetic and copies ran while one was open for 12% -> 9% of each run, Pallas kernels for 30% -> 34%
where the time goes in v10:
time: 195 us; the launch traced here: 194 us
  Pallas kernels  75.6 us (39%)
  waiting for transfers between devices  59.5 us (31%)
  starting transfers between devices  37.4 us (19%)
  other arithmetic  10.5 us (5%)
  local copies, waits for them, and re-layouts  9.86 us (5%)
    ppermute x36, waiting for transfers between devices, swapped(): lax.ppermute(array, axis, [(i, i ^ k) for i in range(lax.axis_size(axis))])  59.5 us
    pallas_call x6, Pallas kernels, call(): pl.pallas_call(kernel, grid=grid, in_specs=specs, out_specs=out_specs, ou...  44.9 us
    ppermute x36, starting transfers between devices, swapped(): lax.ppermute(array, axis, [(i, i ^ k) for i in range(lax.axis_size(axis))])  33.8 us
    pallas_call x4, Pallas kernels, assembled(): pl.pallas_call(functools.partial(assemble_kernel, coil_count, group_plane...  28.6 us
  transfers between devices with their start and end apart: 37, of which 18 were waited for; matrix products, arithmetic and copies ran while one was open for 9% of the time, Pallas kernels for 34%

profile of v10, /device:TPU:0, one launch (start us, length us, event | category | flops | bytes accessed | tf_op | source)
XLA Modules:
  0.0 193.9 jit_solution(7575607117841077576)
XLA Ops:
  1.5 5.1 %collective-permute-start.2 = (bf16[2,2,1024]{2,1,0:T(2,128)(2,1)S(1)}, bf16[2,2,1024]{2,1,0:T(2,128)(2,1)S(1)}, u32[]{:S(2)}, u32[]{:S(2)}) collective-permute-start(bf16[2,2,1024]{2,1,0:T(2,128)(2,1)S(1)} %get-tuple-element.156), channel_id=1, source_target_pairs={{0,12},{4,8},{8,4},{12,0},{1,13},{5,9},{9,5},{13,1},{2,14},{6,10},... | collective-permute-start | bytes 24584 | tf_op jit(solution)/shard_map/ppermute | solution.py:463
  11.2 3.6 %all-to-all-start = ((bf16[4,2,2,128,512]{4,3,2,1,0:T(8,128)(2,1)}), bf16[4,2,2,128,512]{4,3,2,1,0:T(8,128)(2,1)S(1)}, u32[]{:S(2)}, u32[]{:S(2)}) async-start(bf16[4,2,2,128,512]{4,3,2,1,0:T(8,128)(2,1)} %bitcast.45), calls=%async_computation | async-start | bytes 4194304 | tf_op jit(solution)/shard_map/all_to_all | solution.py:504
  24.9 19.8 %collective-permute-done.10.refs_2_.refs_6_ = bf16[32,128,128]{2,1,0:T(8,128)(2,1)} collective-permute-done((bf16[32,128,128]{2,1,0:T(8,128)(2,1)S(1)}, bf16[32,128,128]{2,1,0:T(8,128)(2,1)}, u32[]{:S(2)}, u32[]{:S(2)}) %collective-permute-start.10) | collective-permute-done | bytes 1048608 | tf_op jit(solution)/shard_map/ppermute | solution.py:463
  52.0 10.0 %shard_map.77 = (f32[4,2,2,128,512]{4,3,2,1,0:T(8,128)}, bf16[4,32,128,128]{3,2,1,0:T(8,128)(2,1)}) custom-call(s32[128]{0:T(128)} %reshape.473.block, bf16[32,16,128]{2,1,0:T(8,128)(2,1)} %pad_maximum_fusion.3.samples, bf16[32,128,128]{2,1,0:T(8,128)(2,1)} %refs_4_.1, bf16[32,128,128]{2,1,0:T(8,128)(2,1)} %collective-permute-done.9.refs_1_.refs_5_, ...), custom_call_target="tpu_custom_call" | custom-call | flops 1342177280 | bytes 6423040 | tf_op jit(solution)/shard_map/pallas_call | solution.py:593
  63.3 5.1 %shard_map.78 = (f32[2,2,128,512]{3,2,1,0:T(8,128)}, bf16[2,2,128,512]{3,2,1,0:T(8,128)(2,1)}, f32[8,128]{1,0:T(8,128)}) custom-call(f32[4,2,2,128,512]{4,3,2,1,0:T(8,128)} %get-tuple-element.88.images, bf16[4,2,2,128,512]{4,3,2,1,0:T(8,128)(2,1)} %copy-done, bf16[4,2,2,128,512]{4,3,2,1,0:T(8,128)(2,1)} %copy-done, bf16[4,2,2,128,512]{4,3,2,1,0:T(8,128)(2,1)} %copy-done, ...), custom_call_target="tpu_custom_call" | custom-call | bytes 12582912 | tf_op jit(solution)/shard_map/pallas_call | solution.py:593
  68.4 2.9 %collective-permute-start.19 = (bf16[2,2,128,512]{3,2,1,0:T(8,128)(2,1)}, bf16[2,2,128,512]{3,2,1,0:T(8,128)(2,1)S(1)}, u32[]{:S(2)}, u32[]{:S(2)}) collective-permute-start(bf16[2,2,128,512]{3,2,1,0:T(8,128)(2,1)} %get-tuple-element.132.refs_4_), channel_id=1, source_target_pairs={{0,8},{4,12},{8,0},{12,4},{1,9},{5,13},{9,1},{13,5},{2,10},{6,14},... | collective-permute-start | bytes 1572872 | tf_op jit(solution)/shard_map/ppermute | solution.py:463
  72.8 5.5 %shard_map.79.refs_0_ = bf16[512,128]{1,0:T(8,128)(2,1)} custom-call(s32[128]{0:T(128)} %reshape.472.block, f32[2,2,128,512]{3,2,1,0:T(8,128)} %get-tuple-element.90.picture.refs_16_, bf16[4,2,2,128,512]{4,3,2,1,0:T(8,128)(2,1)} %copy-done, bf16[4,2,2,128,512]{4,3,2,1,0:T(8,128)(2,1)} %copy-done, bf16[4,2,2,128,512]{4,3,2,1,0:T(8,128)(2,1)} %copy-done, ...), custom_call_target="tpu_custom_call" | custom-call | flops 1342177280 | bytes 14156288 | tf_op jit(solution)/shard_map/pallas_call | solution.py:593
  83.3 4.1 %collective-permute-done.14.refs_3_ = bf16[512,128]{1,0:T(8,128)(2,1)S(1)} collective-permute-done((bf16[512,128]{1,0:T(8,128)(2,1)}, bf16[512,128]{1,0:T(8,128)(2,1)S(1)}, u32[]{:S(2)}, u32[]{:S(2)}) %collective-permute-start.14) | collective-permute-done | bytes 131104 | tf_op jit(solution)/shard_map/ppermute | solution.py:463
  87.4 2.6 %collective-permute-done.13.refs_2_ = bf16[512,128]{1,0:T(8,128)(2,1)S(1)} collective-permute-done((bf16[512,128]{1,0:T(8,128)(2,1)}, bf16[512,128]{1,0:T(8,128)(2,1)S(1)}, u32[]{:S(2)}, u32[]{:S(2)}) %collective-permute-start.13) | collective-permute-done | bytes 131104 | tf_op jit(solution)/shard_map/ppermute | solution.py:463
  90.0 4.9 %collective-permute-done.19.refs_8_.refs_4_ = bf16[2,2,128,512]{3,2,1,0:T(8,128)(2,1)S(1)} collective-permute-done((bf16[2,2,128,512]{3,2,1,0:T(8,128)(2,1)}, bf16[2,2,128,512]{3,2,1,0:T(8,128)(2,1)S(1)}, u32[]{:S(2)}, u32[]{:S(2)}) %collective-permute-start.19) | collective-permute-done | bytes 524320 | tf_op jit(solution)/shard_map/ppermute | solution.py:463
  96.7 9.7 %shard_map.80 = (f32[2,2,128,512]{3,2,1,0:T(8,128)}, bf16[2,2,128,512]{3,2,1,0:T(8,128)(2,1)}, f32[8,128]{1,0:T(8,128)}, f32[8,128]{1,0:T(8,128)}, f32[512,128]{1,0:T(8,128)}) custom-call(s32[128]{0:T(128)} %reshape.472.block, bf16[512,128]{1,0:T(8,128)(2,1)} %shard_map.79.refs_0_, bf16[512,128]{1,0:T(8,128)(2,1)} %copy-done.16, ...), custom_call_target="tpu_custom_call" | custom-call | flops 1342177280 | bytes 16269824 | tf_op jit(solution)/shard_map/pallas_call | solution.py:593
  110.4 2.4 %collective-permute-start.31 = (bf16[2,2,128,512]{3,2,1,0:T(8,128)(2,1)}, bf16[2,2,128,512]{3,2,1,0:T(8,128)(2,1)S(1)}, u32[]{:S(2)}, u32[]{:S(2)}) collective-permute-start(bf16[2,2,128,512]{3,2,1,0:T(8,128)(2,1)} %get-tuple-element.140.refs_5_), channel_id=1, source_target_pairs={{0,8},{4,12},{8,0},{12,4},{1,9},{5,13},{9,1},{13,5},{2,10},{6,14},... | collective-permute-start | bytes 1572872 | tf_op jit(solution)/shard_map/ppermute | solution.py:463
  113.1 5.5 %shard_map.81.refs_0_ = bf16[512,128]{1,0:T(8,128)(2,1)} custom-call(s32[128]{0:T(128)} %reshape.472.block, f32[2,2,128,512]{3,2,1,0:T(8,128)} %get-tuple-element.112.picture.refs_13_, bf16[4,2,2,128,512]{4,3,2,1,0:T(8,128)(2,1)} %copy-done, bf16[4,2,2,128,512]{4,3,2,1,0:T(8,128)(2,1)} %copy-done, bf16[4,2,2,128,512]{4,3,2,1,0:T(8,128)(2,1)} %copy-done, ...), custom_call_target="tpu_custom_call" | custom-call | flops 1342177280 | bytes 14156288 | tf_op jit(solution)/shard_map/pallas_call | solution.py:593
  120.5 4.1 %collective-permute-done.26.refs_3_ = bf16[512,128]{1,0:T(8,128)(2,1)S(1)} collective-permute-done((bf16[512,128]{1,0:T(8,128)(2,1)}, bf16[512,128]{1,0:T(8,128)(2,1)S(1)}, u32[]{:S(2)}, u32[]{:S(2)}) %collective-permute-start.26) | collective-permute-done | bytes 131104 | tf_op jit(solution)/shard_map/ppermute | solution.py:463
  124.6 2.9 %collective-permute-done.25.refs_2_ = bf16[512,128]{1,0:T(8,128)(2,1)S(1)} collective-permute-done((bf16[512,128]{1,0:T(8,128)(2,1)}, bf16[512,128]{1,0:T(8,128)(2,1)S(1)}, u32[]{:S(2)}, u32[]{:S(2)}) %collective-permute-start.25) | collective-permute-done | bytes 131104 | tf_op jit(solution)/shard_map/ppermute | solution.py:463
  128.2 2.1 %shard_map.82.refs_12_ = f32[8,128]{1,0:T(8,128)} custom-call(bf16[512,128]{1,0:T(8,128)(2,1)} %shard_map.81.refs_0_, bf16[512,128]{1,0:T(8,128)(2,1)} %copy-done.10, bf16[512,128]{1,0:T(8,128)(2,1)} %copy-done.9, bf16[512,128]{1,0:T(8,128)(2,1)} %copy-done.8, f32[8,128]{1,0:T(8,128)} %get-tuple-element.121.refs_4_, f32[8,128]{1,0:T(8,128)} %copy-done.22, ...), custom_call_target="tpu_custom_call" | custom-call | tf_op jit(solution)/shard_map/pallas_call | solution.py:701
  130.8 2.4 %collective-permute-start.28 = (f32[1,8,128]{2,1,0:T(8,128)}, f32[1,8,128]{2,1,0:T(8,128)S(1)}, u32[]{:S(2)}, u32[]{:S(2)}) collective-permute-start(f32[1,8,128]{2,1,0:T(8,128)} %bitcast.47), channel_id=1, source_target_pairs={{0,8},{4,12},{8,0},{12,4},{1,9},{5,13},{9,1},{13,5},{2,10},{6,14},... | collective-permute-start | bytes 12296 | tf_op jit(solution)/shard_map/ppermute | solution.py:463
  138.5 9.2 %shard_map.83.refs_6_ = bf16[2,2,128,512]{3,2,1,0:T(8,128)(2,1)} custom-call(s32[128]{0:T(128)} %reshape.472.block, bf16[512,128]{1,0:T(8,128)(2,1)} %shard_map.81.refs_0_, bf16[512,128]{1,0:T(8,128)(2,1)} %copy-done.10, bf16[512,128]{1,0:T(8,128)(2,1)} %copy-done.9, bf16[512,128]{1,0:T(8,128)(2,1)} %copy-done.8, ...), custom_call_target="tpu_custom_call" | custom-call | flops 1342177280 | bytes 16257536 | tf_op jit(solution)/shard_map/pallas_call | solution.py:593
  147.7 2.7 %collective-permute-done.32.refs_11_.refs_5_ = bf16[2,2,128,512]{3,2,1,0:T(8,128)(2,1)S(1)} collective-permute-done((bf16[2,2,128,512]{3,2,1,0:T(8,128)(2,1)S(1)}, bf16[2,2,128,512]{3,2,1,0:T(8,128)(2,1)S(1)}, u32[]{:S(2)}, u32[]{:S(2)}) %collective-permute-start.32) | collective-permute-done | bytes 524320 | tf_op jit(solution)/shard_map/ppermute | solution.py:463
  152.9 12.2 %shard_map.84 = f32[8,2,128,512]{3,2,1,0:T(8,128)} custom-call(s32[8]{0:T(128)} %stack.95.order, f32[1,8,128]{2,1,0:T(8,128)} %bitcast.49, f32[1,8,128]{2,1,0:T(8,128)} %copy-done.19, f32[1,8,128]{2,1,0:T(8,128)} %copy-done.18, f32[1,8,128]{2,1,0:T(8,128)} %copy-done.17, bf16[2,2,128,512]{3,2,1,0:T(8,128)(2,1)} %get-tuple-element.132.refs_4_, ...), custom_call_target="tpu_custom_call" | custom-call | tf_op jit(solution)/shard_map/pallas_call | solution.py:737
  165.1 9.4 %collective-permute-done.34.refs_6_ = bf16[2,2,128,512]{3,2,1,0:T(8,128)(2,1)S(1)} collective-permute-done((bf16[2,2,128,512]{3,2,1,0:T(8,128)(2,1)}, bf16[2,2,128,512]{3,2,1,0:T(8,128)(2,1)S(1)}, u32[]{:S(2)}, u32[]{:S(2)}) %collective-permute-start.34) | collective-permute-done | bytes 524320 | tf_op jit(solution)/shard_map/ppermute | solution.py:463
  176.6 7.3 %shard_map.85.refs_7_ = f32[8,2,128,512]{3,2,1,0:T(8,128)} custom-call(s32[4]{0:T(128)} %pad_add_fusion.4.order, f32[1,8,128]{2,1,0:T(8,128)} %bitcast.50, f32[1,8,128]{2,1,0:T(8,128)} %copy-done.19, f32[1,8,128]{2,1,0:T(8,128)} %copy-done.18, f32[1,8,128]{2,1,0:T(8,128)} %copy-done.17, bf16[2,2,128,512]{3,2,1,0:T(8,128)(2,1)} %get-tuple-element.132.refs_4_, ...), custom_call_target="tpu_custom_call" | custom-call | tf_op jit(solution)/shard_map/pallas_call | solution.py:737
  183.9 4.6 %shard_map.86.refs_7_ = f32[8,2,128,512]{3,2,1,0:T(8,128)} custom-call(s32[2]{0:T(128)} %pad_add_fusion.3.order, f32[1,8,128]{2,1,0:T(8,128)} %bitcast.51, f32[1,8,128]{2,1,0:T(8,128)} %copy-done.19, f32[1,8,128]{2,1,0:T(8,128)} %copy-done.18, f32[1,8,128]{2,1,0:T(8,128)} %copy-done.17, ...), custom_call_target="tpu_custom_call", output_to_operand_aliasing={{}: (8, {})} | custom-call | tf_op jit(solution)/shard_map/pallas_call | solution.py:737
  189.3 4.6 %shard_map.87 = f32[8,2,128,512]{3,2,1,0:T(8,128)} custom-call(s32[2]{0:T(128)} %pad_add_fusion.2.order, f32[1,8,128]{2,1,0:T(8,128)} %bitcast.52, f32[1,8,128]{2,1,0:T(8,128)} %copy-done.19, f32[1,8,128]{2,1,0:T(8,128)} %copy-done.18, f32[1,8,128]{2,1,0:T(8,128)} %copy-done.17, bf16[2,2,128,512]{3,2,1,0:T(8,128)(2,1)} %copy-done.3, ...), custom_call_target="tpu_custom_call", output_to_operand_aliasing={{}: (8, {})} | custom-call | tf_op jit(solution)/shard_map/pallas_call | solution.py:737
  (163 shorter events, 50.3 us)
Async XLA Ops:
  1.5 7.9 %collective-permute-start.2 = (bf16[2,2,1024]{2,1,0:T(2,128)(2,1)S(1)}, bf16[2,2,1024]{2,1,0:T(2,128)(2,1)S(1)}, u32[]{:S(2)}, u32[]{:S(2)}) collective-permute-start(bf16[2,2,1024]{2,1,0:T(2,128)(2,1)S(1)} %get-tuple-element.156), channel_id=1, source_target_pairs={{0,12},{4,8},{8,4},{12,0},{1,13},{5,9},{9,5},{13,1},{2,14},{6,10},... | collective-permute-start | bytes 24584 | tf_op jit(solution)/shard_map/ppermute | solution.py:463
  11.2 50.8 %all-to-all-start = ((bf16[4,2,2,128,512]{4,3,2,1,0:T(8,128)(2,1)}), bf16[4,2,2,128,512]{4,3,2,1,0:T(8,128)(2,1)S(1)}, u32[]{:S(2)}, u32[]{:S(2)}) async-start(bf16[4,2,2,128,512]{4,3,2,1,0:T(8,128)(2,1)} %bitcast.45), calls=%async_computation | async-start | bytes 4194304 | tf_op jit(solution)/shard_map/all_to_all | solution.py:504
  18.5 26.1 %collective-permute-start.10 = (bf16[32,128,128]{2,1,0:T(8,128)(2,1)S(1)}, bf16[32,128,128]{2,1,0:T(8,128)(2,1)}, u32[]{:S(2)}, u32[]{:S(2)}) collective-permute-start(bf16[32,128,128]{2,1,0:T(8,128)(2,1)S(1)} %copy-done.1), channel_id=1, source_target_pairs={{0,2},{1,3},{2,0},{3,1},{4,6},{5,7},{6,4},{7,5},{8,10},{9,11},{10,... | collective-permute-start | bytes 3145736 | tf_op jit(solution)/shard_map/ppermute | solution.py:463
  19.9 28.9 %collective-permute-start.4 = (bf16[8,16,128]{2,1,0:T(8,128)(2,1)S(1)}, bf16[8,16,128]{2,1,0:T(8,128)(2,1)S(1)}, u32[]{:S(2)}, u32[]{:S(2)}) collective-permute-start(bf16[8,16,128]{2,1,0:T(8,128)(2,1)S(1)} %fusion.14), channel_id=1, source_target_pairs={{0,2},{1,3},{2,0},{3,1},{4,6},{5,7},{6,4},{7,5},{8,10},{9,11},{10,... | collective-permute-start | bytes 98312 | tf_op jit(solution)/shard_map/ppermute | solution.py:463
  21.4 29.9 %collective-permute-start.3 = (bf16[8,16,128]{2,1,0:T(8,128)(2,1)S(1)}, bf16[8,16,128]{2,1,0:T(8,128)(2,1)S(1)}, u32[]{:S(2)}, u32[]{:S(2)}) collective-permute-start(bf16[8,16,128]{2,1,0:T(8,128)(2,1)S(1)} %fusion.14), channel_id=1, source_target_pairs={{0,1},{1,0},{2,3},{3,2},{4,5},{5,4},{6,7},{7,6},{8,9},{9,8},{10,11... | collective-permute-start | bytes 98312 | tf_op jit(solution)/shard_map/ppermute | solution.py:463
  21.7 30.3 %collective-permute-start.9 = (bf16[32,128,128]{2,1,0:T(8,128)(2,1)S(1)}, bf16[32,128,128]{2,1,0:T(8,128)(2,1)}, u32[]{:S(2)}, u32[]{:S(2)}) collective-permute-start(bf16[32,128,128]{2,1,0:T(8,128)(2,1)S(1)} %copy-done.1), channel_id=1, source_target_pairs={{0,1},{1,0},{2,3},{3,2},{4,5},{5,4},{6,7},{7,6},{8,9},{9,8},{10,11... | collective-permute-start | bytes 3145736 | tf_op jit(solution)/shard_map/ppermute | solution.py:463
  44.6 7.4 %collective-permute-start.11 = (bf16[32,128,128]{2,1,0:T(8,128)(2,1)}, bf16[32,128,128]{2,1,0:T(8,128)(2,1)}, u32[]{:S(2)}, u32[]{:S(2)}) collective-permute-start(bf16[32,128,128]{2,1,0:T(8,128)(2,1)} %collective-permute-done.10.refs_2_.refs_6_), channel_id=1, source_target_pairs={{0,1},{1,0},{2,3},{3,2},{4,5},{5,4},{6,7},{7,6},{8,9},{9,8},{10,11... | collective-permute-start | bytes 3145736 | tf_op jit(solution)/shard_map/ppermute | solution.py:463
  68.4 26.5 %collective-permute-start.19 = (bf16[2,2,128,512]{3,2,1,0:T(8,128)(2,1)}, bf16[2,2,128,512]{3,2,1,0:T(8,128)(2,1)S(1)}, u32[]{:S(2)}, u32[]{:S(2)}) collective-permute-start(bf16[2,2,128,512]{3,2,1,0:T(8,128)(2,1)} %get-tuple-element.132.refs_4_), channel_id=1, source_target_pairs={{0,8},{4,12},{8,0},{12,4},{1,9},{5,13},{9,1},{13,5},{2,10},{6,14},... | collective-permute-start | bytes 1572872 | tf_op jit(solution)/shard_map/ppermute | solution.py:463
  71.3 23.7 %collective-permute-start.18 = (bf16[2,2,128,512]{3,2,1,0:T(8,128)(2,1)}, bf16[2,2,128,512]{3,2,1,0:T(8,128)(2,1)S(1)}, u32[]{:S(2)}, u32[]{:S(2)}) collective-permute-start(bf16[2,2,128,512]{3,2,1,0:T(8,128)(2,1)} %get-tuple-element.132.refs_4_), channel_id=1, source_target_pairs={{0,4},{4,0},{8,12},{12,8},{1,5},{5,1},{9,13},{13,9},{2,6},{6,2},{1... | collective-permute-start | bytes 1572872 | tf_op jit(solution)/shard_map/ppermute | solution.py:463
  81.4 6.0 %collective-permute-start.14 = (bf16[512,128]{1,0:T(8,128)(2,1)}, bf16[512,128]{1,0:T(8,128)(2,1)S(1)}, u32[]{:S(2)}, u32[]{:S(2)}) collective-permute-start(bf16[512,128]{1,0:T(8,128)(2,1)} %shard_map.79.refs_0_), channel_id=1, source_target_pairs={{0,3},{1,2},{2,1},{3,0},{4,7},{5,6},{6,5},{7,4},{8,11},{9,10},{10,... | collective-permute-start | bytes 393224 | tf_op jit(solution)/shard_map/ppermute | solution.py:463
  82.0 8.0 %collective-permute-start.13 = (bf16[512,128]{1,0:T(8,128)(2,1)}, bf16[512,128]{1,0:T(8,128)(2,1)S(1)}, u32[]{:S(2)}, u32[]{:S(2)}) collective-permute-start(bf16[512,128]{1,0:T(8,128)(2,1)} %shard_map.79.refs_0_), channel_id=1, source_target_pairs={{0,2},{1,3},{2,0},{3,1},{4,6},{5,7},{6,4},{7,5},{8,10},{9,11},{10,... | collective-permute-start | bytes 393224 | tf_op jit(solution)/shard_map/ppermute | solution.py:463
  83.0 7.0 %collective-permute-start.12 = (bf16[512,128]{1,0:T(8,128)(2,1)}, bf16[512,128]{1,0:T(8,128)(2,1)S(1)}, u32[]{:S(2)}, u32[]{:S(2)}) collective-permute-start(bf16[512,128]{1,0:T(8,128)(2,1)} %shard_map.79.refs_0_), channel_id=1, source_target_pairs={{0,1},{1,0},{2,3},{3,2},{4,5},{5,4},{6,7},{7,6},{8,9},{9,8},{10,11... | collective-permute-start | bytes 393224 | tf_op jit(solution)/shard_map/ppermute | solution.py:463
  95.0 15.3 %collective-permute-start.23 = (bf16[2,2,128,512]{3,2,1,0:T(8,128)(2,1)S(1)}, bf16[2,2,128,512]{3,2,1,0:T(8,128)(2,1)S(1)}, u32[]{:S(2)}, u32[]{:S(2)}) collective-permute-start(bf16[2,2,128,512]{3,2,1,0:T(8,128)(2,1)S(1)} %collective-permute-done.19.refs_8_.refs_4_), channel_id=1, source_target_pairs={{0,4},{4,0},{8,12},{12,8},{1,5},{5,1},{9,13},{13,9},{2,6},{6,2},{1... | collective-permute-start | bytes 1572872 | tf_op jit(solution)/shard_map/ppermute | solution.py:463
  110.4 27.1 %collective-permute-start.31 = (bf16[2,2,128,512]{3,2,1,0:T(8,128)(2,1)}, bf16[2,2,128,512]{3,2,1,0:T(8,128)(2,1)S(1)}, u32[]{:S(2)}, u32[]{:S(2)}) collective-permute-start(bf16[2,2,128,512]{3,2,1,0:T(8,128)(2,1)} %get-tuple-element.140.refs_5_), channel_id=1, source_target_pairs={{0,8},{4,12},{8,0},{12,4},{1,9},{5,13},{9,1},{13,5},{2,10},{6,14},... | collective-permute-start | bytes 1572872 | tf_op jit(solution)/shard_map/ppermute | solution.py:463
  112.8 24.6 %collective-permute-start.30 = (bf16[2,2,128,512]{3,2,1,0:T(8,128)(2,1)}, bf16[2,2,128,512]{3,2,1,0:T(8,128)(2,1)S(1)}, u32[]{:S(2)}, u32[]{:S(2)}) collective-permute-start(bf16[2,2,128,512]{3,2,1,0:T(8,128)(2,1)} %get-tuple-element.140.refs_5_), channel_id=1, source_target_pairs={{0,4},{4,0},{8,12},{12,8},{1,5},{5,1},{9,13},{13,9},{2,6},{6,2},{1... | collective-permute-start | bytes 1572872 | tf_op jit(solution)/shard_map/ppermute | solution.py:463
  118.6 6.0 %collective-permute-start.26 = (bf16[512,128]{1,0:T(8,128)(2,1)}, bf16[512,128]{1,0:T(8,128)(2,1)S(1)}, u32[]{:S(2)}, u32[]{:S(2)}) collective-permute-start(bf16[512,128]{1,0:T(8,128)(2,1)} %shard_map.81.refs_0_), channel_id=1, source_target_pairs={{0,3},{1,2},{2,1},{3,0},{4,7},{5,6},{6,5},{7,4},{8,11},{9,10},{10,... | collective-permute-start | bytes 393224 | tf_op jit(solution)/shard_map/ppermute | solution.py:463
  118.8 8.6 %collective-permute-start.25 = (bf16[512,128]{1,0:T(8,128)(2,1)}, bf16[512,128]{1,0:T(8,128)(2,1)S(1)}, u32[]{:S(2)}, u32[]{:S(2)}) collective-permute-start(bf16[512,128]{1,0:T(8,128)(2,1)} %shard_map.81.refs_0_), channel_id=1, source_target_pairs={{0,2},{1,3},{2,0},{3,1},{4,6},{5,7},{6,4},{7,5},{8,10},{9,11},{10,... | collective-permute-start | bytes 393224 | tf_op jit(solution)/shard_map/ppermute | solution.py:463
  120.2 7.2 %collective-permute-start.24 = (bf16[512,128]{1,0:T(8,128)(2,1)}, bf16[512,128]{1,0:T(8,128)(2,1)S(1)}, u32[]{:S(2)}, u32[]{:S(2)}) collective-permute-start(bf16[512,128]{1,0:T(8,128)(2,1)} %shard_map.81.refs_0_), channel_id=1, source_target_pairs={{0,1},{1,0},{2,3},{3,2},{4,5},{5,4},{6,7},{7,6},{8,9},{9,8},{10,11... | collective-permute-start | bytes 393224 | tf_op jit(solution)/shard_map/ppermute | solution.py:463
  130.2 6.0 %collective-permute-start.29 = (f32[1,8,128]{2,1,0:T(8,128)}, f32[1,8,128]{2,1,0:T(8,128)S(1)}, u32[]{:S(2)}, u32[]{:S(2)}) collective-permute-start(f32[1,8,128]{2,1,0:T(8,128)} %bitcast.46), channel_id=1, source_target_pairs={{0,12},{4,8},{8,4},{12,0},{1,13},{5,9},{9,5},{13,1},{2,14},{6,10},... | collective-permute-start | bytes 12296 | tf_op jit(solution)/shard_map/ppermute | solution.py:463
  130.8 5.5 %collective-permute-start.28 = (f32[1,8,128]{2,1,0:T(8,128)}, f32[1,8,128]{2,1,0:T(8,128)S(1)}, u32[]{:S(2)}, u32[]{:S(2)}) collective-permute-start(f32[1,8,128]{2,1,0:T(8,128)} %bitcast.47), channel_id=1, source_target_pairs={{0,8},{4,12},{8,0},{12,4},{1,9},{5,13},{9,1},{13,5},{2,10},{6,14},... | collective-permute-start | bytes 12296 | tf_op jit(solution)/shard_map/ppermute | solution.py:463
  137.5 13.0 %collective-permute-start.32 = (bf16[2,2,128,512]{3,2,1,0:T(8,128)(2,1)S(1)}, bf16[2,2,128,512]{3,2,1,0:T(8,128)(2,1)S(1)}, u32[]{:S(2)}, u32[]{:S(2)}) collective-permute-start(bf16[2,2,128,512]{3,2,1,0:T(8,128)(2,1)S(1)} %collective-permute-done.31.refs_9_.refs_5_), channel_id=1, source_target_pairs={{0,4},{4,0},{8,12},{12,8},{1,5},{5,1},{9,13},{13,9},{2,6},{6,2},{1... | collective-permute-start | bytes 1572872 | tf_op jit(solution)/shard_map/ppermute | solution.py:463
  150.4 24.1 %collective-permute-start.34 = (bf16[2,2,128,512]{3,2,1,0:T(8,128)(2,1)}, bf16[2,2,128,512]{3,2,1,0:T(8,128)(2,1)S(1)}, u32[]{:S(2)}, u32[]{:S(2)}) collective-permute-start(bf16[2,2,128,512]{3,2,1,0:T(8,128)(2,1)} %shard_map.83.refs_6_), channel_id=1, source_target_pairs={{0,8},{4,12},{8,0},{12,4},{1,9},{5,13},{9,1},{13,5},{2,10},{6,14},... | collective-permute-start | bytes 1572872 | tf_op jit(solution)/shard_map/ppermute | solution.py:463
  150.9 23.6 %collective-permute-start.33 = (bf16[2,2,128,512]{3,2,1,0:T(8,128)(2,1)}, bf16[2,2,128,512]{3,2,1,0:T(8,128)(2,1)S(1)}, u32[]{:S(2)}, u32[]{:S(2)}) collective-permute-start(bf16[2,2,128,512]{3,2,1,0:T(8,128)(2,1)} %shard_map.83.refs_6_), channel_id=1, source_target_pairs={{0,4},{4,0},{8,12},{12,8},{1,5},{5,1},{9,13},{13,9},{2,6},{6,2},{1... | collective-permute-start | bytes 1572872 | tf_op jit(solution)/shard_map/ppermute | solution.py:463
  174.5 14.0 %collective-permute-start.35 = (bf16[2,2,128,512]{3,2,1,0:T(8,128)(2,1)S(1)}, bf16[2,2,128,512]{3,2,1,0:T(8,128)(2,1)S(1)}, u32[]{:S(2)}, u32[]{:S(2)}) collective-permute-start(bf16[2,2,128,512]{3,2,1,0:T(8,128)(2,1)S(1)} %collective-permute-done.34.refs_6_), channel_id=1, source_target_pairs={{0,4},{4,0},{8,12},{12,8},{1,5},{5,1},{9,13},{13,9},{2,6},{6,2},{1... | collective-permute-start | bytes 1572872 | tf_op jit(solution)/shard_map/ppermute | solution.py:463
  (40 other events, 265.0 us)

commit v11 on v10

--- a/solution.py
+++ b/solution.py
@@ -321,11 +321,13 @@
 
 def second_kernel(peers, coils, block, *refs):
     samples, weights, sens = refs[:peers], refs[peers], refs[peers + 1 :][:coils]
-    mx, eb, turn, facts, residual, rounded, grid, parts = refs[peers + 1 + coils :]
+    mx, eb, turn, facts, *infos = refs[peers + 1 + coils :][: 4 + coils]
+    right_side, residual, rounded, grid, parts, kept = refs[-6:]
     plane = pl.program_id(0)
 
     @pl.when(plane == 0)
     def _():
+        kept_coefficients(infos, kept, [0], True)
         summed_parts(samples, parts)
         spread_tiles(block, [weights.at[k] for k in range(peers)], parts, grid)
 
@@ -334,8 +336,9 @@
     scale = step_of(facts[0:1, 0:1], facts[1:2, 0:1])
     for part in range(2):
         vector = residual[0, part]
-        again = total[part] + damping * vector
-        rounded[0, part] = (vector - scale * again).astype(bf16)
+        mixed = vector - scale * (total[part] + damping * vector)
+        value = kept[0, 0:1, 0:1] * right_side[0, part] + kept[0, 1:2, 0:1] * vector
+        rounded[0, part] = (value + kept[0, 2:3, 0:1] * mixed).astype(bf16)
 
 
 def facts_kernel(peers, *refs):
@@ -399,38 +402,57 @@
     return picture, residual
 
 
-def assemble_kernel(coils, group_steps, combos, is_residual, order, *refs):
+def kept_coefficients(infos, kept, ks, is_residual):
+    numbers = [
+        [[info[0, row : row + 1, 0:1]] for info in infos] for row in range(6)
+    ]
+    factors = coefficients(*numbers)[is_residual]
+    rows = lax.broadcasted_iota(jnp.int32, kept.shape[1:], 0)
+    for place, k in enumerate(ks):
+        total = jnp.zeros(kept.shape[1:], f32)
+        for row, factor in enumerate(factors[k][0]):
+            total = jnp.where(rows == row, factor, total)
+        kept[place] = total
+
+
+def assemble_kernel(coils, ks, counts, order, *refs):
     infos, pieces, (out, kept) = refs[:coils], refs[coils:-2], refs[-2:]
-    groups = infos[0].shape[0]
-    count = 3 if is_residual else 2
+
+    if max(counts) > 1:
+
+        @pl.when(pl.program_id(0) == 0)
+        def _():
+            kept_coefficients(infos, kept, ks, False)
+
+    def write(place, used):
+        @pl.when(pl.program_id(0) == place)
+        def _():
+            if len(used) == 1:
+                out[...] = used[0][...].astype(f32)
+            else:
+                total = 0.0
+                for row, piece in enumerate(used):
+                    factor = kept[place // len(counts), row : row + 1, 0:1]
+                    total += factor.reshape(1, 1, 1, 1) * piece[...].astype(f32)
+                out[...] = total
+
+    first = 0
+    for place in range(len(ks) * len(counts)):
+        count = counts[place % len(counts)]
+        write(place, pieces[first : first + count])
+        first += count
+
+
+def picture_kernel(coils, *refs):
+    infos, (right_side, residual, out, kept) = refs[:coils], refs[coils:]
 
     @pl.when(pl.program_id(0) == 0)
     def _():
-        numbers = [
-            [[info[g, row : row + 1, 0:1] for g in range(groups)] for info in infos]
-            for row in range(6)
-        ]
-        factors = coefficients(*numbers)[is_residual]
-        rows = lax.broadcasted_iota(jnp.int32, kept.shape[1:], 0)
-        for place, (k, g) in enumerate(combos):
-            total = jnp.zeros(kept.shape[1:], f32)
-            for row, factor in enumerate(factors[k][g]):
-                total = jnp.where(rows == row, factor, total)
-            kept[place] = total
-
-    for place in range(len(combos)):
-
-        @pl.when(pl.program_id(0) // group_steps == place)
-        def _():
-            total = 0.0
-            for row, piece in enumerate(pieces[place * count :][:count]):
-                factor = kept[place, row : row + 1, 0:1].reshape(1, 1, 1, 1)
-                total += factor * piece[...].astype(f32)
-            out[...] = total
-
-
-def group_count_of(own_planes):
-    return 1
+        kept_coefficients(infos, kept, [0], False)
+
+    for part in range(2):
+        value = kept[0, 0:1, 0:1] * right_side[0, part] + kept[0, 1:2, 0:1] * residual[0, part]
+        out[0, part] = value.astype(bf16)
 
 
 def whole_block(array):
@@ -492,7 +514,7 @@
             pieces.append(swapped(part, "coil", k) if k > 0 else part)
         return pieces
 
-    group_planes = own_planes // group_count_of(own_planes)
+    group_planes = own_planes
     groups = range(own_planes // group_planes)
     measured = to_planes(kspace[0])
     packed = jnp.concatenate([tile_slot, tile_block, send_list.reshape(-1)])
@@ -666,7 +688,7 @@
                 group_images,
             )
 
-        def back(kernel, samples, tables, vectors, g, outs, out_specs):
+        def back(kernel, samples, tables, vectors, g, outs, out_specs, scratch=()):
             inputs = [*samples, turned_weights]
             tables = tail_tables + tables
             return call(
@@ -680,7 +702,7 @@
                 + [plane_spec] * len(vectors),
                 outs,
                 out_specs,
-                [grid_scratch, pltpu.VMEM((blocks, 2 * group_channels, size), bf16)],
+                [grid_scratch, pltpu.VMEM((blocks, 2 * group_channels, size), bf16), *scratch],
                 group_images,
             )
 
@@ -706,65 +728,68 @@
                 compiler_params=params,
             )(*inputs)
 
-        def assembled(infos, vectors, ks, out=None):
-            combos = [(k, g) for k in ks for g in groups]
+        def assembled(infos, parts, ks, out=None):
+            step = own_planes // len(parts)
             order = jnp.stack(
-                [
-                    (coil_index ^ k) * own_planes + g * group_planes + p
-                    for k, g in combos
-                    for p in range(group_planes)
-                ]
+                [(coil_index ^ k) * len(parts) + h for k in ks for h in range(len(parts))]
             ).astype(jnp.int32)
-            chunks = rows // 64
-            inputs = [vector[g][k] for k, g in combos for vector in vectors]
-
-            def spec(place):
-                first = place // len(vectors) * group_planes * chunks
-
-                def part_of(i, o):
-                    i = jnp.clip(i - first, 0, group_planes * chunks - 1)
-                    return i // chunks, 0, i % chunks, 0
-
-                return pl.BlockSpec((1, 2, 64, columns), part_of)
-
-            specs = [pl.BlockSpec(infos[0].shape, lambda i, o: (0, 0, 0))] * len(infos)
-            specs += [spec(place) for place in range(len(inputs))]
+            inputs, specs = [], [pl.BlockSpec(infos[0].shape, lambda i, o: (0, 0, 0))] * len(infos)
+            for k in ks:
+                for vectors, h in parts:
+                    for vector in vectors:
+                        inputs.append(vector[k])
+                        specs.append(
+                            pl.BlockSpec(
+                                (step, 2, rows, columns),
+                                functools.partial(lambda h, i, o: (h, 0, 0, 0), h),
+                            )
+                        )
             aliases = {}
             if out is not None:
                 aliases = {1 + len(infos) + len(inputs): 0}
-                inputs = inputs + [out]
+                inputs.append(out)
                 specs.append(pl.BlockSpec(memory_space=pl.ANY))
+            counts = [len(vectors) for vectors, h in parts]
             return pl.pallas_call(
-                functools.partial(
-                    assemble_kernel,
-                    coil_count,
-                    group_planes * chunks,
-                    combos,
-                    len(vectors) == 3,
-                ),
+                functools.partial(assemble_kernel, coil_count, list(ks), counts),
                 grid_spec=pltpu.PrefetchScalarGridSpec(
                     num_scalar_prefetch=1,
-                    grid=(len(combos) * group_planes * chunks,),
+                    grid=(len(ks) * len(parts),),
                     in_specs=specs,
                     out_specs=pl.BlockSpec(
-                        (1, 2, 64, columns), lambda i, o: (o[i // chunks], 0, i % chunks, 0)
+                        (step, 2, rows, columns), lambda i, o: (o[i], 0, 0, 0)
                     ),
-                    scratch_shapes=[pltpu.VMEM((len(combos), 8, 128), f32)],
+                    scratch_shapes=[pltpu.VMEM((len(ks), 8, 128), f32)],
                 ),
                 out_shape=shaped((planes, 2, rows, columns)),
                 input_output_aliases=aliases,
                 compiler_params=params,
             )(order, *infos, *inputs)
 
-        def second(samples, facts, residual, g):
+        def own_picture(infos, right_side, residual, first_plane):
+            count = own_planes - first_plane
+            spec = pl.BlockSpec((1, 2, rows, columns), lambda p: (p + first_plane, 0, 0, 0))
+            small = pl.BlockSpec(infos[0].shape, lambda p: (0, 0, 0))
+            return pl.pallas_call(
+                functools.partial(picture_kernel, coil_count),
+                grid=(count,),
+                in_specs=[small] * len(infos) + [spec] * 2,
+                out_specs=plane_spec,
+                out_shape=shaped((count, 2, rows, columns), bf16),
+                scratch_shapes=[pltpu.VMEM((1, 8, 128), f32)],
+                compiler_params=params,
+            )(*infos, right_side, residual)
+
+        def second(samples, facts, infos, right_side, residual, g):
             return back(
                 second_kernel,
                 samples,
-                [facts],
-                [residual],
+                [facts, *infos],
+                [right_side, residual],
                 g,
                 shaped(group_shape, bf16),
                 plane_spec,
+                [pltpu.VMEM((1, 8, 128), f32)],
             )
 
     else:
@@ -858,26 +883,36 @@
             values += [jnp.sum(total * total), jnp.sum(total * start_total)]
             return stacked_dots(values)
 
-        def assembled(infos, vectors, ks, out=None):
-            numbers = [
-                [[info[g, row, 0] for g in groups] for info in infos] for row in range(6)
-            ]
-            factors = coefficients(*numbers)[len(vectors) == 3]
+        def factors_of(infos, is_residual):
+            numbers = [[[info[0, row, 0]] for info in infos] for row in range(6)]
+            return [factors[0] for factors in coefficients(*numbers)[is_residual]]
+
+        def mixture(factors, vectors):
+            return sum(factor * vector.astype(f32) for factor, vector in zip(factors, vectors))
+
+        def assembled(infos, parts, ks, out=None):
+            factors = factors_of(infos, False)
+            step = own_planes // len(parts)
             if out is None:
                 out = jnp.zeros((planes, 2, rows, columns), f32)
             for k in ks:
-                for g in groups:
-                    place = ((coil_index ^ k) * own_planes + g * group_planes, 0, 0, 0)
-                    piece = sum(
-                        factor * vector[g][k].astype(f32)
-                        for factor, vector in zip(factors[k][g], vectors)
-                    )
+                for h, (vectors, at) in enumerate(parts):
+                    place = ((coil_index ^ k) * own_planes + h * step, 0, 0, 0)
+                    pieces = [vector[k][at * step : (at + 1) * step] for vector in vectors]
+                    if len(pieces) == 1:
+                        piece = pieces[0].astype(f32)
+                    else:
+                        piece = mixture(factors[k], pieces)
                     out = lax.dynamic_update_slice(out, piece, place)
             return out
 
-        def second(samples, facts, residual, g):
-            again = applied_to(samples, residual, g)
-            return (residual - step_of(facts[0, 0], facts[1, 0]) * again).astype(bf16)
+        def own_picture(infos, right_side, residual, first_plane):
+            vectors = [right_side[first_plane:], residual[first_plane:]]
+            return mixture(factors_of(infos, False)[0], vectors).astype(bf16)
+
+        def second(samples, facts, infos, right_side, residual, g):
+            mixed = residual - step_of(facts[0, 0], facts[1, 0]) * applied_to(samples, residual, g)
+            return mixture(factors_of(infos, True)[0], [right_side, residual, mixed]).astype(bf16)
 
     def added(samples):
         return tree_sum([part.astype(f32) for part in samples])
@@ -886,49 +921,51 @@
         return [swapped(own, "coil", k) for k in first_bits]
 
     images, turned_weights = measured_images()
-    start_pieces, residual_pieces, mixed_own, mixed_sent, infos = [], [], [], [], []
-    for g in groups:
-        right_side, start_own, norm = start(images, g)
-        start_sent = sent_by_bits(start_own)
-        samples, norm = lax.optimization_barrier((forward(right_side, g), norm))
-        samples = exchanged(samples)
-        norms = exchanged(norm)
-        samples, norms, start_sent = lax.optimization_barrier((samples, norms, start_sent))
-        residual, residual_own, facts, dots, start_total = first(samples, norms, right_side, g)
-        dots = exchanged(dots)
-        residual, residual_own, dots, pieces = lax.optimization_barrier(
-            (residual, residual_own, dots, completed(start_own, start_sent))
-        )
-        start_pieces.append(pieces)
-        residual_sent = sent_by_bits(residual_own)
-        samples = exchanged(forward(residual, g))
-        samples, dots = lax.optimization_barrier((samples, dots))
-        info = facts_of(samples, dots, start_total, facts)
-        infos.append(info)
-        others = exchanged(jnp.stack(infos), "coil") if g == groups[-1] else []
-        samples, info, others, residual_sent = lax.optimization_barrier(
-            (samples, info, others, residual_sent)
-        )
-        rounded = second(samples, info, residual, g)
-        rounded, pieces = lax.optimization_barrier(
-            (rounded, completed(residual_own, residual_sent))
-        )
-        residual_pieces.append(pieces)
-        mixed_own.append(rounded)
-        mixed_sent.append(sent_by_bits(rounded))
-
-    picture = assembled(others, [start_pieces, residual_pieces], range(coil_count))
-    early = [
-        [own, sent[0]] + [None] * (coil_count - 2)
-        for own, sent in zip(mixed_own, mixed_sent)
-    ]
-    out = assembled(others, [start_pieces, residual_pieces, early], range(2))
-    picture, mixed_sent = lax.optimization_barrier((picture, mixed_sent))
-    mixed_pieces = [completed(own, sent) for own, sent in zip(mixed_own, mixed_sent)]
-    vectors = [start_pieces, residual_pieces, mixed_pieces]
+    halves = 2 if own_planes % 2 == 0 else 1
+    early = own_planes // 2 if halves == 2 else 0
+
+    def first_planes(own):
+        return own[:early]
+
+    right_side, start_own, norm = start(images, 0)
+    start_sent = sent_by_bits(first_planes(start_own)) if early else []
+    samples, norm = lax.optimization_barrier((forward(right_side, 0), norm))
+    samples = exchanged(samples)
+    norms = exchanged(norm)
+    samples, norms, start_sent = lax.optimization_barrier((samples, norms, start_sent))
+    residual, residual_own, facts, dots, start_total = first(samples, norms, right_side, 0)
+    dots = exchanged(dots)
+    start_pieces = completed(first_planes(start_own), start_sent) if early else []
+    residual, residual_own, dots, start_pieces = lax.optimization_barrier(
+        (residual, residual_own, dots, start_pieces)
+    )
+    residual_sent = sent_by_bits(first_planes(residual_own)) if early else []
+    samples = exchanged(forward(residual, 0))
+    samples, dots = lax.optimization_barrier((samples, dots))
+    info = facts_of(samples, dots, start_total, facts)
+    others = exchanged(info[None], "coil")
+    picture_own = own_picture(others, right_side, residual, early)
+    samples, others, picture_own, residual_sent = lax.optimization_barrier(
+        (samples, others, picture_own, residual_sent)
+    )
+    residual_pieces = completed(first_planes(residual_own), residual_sent) if early else []
+    picture_sent = sent_by_bits(picture_own)
+    final_own = second(samples, info, others, right_side, residual, 0)
+    final_own, picture_sent, residual_pieces = lax.optimization_barrier(
+        (final_own, picture_sent, residual_pieces)
+    )
+    final_sent = sent_by_bits(final_own)
+    picture_pieces = completed(picture_own, picture_sent)
+    parts = [([start_pieces, residual_pieces], 0)] * (halves - 1) + [([picture_pieces], 0)]
+    picture = assembled(others, parts, range(coil_count))
+    near = [final_own, final_sent[0]] + [None] * (coil_count - 2)
+    out = assembled(others, [([near], h) for h in range(halves)], range(2))
+    picture, final_sent = lax.optimization_barrier((picture, final_sent))
+    final_pieces = completed(final_own, final_sent)
+    parts = [([final_pieces], h) for h in range(halves)]
     late = coil_count - 1
-    out = assembled(others, vectors, range(2, late), out)
-    out = assembled(others, vectors, [late], out)
+    out = assembled(others, parts, range(2, late), out)
+    out = assembled(others, parts, [late], out)
     return picture, out
 
 

time: 195 us -> 206 us (1.056)
  waiting for transfers between devices: 59.5 us -> 74.7 us
  Pallas kernels: 75.6 us -> 65.4 us
  local copies, waits for them, and re-layouts: 9.86 us -> 13.8 us
  starting transfers between devices: 37.4 us -> 39.9 us
    ppermute x36 -> x39, waiting for transfers between devices: 59.5 us -> 74.7 us  [swapped(): lax.ppermute(array, axis, [(i, i ^ k) for i in range(lax.axis_size(axis))])]
    pallas_call x4 -> x5, Pallas kernels: 28.6 us -> 18.1 us  [the longest x4 16 us: assembled(): pl.pallas_call(functools.partial(assemble_kernel, coil_count, list(ks), c...]
    ppermute x36 -> x39, starting transfers between devices: 33.8 us -> 36.3 us  [swapped(): lax.ppermute(array, axis, [(i, i ^ k) for i in range(lax.axis_size(axis))])]
    unnamed x54 -> x64, local copies, waits for them, and re-layouts: 2.9 us -> 4.75 us
  transfers between devices with their start and end apart: 37 -> 40, of which waited for: 18 -> 18; matrix products, arithmetic and copies ran while one was open for 9% -> 8% of each run, Pallas kernels for 34% -> 28%
where the time goes in v11:
time: 206 us; the launch traced here: 205 us
  waiting for transfers between devices  74.7 us (36%)
  Pallas kernels  65.4 us (32%)
  starting transfers between devices  39.9 us (19%)
  local copies, waits for them, and re-layouts  13.8 us (7%)
  other arithmetic  10.4 us (5%)
    ppermute x39, waiting for transfers between devices, swapped(): lax.ppermute(array, axis, [(i, i ^ k) for i in range(lax.axis_size(axis))])  74.7 us
    pallas_call x6, Pallas kernels, call(): pl.pallas_call(kernel, grid=grid, in_specs=specs, out_specs=out_specs, ou...  45.3 us
    ppermute x39, starting transfers between devices, swapped(): lax.ppermute(array, axis, [(i, i ^ k) for i in range(lax.axis_size(axis))])  36.3 us
    pallas_call x4, Pallas kernels, assembled(): pl.pallas_call(functools.partial(assemble_kernel, coil_count, list(ks), c...  16 us
    unnamed x64, local copies, waits for them, and re-layouts  4.75 us
  transfers between devices with their start and end apart: 40, of which 18 were waited for; matrix products, arithmetic and copies ran while one was open for 8% of the time, Pallas kernels for 28%

profile of v11, /device:TPU:0, one launch (start us, length us, event | category | flops | bytes accessed | tf_op | source)
XLA Modules:
  0.0 205.3 jit_solution(7958275967230323529)
XLA Ops:
  1.5 5.1 %collective-permute-start.2 = (bf16[2,2,1024]{2,1,0:T(2,128)(2,1)S(1)}, bf16[2,2,1024]{2,1,0:T(2,128)(2,1)S(1)}, u32[]{:S(2)}, u32[]{:S(2)}) collective-permute-start(bf16[2,2,1024]{2,1,0:T(2,128)(2,1)S(1)} %get-tuple-element.160), channel_id=1, source_target_pairs={{0,12},{4,8},{8,4},{12,0},{1,13},{5,9},{9,5},{13,1},{2,14},{6,10},... | collective-permute-start | bytes 24584 | tf_op jit(solution)/shard_map/ppermute | solution.py:485
  11.2 3.6 %all-to-all-start = ((bf16[4,2,2,128,512]{4,3,2,1,0:T(8,128)(2,1)}), bf16[4,2,2,128,512]{4,3,2,1,0:T(8,128)(2,1)S(1)}, u32[]{:S(2)}, u32[]{:S(2)}) async-start(bf16[4,2,2,128,512]{4,3,2,1,0:T(8,128)(2,1)} %bitcast.45), calls=%async_computation | async-start | bytes 4194304 | tf_op jit(solution)/shard_map/all_to_all | solution.py:526
  24.9 19.8 %collective-permute-done.10.refs_2_.refs_6_ = bf16[32,128,128]{2,1,0:T(8,128)(2,1)} collective-permute-done((bf16[32,128,128]{2,1,0:T(8,128)(2,1)S(1)}, bf16[32,128,128]{2,1,0:T(8,128)(2,1)}, u32[]{:S(2)}, u32[]{:S(2)}) %collective-permute-start.10) | collective-permute-done | bytes 1048608 | tf_op jit(solution)/shard_map/ppermute | solution.py:485
  52.0 10.0 %shard_map.77 = (f32[4,2,2,128,512]{4,3,2,1,0:T(8,128)}, bf16[4,32,128,128]{3,2,1,0:T(8,128)(2,1)}) custom-call(s32[128]{0:T(128)} %reshape.473.block, bf16[32,16,128]{2,1,0:T(8,128)(2,1)} %pad_maximum_fusion.3.samples, bf16[32,128,128]{2,1,0:T(8,128)(2,1)} %refs_4_.1, bf16[32,128,128]{2,1,0:T(8,128)(2,1)} %collective-permute-done.9.refs_1_.refs_5_, ...), custom_call_target="tpu_custom_call" | custom-call | flops 1342177280 | bytes 6423040 | tf_op jit(solution)/shard_map/pallas_call | solution.py:615
  63.3 5.1 %shard_map.78 = (f32[2,2,128,512]{3,2,1,0:T(8,128)}, bf16[2,2,128,512]{3,2,1,0:T(8,128)(2,1)}, f32[8,128]{1,0:T(8,128)}) custom-call(f32[4,2,2,128,512]{4,3,2,1,0:T(8,128)} %get-tuple-element.90.images, bf16[4,2,2,128,512]{4,3,2,1,0:T(8,128)(2,1)} %copy-done, bf16[4,2,2,128,512]{4,3,2,1,0:T(8,128)(2,1)} %copy-done, bf16[4,2,2,128,512]{4,3,2,1,0:T(8,128)(2,1)} %copy-done, ...), custom_call_target="tpu_custom_call" | custom-call | bytes 12582912 | tf_op jit(solution)/shard_map/pallas_call | solution.py:615
  69.4 2.9 %collective-permute-start.19 = (bf16[1,2,128,512]{3,2,1,0:T(8,128)(2,1)S(1)}, bf16[1,2,128,512]{3,2,1,0:T(8,128)(2,1)S(1)}, u32[]{:S(2)}, u32[]{:S(2)}) collective-permute-start(bf16[1,2,128,512]{3,2,1,0:T(8,128)(2,1)S(1)} %slice.21.refs_4_), channel_id=1, source_target_pairs={{0,8},{4,12},{8,0},{12,4},{1,9},{5,13},{9,1},{13,5},{2,10},{6,14},... | collective-permute-start | bytes 786440 | tf_op jit(solution)/shard_map/ppermute | solution.py:485
  73.8 5.5 %shard_map.79.refs_0_ = bf16[512,128]{1,0:T(8,128)(2,1)} custom-call(s32[128]{0:T(128)} %reshape.472.block, f32[2,2,128,512]{3,2,1,0:T(8,128)} %get-tuple-element.92.picture.refs_16_.refs_4_.refs_17_, bf16[4,2,2,128,512]{4,3,2,1,0:T(8,128)(2,1)} %copy-done, bf16[4,2,2,128,512]{4,3,2,1,0:T(8,128)(2,1)} %copy-done, bf16[4,2,2,128,512]{4,3,2,1,0:T(8,128)(2,1)} %copy-done, ...), custom_call_target="tpu_custom_call" | custom-call | flops 1342177280 | bytes 14156288 | tf_op jit(solution)/shard_map/pallas_call | solution.py:615
  84.3 4.1 %collective-permute-done.14.refs_3_ = bf16[512,128]{1,0:T(8,128)(2,1)S(1)} collective-permute-done((bf16[512,128]{1,0:T(8,128)(2,1)}, bf16[512,128]{1,0:T(8,128)(2,1)S(1)}, u32[]{:S(2)}, u32[]{:S(2)}) %collective-permute-start.14) | collective-permute-done | bytes 131104 | tf_op jit(solution)/shard_map/ppermute | solution.py:485
  88.4 2.6 %collective-permute-done.13.refs_2_ = bf16[512,128]{1,0:T(8,128)(2,1)S(1)} collective-permute-done((bf16[512,128]{1,0:T(8,128)(2,1)}, bf16[512,128]{1,0:T(8,128)(2,1)S(1)}, u32[]{:S(2)}, u32[]{:S(2)}) %collective-permute-start.13) | collective-permute-done | bytes 131104 | tf_op jit(solution)/shard_map/ppermute | solution.py:485
  91.7 9.7 %shard_map.80 = (f32[2,2,128,512]{3,2,1,0:T(8,128)}, bf16[2,2,128,512]{3,2,1,0:T(8,128)(2,1)}, f32[8,128]{1,0:T(8,128)}, f32[8,128]{1,0:T(8,128)}, f32[512,128]{1,0:T(8,128)}) custom-call(s32[128]{0:T(128)} %reshape.472.block, bf16[512,128]{1,0:T(8,128)(2,1)} %shard_map.79.refs_0_, bf16[512,128]{1,0:T(8,128)(2,1)} %copy-done.24, ...), custom_call_target="tpu_custom_call" | custom-call | flops 1342177280 | bytes 16269824 | tf_op jit(solution)/shard_map/pallas_call | solution.py:615
  108.6 5.4 %shard_map.81.refs_0_ = bf16[512,128]{1,0:T(8,128)(2,1)} custom-call(s32[128]{0:T(128)} %reshape.472.block, f32[2,2,128,512]{3,2,1,0:T(8,128)} %get-tuple-element.114.picture.refs_5_.refs_18_, bf16[4,2,2,128,512]{4,3,2,1,0:T(8,128)(2,1)} %copy-done, bf16[4,2,2,128,512]{4,3,2,1,0:T(8,128)(2,1)} %copy-done, bf16[4,2,2,128,512]{4,3,2,1,0:T(8,128)(2,1)} %copy-done, ...), custom_call_target="tpu_custom_call" | custom-call | flops 1342177280 | bytes 14156288 | tf_op jit(solution)/shard_map/pallas_call | solution.py:615
  116.1 4.1 %collective-permute-done.26.refs_3_ = bf16[512,128]{1,0:T(8,128)(2,1)S(1)} collective-permute-done((bf16[512,128]{1,0:T(8,128)(2,1)}, bf16[512,128]{1,0:T(8,128)(2,1)S(1)}, u32[]{:S(2)}, u32[]{:S(2)}) %collective-permute-start.26) | collective-permute-done | bytes 131104 | tf_op jit(solution)/shard_map/ppermute | solution.py:485
  120.2 2.7 %collective-permute-done.25.refs_2_ = bf16[512,128]{1,0:T(8,128)(2,1)S(1)} collective-permute-done((bf16[512,128]{1,0:T(8,128)(2,1)}, bf16[512,128]{1,0:T(8,128)(2,1)S(1)}, u32[]{:S(2)}, u32[]{:S(2)}) %collective-permute-start.25) | collective-permute-done | bytes 131104 | tf_op jit(solution)/shard_map/ppermute | solution.py:485
  123.6 2.0 shard_map.82.refs_12_
  125.6 2.5 %collective-permute-start.29 = (f32[1,8,128]{2,1,0:T(8,128)}, f32[1,8,128]{2,1,0:T(8,128)S(1)}, u32[]{:S(2)}, u32[]{:S(2)}) collective-permute-start(f32[1,8,128]{2,1,0:T(8,128)} %bitcast.46), channel_id=1, source_target_pairs={{0,12},{4,8},{8,4},{12,0},{1,13},{5,9},{9,5},{13,1},{2,14},{6,10},... | collective-permute-start | bytes 12296 | tf_op jit(solution)/shard_map/ppermute | solution.py:485
  128.1 1.9 collective-permute-start.27
  134.0 2.1 %shard_map.83.refs_6_ = bf16[1,2,128,512]{3,2,1,0:T(8,128)(2,1)} custom-call(f32[1,8,128]{2,1,0:T(8,128)} %bitcast.49, f32[1,8,128]{2,1,0:T(8,128)} %copy-done.21, f32[1,8,128]{2,1,0:T(8,128)} %copy-done.20, f32[1,8,128]{2,1,0:T(8,128)} %copy-done.19, f32[2,2,128,512]{3,2,1,0:T(8,128)} %get-tuple-element.92.picture.refs_16_.refs_4_.refs_17_, ...), custom_call_target="tpu_custom_call" | custom-call | tf_op jit(solution)/shard_map/pallas_call | solution.py:773
  139.7 9.6 %shard_map.84.refs_4_.refs_5_ = bf16[2,2,128,512]{3,2,1,0:T(8,128)(2,1)} custom-call(s32[128]{0:T(128)} %reshape.472.block, bf16[512,128]{1,0:T(8,128)(2,1)} %shard_map.81.refs_0_, bf16[512,128]{1,0:T(8,128)(2,1)} %copy-done.9, bf16[512,128]{1,0:T(8,128)(2,1)} %copy-done.8, bf16[512,128]{1,0:T(8,128)(2,1)} %copy-done.7, ...), custom_call_target="tpu_custom_call" | custom-call | flops 1342177280 | bytes 17322496 | tf_op jit(solution)/shard_map/pallas_call | solution.py:615
  150.1 4.1 %collective-permute-done.32.refs_9_ = bf16[1,2,128,512]{3,2,1,0:T(8,128)(2,1)S(1)} collective-permute-done((bf16[1,2,128,512]{3,2,1,0:T(8,128)(2,1)}, bf16[1,2,128,512]{3,2,1,0:T(8,128)(2,1)S(1)}, u32[]{:S(2)}, u32[]{:S(2)}) %collective-permute-start.32) | collective-permute-done | bytes 262176 | tf_op jit(solution)/shard_map/ppermute | solution.py:485
  158.0 25.7 %collective-permute-done.35.refs_15_ = bf16[1,2,128,512]{3,2,1,0:T(8,128)(2,1)S(1)} collective-permute-done((bf16[1,2,128,512]{3,2,1,0:T(8,128)(2,1)S(1)}, bf16[1,2,128,512]{3,2,1,0:T(8,128)(2,1)S(1)}, u32[]{:S(2)}, u32[]{:S(2)}) %collective-permute-start.35) | collective-permute-done | bytes 262176 | tf_op jit(solution)/shard_map/ppermute | solution.py:485
  184.4 6.7 %shard_map.85 = f32[8,2,128,512]{3,2,1,0:T(8,128)} custom-call(s32[8]{0:T(128)} %stack.92.order, f32[1,8,128]{2,1,0:T(8,128)} %bitcast.51, f32[1,8,128]{2,1,0:T(8,128)} %copy-done.21, f32[1,8,128]{2,1,0:T(8,128)} %copy-done.20, f32[1,8,128]{2,1,0:T(8,128)} %copy-done.19, bf16[1,2,128,512]{3,2,1,0:T(8,128)(2,1)} %copy-done.5, ...), custom_call_target="tpu_custom_call" | custom-call | tf_op jit(solution)/shard_map/pallas_call | solution.py:753
  193.5 3.8 %shard_map.86.refs_6_ = f32[8,2,128,512]{3,2,1,0:T(8,128)} custom-call(s32[4]{0:T(128)} %pad_add_fusion.4.order, f32[1,8,128]{2,1,0:T(8,128)} %bitcast.52, f32[1,8,128]{2,1,0:T(8,128)} %copy-done.21, f32[1,8,128]{2,1,0:T(8,128)} %copy-done.20, f32[1,8,128]{2,1,0:T(8,128)} %copy-done.19, bf16[2,2,128,512]{3,2,1,0:T(8,128)(2,1)} %shard_map.84.refs_4_.refs_5_, ...), custom_call_target="tpu_custom_call" | custom-call | tf_op jit(solution)/shard_map/pallas_call | solution.py:753
  197.2 2.7 %shard_map.87.refs_6_ = f32[8,2,128,512]{3,2,1,0:T(8,128)} custom-call(s32[2]{0:T(128)} %pad_add_fusion.3.order, f32[1,8,128]{2,1,0:T(8,128)} %bitcast.53, f32[1,8,128]{2,1,0:T(8,128)} %copy-done.21, f32[1,8,128]{2,1,0:T(8,128)} %copy-done.20, f32[1,8,128]{2,1,0:T(8,128)} %copy-done.19, ...), custom_call_target="tpu_custom_call", output_to_operand_aliasing={{}: (7, {})} | custom-call | tf_op jit(solution)/shard_map/pallas_call | solution.py:753
  202.6 2.7 %shard_map.88 = f32[8,2,128,512]{3,2,1,0:T(8,128)} custom-call(s32[2]{0:T(128)} %pad_add_fusion.2.order, f32[1,8,128]{2,1,0:T(8,128)} %bitcast.54, f32[1,8,128]{2,1,0:T(8,128)} %copy-done.21, f32[1,8,128]{2,1,0:T(8,128)} %copy-done.20, f32[1,8,128]{2,1,0:T(8,128)} %copy-done.19, bf16[2,2,128,512]{3,2,1,0:T(8,128)(2,1)} %copy-done.4, ...), custom_call_target="tpu_custom_call", output_to_operand_aliasing={{}: (7, {})} | custom-call | tf_op jit(solution)/shard_map/pallas_call | solution.py:753
  (182 shorter events, 59.6 us)
Async XLA Ops:
  1.5 7.9 %collective-permute-start.2 = (bf16[2,2,1024]{2,1,0:T(2,128)(2,1)S(1)}, bf16[2,2,1024]{2,1,0:T(2,128)(2,1)S(1)}, u32[]{:S(2)}, u32[]{:S(2)}) collective-permute-start(bf16[2,2,1024]{2,1,0:T(2,128)(2,1)S(1)} %get-tuple-element.160), channel_id=1, source_target_pairs={{0,12},{4,8},{8,4},{12,0},{1,13},{5,9},{9,5},{13,1},{2,14},{6,10},... | collective-permute-start | bytes 24584 | tf_op jit(solution)/shard_map/ppermute | solution.py:485
  11.2 50.8 %all-to-all-start = ((bf16[4,2,2,128,512]{4,3,2,1,0:T(8,128)(2,1)}), bf16[4,2,2,128,512]{4,3,2,1,0:T(8,128)(2,1)S(1)}, u32[]{:S(2)}, u32[]{:S(2)}) async-start(bf16[4,2,2,128,512]{4,3,2,1,0:T(8,128)(2,1)} %bitcast.45), calls=%async_computation | async-start | bytes 4194304 | tf_op jit(solution)/shard_map/all_to_all | solution.py:526
  18.6 26.1 %collective-permute-start.10 = (bf16[32,128,128]{2,1,0:T(8,128)(2,1)S(1)}, bf16[32,128,128]{2,1,0:T(8,128)(2,1)}, u32[]{:S(2)}, u32[]{:S(2)}) collective-permute-start(bf16[32,128,128]{2,1,0:T(8,128)(2,1)S(1)} %copy-done.1), channel_id=1, source_target_pairs={{0,2},{1,3},{2,0},{3,1},{4,6},{5,7},{6,4},{7,5},{8,10},{9,11},{10,... | collective-permute-start | bytes 3145736 | tf_op jit(solution)/shard_map/ppermute | solution.py:485
  19.9 28.9 %collective-permute-start.4 = (bf16[8,16,128]{2,1,0:T(8,128)(2,1)S(1)}, bf16[8,16,128]{2,1,0:T(8,128)(2,1)S(1)}, u32[]{:S(2)}, u32[]{:S(2)}) collective-permute-start(bf16[8,16,128]{2,1,0:T(8,128)(2,1)S(1)} %fusion.14), channel_id=1, source_target_pairs={{0,2},{1,3},{2,0},{3,1},{4,6},{5,7},{6,4},{7,5},{8,10},{9,11},{10,... | collective-permute-start | bytes 98312 | tf_op jit(solution)/shard_map/ppermute | solution.py:485
  21.5 29.9 %collective-permute-start.3 = (bf16[8,16,128]{2,1,0:T(8,128)(2,1)S(1)}, bf16[8,16,128]{2,1,0:T(8,128)(2,1)S(1)}, u32[]{:S(2)}, u32[]{:S(2)}) collective-permute-start(bf16[8,16,128]{2,1,0:T(8,128)(2,1)S(1)} %fusion.14), channel_id=1, source_target_pairs={{0,1},{1,0},{2,3},{3,2},{4,5},{5,4},{6,7},{7,6},{8,9},{9,8},{10,11... | collective-permute-start | bytes 98312 | tf_op jit(solution)/shard_map/ppermute | solution.py:485
  21.7 30.3 %collective-permute-start.9 = (bf16[32,128,128]{2,1,0:T(8,128)(2,1)S(1)}, bf16[32,128,128]{2,1,0:T(8,128)(2,1)}, u32[]{:S(2)}, u32[]{:S(2)}) collective-permute-start(bf16[32,128,128]{2,1,0:T(8,128)(2,1)S(1)} %copy-done.1), channel_id=1, source_target_pairs={{0,1},{1,0},{2,3},{3,2},{4,5},{5,4},{6,7},{7,6},{8,9},{9,8},{10,11... | collective-permute-start | bytes 3145736 | tf_op jit(solution)/shard_map/ppermute | solution.py:485
  44.6 7.4 %collective-permute-start.11 = (bf16[32,128,128]{2,1,0:T(8,128)(2,1)}, bf16[32,128,128]{2,1,0:T(8,128)(2,1)}, u32[]{:S(2)}, u32[]{:S(2)}) collective-permute-start(bf16[32,128,128]{2,1,0:T(8,128)(2,1)} %collective-permute-done.10.refs_2_.refs_6_), channel_id=1, source_target_pairs={{0,1},{1,0},{2,3},{3,2},{4,5},{5,4},{6,7},{7,6},{8,9},{9,8},{10,11... | collective-permute-start | bytes 3145736 | tf_op jit(solution)/shard_map/ppermute | solution.py:485
  69.4 21.6 %collective-permute-start.19 = (bf16[1,2,128,512]{3,2,1,0:T(8,128)(2,1)S(1)}, bf16[1,2,128,512]{3,2,1,0:T(8,128)(2,1)S(1)}, u32[]{:S(2)}, u32[]{:S(2)}) collective-permute-start(bf16[1,2,128,512]{3,2,1,0:T(8,128)(2,1)S(1)} %slice.21.refs_4_), channel_id=1, source_target_pairs={{0,8},{4,12},{8,0},{12,4},{1,9},{5,13},{9,1},{13,5},{2,10},{6,14},... | collective-permute-start | bytes 786440 | tf_op jit(solution)/shard_map/ppermute | solution.py:485
  72.3 18.7 %collective-permute-start.18 = (bf16[1,2,128,512]{3,2,1,0:T(8,128)(2,1)S(1)}, bf16[1,2,128,512]{3,2,1,0:T(8,128)(2,1)S(1)}, u32[]{:S(2)}, u32[]{:S(2)}) collective-permute-start(bf16[1,2,128,512]{3,2,1,0:T(8,128)(2,1)S(1)} %slice.21.refs_4_), channel_id=1, source_target_pairs={{0,4},{4,0},{8,12},{12,8},{1,5},{5,1},{9,13},{13,9},{2,6},{6,2},{1... | collective-permute-start | bytes 786440 | tf_op jit(solution)/shard_map/ppermute | solution.py:485
  83.1 8.0 %collective-permute-start.13 = (bf16[512,128]{1,0:T(8,128)(2,1)}, bf16[512,128]{1,0:T(8,128)(2,1)S(1)}, u32[]{:S(2)}, u32[]{:S(2)}) collective-permute-start(bf16[512,128]{1,0:T(8,128)(2,1)} %shard_map.79.refs_0_), channel_id=1, source_target_pairs={{0,2},{1,3},{2,0},{3,1},{4,6},{5,7},{6,4},{7,5},{8,10},{9,11},{10,... | collective-permute-start | bytes 393224 | tf_op jit(solution)/shard_map/ppermute | solution.py:485
  84.0 7.0 %collective-permute-start.12 = (bf16[512,128]{1,0:T(8,128)(2,1)}, bf16[512,128]{1,0:T(8,128)(2,1)S(1)}, u32[]{:S(2)}, u32[]{:S(2)}) collective-permute-start(bf16[512,128]{1,0:T(8,128)(2,1)} %shard_map.79.refs_0_), channel_id=1, source_target_pairs={{0,1},{1,0},{2,3},{3,2},{4,5},{5,4},{6,7},{7,6},{8,9},{9,8},{10,11... | collective-permute-start | bytes 393224 | tf_op jit(solution)/shard_map/ppermute | solution.py:485
  91.1 14.4 %collective-permute-start.23 = (bf16[1,2,128,512]{3,2,1,0:T(8,128)(2,1)S(1)}, bf16[1,2,128,512]{3,2,1,0:T(8,128)(2,1)S(1)}, u32[]{:S(2)}, u32[]{:S(2)}) collective-permute-start(bf16[1,2,128,512]{3,2,1,0:T(8,128)(2,1)S(1)} %collective-permute-done.19.refs_10_), channel_id=1, source_target_pairs={{0,4},{4,0},{8,12},{12,8},{1,5},{5,1},{9,13},{13,9},{2,6},{6,2},{1... | collective-permute-start | bytes 786440 | tf_op jit(solution)/shard_map/ppermute | solution.py:485
  106.6 29.6 %collective-permute-start.31 = (bf16[1,2,128,512]{3,2,1,0:T(8,128)(2,1)S(1)}, bf16[1,2,128,512]{3,2,1,0:T(8,128)(2,1)S(1)}, u32[]{:S(2)}, u32[]{:S(2)}) collective-permute-start(bf16[1,2,128,512]{3,2,1,0:T(8,128)(2,1)S(1)} %slice.22.refs_5_), channel_id=1, source_target_pairs={{0,8},{4,12},{8,0},{12,4},{1,9},{5,13},{9,1},{13,5},{2,10},{6,14},... | collective-permute-start | bytes 786440 | tf_op jit(solution)/shard_map/ppermute | solution.py:485
  107.2 28.9 %collective-permute-start.30 = (bf16[1,2,128,512]{3,2,1,0:T(8,128)(2,1)S(1)}, bf16[1,2,128,512]{3,2,1,0:T(8,128)(2,1)S(1)}, u32[]{:S(2)}, u32[]{:S(2)}) collective-permute-start(bf16[1,2,128,512]{3,2,1,0:T(8,128)(2,1)S(1)} %slice.22.refs_5_), channel_id=1, source_target_pairs={{0,4},{4,0},{8,12},{12,8},{1,5},{5,1},{9,13},{13,9},{2,6},{6,2},{1... | collective-permute-start | bytes 786440 | tf_op jit(solution)/shard_map/ppermute | solution.py:485
  114.1 6.1 %collective-permute-start.26 = (bf16[512,128]{1,0:T(8,128)(2,1)}, bf16[512,128]{1,0:T(8,128)(2,1)S(1)}, u32[]{:S(2)}, u32[]{:S(2)}) collective-permute-start(bf16[512,128]{1,0:T(8,128)(2,1)} %shard_map.81.refs_0_), channel_id=1, source_target_pairs={{0,3},{1,2},{2,1},{3,0},{4,7},{5,6},{6,5},{7,4},{8,11},{9,10},{10,... | collective-permute-start | bytes 393224 | tf_op jit(solution)/shard_map/ppermute | solution.py:485
  114.2 8.7 %collective-permute-start.25 = (bf16[512,128]{1,0:T(8,128)(2,1)}, bf16[512,128]{1,0:T(8,128)(2,1)S(1)}, u32[]{:S(2)}, u32[]{:S(2)}) collective-permute-start(bf16[512,128]{1,0:T(8,128)(2,1)} %shard_map.81.refs_0_), channel_id=1, source_target_pairs={{0,2},{1,3},{2,0},{3,1},{4,6},{5,7},{6,4},{7,5},{8,10},{9,11},{10,... | collective-permute-start | bytes 393224 | tf_op jit(solution)/shard_map/ppermute | solution.py:485
  115.7 7.2 %collective-permute-start.24 = (bf16[512,128]{1,0:T(8,128)(2,1)}, bf16[512,128]{1,0:T(8,128)(2,1)S(1)}, u32[]{:S(2)}, u32[]{:S(2)}) collective-permute-start(bf16[512,128]{1,0:T(8,128)(2,1)} %shard_map.81.refs_0_), channel_id=1, source_target_pairs={{0,1},{1,0},{2,3},{3,2},{4,5},{5,4},{6,7},{7,6},{8,9},{9,8},{10,11... | collective-permute-start | bytes 393224 | tf_op jit(solution)/shard_map/ppermute | solution.py:485
  136.2 14.0 %collective-permute-start.34 = (bf16[1,2,128,512]{3,2,1,0:T(8,128)(2,1)S(1)}, bf16[1,2,128,512]{3,2,1,0:T(8,128)(2,1)S(1)}, u32[]{:S(2)}, u32[]{:S(2)}) collective-permute-start(bf16[1,2,128,512]{3,2,1,0:T(8,128)(2,1)S(1)} %collective-permute-done.31.refs_11_), channel_id=1, source_target_pairs={{0,4},{4,0},{8,12},{12,8},{1,5},{5,1},{9,13},{13,9},{2,6},{6,2},{1... | collective-permute-start | bytes 786440 | tf_op jit(solution)/shard_map/ppermute | solution.py:485
  136.6 13.5 %collective-permute-start.33 = (bf16[1,2,128,512]{3,2,1,0:T(8,128)(2,1)}, bf16[1,2,128,512]{3,2,1,0:T(8,128)(2,1)S(1)}, u32[]{:S(2)}, u32[]{:S(2)}) collective-permute-start(bf16[1,2,128,512]{3,2,1,0:T(8,128)(2,1)} %shard_map.83.refs_6_), channel_id=1, source_target_pairs={{0,8},{4,12},{8,0},{12,4},{1,9},{5,13},{9,1},{13,5},{2,10},{6,14},... | collective-permute-start | bytes 786440 | tf_op jit(solution)/shard_map/ppermute | solution.py:485
  138.1 16.1 %collective-permute-start.32 = (bf16[1,2,128,512]{3,2,1,0:T(8,128)(2,1)}, bf16[1,2,128,512]{3,2,1,0:T(8,128)(2,1)S(1)}, u32[]{:S(2)}, u32[]{:S(2)}) collective-permute-start(bf16[1,2,128,512]{3,2,1,0:T(8,128)(2,1)} %shard_map.83.refs_6_), channel_id=1, source_target_pairs={{0,4},{4,0},{8,12},{12,8},{1,5},{5,1},{9,13},{13,9},{2,6},{6,2},{1... | collective-permute-start | bytes 786440 | tf_op jit(solution)/shard_map/ppermute | solution.py:485
  154.2 36.9 %collective-permute-start.37 = (bf16[2,2,128,512]{3,2,1,0:T(8,128)(2,1)}, bf16[2,2,128,512]{3,2,1,0:T(8,128)(2,1)S(1)}, u32[]{:S(2)}, u32[]{:S(2)}) collective-permute-start(bf16[2,2,128,512]{3,2,1,0:T(8,128)(2,1)} %shard_map.84.refs_4_.refs_5_), channel_id=1, source_target_pairs={{0,8},{4,12},{8,0},{12,4},{1,9},{5,13},{9,1},{13,5},{2,10},{6,14},... | collective-permute-start | bytes 1572872 | tf_op jit(solution)/shard_map/ppermute | solution.py:485
  155.4 35.8 %collective-permute-start.36 = (bf16[2,2,128,512]{3,2,1,0:T(8,128)(2,1)}, bf16[2,2,128,512]{3,2,1,0:T(8,128)(2,1)S(1)}, u32[]{:S(2)}, u32[]{:S(2)}) collective-permute-start(bf16[2,2,128,512]{3,2,1,0:T(8,128)(2,1)} %shard_map.84.refs_4_.refs_5_), channel_id=1, source_target_pairs={{0,4},{4,0},{8,12},{12,8},{1,5},{5,1},{9,13},{13,9},{2,6},{6,2},{1... | collective-permute-start | bytes 1572872 | tf_op jit(solution)/shard_map/ppermute | solution.py:485
  156.3 27.5 %collective-permute-start.35 = (bf16[1,2,128,512]{3,2,1,0:T(8,128)(2,1)S(1)}, bf16[1,2,128,512]{3,2,1,0:T(8,128)(2,1)S(1)}, u32[]{:S(2)}, u32[]{:S(2)}) collective-permute-start(bf16[1,2,128,512]{3,2,1,0:T(8,128)(2,1)S(1)} %collective-permute-done.33.refs_12_), channel_id=1, source_target_pairs={{0,4},{4,0},{8,12},{12,8},{1,5},{5,1},{9,13},{13,9},{2,6},{6,2},{1... | collective-permute-start | bytes 786440 | tf_op jit(solution)/shard_map/ppermute | solution.py:485
  191.2 10.5 %collective-permute-start.38 = (bf16[2,2,128,512]{3,2,1,0:T(8,128)(2,1)S(1)}, bf16[2,2,128,512]{3,2,1,0:T(8,128)(2,1)S(1)}, u32[]{:S(2)}, u32[]{:S(2)}) collective-permute-start(bf16[2,2,128,512]{3,2,1,0:T(8,128)(2,1)S(1)} %collective-permute-done.37.refs_4_.refs_5_), channel_id=1, source_target_pairs={{0,4},{4,0},{8,12},{12,8},{1,5},{5,1},{9,13},{13,9},{2,6},{6,2},{1... | collective-permute-start | bytes 1572872 | tf_op jit(solution)/shard_map/ppermute | solution.py:485
  (48 other events, 329.1 us)

commit v12 on v11

--- a/solution.py
+++ b/solution.py
@@ -441,18 +441,6 @@
         count = counts[place % len(counts)]
         write(place, pieces[first : first + count])
         first += count
-
-
-def picture_kernel(coils, *refs):
-    infos, (right_side, residual, out, kept) = refs[:coils], refs[coils:]
-
-    @pl.when(pl.program_id(0) == 0)
-    def _():
-        kept_coefficients(infos, kept, [0], False)
-
-    for part in range(2):
-        value = kept[0, 0:1, 0:1] * right_side[0, part] + kept[0, 1:2, 0:1] * residual[0, part]
-        out[0, part] = value.astype(bf16)
 
 
 def whole_block(array):
@@ -766,20 +754,6 @@
                 compiler_params=params,
             )(order, *infos, *inputs)
 
-        def own_picture(infos, right_side, residual, first_plane):
-            count = own_planes - first_plane
-            spec = pl.BlockSpec((1, 2, rows, columns), lambda p: (p + first_plane, 0, 0, 0))
-            small = pl.BlockSpec(infos[0].shape, lambda p: (0, 0, 0))
-            return pl.pallas_call(
-                functools.partial(picture_kernel, coil_count),
-                grid=(count,),
-                in_specs=[small] * len(infos) + [spec] * 2,
-                out_specs=plane_spec,
-                out_shape=shaped((count, 2, rows, columns), bf16),
-                scratch_shapes=[pltpu.VMEM((1, 8, 128), f32)],
-                compiler_params=params,
-            )(*infos, right_side, residual)
-
         def second(samples, facts, infos, right_side, residual, g):
             return back(
                 second_kernel,
@@ -906,10 +880,6 @@
                     out = lax.dynamic_update_slice(out, piece, place)
             return out
 
-        def own_picture(infos, right_side, residual, first_plane):
-            vectors = [right_side[first_plane:], residual[first_plane:]]
-            return mixture(factors_of(infos, False)[0], vectors).astype(bf16)
-
         def second(samples, facts, infos, right_side, residual, g):
             mixed = residual - step_of(facts[0, 0], facts[1, 0]) * applied_to(samples, residual, g)
             return mixture(factors_of(infos, True)[0], [right_side, residual, mixed]).astype(bf16)
@@ -921,48 +891,34 @@
         return [swapped(own, "coil", k) for k in first_bits]
 
     images, turned_weights = measured_images()
-    halves = 2 if own_planes % 2 == 0 else 1
-    early = own_planes // 2 if halves == 2 else 0
-
-    def first_planes(own):
-        return own[:early]
-
     right_side, start_own, norm = start(images, 0)
-    start_sent = sent_by_bits(first_planes(start_own)) if early else []
+    start_sent = sent_by_bits(start_own)
     samples, norm = lax.optimization_barrier((forward(right_side, 0), norm))
     samples = exchanged(samples)
     norms = exchanged(norm)
     samples, norms, start_sent = lax.optimization_barrier((samples, norms, start_sent))
     residual, residual_own, facts, dots, start_total = first(samples, norms, right_side, 0)
     dots = exchanged(dots)
-    start_pieces = completed(first_planes(start_own), start_sent) if early else []
     residual, residual_own, dots, start_pieces = lax.optimization_barrier(
-        (residual, residual_own, dots, start_pieces)
-    )
-    residual_sent = sent_by_bits(first_planes(residual_own)) if early else []
+        (residual, residual_own, dots, completed(start_own, start_sent))
+    )
+    residual_sent = sent_by_bits(residual_own)
     samples = exchanged(forward(residual, 0))
     samples, dots = lax.optimization_barrier((samples, dots))
     info = facts_of(samples, dots, start_total, facts)
     others = exchanged(info[None], "coil")
-    picture_own = own_picture(others, right_side, residual, early)
-    samples, others, picture_own, residual_sent = lax.optimization_barrier(
-        (samples, others, picture_own, residual_sent)
-    )
-    residual_pieces = completed(first_planes(residual_own), residual_sent) if early else []
-    picture_sent = sent_by_bits(picture_own)
+    samples, others, residual_sent = lax.optimization_barrier((samples, others, residual_sent))
     final_own = second(samples, info, others, right_side, residual, 0)
-    final_own, picture_sent, residual_pieces = lax.optimization_barrier(
-        (final_own, picture_sent, residual_pieces)
+    final_own, residual_pieces = lax.optimization_barrier(
+        (final_own, completed(residual_own, residual_sent))
     )
     final_sent = sent_by_bits(final_own)
-    picture_pieces = completed(picture_own, picture_sent)
-    parts = [([start_pieces, residual_pieces], 0)] * (halves - 1) + [([picture_pieces], 0)]
-    picture = assembled(others, parts, range(coil_count))
+
+    picture = assembled(others, [([start_pieces, residual_pieces], 0)], range(coil_count))
     near = [final_own, final_sent[0]] + [None] * (coil_count - 2)
-    out = assembled(others, [([near], h) for h in range(halves)], range(2))
+    out = assembled(others, [([near], 0)], range(2))
     picture, final_sent = lax.optimization_barrier((picture, final_sent))
-    final_pieces = completed(final_own, final_sent)
-    parts = [([final_pieces], h) for h in range(halves)]
+    parts = [([completed(final_own, final_sent)], 0)]
     late = coil_count - 1
     out = assembled(others, parts, range(2, late), out)
     out = assembled(others, parts, [late], out)

time: 206 us -> 192 us (0.932)
  local copies, waits for them, and re-layouts: 13.8 us -> 9.23 us
  Pallas kernels: 65.4 us -> 61 us
  starting transfers between devices: 39.9 us -> 37.4 us
    ppermute x39 -> x36, starting transfers between devices: 36.3 us -> 33.8 us  [swapped(): lax.ppermute(array, axis, [(i, i ^ k) for i in range(lax.axis_size(axis))])]
    pallas_call x4, Pallas kernels: 16 us -> 13.5 us  [assembled(): pl.pallas_call(functools.partial(assemble_kernel, coil_count, list(ks), c...]
    pallas_call x1 -> x0, Pallas kernels: 2.11 us -> none  [own_picture(): pl.pallas_call(functools.partial(picture_kernel, coil_count), grid=(count...]
    ppermute x39 -> x36, waiting for transfers between devices: 74.7 us -> 72.9 us  [swapped(): lax.ppermute(array, axis, [(i, i ^ k) for i in range(lax.axis_size(axis))])]
    unnamed x64 -> x54, local copies, waits for them, and re-layouts: 4.75 us -> 2.95 us
  transfers between devices with their start and end apart: 40 -> 37, of which waited for: 18 -> 19; matrix products, arithmetic and copies ran while one was open for 8% -> 8% of each run, Pallas kernels for 28% -> 28%
where the time goes in v12:
time: 192 us; the launch traced here: 191 us
  waiting for transfers between devices  72.9 us (38%)
  Pallas kernels  61 us (32%)
  starting transfers between devices  37.4 us (19%)
  other arithmetic  9.79 us (5%)
  local copies, waits for them, and re-layouts  9.23 us (5%)
    ppermute x36, waiting for transfers between devices, swapped(): lax.ppermute(array, axis, [(i, i ^ k) for i in range(lax.axis_size(axis))])  72.9 us
    pallas_call x6, Pallas kernels, call(): pl.pallas_call(kernel, grid=grid, in_specs=specs, out_specs=out_specs, ou...  45.4 us
    ppermute x36, starting transfers between devices, swapped(): lax.ppermute(array, axis, [(i, i ^ k) for i in range(lax.axis_size(axis))])  33.8 us
    pallas_call x4, Pallas kernels, assembled(): pl.pallas_call(functools.partial(assemble_kernel, coil_count, list(ks), c...  13.5 us
  transfers between devices with their start and end apart: 37, of which 19 were waited for; matrix products, arithmetic and copies ran while one was open for 8% of the time, Pallas kernels for 28%

profile of v12, /device:TPU:0, one launch (start us, length us, event | category | flops | bytes accessed | tf_op | source)
XLA Modules:
  0.0 191.3 jit_solution(12882261421532051003)
XLA Ops:
  1.5 5.1 %collective-permute-start.2 = (bf16[2,2,1024]{2,1,0:T(2,128)(2,1)S(1)}, bf16[2,2,1024]{2,1,0:T(2,128)(2,1)S(1)}, u32[]{:S(2)}, u32[]{:S(2)}) collective-permute-start(bf16[2,2,1024]{2,1,0:T(2,128)(2,1)S(1)} %get-tuple-element.154), channel_id=1, source_target_pairs={{0,12},{4,8},{8,4},{12,0},{1,13},{5,9},{9,5},{13,1},{2,14},{6,10},... | collective-permute-start | bytes 24584 | tf_op jit(solution)/shard_map/ppermute | solution.py:473
  11.2 3.6 %all-to-all-start = ((bf16[4,2,2,128,512]{4,3,2,1,0:T(8,128)(2,1)}), bf16[4,2,2,128,512]{4,3,2,1,0:T(8,128)(2,1)S(1)}, u32[]{:S(2)}, u32[]{:S(2)}) async-start(bf16[4,2,2,128,512]{4,3,2,1,0:T(8,128)(2,1)} %bitcast.41), calls=%async_computation | async-start | bytes 4194304 | tf_op jit(solution)/shard_map/all_to_all | solution.py:514
  24.8 19.8 %collective-permute-done.10.refs_2_.refs_6_ = bf16[32,128,128]{2,1,0:T(8,128)(2,1)} collective-permute-done((bf16[32,128,128]{2,1,0:T(8,128)(2,1)S(1)}, bf16[32,128,128]{2,1,0:T(8,128)(2,1)}, u32[]{:S(2)}, u32[]{:S(2)}) %collective-permute-start.10) | collective-permute-done | bytes 1048608 | tf_op jit(solution)/shard_map/ppermute | solution.py:473
  51.9 10.0 %shard_map.77 = (f32[4,2,2,128,512]{4,3,2,1,0:T(8,128)}, bf16[4,32,128,128]{3,2,1,0:T(8,128)(2,1)}) custom-call(s32[128]{0:T(128)} %reshape.473.block, bf16[32,16,128]{2,1,0:T(8,128)(2,1)} %pad_maximum_fusion.3.samples, bf16[32,128,128]{2,1,0:T(8,128)(2,1)} %refs_4_.1, bf16[32,128,128]{2,1,0:T(8,128)(2,1)} %collective-permute-done.9.refs_1_.refs_5_, ...), custom_call_target="tpu_custom_call" | custom-call | flops 1342177280 | bytes 6423040 | tf_op jit(solution)/shard_map/pallas_call | solution.py:603
  63.2 5.1 %shard_map.78 = (f32[2,2,128,512]{3,2,1,0:T(8,128)}, bf16[2,2,128,512]{3,2,1,0:T(8,128)(2,1)}, f32[8,128]{1,0:T(8,128)}) custom-call(f32[4,2,2,128,512]{4,3,2,1,0:T(8,128)} %get-tuple-element.87.images, bf16[4,2,2,128,512]{4,3,2,1,0:T(8,128)(2,1)} %copy-done, bf16[4,2,2,128,512]{4,3,2,1,0:T(8,128)(2,1)} %copy-done, bf16[4,2,2,128,512]{4,3,2,1,0:T(8,128)(2,1)} %copy-done, ...), custom_call_target="tpu_custom_call" | custom-call | bytes 12582912 | tf_op jit(solution)/shard_map/pallas_call | solution.py:603
  68.3 2.9 %collective-permute-start.19 = (bf16[2,2,128,512]{3,2,1,0:T(8,128)(2,1)}, bf16[2,2,128,512]{3,2,1,0:T(8,128)(2,1)S(1)}, u32[]{:S(2)}, u32[]{:S(2)}) collective-permute-start(bf16[2,2,128,512]{3,2,1,0:T(8,128)(2,1)} %get-tuple-element.131.refs_4_), channel_id=1, source_target_pairs={{0,8},{4,12},{8,0},{12,4},{1,9},{5,13},{9,1},{13,5},{2,10},{6,14},... | collective-permute-start | bytes 1572872 | tf_op jit(solution)/shard_map/ppermute | solution.py:473
  72.7 5.4 %shard_map.79.refs_0_ = bf16[512,128]{1,0:T(8,128)(2,1)} custom-call(s32[128]{0:T(128)} %reshape.472.block, f32[2,2,128,512]{3,2,1,0:T(8,128)} %get-tuple-element.89.picture.refs_16_.refs_17_, bf16[4,2,2,128,512]{4,3,2,1,0:T(8,128)(2,1)} %copy-done, bf16[4,2,2,128,512]{4,3,2,1,0:T(8,128)(2,1)} %copy-done, bf16[4,2,2,128,512]{4,3,2,1,0:T(8,128)(2,1)} %copy-done, ...), custom_call_target="tpu_custom_call" | custom-call | flops 1342177280 | bytes 14156288 | tf_op jit(solution)/shard_map/pallas_call | solution.py:603
  83.2 4.1 %collective-permute-done.14.refs_3_ = bf16[512,128]{1,0:T(8,128)(2,1)S(1)} collective-permute-done((bf16[512,128]{1,0:T(8,128)(2,1)}, bf16[512,128]{1,0:T(8,128)(2,1)S(1)}, u32[]{:S(2)}, u32[]{:S(2)}) %collective-permute-start.14) | collective-permute-done | bytes 131104 | tf_op jit(solution)/shard_map/ppermute | solution.py:473
  87.3 2.7 %collective-permute-done.13.refs_2_ = bf16[512,128]{1,0:T(8,128)(2,1)S(1)} collective-permute-done((bf16[512,128]{1,0:T(8,128)(2,1)}, bf16[512,128]{1,0:T(8,128)(2,1)S(1)}, u32[]{:S(2)}, u32[]{:S(2)}) %collective-permute-start.13) | collective-permute-done | bytes 131104 | tf_op jit(solution)/shard_map/ppermute | solution.py:473
  90.0 4.9 %collective-permute-done.19.refs_8_ = bf16[2,2,128,512]{3,2,1,0:T(8,128)(2,1)S(1)} collective-permute-done((bf16[2,2,128,512]{3,2,1,0:T(8,128)(2,1)}, bf16[2,2,128,512]{3,2,1,0:T(8,128)(2,1)S(1)}, u32[]{:S(2)}, u32[]{:S(2)}) %collective-permute-start.19) | collective-permute-done | bytes 524320 | tf_op jit(solution)/shard_map/ppermute | solution.py:473
  96.6 9.7 %shard_map.80 = (f32[2,2,128,512]{3,2,1,0:T(8,128)}, bf16[2,2,128,512]{3,2,1,0:T(8,128)(2,1)}, f32[8,128]{1,0:T(8,128)}, f32[8,128]{1,0:T(8,128)}, f32[512,128]{1,0:T(8,128)}) custom-call(s32[128]{0:T(128)} %reshape.472.block, bf16[512,128]{1,0:T(8,128)(2,1)} %shard_map.79.refs_0_, bf16[512,128]{1,0:T(8,128)(2,1)} %copy-done.16, ...), custom_call_target="tpu_custom_call" | custom-call | flops 1342177280 | bytes 16269824 | tf_op jit(solution)/shard_map/pallas_call | solution.py:603
  110.3 2.4 %collective-permute-start.31 = (bf16[2,2,128,512]{3,2,1,0:T(8,128)(2,1)}, bf16[2,2,128,512]{3,2,1,0:T(8,128)(2,1)S(1)}, u32[]{:S(2)}, u32[]{:S(2)}) collective-permute-start(bf16[2,2,128,512]{3,2,1,0:T(8,128)(2,1)} %get-tuple-element.138.refs_5_), channel_id=1, source_target_pairs={{0,8},{4,12},{8,0},{12,4},{1,9},{5,13},{9,1},{13,5},{2,10},{6,14},... | collective-permute-start | bytes 1572872 | tf_op jit(solution)/shard_map/ppermute | solution.py:473
  113.0 5.5 %shard_map.81.refs_0_ = bf16[512,128]{1,0:T(8,128)(2,1)} custom-call(s32[128]{0:T(128)} %reshape.472.block, f32[2,2,128,512]{3,2,1,0:T(8,128)} %get-tuple-element.111.picture.refs_18_, bf16[4,2,2,128,512]{4,3,2,1,0:T(8,128)(2,1)} %copy-done, bf16[4,2,2,128,512]{4,3,2,1,0:T(8,128)(2,1)} %copy-done, bf16[4,2,2,128,512]{4,3,2,1,0:T(8,128)(2,1)} %copy-done, ...), custom_call_target="tpu_custom_call" | custom-call | flops 1342177280 | bytes 14156288 | tf_op jit(solution)/shard_map/pallas_call | solution.py:603
  120.5 4.1 %collective-permute-done.26.refs_3_ = bf16[512,128]{1,0:T(8,128)(2,1)S(1)} collective-permute-done((bf16[512,128]{1,0:T(8,128)(2,1)}, bf16[512,128]{1,0:T(8,128)(2,1)S(1)}, u32[]{:S(2)}, u32[]{:S(2)}) %collective-permute-start.26) | collective-permute-done | bytes 131104 | tf_op jit(solution)/shard_map/ppermute | solution.py:473
  124.5 2.9 %collective-permute-done.25.refs_2_ = bf16[512,128]{1,0:T(8,128)(2,1)S(1)} collective-permute-done((bf16[512,128]{1,0:T(8,128)(2,1)}, bf16[512,128]{1,0:T(8,128)(2,1)S(1)}, u32[]{:S(2)}, u32[]{:S(2)}) %collective-permute-start.25) | collective-permute-done | bytes 131104 | tf_op jit(solution)/shard_map/ppermute | solution.py:473
  130.7 2.3 %collective-permute-start.28 = (f32[1,8,128]{2,1,0:T(8,128)}, f32[1,8,128]{2,1,0:T(8,128)S(1)}, u32[]{:S(2)}, u32[]{:S(2)}) collective-permute-start(f32[1,8,128]{2,1,0:T(8,128)} %bitcast.43), channel_id=1, source_target_pairs={{0,8},{4,12},{8,0},{12,4},{1,9},{5,13},{9,1},{13,5},{2,10},{6,14},... | collective-permute-start | bytes 12296 | tf_op jit(solution)/shard_map/ppermute | solution.py:473
  138.5 9.6 %shard_map.83.refs_4_ = bf16[2,2,128,512]{3,2,1,0:T(8,128)(2,1)} custom-call(s32[128]{0:T(128)} %reshape.472.block, bf16[512,128]{1,0:T(8,128)(2,1)} %shard_map.81.refs_0_, bf16[512,128]{1,0:T(8,128)(2,1)} %copy-done.4, bf16[512,128]{1,0:T(8,128)(2,1)} %copy-done.3, bf16[512,128]{1,0:T(8,128)(2,1)} %copy-done.2, ...), custom_call_target="tpu_custom_call" | custom-call | flops 1342177280 | bytes 17322496 | tf_op jit(solution)/shard_map/pallas_call | solution.py:603
  148.1 2.2 %collective-permute-done.32.refs_11_ = bf16[2,2,128,512]{3,2,1,0:T(8,128)(2,1)S(1)} collective-permute-done((bf16[2,2,128,512]{3,2,1,0:T(8,128)(2,1)S(1)}, bf16[2,2,128,512]{3,2,1,0:T(8,128)(2,1)S(1)}, u32[]{:S(2)}, u32[]{:S(2)}) %collective-permute-start.32) | collective-permute-done | bytes 524320 | tf_op jit(solution)/shard_map/ppermute | solution.py:473
  152.9 6.1 %shard_map.84 = f32[8,2,128,512]{3,2,1,0:T(8,128)} custom-call(s32[4]{0:T(128)} %pad_add_fusion.1.order, f32[1,8,128]{2,1,0:T(8,128)} %bitcast.46, f32[1,8,128]{2,1,0:T(8,128)} %copy-done.19, f32[1,8,128]{2,1,0:T(8,128)} %copy-done.18, f32[1,8,128]{2,1,0:T(8,128)} %copy-done.17, bf16[2,2,128,512]{3,2,1,0:T(8,128)(2,1)} %get-tuple-element.131.refs_4_, ...), custom_call_target="tpu_custom_call" | custom-call | tf_op jit(solution)/shard_map/pallas_call | solution.py:741
  158.9 15.5 %collective-permute-done.34.refs_4_ = bf16[2,2,128,512]{3,2,1,0:T(8,128)(2,1)S(1)} collective-permute-done((bf16[2,2,128,512]{3,2,1,0:T(8,128)(2,1)}, bf16[2,2,128,512]{3,2,1,0:T(8,128)(2,1)S(1)}, u32[]{:S(2)}, u32[]{:S(2)}) %collective-permute-start.34) | collective-permute-done | bytes 524320 | tf_op jit(solution)/shard_map/ppermute | solution.py:473
  175.3 3.3 %shard_map.85.refs_5_ = f32[8,2,128,512]{3,2,1,0:T(8,128)} custom-call(s32[2]{0:T(128)} %pad_add_fusion.3.order, f32[1,8,128]{2,1,0:T(8,128)} %bitcast.47, f32[1,8,128]{2,1,0:T(8,128)} %copy-done.19, f32[1,8,128]{2,1,0:T(8,128)} %copy-done.18, f32[1,8,128]{2,1,0:T(8,128)} %copy-done.17, bf16[2,2,128,512]{3,2,1,0:T(8,128)(2,1)} %shard_map.83.refs_4_, ...), custom_call_target="tpu_custom_call" | custom-call | tf_op jit(solution)/shard_map/pallas_call | solution.py:741
  178.6 2.1 %shard_map.86.refs_5_ = f32[8,2,128,512]{3,2,1,0:T(8,128)} custom-call(s32[1]{0:T(128)} %bitcast.2.order, f32[1,8,128]{2,1,0:T(8,128)} %bitcast.48, f32[1,8,128]{2,1,0:T(8,128)} %copy-done.19, f32[1,8,128]{2,1,0:T(8,128)} %copy-done.18, f32[1,8,128]{2,1,0:T(8,128)} %copy-done.17, ...), custom_call_target="tpu_custom_call", output_to_operand_aliasing={{}: (6, {})} | custom-call | tf_op jit(solution)/shard_map/pallas_call | solution.py:741
  180.7 7.7 %collective-permute-done.35.refs_4_ = bf16[2,2,128,512]{3,2,1,0:T(8,128)(2,1)S(1)} collective-permute-done((bf16[2,2,128,512]{3,2,1,0:T(8,128)(2,1)S(1)}, bf16[2,2,128,512]{3,2,1,0:T(8,128)(2,1)S(1)}, u32[]{:S(2)}, u32[]{:S(2)}) %collective-permute-start.35) | collective-permute-done | bytes 524320 | tf_op jit(solution)/shard_map/ppermute | solution.py:473
  189.2 2.1 %shard_map.87 = f32[8,2,128,512]{3,2,1,0:T(8,128)} custom-call(s32[1]{0:T(128)} %bitcast.3.order, f32[1,8,128]{2,1,0:T(8,128)} %bitcast.49, f32[1,8,128]{2,1,0:T(8,128)} %copy-done.19, f32[1,8,128]{2,1,0:T(8,128)} %copy-done.18, f32[1,8,128]{2,1,0:T(8,128)} %copy-done.17, bf16[2,2,128,512]{3,2,1,0:T(8,128)(2,1)} %copy-done.12, ...), custom_call_target="tpu_custom_call", output_to_operand_aliasing={{}: (6, {})} | custom-call | tf_op jit(solution)/shard_map/pallas_call | solution.py:741
  (161 shorter events, 51.0 us)
Async XLA Ops:
  1.5 7.9 %collective-permute-start.2 = (bf16[2,2,1024]{2,1,0:T(2,128)(2,1)S(1)}, bf16[2,2,1024]{2,1,0:T(2,128)(2,1)S(1)}, u32[]{:S(2)}, u32[]{:S(2)}) collective-permute-start(bf16[2,2,1024]{2,1,0:T(2,128)(2,1)S(1)} %get-tuple-element.154), channel_id=1, source_target_pairs={{0,12},{4,8},{8,4},{12,0},{1,13},{5,9},{9,5},{13,1},{2,14},{6,10},... | collective-permute-start | bytes 24584 | tf_op jit(solution)/shard_map/ppermute | solution.py:473
  11.2 50.7 %all-to-all-start = ((bf16[4,2,2,128,512]{4,3,2,1,0:T(8,128)(2,1)}), bf16[4,2,2,128,512]{4,3,2,1,0:T(8,128)(2,1)S(1)}, u32[]{:S(2)}, u32[]{:S(2)}) async-start(bf16[4,2,2,128,512]{4,3,2,1,0:T(8,128)(2,1)} %bitcast.41), calls=%async_computation | async-start | bytes 4194304 | tf_op jit(solution)/shard_map/all_to_all | solution.py:514
  18.5 26.1 %collective-permute-start.10 = (bf16[32,128,128]{2,1,0:T(8,128)(2,1)S(1)}, bf16[32,128,128]{2,1,0:T(8,128)(2,1)}, u32[]{:S(2)}, u32[]{:S(2)}) collective-permute-start(bf16[32,128,128]{2,1,0:T(8,128)(2,1)S(1)} %copy-done.1), channel_id=1, source_target_pairs={{0,2},{1,3},{2,0},{3,1},{4,6},{5,7},{6,4},{7,5},{8,10},{9,11},{10,... | collective-permute-start | bytes 3145736 | tf_op jit(solution)/shard_map/ppermute | solution.py:473
  19.9 28.9 %collective-permute-start.4 = (bf16[8,16,128]{2,1,0:T(8,128)(2,1)S(1)}, bf16[8,16,128]{2,1,0:T(8,128)(2,1)S(1)}, u32[]{:S(2)}, u32[]{:S(2)}) collective-permute-start(bf16[8,16,128]{2,1,0:T(8,128)(2,1)S(1)} %fusion.14), channel_id=1, source_target_pairs={{0,2},{1,3},{2,0},{3,1},{4,6},{5,7},{6,4},{7,5},{8,10},{9,11},{10,... | collective-permute-start | bytes 98312 | tf_op jit(solution)/shard_map/ppermute | solution.py:473
  21.4 29.8 %collective-permute-start.3 = (bf16[8,16,128]{2,1,0:T(8,128)(2,1)S(1)}, bf16[8,16,128]{2,1,0:T(8,128)(2,1)S(1)}, u32[]{:S(2)}, u32[]{:S(2)}) collective-permute-start(bf16[8,16,128]{2,1,0:T(8,128)(2,1)S(1)} %fusion.14), channel_id=1, source_target_pairs={{0,1},{1,0},{2,3},{3,2},{4,5},{5,4},{6,7},{7,6},{8,9},{9,8},{10,11... | collective-permute-start | bytes 98312 | tf_op jit(solution)/shard_map/ppermute | solution.py:473
  21.7 30.2 %collective-permute-start.9 = (bf16[32,128,128]{2,1,0:T(8,128)(2,1)S(1)}, bf16[32,128,128]{2,1,0:T(8,128)(2,1)}, u32[]{:S(2)}, u32[]{:S(2)}) collective-permute-start(bf16[32,128,128]{2,1,0:T(8,128)(2,1)S(1)} %copy-done.1), channel_id=1, source_target_pairs={{0,1},{1,0},{2,3},{3,2},{4,5},{5,4},{6,7},{7,6},{8,9},{9,8},{10,11... | collective-permute-start | bytes 3145736 | tf_op jit(solution)/shard_map/ppermute | solution.py:473
  44.6 7.3 %collective-permute-start.11 = (bf16[32,128,128]{2,1,0:T(8,128)(2,1)}, bf16[32,128,128]{2,1,0:T(8,128)(2,1)}, u32[]{:S(2)}, u32[]{:S(2)}) collective-permute-start(bf16[32,128,128]{2,1,0:T(8,128)(2,1)} %collective-permute-done.10.refs_2_.refs_6_), channel_id=1, source_target_pairs={{0,1},{1,0},{2,3},{3,2},{4,5},{5,4},{6,7},{7,6},{8,9},{9,8},{10,11... | collective-permute-start | bytes 3145736 | tf_op jit(solution)/shard_map/ppermute | solution.py:473
  68.3 26.6 %collective-permute-start.19 = (bf16[2,2,128,512]{3,2,1,0:T(8,128)(2,1)}, bf16[2,2,128,512]{3,2,1,0:T(8,128)(2,1)S(1)}, u32[]{:S(2)}, u32[]{:S(2)}) collective-permute-start(bf16[2,2,128,512]{3,2,1,0:T(8,128)(2,1)} %get-tuple-element.131.refs_4_), channel_id=1, source_target_pairs={{0,8},{4,12},{8,0},{12,4},{1,9},{5,13},{9,1},{13,5},{2,10},{6,14},... | collective-permute-start | bytes 1572872 | tf_op jit(solution)/shard_map/ppermute | solution.py:473
  71.3 23.7 %collective-permute-start.18 = (bf16[2,2,128,512]{3,2,1,0:T(8,128)(2,1)}, bf16[2,2,128,512]{3,2,1,0:T(8,128)(2,1)S(1)}, u32[]{:S(2)}, u32[]{:S(2)}) collective-permute-start(bf16[2,2,128,512]{3,2,1,0:T(8,128)(2,1)} %get-tuple-element.131.refs_4_), channel_id=1, source_target_pairs={{0,4},{4,0},{8,12},{12,8},{1,5},{5,1},{9,13},{13,9},{2,6},{6,2},{1... | collective-permute-start | bytes 1572872 | tf_op jit(solution)/shard_map/ppermute | solution.py:473
  81.3 6.0 %collective-permute-start.14 = (bf16[512,128]{1,0:T(8,128)(2,1)}, bf16[512,128]{1,0:T(8,128)(2,1)S(1)}, u32[]{:S(2)}, u32[]{:S(2)}) collective-permute-start(bf16[512,128]{1,0:T(8,128)(2,1)} %shard_map.79.refs_0_), channel_id=1, source_target_pairs={{0,3},{1,2},{2,1},{3,0},{4,7},{5,6},{6,5},{7,4},{8,11},{9,10},{10,... | collective-permute-start | bytes 393224 | tf_op jit(solution)/shard_map/ppermute | solution.py:473
  82.0 8.0 %collective-permute-start.13 = (bf16[512,128]{1,0:T(8,128)(2,1)}, bf16[512,128]{1,0:T(8,128)(2,1)S(1)}, u32[]{:S(2)}, u32[]{:S(2)}) collective-permute-start(bf16[512,128]{1,0:T(8,128)(2,1)} %shard_map.79.refs_0_), channel_id=1, source_target_pairs={{0,2},{1,3},{2,0},{3,1},{4,6},{5,7},{6,4},{7,5},{8,10},{9,11},{10,... | collective-permute-start | bytes 393224 | tf_op jit(solution)/shard_map/ppermute | solution.py:473
  83.0 7.0 %collective-permute-start.12 = (bf16[512,128]{1,0:T(8,128)(2,1)}, bf16[512,128]{1,0:T(8,128)(2,1)S(1)}, u32[]{:S(2)}, u32[]{:S(2)}) collective-permute-start(bf16[512,128]{1,0:T(8,128)(2,1)} %shard_map.79.refs_0_), channel_id=1, source_target_pairs={{0,1},{1,0},{2,3},{3,2},{4,5},{5,4},{6,7},{7,6},{8,9},{9,8},{10,11... | collective-permute-start | bytes 393224 | tf_op jit(solution)/shard_map/ppermute | solution.py:473
  95.0 15.4 %collective-permute-start.23 = (bf16[2,2,128,512]{3,2,1,0:T(8,128)(2,1)S(1)}, bf16[2,2,128,512]{3,2,1,0:T(8,128)(2,1)S(1)}, u32[]{:S(2)}, u32[]{:S(2)}) collective-permute-start(bf16[2,2,128,512]{3,2,1,0:T(8,128)(2,1)S(1)} %collective-permute-done.19.refs_8_), channel_id=1, source_target_pairs={{0,4},{4,0},{8,12},{12,8},{1,5},{5,1},{9,13},{13,9},{2,6},{6,2},{1... | collective-permute-start | bytes 1572872 | tf_op jit(solution)/shard_map/ppermute | solution.py:473
  110.3 27.1 %collective-permute-start.31 = (bf16[2,2,128,512]{3,2,1,0:T(8,128)(2,1)}, bf16[2,2,128,512]{3,2,1,0:T(8,128)(2,1)S(1)}, u32[]{:S(2)}, u32[]{:S(2)}) collective-permute-start(bf16[2,2,128,512]{3,2,1,0:T(8,128)(2,1)} %get-tuple-element.138.refs_5_), channel_id=1, source_target_pairs={{0,8},{4,12},{8,0},{12,4},{1,9},{5,13},{9,1},{13,5},{2,10},{6,14},... | collective-permute-start | bytes 1572872 | tf_op jit(solution)/shard_map/ppermute | solution.py:473
  112.8 24.6 %collective-permute-start.30 = (bf16[2,2,128,512]{3,2,1,0:T(8,128)(2,1)}, bf16[2,2,128,512]{3,2,1,0:T(8,128)(2,1)S(1)}, u32[]{:S(2)}, u32[]{:S(2)}) collective-permute-start(bf16[2,2,128,512]{3,2,1,0:T(8,128)(2,1)} %get-tuple-element.138.refs_5_), channel_id=1, source_target_pairs={{0,4},{4,0},{8,12},{12,8},{1,5},{5,1},{9,13},{13,9},{2,6},{6,2},{1... | collective-permute-start | bytes 1572872 | tf_op jit(solution)/shard_map/ppermute | solution.py:473
  118.5 6.0 %collective-permute-start.26 = (bf16[512,128]{1,0:T(8,128)(2,1)}, bf16[512,128]{1,0:T(8,128)(2,1)S(1)}, u32[]{:S(2)}, u32[]{:S(2)}) collective-permute-start(bf16[512,128]{1,0:T(8,128)(2,1)} %shard_map.81.refs_0_), channel_id=1, source_target_pairs={{0,3},{1,2},{2,1},{3,0},{4,7},{5,6},{6,5},{7,4},{8,11},{9,10},{10,... | collective-permute-start | bytes 393224 | tf_op jit(solution)/shard_map/ppermute | solution.py:473
  118.8 8.6 %collective-permute-start.25 = (bf16[512,128]{1,0:T(8,128)(2,1)}, bf16[512,128]{1,0:T(8,128)(2,1)S(1)}, u32[]{:S(2)}, u32[]{:S(2)}) collective-permute-start(bf16[512,128]{1,0:T(8,128)(2,1)} %shard_map.81.refs_0_), channel_id=1, source_target_pairs={{0,2},{1,3},{2,0},{3,1},{4,6},{5,7},{6,4},{7,5},{8,10},{9,11},{10,... | collective-permute-start | bytes 393224 | tf_op jit(solution)/shard_map/ppermute | solution.py:473
  120.2 7.2 %collective-permute-start.24 = (bf16[512,128]{1,0:T(8,128)(2,1)}, bf16[512,128]{1,0:T(8,128)(2,1)S(1)}, u32[]{:S(2)}, u32[]{:S(2)}) collective-permute-start(bf16[512,128]{1,0:T(8,128)(2,1)} %shard_map.81.refs_0_), channel_id=1, source_target_pairs={{0,1},{1,0},{2,3},{3,2},{4,5},{5,4},{6,7},{7,6},{8,9},{9,8},{10,11... | collective-permute-start | bytes 393224 | tf_op jit(solution)/shard_map/ppermute | solution.py:473
  130.2 6.0 %collective-permute-start.29 = (f32[1,8,128]{2,1,0:T(8,128)}, f32[1,8,128]{2,1,0:T(8,128)S(1)}, u32[]{:S(2)}, u32[]{:S(2)}) collective-permute-start(f32[1,8,128]{2,1,0:T(8,128)} %bitcast.42), channel_id=1, source_target_pairs={{0,12},{4,8},{8,4},{12,0},{1,13},{5,9},{9,5},{13,1},{2,14},{6,10},... | collective-permute-start | bytes 12296 | tf_op jit(solution)/shard_map/ppermute | solution.py:473
  130.7 5.5 %collective-permute-start.28 = (f32[1,8,128]{2,1,0:T(8,128)}, f32[1,8,128]{2,1,0:T(8,128)S(1)}, u32[]{:S(2)}, u32[]{:S(2)}) collective-permute-start(f32[1,8,128]{2,1,0:T(8,128)} %bitcast.43), channel_id=1, source_target_pairs={{0,8},{4,12},{8,0},{12,4},{1,9},{5,13},{9,1},{13,5},{2,10},{6,14},... | collective-permute-start | bytes 12296 | tf_op jit(solution)/shard_map/ppermute | solution.py:473
  137.4 13.0 %collective-permute-start.32 = (bf16[2,2,128,512]{3,2,1,0:T(8,128)(2,1)S(1)}, bf16[2,2,128,512]{3,2,1,0:T(8,128)(2,1)S(1)}, u32[]{:S(2)}, u32[]{:S(2)}) collective-permute-start(bf16[2,2,128,512]{3,2,1,0:T(8,128)(2,1)S(1)} %collective-permute-done.31.refs_9_), channel_id=1, source_target_pairs={{0,4},{4,0},{8,12},{12,8},{1,5},{5,1},{9,13},{13,9},{2,6},{6,2},{1... | collective-permute-start | bytes 1572872 | tf_op jit(solution)/shard_map/ppermute | solution.py:473
  150.4 24.1 %collective-permute-start.34 = (bf16[2,2,128,512]{3,2,1,0:T(8,128)(2,1)}, bf16[2,2,128,512]{3,2,1,0:T(8,128)(2,1)S(1)}, u32[]{:S(2)}, u32[]{:S(2)}) collective-permute-start(bf16[2,2,128,512]{3,2,1,0:T(8,128)(2,1)} %shard_map.83.refs_4_), channel_id=1, source_target_pairs={{0,8},{4,12},{8,0},{12,4},{1,9},{5,13},{9,1},{13,5},{2,10},{6,14},... | collective-permute-start | bytes 1572872 | tf_op jit(solution)/shard_map/ppermute | solution.py:473
  150.9 23.6 %collective-permute-start.33 = (bf16[2,2,128,512]{3,2,1,0:T(8,128)(2,1)}, bf16[2,2,128,512]{3,2,1,0:T(8,128)(2,1)S(1)}, u32[]{:S(2)}, u32[]{:S(2)}) collective-permute-start(bf16[2,2,128,512]{3,2,1,0:T(8,128)(2,1)} %shard_map.83.refs_4_), channel_id=1, source_target_pairs={{0,4},{4,0},{8,12},{12,8},{1,5},{5,1},{9,13},{13,9},{2,6},{6,2},{1... | collective-permute-start | bytes 1572872 | tf_op jit(solution)/shard_map/ppermute | solution.py:473
  174.5 13.9 %collective-permute-start.35 = (bf16[2,2,128,512]{3,2,1,0:T(8,128)(2,1)S(1)}, bf16[2,2,128,512]{3,2,1,0:T(8,128)(2,1)S(1)}, u32[]{:S(2)}, u32[]{:S(2)}) collective-permute-start(bf16[2,2,128,512]{3,2,1,0:T(8,128)(2,1)S(1)} %collective-permute-done.34.refs_4_), channel_id=1, source_target_pairs={{0,4},{4,0},{8,12},{12,8},{1,5},{5,1},{9,13},{13,9},{2,6},{6,2},{1... | collective-permute-start | bytes 1572872 | tf_op jit(solution)/shard_map/ppermute | solution.py:473
  (40 other events, 231.9 us)

commit v13 on v12

--- a/solution.py
+++ b/solution.py
@@ -634,7 +634,7 @@
             )
 
         def start(images, g):
-            chunk = 64
+            chunk = rows
             spec = pl.BlockSpec((1, 2, chunk, columns), lambda p, r: (p, 0, r, 0))
             images_spec = pl.BlockSpec(
                 (coil_count, 1, 2, chunk, columns),

time: 192 us -> 191 us (level)
  no operation moved by 1% of the time
where the time goes in v13:
time: 191 us; the launch traced here: 190 us
  waiting for transfers between devices  72.9 us (38%)
  Pallas kernels  59.9 us (31%)
  starting transfers between devices  37.4 us (20%)
  other arithmetic  9.79 us (5%)
  local copies, waits for them, and re-layouts  9.23 us (5%)
    ppermute x36, waiting for transfers between devices, swapped(): lax.ppermute(array, axis, [(i, i ^ k) for i in range(lax.axis_size(axis))])  72.9 us
    pallas_call x6, Pallas kernels, call(): pl.pallas_call(kernel, grid=grid, in_specs=specs, out_specs=out_specs, ou...  44.3 us
    ppermute x36, starting transfers between devices, swapped(): lax.ppermute(array, axis, [(i, i ^ k) for i in range(lax.axis_size(axis))])  33.8 us
    pallas_call x4, Pallas kernels, assembled(): pl.pallas_call(functools.partial(assemble_kernel, coil_count, list(ks), c...  13.5 us
  transfers between devices with their start and end apart: 37, of which 19 were waited for; matrix products, arithmetic and copies ran while one was open for 8% of the time, Pallas kernels for 28%

profile of v13, /device:TPU:0, one launch (start us, length us, event | category | flops | bytes accessed | tf_op | source)
XLA Modules:
  0.0 190.2 jit_solution(14710889782735866800)
XLA Ops:
  1.5 5.1 %collective-permute-start.2 = (bf16[2,2,1024]{2,1,0:T(2,128)(2,1)S(1)}, bf16[2,2,1024]{2,1,0:T(2,128)(2,1)S(1)}, u32[]{:S(2)}, u32[]{:S(2)}) collective-permute-start(bf16[2,2,1024]{2,1,0:T(2,128)(2,1)S(1)} %get-tuple-element.154), channel_id=1, source_target_pairs={{0,12},{4,8},{8,4},{12,0},{1,13},{5,9},{9,5},{13,1},{2,14},{6,10},... | collective-permute-start | bytes 24584 | tf_op jit(solution)/shard_map/ppermute | solution.py:473
  11.2 3.6 %all-to-all-start = ((bf16[4,2,2,128,512]{4,3,2,1,0:T(8,128)(2,1)}), bf16[4,2,2,128,512]{4,3,2,1,0:T(8,128)(2,1)S(1)}, u32[]{:S(2)}, u32[]{:S(2)}) async-start(bf16[4,2,2,128,512]{4,3,2,1,0:T(8,128)(2,1)} %bitcast.41), calls=%async_computation | async-start | bytes 4194304 | tf_op jit(solution)/shard_map/all_to_all | solution.py:514
  24.8 19.8 %collective-permute-done.10.refs_2_.refs_6_ = bf16[32,128,128]{2,1,0:T(8,128)(2,1)} collective-permute-done((bf16[32,128,128]{2,1,0:T(8,128)(2,1)S(1)}, bf16[32,128,128]{2,1,0:T(8,128)(2,1)}, u32[]{:S(2)}, u32[]{:S(2)}) %collective-permute-start.10) | collective-permute-done | bytes 1048608 | tf_op jit(solution)/shard_map/ppermute | solution.py:473
  51.9 10.0 %shard_map.77 = (f32[4,2,2,128,512]{4,3,2,1,0:T(8,128)}, bf16[4,32,128,128]{3,2,1,0:T(8,128)(2,1)}) custom-call(s32[128]{0:T(128)} %reshape.473.block, bf16[32,16,128]{2,1,0:T(8,128)(2,1)} %pad_maximum_fusion.3.samples, bf16[32,128,128]{2,1,0:T(8,128)(2,1)} %refs_4_.1, bf16[32,128,128]{2,1,0:T(8,128)(2,1)} %collective-permute-done.9.refs_1_.refs_5_, ...), custom_call_target="tpu_custom_call" | custom-call | flops 1342177280 | bytes 6423040 | tf_op jit(solution)/shard_map/pallas_call | solution.py:603
  63.2 4.1 %shard_map.78 = (f32[2,2,128,512]{3,2,1,0:T(8,128)}, bf16[2,2,128,512]{3,2,1,0:T(8,128)(2,1)}, f32[8,128]{1,0:T(8,128)}) custom-call(f32[4,2,2,128,512]{4,3,2,1,0:T(8,128)} %get-tuple-element.87.images, bf16[4,2,2,128,512]{4,3,2,1,0:T(8,128)(2,1)} %copy-done, bf16[4,2,2,128,512]{4,3,2,1,0:T(8,128)(2,1)} %copy-done, bf16[4,2,2,128,512]{4,3,2,1,0:T(8,128)(2,1)} %copy-done, ...), custom_call_target="tpu_custom_call" | custom-call | bytes 12582912 | tf_op jit(solution)/shard_map/pallas_call | solution.py:603
  67.3 3.0 %collective-permute-start.19 = (bf16[2,2,128,512]{3,2,1,0:T(8,128)(2,1)}, bf16[2,2,128,512]{3,2,1,0:T(8,128)(2,1)S(1)}, u32[]{:S(2)}, u32[]{:S(2)}) collective-permute-start(bf16[2,2,128,512]{3,2,1,0:T(8,128)(2,1)} %get-tuple-element.131.refs_4_), channel_id=1, source_target_pairs={{0,8},{4,12},{8,0},{12,4},{1,9},{5,13},{9,1},{13,5},{2,10},{6,14},... | collective-permute-start | bytes 1572872 | tf_op jit(solution)/shard_map/ppermute | solution.py:473
  71.7 5.4 %shard_map.79.refs_0_ = bf16[512,128]{1,0:T(8,128)(2,1)} custom-call(s32[128]{0:T(128)} %reshape.472.block, f32[2,2,128,512]{3,2,1,0:T(8,128)} %get-tuple-element.89.picture.refs_16_.refs_17_, bf16[4,2,2,128,512]{4,3,2,1,0:T(8,128)(2,1)} %copy-done, bf16[4,2,2,128,512]{4,3,2,1,0:T(8,128)(2,1)} %copy-done, bf16[4,2,2,128,512]{4,3,2,1,0:T(8,128)(2,1)} %copy-done, ...), custom_call_target="tpu_custom_call" | custom-call | flops 1342177280 | bytes 14156288 | tf_op jit(solution)/shard_map/pallas_call | solution.py:603
  82.1 4.1 %collective-permute-done.14.refs_3_ = bf16[512,128]{1,0:T(8,128)(2,1)S(1)} collective-permute-done((bf16[512,128]{1,0:T(8,128)(2,1)}, bf16[512,128]{1,0:T(8,128)(2,1)S(1)}, u32[]{:S(2)}, u32[]{:S(2)}) %collective-permute-start.14) | collective-permute-done | bytes 131104 | tf_op jit(solution)/shard_map/ppermute | solution.py:473
  86.3 2.7 %collective-permute-done.13.refs_2_ = bf16[512,128]{1,0:T(8,128)(2,1)S(1)} collective-permute-done((bf16[512,128]{1,0:T(8,128)(2,1)}, bf16[512,128]{1,0:T(8,128)(2,1)S(1)}, u32[]{:S(2)}, u32[]{:S(2)}) %collective-permute-start.13) | collective-permute-done | bytes 131104 | tf_op jit(solution)/shard_map/ppermute | solution.py:473
  88.9 4.9 %collective-permute-done.19.refs_8_ = bf16[2,2,128,512]{3,2,1,0:T(8,128)(2,1)S(1)} collective-permute-done((bf16[2,2,128,512]{3,2,1,0:T(8,128)(2,1)}, bf16[2,2,128,512]{3,2,1,0:T(8,128)(2,1)S(1)}, u32[]{:S(2)}, u32[]{:S(2)}) %collective-permute-start.19) | collective-permute-done | bytes 524320 | tf_op jit(solution)/shard_map/ppermute | solution.py:473
  95.6 9.7 %shard_map.80 = (f32[2,2,128,512]{3,2,1,0:T(8,128)}, bf16[2,2,128,512]{3,2,1,0:T(8,128)(2,1)}, f32[8,128]{1,0:T(8,128)}, f32[8,128]{1,0:T(8,128)}, f32[512,128]{1,0:T(8,128)}) custom-call(s32[128]{0:T(128)} %reshape.472.block, bf16[512,128]{1,0:T(8,128)(2,1)} %shard_map.79.refs_0_, bf16[512,128]{1,0:T(8,128)(2,1)} %copy-done.16, ...), custom_call_target="tpu_custom_call" | custom-call | flops 1342177280 | bytes 16269824 | tf_op jit(solution)/shard_map/pallas_call | solution.py:603
  109.3 2.4 %collective-permute-start.31 = (bf16[2,2,128,512]{3,2,1,0:T(8,128)(2,1)}, bf16[2,2,128,512]{3,2,1,0:T(8,128)(2,1)S(1)}, u32[]{:S(2)}, u32[]{:S(2)}) collective-permute-start(bf16[2,2,128,512]{3,2,1,0:T(8,128)(2,1)} %get-tuple-element.138.refs_5_), channel_id=1, source_target_pairs={{0,8},{4,12},{8,0},{12,4},{1,9},{5,13},{9,1},{13,5},{2,10},{6,14},... | collective-permute-start | bytes 1572872 | tf_op jit(solution)/shard_map/ppermute | solution.py:473
  112.0 5.5 %shard_map.81.refs_0_ = bf16[512,128]{1,0:T(8,128)(2,1)} custom-call(s32[128]{0:T(128)} %reshape.472.block, f32[2,2,128,512]{3,2,1,0:T(8,128)} %get-tuple-element.111.picture.refs_18_, bf16[4,2,2,128,512]{4,3,2,1,0:T(8,128)(2,1)} %copy-done, bf16[4,2,2,128,512]{4,3,2,1,0:T(8,128)(2,1)} %copy-done, bf16[4,2,2,128,512]{4,3,2,1,0:T(8,128)(2,1)} %copy-done, ...), custom_call_target="tpu_custom_call" | custom-call | flops 1342177280 | bytes 14156288 | tf_op jit(solution)/shard_map/pallas_call | solution.py:603
  119.4 4.1 %collective-permute-done.26.refs_3_ = bf16[512,128]{1,0:T(8,128)(2,1)S(1)} collective-permute-done((bf16[512,128]{1,0:T(8,128)(2,1)}, bf16[512,128]{1,0:T(8,128)(2,1)S(1)}, u32[]{:S(2)}, u32[]{:S(2)}) %collective-permute-start.26) | collective-permute-done | bytes 131104 | tf_op jit(solution)/shard_map/ppermute | solution.py:473
  123.5 2.9 %collective-permute-done.25.refs_2_ = bf16[512,128]{1,0:T(8,128)(2,1)S(1)} collective-permute-done((bf16[512,128]{1,0:T(8,128)(2,1)}, bf16[512,128]{1,0:T(8,128)(2,1)S(1)}, u32[]{:S(2)}, u32[]{:S(2)}) %collective-permute-start.25) | collective-permute-done | bytes 131104 | tf_op jit(solution)/shard_map/ppermute | solution.py:473
  129.7 2.3 %collective-permute-start.28 = (f32[1,8,128]{2,1,0:T(8,128)}, f32[1,8,128]{2,1,0:T(8,128)S(1)}, u32[]{:S(2)}, u32[]{:S(2)}) collective-permute-start(f32[1,8,128]{2,1,0:T(8,128)} %bitcast.43), channel_id=1, source_target_pairs={{0,8},{4,12},{8,0},{12,4},{1,9},{5,13},{9,1},{13,5},{2,10},{6,14},... | collective-permute-start | bytes 12296 | tf_op jit(solution)/shard_map/ppermute | solution.py:473
  137.4 9.7 %shard_map.83.refs_4_ = bf16[2,2,128,512]{3,2,1,0:T(8,128)(2,1)} custom-call(s32[128]{0:T(128)} %reshape.472.block, bf16[512,128]{1,0:T(8,128)(2,1)} %shard_map.81.refs_0_, bf16[512,128]{1,0:T(8,128)(2,1)} %copy-done.4, bf16[512,128]{1,0:T(8,128)(2,1)} %copy-done.3, bf16[512,128]{1,0:T(8,128)(2,1)} %copy-done.2, ...), custom_call_target="tpu_custom_call" | custom-call | flops 1342177280 | bytes 17322496 | tf_op jit(solution)/shard_map/pallas_call | solution.py:603
  147.1 2.2 %collective-permute-done.32.refs_11_ = bf16[2,2,128,512]{3,2,1,0:T(8,128)(2,1)S(1)} collective-permute-done((bf16[2,2,128,512]{3,2,1,0:T(8,128)(2,1)S(1)}, bf16[2,2,128,512]{3,2,1,0:T(8,128)(2,1)S(1)}, u32[]{:S(2)}, u32[]{:S(2)}) %collective-permute-start.32) | collective-permute-done | bytes 524320 | tf_op jit(solution)/shard_map/ppermute | solution.py:473
  151.8 6.1 %shard_map.84 = f32[8,2,128,512]{3,2,1,0:T(8,128)} custom-call(s32[4]{0:T(128)} %pad_add_fusion.1.order, f32[1,8,128]{2,1,0:T(8,128)} %bitcast.46, f32[1,8,128]{2,1,0:T(8,128)} %copy-done.19, f32[1,8,128]{2,1,0:T(8,128)} %copy-done.18, f32[1,8,128]{2,1,0:T(8,128)} %copy-done.17, bf16[2,2,128,512]{3,2,1,0:T(8,128)(2,1)} %get-tuple-element.131.refs_4_, ...), custom_call_target="tpu_custom_call" | custom-call | tf_op jit(solution)/shard_map/pallas_call | solution.py:741
  157.9 15.5 %collective-permute-done.34.refs_4_ = bf16[2,2,128,512]{3,2,1,0:T(8,128)(2,1)S(1)} collective-permute-done((bf16[2,2,128,512]{3,2,1,0:T(8,128)(2,1)}, bf16[2,2,128,512]{3,2,1,0:T(8,128)(2,1)S(1)}, u32[]{:S(2)}, u32[]{:S(2)}) %collective-permute-start.34) | collective-permute-done | bytes 524320 | tf_op jit(solution)/shard_map/ppermute | solution.py:473
  174.2 3.3 %shard_map.85.refs_5_ = f32[8,2,128,512]{3,2,1,0:T(8,128)} custom-call(s32[2]{0:T(128)} %pad_add_fusion.3.order, f32[1,8,128]{2,1,0:T(8,128)} %bitcast.47, f32[1,8,128]{2,1,0:T(8,128)} %copy-done.19, f32[1,8,128]{2,1,0:T(8,128)} %copy-done.18, f32[1,8,128]{2,1,0:T(8,128)} %copy-done.17, bf16[2,2,128,512]{3,2,1,0:T(8,128)(2,1)} %shard_map.83.refs_4_, ...), custom_call_target="tpu_custom_call" | custom-call | tf_op jit(solution)/shard_map/pallas_call | solution.py:741
  177.5 2.1 %shard_map.86.refs_5_ = f32[8,2,128,512]{3,2,1,0:T(8,128)} custom-call(s32[1]{0:T(128)} %bitcast.2.order, f32[1,8,128]{2,1,0:T(8,128)} %bitcast.48, f32[1,8,128]{2,1,0:T(8,128)} %copy-done.19, f32[1,8,128]{2,1,0:T(8,128)} %copy-done.18, f32[1,8,128]{2,1,0:T(8,128)} %copy-done.17, ...), custom_call_target="tpu_custom_call", output_to_operand_aliasing={{}: (6, {})} | custom-call | tf_op jit(solution)/shard_map/pallas_call | solution.py:741
  179.6 7.7 %collective-permute-done.35.refs_4_ = bf16[2,2,128,512]{3,2,1,0:T(8,128)(2,1)S(1)} collective-permute-done((bf16[2,2,128,512]{3,2,1,0:T(8,128)(2,1)S(1)}, bf16[2,2,128,512]{3,2,1,0:T(8,128)(2,1)S(1)}, u32[]{:S(2)}, u32[]{:S(2)}) %collective-permute-start.35) | collective-permute-done | bytes 524320 | tf_op jit(solution)/shard_map/ppermute | solution.py:473
  188.1 2.1 %shard_map.87 = f32[8,2,128,512]{3,2,1,0:T(8,128)} custom-call(s32[1]{0:T(128)} %bitcast.3.order, f32[1,8,128]{2,1,0:T(8,128)} %bitcast.49, f32[1,8,128]{2,1,0:T(8,128)} %copy-done.19, f32[1,8,128]{2,1,0:T(8,128)} %copy-done.18, f32[1,8,128]{2,1,0:T(8,128)} %copy-done.17, bf16[2,2,128,512]{3,2,1,0:T(8,128)(2,1)} %copy-done.12, ...), custom_call_target="tpu_custom_call", output_to_operand_aliasing={{}: (6, {})} | custom-call | tf_op jit(solution)/shard_map/pallas_call | solution.py:741
  (161 shorter events, 51.0 us)
Async XLA Ops:
  1.5 7.9 %collective-permute-start.2 = (bf16[2,2,1024]{2,1,0:T(2,128)(2,1)S(1)}, bf16[2,2,1024]{2,1,0:T(2,128)(2,1)S(1)}, u32[]{:S(2)}, u32[]{:S(2)}) collective-permute-start(bf16[2,2,1024]{2,1,0:T(2,128)(2,1)S(1)} %get-tuple-element.154), channel_id=1, source_target_pairs={{0,12},{4,8},{8,4},{12,0},{1,13},{5,9},{9,5},{13,1},{2,14},{6,10},... | collective-permute-start | bytes 24584 | tf_op jit(solution)/shard_map/ppermute | solution.py:473
  11.2 50.7 %all-to-all-start = ((bf16[4,2,2,128,512]{4,3,2,1,0:T(8,128)(2,1)}), bf16[4,2,2,128,512]{4,3,2,1,0:T(8,128)(2,1)S(1)}, u32[]{:S(2)}, u32[]{:S(2)}) async-start(bf16[4,2,2,128,512]{4,3,2,1,0:T(8,128)(2,1)} %bitcast.41), calls=%async_computation | async-start | bytes 4194304 | tf_op jit(solution)/shard_map/all_to_all | solution.py:514
  18.5 26.1 %collective-permute-start.10 = (bf16[32,128,128]{2,1,0:T(8,128)(2,1)S(1)}, bf16[32,128,128]{2,1,0:T(8,128)(2,1)}, u32[]{:S(2)}, u32[]{:S(2)}) collective-permute-start(bf16[32,128,128]{2,1,0:T(8,128)(2,1)S(1)} %copy-done.1), channel_id=1, source_target_pairs={{0,2},{1,3},{2,0},{3,1},{4,6},{5,7},{6,4},{7,5},{8,10},{9,11},{10,... | collective-permute-start | bytes 3145736 | tf_op jit(solution)/shard_map/ppermute | solution.py:473
  19.9 28.9 %collective-permute-start.4 = (bf16[8,16,128]{2,1,0:T(8,128)(2,1)S(1)}, bf16[8,16,128]{2,1,0:T(8,128)(2,1)S(1)}, u32[]{:S(2)}, u32[]{:S(2)}) collective-permute-start(bf16[8,16,128]{2,1,0:T(8,128)(2,1)S(1)} %fusion.14), channel_id=1, source_target_pairs={{0,2},{1,3},{2,0},{3,1},{4,6},{5,7},{6,4},{7,5},{8,10},{9,11},{10,... | collective-permute-start | bytes 98312 | tf_op jit(solution)/shard_map/ppermute | solution.py:473
  21.4 29.8 %collective-permute-start.3 = (bf16[8,16,128]{2,1,0:T(8,128)(2,1)S(1)}, bf16[8,16,128]{2,1,0:T(8,128)(2,1)S(1)}, u32[]{:S(2)}, u32[]{:S(2)}) collective-permute-start(bf16[8,16,128]{2,1,0:T(8,128)(2,1)S(1)} %fusion.14), channel_id=1, source_target_pairs={{0,1},{1,0},{2,3},{3,2},{4,5},{5,4},{6,7},{7,6},{8,9},{9,8},{10,11... | collective-permute-start | bytes 98312 | tf_op jit(solution)/shard_map/ppermute | solution.py:473
  21.7 30.2 %collective-permute-start.9 = (bf16[32,128,128]{2,1,0:T(8,128)(2,1)S(1)}, bf16[32,128,128]{2,1,0:T(8,128)(2,1)}, u32[]{:S(2)}, u32[]{:S(2)}) collective-permute-start(bf16[32,128,128]{2,1,0:T(8,128)(2,1)S(1)} %copy-done.1), channel_id=1, source_target_pairs={{0,1},{1,0},{2,3},{3,2},{4,5},{5,4},{6,7},{7,6},{8,9},{9,8},{10,11... | collective-permute-start | bytes 3145736 | tf_op jit(solution)/shard_map/ppermute | solution.py:473
  44.6 7.3 %collective-permute-start.11 = (bf16[32,128,128]{2,1,0:T(8,128)(2,1)}, bf16[32,128,128]{2,1,0:T(8,128)(2,1)}, u32[]{:S(2)}, u32[]{:S(2)}) collective-permute-start(bf16[32,128,128]{2,1,0:T(8,128)(2,1)} %collective-permute-done.10.refs_2_.refs_6_), channel_id=1, source_target_pairs={{0,1},{1,0},{2,3},{3,2},{4,5},{5,4},{6,7},{7,6},{8,9},{9,8},{10,11... | collective-permute-start | bytes 3145736 | tf_op jit(solution)/shard_map/ppermute | solution.py:473
  67.3 26.6 %collective-permute-start.19 = (bf16[2,2,128,512]{3,2,1,0:T(8,128)(2,1)}, bf16[2,2,128,512]{3,2,1,0:T(8,128)(2,1)S(1)}, u32[]{:S(2)}, u32[]{:S(2)}) collective-permute-start(bf16[2,2,128,512]{3,2,1,0:T(8,128)(2,1)} %get-tuple-element.131.refs_4_), channel_id=1, source_target_pairs={{0,8},{4,12},{8,0},{12,4},{1,9},{5,13},{9,1},{13,5},{2,10},{6,14},... | collective-permute-start | bytes 1572872 | tf_op jit(solution)/shard_map/ppermute | solution.py:473
  70.2 23.7 %collective-permute-start.18 = (bf16[2,2,128,512]{3,2,1,0:T(8,128)(2,1)}, bf16[2,2,128,512]{3,2,1,0:T(8,128)(2,1)S(1)}, u32[]{:S(2)}, u32[]{:S(2)}) collective-permute-start(bf16[2,2,128,512]{3,2,1,0:T(8,128)(2,1)} %get-tuple-element.131.refs_4_), channel_id=1, source_target_pairs={{0,4},{4,0},{8,12},{12,8},{1,5},{5,1},{9,13},{13,9},{2,6},{6,2},{1... | collective-permute-start | bytes 1572872 | tf_op jit(solution)/shard_map/ppermute | solution.py:473
  80.3 6.0 %collective-permute-start.14 = (bf16[512,128]{1,0:T(8,128)(2,1)}, bf16[512,128]{1,0:T(8,128)(2,1)S(1)}, u32[]{:S(2)}, u32[]{:S(2)}) collective-permute-start(bf16[512,128]{1,0:T(8,128)(2,1)} %shard_map.79.refs_0_), channel_id=1, source_target_pairs={{0,3},{1,2},{2,1},{3,0},{4,7},{5,6},{6,5},{7,4},{8,11},{9,10},{10,... | collective-permute-start | bytes 393224 | tf_op jit(solution)/shard_map/ppermute | solution.py:473
  80.9 8.0 %collective-permute-start.13 = (bf16[512,128]{1,0:T(8,128)(2,1)}, bf16[512,128]{1,0:T(8,128)(2,1)S(1)}, u32[]{:S(2)}, u32[]{:S(2)}) collective-permute-start(bf16[512,128]{1,0:T(8,128)(2,1)} %shard_map.79.refs_0_), channel_id=1, source_target_pairs={{0,2},{1,3},{2,0},{3,1},{4,6},{5,7},{6,4},{7,5},{8,10},{9,11},{10,... | collective-permute-start | bytes 393224 | tf_op jit(solution)/shard_map/ppermute | solution.py:473
  81.9 7.0 %collective-permute-start.12 = (bf16[512,128]{1,0:T(8,128)(2,1)}, bf16[512,128]{1,0:T(8,128)(2,1)S(1)}, u32[]{:S(2)}, u32[]{:S(2)}) collective-permute-start(bf16[512,128]{1,0:T(8,128)(2,1)} %shard_map.79.refs_0_), channel_id=1, source_target_pairs={{0,1},{1,0},{2,3},{3,2},{4,5},{5,4},{6,7},{7,6},{8,9},{9,8},{10,11... | collective-permute-start | bytes 393224 | tf_op jit(solution)/shard_map/ppermute | solution.py:473
  93.9 15.4 %collective-permute-start.23 = (bf16[2,2,128,512]{3,2,1,0:T(8,128)(2,1)S(1)}, bf16[2,2,128,512]{3,2,1,0:T(8,128)(2,1)S(1)}, u32[]{:S(2)}, u32[]{:S(2)}) collective-permute-start(bf16[2,2,128,512]{3,2,1,0:T(8,128)(2,1)S(1)} %collective-permute-done.19.refs_8_), channel_id=1, source_target_pairs={{0,4},{4,0},{8,12},{12,8},{1,5},{5,1},{9,13},{13,9},{2,6},{6,2},{1... | collective-permute-start | bytes 1572872 | tf_op jit(solution)/shard_map/ppermute | solution.py:473
  109.3 27.1 %collective-permute-start.31 = (bf16[2,2,128,512]{3,2,1,0:T(8,128)(2,1)}, bf16[2,2,128,512]{3,2,1,0:T(8,128)(2,1)S(1)}, u32[]{:S(2)}, u32[]{:S(2)}) collective-permute-start(bf16[2,2,128,512]{3,2,1,0:T(8,128)(2,1)} %get-tuple-element.138.refs_5_), channel_id=1, source_target_pairs={{0,8},{4,12},{8,0},{12,4},{1,9},{5,13},{9,1},{13,5},{2,10},{6,14},... | collective-permute-start | bytes 1572872 | tf_op jit(solution)/shard_map/ppermute | solution.py:473
  111.7 24.6 %collective-permute-start.30 = (bf16[2,2,128,512]{3,2,1,0:T(8,128)(2,1)}, bf16[2,2,128,512]{3,2,1,0:T(8,128)(2,1)S(1)}, u32[]{:S(2)}, u32[]{:S(2)}) collective-permute-start(bf16[2,2,128,512]{3,2,1,0:T(8,128)(2,1)} %get-tuple-element.138.refs_5_), channel_id=1, source_target_pairs={{0,4},{4,0},{8,12},{12,8},{1,5},{5,1},{9,13},{13,9},{2,6},{6,2},{1... | collective-permute-start | bytes 1572872 | tf_op jit(solution)/shard_map/ppermute | solution.py:473
  117.5 6.0 %collective-permute-start.26 = (bf16[512,128]{1,0:T(8,128)(2,1)}, bf16[512,128]{1,0:T(8,128)(2,1)S(1)}, u32[]{:S(2)}, u32[]{:S(2)}) collective-permute-start(bf16[512,128]{1,0:T(8,128)(2,1)} %shard_map.81.refs_0_), channel_id=1, source_target_pairs={{0,3},{1,2},{2,1},{3,0},{4,7},{5,6},{6,5},{7,4},{8,11},{9,10},{10,... | collective-permute-start | bytes 393224 | tf_op jit(solution)/shard_map/ppermute | solution.py:473
  117.6 8.8 %collective-permute-start.25 = (bf16[512,128]{1,0:T(8,128)(2,1)}, bf16[512,128]{1,0:T(8,128)(2,1)S(1)}, u32[]{:S(2)}, u32[]{:S(2)}) collective-permute-start(bf16[512,128]{1,0:T(8,128)(2,1)} %shard_map.81.refs_0_), channel_id=1, source_target_pairs={{0,2},{1,3},{2,0},{3,1},{4,6},{5,7},{6,4},{7,5},{8,10},{9,11},{10,... | collective-permute-start | bytes 393224 | tf_op jit(solution)/shard_map/ppermute | solution.py:473
  119.2 7.2 %collective-permute-start.24 = (bf16[512,128]{1,0:T(8,128)(2,1)}, bf16[512,128]{1,0:T(8,128)(2,1)S(1)}, u32[]{:S(2)}, u32[]{:S(2)}) collective-permute-start(bf16[512,128]{1,0:T(8,128)(2,1)} %shard_map.81.refs_0_), channel_id=1, source_target_pairs={{0,1},{1,0},{2,3},{3,2},{4,5},{5,4},{6,7},{7,6},{8,9},{9,8},{10,11... | collective-permute-start | bytes 393224 | tf_op jit(solution)/shard_map/ppermute | solution.py:473
  129.1 6.0 %collective-permute-start.29 = (f32[1,8,128]{2,1,0:T(8,128)}, f32[1,8,128]{2,1,0:T(8,128)S(1)}, u32[]{:S(2)}, u32[]{:S(2)}) collective-permute-start(f32[1,8,128]{2,1,0:T(8,128)} %bitcast.42), channel_id=1, source_target_pairs={{0,12},{4,8},{8,4},{12,0},{1,13},{5,9},{9,5},{13,1},{2,14},{6,10},... | collective-permute-start | bytes 12296 | tf_op jit(solution)/shard_map/ppermute | solution.py:473
  129.7 5.5 %collective-permute-start.28 = (f32[1,8,128]{2,1,0:T(8,128)}, f32[1,8,128]{2,1,0:T(8,128)S(1)}, u32[]{:S(2)}, u32[]{:S(2)}) collective-permute-start(f32[1,8,128]{2,1,0:T(8,128)} %bitcast.43), channel_id=1, source_target_pairs={{0,8},{4,12},{8,0},{12,4},{1,9},{5,13},{9,1},{13,5},{2,10},{6,14},... | collective-permute-start | bytes 12296 | tf_op jit(solution)/shard_map/ppermute | solution.py:473
  136.4 13.0 %collective-permute-start.32 = (bf16[2,2,128,512]{3,2,1,0:T(8,128)(2,1)S(1)}, bf16[2,2,128,512]{3,2,1,0:T(8,128)(2,1)S(1)}, u32[]{:S(2)}, u32[]{:S(2)}) collective-permute-start(bf16[2,2,128,512]{3,2,1,0:T(8,128)(2,1)S(1)} %collective-permute-done.31.refs_9_), channel_id=1, source_target_pairs={{0,4},{4,0},{8,12},{12,8},{1,5},{5,1},{9,13},{13,9},{2,6},{6,2},{1... | collective-permute-start | bytes 1572872 | tf_op jit(solution)/shard_map/ppermute | solution.py:473
  149.3 24.1 %collective-permute-start.34 = (bf16[2,2,128,512]{3,2,1,0:T(8,128)(2,1)}, bf16[2,2,128,512]{3,2,1,0:T(8,128)(2,1)S(1)}, u32[]{:S(2)}, u32[]{:S(2)}) collective-permute-start(bf16[2,2,128,512]{3,2,1,0:T(8,128)(2,1)} %shard_map.83.refs_4_), channel_id=1, source_target_pairs={{0,8},{4,12},{8,0},{12,4},{1,9},{5,13},{9,1},{13,5},{2,10},{6,14},... | collective-permute-start | bytes 1572872 | tf_op jit(solution)/shard_map/ppermute | solution.py:473
  149.8 23.6 %collective-permute-start.33 = (bf16[2,2,128,512]{3,2,1,0:T(8,128)(2,1)}, bf16[2,2,128,512]{3,2,1,0:T(8,128)(2,1)S(1)}, u32[]{:S(2)}, u32[]{:S(2)}) collective-permute-start(bf16[2,2,128,512]{3,2,1,0:T(8,128)(2,1)} %shard_map.83.refs_4_), channel_id=1, source_target_pairs={{0,4},{4,0},{8,12},{12,8},{1,5},{5,1},{9,13},{13,9},{2,6},{6,2},{1... | collective-permute-start | bytes 1572872 | tf_op jit(solution)/shard_map/ppermute | solution.py:473
  173.4 13.9 %collective-permute-start.35 = (bf16[2,2,128,512]{3,2,1,0:T(8,128)(2,1)S(1)}, bf16[2,2,128,512]{3,2,1,0:T(8,128)(2,1)S(1)}, u32[]{:S(2)}, u32[]{:S(2)}) collective-permute-start(bf16[2,2,128,512]{3,2,1,0:T(8,128)(2,1)S(1)} %collective-permute-done.34.refs_4_), channel_id=1, source_target_pairs={{0,4},{4,0},{8,12},{12,8},{1,5},{5,1},{9,13},{13,9},{2,6},{6,2},{1... | collective-permute-start | bytes 1572872 | tf_op jit(solution)/shard_map/ppermute | solution.py:473
  (40 other events, 231.9 us)
